TPU v7x, 32 devices: a whole 2x2x4 slice. The times are simulated.
32 devices in a mesh: dp: 2 (over y), seq: 4 (over x, core), heads: 4 (over z).
Axes of the slice: x: 2, y: 2, z: 4, core: 2. Of those that a mesh axis runs over, the one named last changes fastest.
Arguments:
- tokens: bfloat16 [2, 2, 2048, 2048], P(None, 'dp', ('seq', 'heads')), may hold values from -6 to 6
- lengths: int32 [2, 2, 3], P(None, 'dp'), may hold values from 1 to 2046, as said below
- attention_gain: bfloat16 [2048], P(('dp', 'seq', 'heads')), may hold values from 0.5 to 1.5
- query_weight: bfloat16 [2048, 1792], P(('dp', 'seq'), 'heads'), may hold values from -0.125 to 0.125
- key_value_matrix: bfloat16 [2048, 896], P(('dp', 'seq', 'heads')), may hold values from -0.125 to 0.125
- per_head_gains: bfloat16 [128], P(('dp', 'seq', 'heads')), may hold values from 0.5 to 1.5
- output_weight: bfloat16 [1792, 2048], P(None, ('dp', 'seq', 'heads')), may hold values from -2 to 2
- feed_gain: bfloat16 [2048], P(('dp', 'seq', 'heads')), may hold values from 0.5 to 1.5
- gate_weight: bfloat16 [2048, 6400], P(('dp', 'seq'), 'heads'), may hold values from -0.125 to 0.125
- up_weight: bfloat16 [2048, 6400], P(('dp', 'seq'), 'heads'), may hold values from -0.125 to 0.125
- down_weight: bfloat16 [6400, 2048], P('heads', ('dp', 'seq')), may hold values from -0.078125 to 0.078125
- cotangent: bfloat16 [2, 2, 2048, 2048], P(None, 'dp', ('seq', 'heads')), may hold values from -6 to 6
Outputs:
- layer_out: bfloat16 [2, 2, 2048, 2048], P(None, 'dp', ('seq', 'heads'))
- tokens_grad: float32 [2, 2, 2048, 2048], P(None, 'dp', ('seq', 'heads'))
- attention_gain_grad: float32 [2048], P(('dp', 'seq', 'heads'))
- query_weight_grad: float32 [2048, 1792], P(('dp', 'seq'), 'heads')
- key_value_weight_grad: float32 [2048, 896], P(('dp', 'seq', 'heads'))
- head_gains_grad: float32 [128], P(('dp', 'seq', 'heads'))
- output_weight_grad: float32 [1792, 2048], P(None, ('dp', 'seq', 'heads'))
- feed_gain_grad: float32 [2048], P(('dp', 'seq', 'heads'))
- gate_weight_grad: float32 [2048, 6400], P(('dp', 'seq'), 'heads')
- up_weight_grad: float32 [2048, 6400], P(('dp', 'seq'), 'heads')
- down_weight_grad: float32 [6400, 2048], P('heads', ('dp', 'seq'))
Inputs may be any that keep to these rules, and one draw needn't show every extreme that they name: In each packed row the 3 lengths sum to 2048; the first and the last are shorter than 512, the middle one holds the rest.
All inputs are finite; a program needn't handle non-finite values.
Results may differ from a plain program's by a relative error of at most 0.019.
Values may be sent and summed in bfloat16 or wider, within the bound.
No kernel may reach another device: no remote copies, remote signals or barrier semaphores. Data moves between devices by JAX's collectives and lax.ppermute only.
A program may use at most 320 MiB of HBM per device.

v0:
```python
import math

import jax
import jax.numpy as jnp
from jax import lax
from jax.sharding import PartitionSpec as P

QUERY_HEADS = 28
KEY_VALUE_HEADS = 7
HEAD_SIZE = 64


EPSILON = 1e-06
SCORE_SCALE = 0.125
MASKED = -1e30


def apply_norm(values, gain):
    return values * lax.rsqrt(jnp.mean(values * values, axis=-1, keepdims=True) + EPSILON) * gain


def rotary_tables(places):
    half_width = HEAD_SIZE // 2
    freqs = jnp.exp(
        jnp.arange(half_width, dtype=jnp.float32) * (-2.0 * math.log(10000.0) / HEAD_SIZE)
    )
    angles = places.astype(jnp.float32)[:, None] * freqs[None, :]
    cosine_table = jnp.cos(angles)
    sine_table = jnp.sin(angles)
    return (
        jnp.concatenate([cosine_table, cosine_table], -1)[:, None, :],
        jnp.concatenate([sine_table, sine_table], -1)[:, None, :],
    )


def apply_rotary(values, cosine_table, sine_table):
    half_width = values.shape[-1] // 2
    turned = jnp.concatenate([-values[..., half_width:], values[..., :half_width]], -1)
    return values * cosine_table + turned * sine_table


def documents(sizes, total):
    finish = jnp.cumsum(sizes)
    begin = finish - sizes
    places = jnp.arange(total, dtype=jnp.int32)
    segment = jnp.sum((places[:, None] >= finish[None, :]).astype(jnp.int32), axis=1)
    member = segment[:, None] == jnp.arange(sizes.shape[0], dtype=jnp.int32)[None, :]
    offset = places - jnp.sum(jnp.where(member, begin[None, :], 0), axis=1)
    return (segment, offset)


def by_transpose(left, right):
    return lax.dot_general(
        left, right, (((1,), (1,)), ((), ())), preferred_element_type=jnp.float32
    )


def transpose_by(left, right):
    return lax.dot_general(
        left, right, (((0,), (0,)), ((), ())), preferred_element_type=jnp.float32
    )


def on_device(
    tokens,
    lengths,
    attention_gain,
    query_weight,
    key_value_matrix,
    per_head_gains,
    output_weight,
    feed_gain,
    gate_weight,
    up_weight,
    down_weight,
    cotangent,
):

    def one_batch(batch_index, current):
        (
            query_full,
            gate_full,
            up_full,
            down_full,
            key_value_full,
            output_full,
            attention_low,
            feed_low,
            head_low,
        ) = current
        residual_in = tokens[batch_index, 0].astype(jnp.float32)
        out_cotangent = cotangent[batch_index, 0]
        attention_scale = attention_low.astype(jnp.float32)
        feed_scale = feed_low.astype(jnp.float32)
        head_scale = head_low.astype(jnp.float32)
        query_scale = head_scale[:HEAD_SIZE]
        key_scale = head_scale[HEAD_SIZE:]
        seq_index = lax.axis_index("seq")
        head_index = lax.axis_index("heads")
        rows_here = residual_in.shape[0]
        rows_per_block = rows_here * lax.axis_size("heads")
        sequence_length = rows_per_block * lax.axis_size("seq")
        local_heads = query_full.shape[1] // HEAD_SIZE
        key_total_width = KEY_VALUE_HEADS * HEAD_SIZE
        heads_per_group = QUERY_HEADS // KEY_VALUE_HEADS
        document_owner = (
            head_index * local_heads + jnp.arange(local_heads, dtype=jnp.int32)
        ) // heads_per_group
        choose_float = (
            document_owner[:, None] == jnp.arange(KEY_VALUE_HEADS, dtype=jnp.int32)[None, :]
        ).astype(jnp.float32)
        select_low = choose_float.astype(jnp.bfloat16)
        segment, offset = documents(lengths[batch_index, 0], sequence_length)
        first_row = seq_index * rows_per_block
        segment_here = lax.dynamic_slice_in_dim(segment, first_row, rows_per_block)
        offset_here = lax.dynamic_slice_in_dim(offset, first_row, rows_per_block)
        query_places = first_row + jnp.arange(rows_per_block, dtype=jnp.int32)
        key_places = jnp.arange(sequence_length, dtype=jnp.int32)
        allowed = (segment_here[:, None] == segment[None, :]) & (
            key_places[None, :] <= query_places[:, None]
        )
        cosine_table, sine_table = rotary_tables(offset_here)

        def prepare(query_part, key_part, query_gain, key_gain):
            query_heads = query_part.reshape(query_part.shape[0], -1, HEAD_SIZE)
            key_heads = key_part.reshape(key_part.shape[0], -1, HEAD_SIZE)
            return (
                apply_rotary(apply_norm(query_heads, query_gain), cosine_table, sine_table),
                apply_rotary(apply_norm(key_heads, key_gain), cosine_table, sine_table),
            )

        normed_rows = apply_norm(residual_in, attention_scale).astype(jnp.bfloat16)
        normed_block = lax.all_gather(normed_rows, "heads", axis=0, tiled=True)
        query_raw = jnp.dot(normed_block, query_full, preferred_element_type=jnp.float32)
        key_value_projected = jnp.dot(
            normed_block, key_value_full, preferred_element_type=jnp.float32
        )
        queries_float, keys_float = prepare(
            query_raw, key_value_projected[:, :key_total_width], query_scale, key_scale
        )
        query_rows = queries_float.astype(jnp.bfloat16)
        pair_low = jnp.concatenate(
            [
                keys_float.reshape(rows_per_block, key_total_width),
                key_value_projected[:, key_total_width:],
            ],
            axis=1,
        ).astype(jnp.bfloat16)
        every_pair = lax.all_gather(pair_low, "seq", axis=0, tiled=True)
        key_wide = jnp.einsum(
            "kch,jc->kjh",
            every_pair[:, :key_total_width].reshape(sequence_length, KEY_VALUE_HEADS, HEAD_SIZE),
            select_low,
            preferred_element_type=jnp.float32,
        ).astype(jnp.bfloat16)
        value_wide = jnp.einsum(
            "kch,jc->kjh",
            every_pair[:, key_total_width:].reshape(sequence_length, KEY_VALUE_HEADS, HEAD_SIZE),
            select_low,
            preferred_element_type=jnp.float32,
        ).astype(jnp.bfloat16)

        def score_block():
            scores = (
                jnp.einsum("qjh,kjh->jqk", query_rows, key_wide, preferred_element_type=jnp.float32)
                * SCORE_SCALE
            )
            return jnp.where(allowed[None], scores, MASKED)

        scores = score_block()
        peak = jnp.max(scores, axis=-1, keepdims=True)
        expo = jnp.exp(scores - peak)
        total = jnp.sum(expo, axis=-1, keepdims=True)
        log_total = peak + jnp.log(total)
        probs_low = (expo / total).astype(jnp.bfloat16)
        mixed = jnp.einsum(
            "jqk,kjh->qjh", probs_low, value_wide, preferred_element_type=jnp.float32
        ).astype(jnp.bfloat16)
        mixed = mixed.reshape(rows_per_block, local_heads * HEAD_SIZE)
        mixed_rows = lax.all_to_all(mixed, "heads", split_axis=0, concat_axis=1, tiled=True)
        hidden_in = residual_in + jnp.dot(
            mixed_rows, output_full, preferred_element_type=jnp.float32
        )
        feed_rows = apply_norm(hidden_in, feed_scale).astype(jnp.bfloat16)
        feed_block = lax.all_gather(feed_rows, "heads", axis=0, tiled=True)
        gate_pre = jnp.dot(feed_block, gate_full, preferred_element_type=jnp.float32)
        up_pre = jnp.dot(feed_block, up_full, preferred_element_type=jnp.float32)
        activated = (jax.nn.silu(gate_pre) * up_pre).astype(jnp.bfloat16)
        feed_out = lax.psum_scatter(
            jnp.dot(activated, down_full, preferred_element_type=jnp.float32).astype(jnp.bfloat16),
            "heads",
            scatter_dimension=0,
            tiled=True,
        ).astype(jnp.float32)
        layer_rows = (hidden_in + feed_out).astype(jnp.bfloat16)
        grad_block = lax.all_gather(out_cotangent, "heads", axis=0, tiled=True)
        d_activated = by_transpose(grad_block, down_full)
        grad_down = transpose_by(activated, grad_block)
        unused, pull_gate = jax.vjp(
            lambda gate_part, up_part: jax.nn.silu(gate_part) * up_part, gate_pre, up_pre
        )
        d_gate_float, d_up_float = pull_gate(d_activated)
        d_gate = d_gate_float.astype(jnp.bfloat16)
        d_up = d_up_float.astype(jnp.bfloat16)
        grad_gate = transpose_by(feed_block, d_gate)
        grad_up = transpose_by(feed_block, d_up)
        d_feed = lax.psum_scatter(
            (by_transpose(d_gate, gate_full) + by_transpose(d_up, up_full)).astype(jnp.bfloat16),
            "heads",
            scatter_dimension=0,
            tiled=True,
        ).astype(jnp.float32)
        unused, pull_feed = jax.vjp(apply_norm, hidden_in, feed_scale)
        d_hidden_norm, grad_feed_gain = pull_feed(d_feed)
        d_hidden = out_cotangent.astype(jnp.float32) + d_hidden_norm
        d_attended = d_hidden.astype(jnp.bfloat16)
        grad_output = transpose_by(mixed_rows, d_attended)
        d_mixed_rows = by_transpose(d_attended, output_full).astype(jnp.bfloat16)
        d_mixed = lax.all_to_all(d_mixed_rows, "heads", split_axis=1, concat_axis=0, tiled=True)
        d_mixed = d_mixed.reshape(rows_per_block, local_heads, HEAD_SIZE)
        scores = score_block()
        probs = jnp.exp(scores - log_total)
        probs_low = probs.astype(jnp.bfloat16)
        d_probs = jnp.einsum(
            "qjh,kjh->jqk", d_mixed, value_wide, preferred_element_type=jnp.float32
        )
        balance = jnp.sum(probs * d_probs, axis=-1, keepdims=True)
        d_scores = (probs * (d_probs - balance)).astype(jnp.bfloat16)
        query_gradient = (
            jnp.einsum("jqk,kjh->qjh", d_scores, key_wide, preferred_element_type=jnp.float32)
            * SCORE_SCALE
        )
        d_key_wide = (
            jnp.einsum("jqk,qjh->kjh", d_scores, query_rows, preferred_element_type=jnp.float32)
            * SCORE_SCALE
        )
        d_value_wide = jnp.einsum(
            "jqk,qjh->kjh", probs_low, d_mixed, preferred_element_type=jnp.float32
        )
        d_key_all = jnp.einsum(
            "kjh,jc->kch", d_key_wide, choose_float, precision=lax.Precision.HIGHEST
        )
        d_value_all = jnp.einsum(
            "kjh,jc->kch", d_value_wide, choose_float, precision=lax.Precision.HIGHEST
        )
        d_pair_all = jnp.concatenate(
            [
                d_key_all.reshape(sequence_length, key_total_width),
                d_value_all.reshape(sequence_length, key_total_width),
            ],
            axis=1,
        )
        pair_gradient = lax.psum_scatter(
            d_pair_all.astype(jnp.bfloat16), "seq", scatter_dimension=0, tiled=True
        ).astype(jnp.float32)
        unused, pull_heads = jax.vjp(
            prepare, query_raw, key_value_projected[:, :key_total_width], query_scale, key_scale
        )
        d_query_float, d_key_float, grad_query_gain, grad_key_gain = pull_heads(
            (
                query_gradient,
                pair_gradient[:, :key_total_width].reshape(
                    rows_per_block, KEY_VALUE_HEADS, HEAD_SIZE
                ),
            )
        )
        d_query_raw = d_query_float.astype(jnp.bfloat16)
        d_key_value_raw = jnp.concatenate(
            [d_key_float, pair_gradient[:, key_total_width:]], axis=1
        ).astype(jnp.bfloat16)
        grad_query = transpose_by(normed_block, d_query_raw)
        grad_key_value = transpose_by(normed_block, d_key_value_raw)
        d_normed = lax.psum_scatter(
            (
                by_transpose(d_query_raw, query_full)
                + by_transpose(d_key_value_raw, key_value_full)
            ).astype(jnp.bfloat16),
            "heads",
            scatter_dimension=0,
            tiled=True,
        ).astype(jnp.float32)
        unused, pull_input = jax.vjp(apply_norm, residual_in, attention_scale)
        d_input_norm, grad_attention_gain = pull_input(d_normed)
        input_rows = d_hidden + d_input_norm
        grad_heads = jnp.concatenate([grad_query_gain, grad_key_gain], axis=0)
        grads = (
            grad_query,
            grad_gate,
            grad_up,
            grad_down,
            grad_key_value,
            grad_output,
            grad_attention_gain,
            grad_feed_gain,
            grad_heads,
        )
        return (layer_rows, input_rows, grads)

    layer_list = []
    input_list = []
    running = None
    for batch_index in range(tokens.shape[0]):
        layer_set = (
            lax.all_gather(query_weight, ("dp", "seq"), axis=0, tiled=True),
            lax.all_gather(gate_weight, ("dp", "seq"), axis=0, tiled=True),
            lax.all_gather(up_weight, ("dp", "seq"), axis=0, tiled=True),
            lax.all_gather(down_weight, ("dp", "seq"), axis=1, tiled=True),
        )
        small_set = (
            lax.all_gather(key_value_matrix, ("dp", "seq", "heads"), axis=0, tiled=True),
            lax.all_gather(output_weight, ("dp", "seq", "heads"), axis=1, tiled=True),
            lax.all_gather(attention_gain, ("dp", "seq", "heads"), axis=0, tiled=True),
            lax.all_gather(feed_gain, ("dp", "seq", "heads"), axis=0, tiled=True),
            lax.all_gather(per_head_gains, ("dp", "seq", "heads"), axis=0, tiled=True),
        )
        current = tuple(layer_set) + tuple(small_set)
        layer_rows, input_rows, grads = one_batch(batch_index, current)
        layer_list.append(layer_rows)
        input_list.append(input_rows)
        layer_part = (
            lax.psum_scatter(
                grads[0].astype(jnp.bfloat16), ("dp", "seq"), scatter_dimension=0, tiled=True
            ).astype(jnp.float32),
            lax.psum_scatter(
                grads[1].astype(jnp.bfloat16), ("dp", "seq"), scatter_dimension=0, tiled=True
            ).astype(jnp.float32),
            lax.psum_scatter(
                grads[2].astype(jnp.bfloat16), ("dp", "seq"), scatter_dimension=0, tiled=True
            ).astype(jnp.float32),
            lax.psum_scatter(
                grads[3].astype(jnp.bfloat16), ("dp", "seq"), scatter_dimension=1, tiled=True
            ).astype(jnp.float32),
        )
        shared_part = (
            lax.psum_scatter(grads[4], ("dp", "seq", "heads"), scatter_dimension=0, tiled=True),
            lax.psum_scatter(grads[5], ("dp", "seq", "heads"), scatter_dimension=1, tiled=True),
            lax.psum_scatter(grads[6], ("dp", "seq", "heads"), scatter_dimension=0, tiled=True),
            lax.psum_scatter(grads[7], ("dp", "seq", "heads"), scatter_dimension=0, tiled=True),
            lax.psum_scatter(grads[8], ("dp", "seq", "heads"), scatter_dimension=0, tiled=True),
        )
        shards = tuple(layer_part) + tuple(shared_part)
        running = shards if running is None else jax.tree.map(jnp.add, running, shards)
    layer_out = jnp.stack(layer_list, axis=0)[:, None]
    tokens_grad = jnp.stack(input_list, axis=0)[:, None]
    return (
        layer_out,
        tokens_grad,
        running[6],
        running[0],
        running[4],
        running[8],
        running[5],
        running[7],
        running[1],
        running[2],
        running[3],
    )


def solution(mesh):
    return jax.shard_map(
        on_device,
        mesh=mesh,
        in_specs=(
            P(None, "dp", ("seq", "heads"), None),
            P(None, "dp", None),
            P(("dp", "seq", "heads")),
            P(("dp", "seq"), "heads"),
            P(("dp", "seq", "heads"), None),
            P(("dp", "seq", "heads")),
            P(None, ("dp", "seq", "heads")),
            P(("dp", "seq", "heads")),
            P(("dp", "seq"), "heads"),
            P(("dp", "seq"), "heads"),
            P("heads", ("dp", "seq")),
            P(None, "dp", ("seq", "heads"), None),
        ),
        out_specs=(
            P(None, "dp", ("seq", "heads"), None),
            P(None, "dp", ("seq", "heads"), None),
            P(("dp", "seq", "heads")),
            P(("dp", "seq"), "heads"),
            P(("dp", "seq", "heads"), None),
            P(("dp", "seq", "heads")),
            P(None, ("dp", "seq", "heads")),
            P(("dp", "seq", "heads")),
            P(("dp", "seq"), "heads"),
            P(("dp", "seq"), "heads"),
            P("heads", ("dp", "seq")),
        ),
        check_vma=False,
    )
```

profile of v0, /device:TPU:0, one launch (start us, length us, event | category | flops | bytes accessed | tf_op | source)
XLA Modules:
  0.0 2293.8 jit_solution(14578681344874961842)
XLA Ops:
  11.9 42.2 %all-reduce.15 = (bf16[128]{0:T(256)(128)(2,1)S(1)}, bf16[2048]{0:T(1024)(128)(2,1)S(1)}, bf16[2048]{0:T(1024)(128)(2,1)S(1)}) all-reduce(bf16[128]{0:T(256)(128)(2,1)S(1)} %dynamic-update-slice.1, bf16[2048]{0:T(1024)(128)(2,1)S(1)} %dynamic-update-slice, ...), channel_id=1, replica_groups=mesh['dp'=2,'seq'=4,'heads'=4] {'dp','seq','heads'}, use_global_device_ids=true, to_apply=%add.9 | all-reduce | flops 4224 | bytes 16896
  63.9 39.1 %all-gather.35.cloned.1.call-done = bf16[512,2048]{1,0:T(8,128)(2,1)} async-done(((bf16[128,2048]{1,0:T(8,128)(2,1)}), bf16[512,2048]{1,0:T(8,128)(2,1)}) %all-gather.35.cloned.1.call-update) | async-done | bytes 2097168 | tf_op jit(solution)/shard_map/all_gather | solution.py:133
  103.1 27.7 %all-gather.23.cloned.1.call-done = bf16[2048,448]{0,1:T(8,128)(2,1)} async-done(((bf16[256,448]{0,1:T(8,128)(2,1)}), bf16[2048,448]{0,1:T(8,128)(2,1)}) %all-gather.23.cloned.1.call-update) | async-done | bytes 1835024 | tf_op jit(solution)/shard_map/all_gather | solution.py:304
  134.3 44.6 %all-gather.17.cloned.1.call-done = bf16[512,2048]{1,0:T(8,128)(2,1)} async-done(((bf16[128,2048]{1,0:T(8,128)(2,1)}), bf16[512,2048]{1,0:T(8,128)(2,1)}) %all-gather.17.cloned.1.call-update) | async-done | bytes 2097168 | tf_op jit(solution)/shard_map/all_gather | solution.py:133
  183.9 56.8 %all-gather.19.cloned.1.call-done = bf16[2048,896]{1,0:T(8,128)(2,1)} async-done(((bf16[64,896]{1,0:T(8,128)(2,1)}), bf16[2048,896]{1,0:T(8,128)(2,1)}) %all-gather.19.cloned.1.call-update) | async-done | bytes 3670032 | tf_op jit(solution)/shard_map/all_gather | solution.py:310
  260.3 24.7 %all-gather.21.cloned.1.call-done = bf16[2048,896]{0,1:T(8,128)(2,1)} async-done(((bf16[512,896]{0,1:T(8,128)(2,1)}), bf16[2048,896]{0,1:T(8,128)(2,1)}) %all-gather.21.cloned.1.call-update) | async-done | bytes 3670032 | tf_op jit(solution)/shard_map/all_gather | solution.py:149
  291.7 13.3 fusion.198
  305.0 12.1 fusion
  317.1 15.2 fusion.106
  337.8 26.1 %all-to-all-done = bf16[4,128,448]{1,2,0:T(8,128)(2,1)S(1)} async-done(((bf16[4,128,448]{1,2,0:T(8,128)(2,1)}), bf16[4,128,448]{1,2,0:T(8,128)(2,1)S(1)}, u32[]{:S(2)}, u32[]{:S(2)}) %all-to-all-start) | async-done | bytes 458784 | tf_op jit(solution)/shard_map/all_to_all | solution.py:180
  379.3 22.1 all-gather.37.cloned.1.call-done
  408.2 13.4 fusion.199
  421.5 13.0 fusion.1
  434.6 16.7 all-gather.31.cloned.1.call-done
  451.2 48.1 %all-gather.27.cloned.1.call-done = bf16[512,2048]{1,0:T(8,128)(2,1)} async-done(((bf16[128,2048]{1,0:T(8,128)(2,1)}), bf16[512,2048]{1,0:T(8,128)(2,1)}) %all-gather.27.cloned.1.call-update) | async-done | bytes 2097168 | tf_op jit(solution)/shard_map/all_gather | solution.py:185
  508.2 39.5 %all-gather.29.cloned.1.call-done = bf16[2048,1600]{0,1:T(8,128)(2,1)} async-done(((bf16[256,1600]{0,1:T(8,128)(2,1)}), bf16[2048,1600]{0,1:T(8,128)(2,1)}) %all-gather.29.cloned.1.call-update) | async-done | bytes 6553616 | tf_op jit(solution)/shard_map/all_gather | solution.py:305
  547.6 8.9 fusion.202
  556.5 39.3 %all-gather.41.cloned.1.call-done = bf16[1,1,512,2048]{3,2,1,0:T(8,128)(2,1)} async-done(((bf16[1,1,128,2048]{3,2,1,0:T(8,128)(2,1)}), bf16[1,1,512,2048]{3,2,1,0:T(8,128)(2,1)}) %all-gather.41.cloned.1.call-update) | async-done | bytes 2097168 | tf_op jit(solution)/shard_map/all_gather | solution.py:196
  595.8 48.3 %all-gather.33.cloned.1.call-done = bf16[1600,2048]{1,0:T(8,128)(2,1)} async-done(((bf16[1600,256]{1,0:T(8,128)(2,1)}), bf16[1600,2048]{1,0:T(8,128)(2,1)}) %all-gather.33.cloned.1.call-update) | async-done | bytes 6553616 | tf_op jit(solution)/shard_map/all_gather | solution.py:307
  644.1 11.7 multiply_convert_fusion.3
  668.4 14.8 fusion.109
  683.4 30.6 %all_to_all.70 = bf16[4,128,448]{1,2,0:T(8,128)(2,1)S(1)} all-to-all(bf16[4,128,448]{1,2,0:T(8,128)(2,1)S(1)} %copy.200), channel_id=1, replica_groups=mesh['dp'=2,'seq'=4,'heads'=4] {'heads'}, dimensions={0} | all-to-all | bytes 917504 | tf_op jit(solution)/shard_map/all_to_all | solution.py:180
  723.9 45.2 %all-gather.39.cloned.1.call-done = bf16[512,2048]{1,0:T(8,128)(2,1)} async-done(((bf16[128,2048]{1,0:T(8,128)(2,1)}), bf16[512,2048]{1,0:T(8,128)(2,1)}) %all-gather.39.cloned.1.call-update) | async-done | bytes 2097168 | tf_op jit(solution)/shard_map/all_gather | solution.py:185
  769.1 9.0 fusion.207
  786.4 29.4 %all-gather.43.cloned.1.call-done = bf16[1,1,512,2048]{3,2,1,0:T(8,128)(2,1)} async-done(((bf16[1,1,128,2048]{3,2,1,0:T(8,128)(2,1)}), bf16[1,1,512,2048]{3,2,1,0:T(8,128)(2,1)}) %all-gather.43.cloned.1.call-update) | async-done | bytes 2097168 | tf_op jit(solution)/shard_map/all_gather | solution.py:196
  815.9 11.6 multiply_convert_fusion.2
  861.0 24.8 %reduce-scatter.29.cloned.1.call-done = bf16[128,2048]{1,0:T(8,128)(2,1)} async-done(((bf16[512,2048]{1,0:T(8,128)(2,1)}), bf16[128,2048]{1,0:T(8,128)(2,1)}) %reduce-scatter.29.cloned.1.call-update) | async-done | bytes 524304 | tf_op jit(solution)/shard_map/reduce_scatter | solution.py:207
  887.8 43.4 %reduce-scatter.19.cloned.1.call-done = bf16[128,2048]{1,0:T(8,128)(2,1)} async-done(((bf16[512,2048]{1,0:T(8,128)(2,1)}), bf16[128,2048]{1,0:T(8,128)(2,1)}) %reduce-scatter.19.cloned.1.call-update) | async-done | bytes 524304 | tf_op jit(solution)/shard_map/reduce_scatter | solution.py:189
  931.1 45.5 %reduce-scatter.21.cloned.1.call-done = bf16[128,2048]{1,0:T(8,128)(2,1)} async-done(((bf16[512,2048]{1,0:T(8,128)(2,1)}), bf16[128,2048]{1,0:T(8,128)(2,1)}) %reduce-scatter.21.cloned.1.call-update) | async-done | bytes 524304 | tf_op jit(solution)/shard_map/reduce_scatter | solution.py:189
  1009.9 24.5 %multiply_reduce_fusion.1 = (f32[7,512]{1,0:T(8,128)S(1)}, f32[7,512,2048]{2,1,0:T(8,128)}) fusion(f32[7,512,2048]{2,1,0:T(8,128)} %get-tuple-element.177, f32[7,512]{1,0:T(8,128)S(1)} %log_add_fusion.1, bf16[512,7,64]{0,2,1:T(8,128)(2,1)S(1)} %reshape.506, bf16[2048,7,64]{0,1,2:T(8,128)(2,1)S(1)} %copy-done.18), kind=kOutput, calls=%fused_computation.4 | convolution fusion | flops 961540608 | bytes 61042688 | tf_op jit(solution)/shard_map/qjh,kjh->jqk/dot_general | solution.py:224
  1034.4 13.7 fusion.30
  1049.6 12.4 fusion.33
  1073.6 24.8 %multiply_convert_fusion.1 = bf16[7,512,2048]{2,1,0:T(8,128)(2,1)} fusion(f32[7,512,2048]{2,1,0:T(8,128)} %get-tuple-element.185, f32[7,512,2048]{2,1,0:T(8,128)} %get-tuple-element.177, f32[7,512]{1,0:T(8,128)S(1)} %get-tuple-element.184, f32[7,512]{1,0:T(8,128)S(1)} %log_add_fusion.1), kind=kLoop, calls=%fused_computation.3 | loop fusion | flops 29360128 | bytes 73428992 | tf_op jit(solution)/shard_map/convert_element_type | solution.py:228
  1115.0 25.1 %multiply_reduce_fusion = (f32[7,512]{1,0:T(8,128)S(1)}, f32[7,512,2048]{2,1,0:T(8,128)}) fusion(f32[7,512,2048]{2,1,0:T(8,128)} %get-tuple-element.181, f32[7,512]{1,0:T(8,128)S(1)} %log_add_fusion, bf16[512,7,64]{0,2,1:T(8,128)(2,1)S(1)} %reshape.512, bf16[2048,7,64]{0,1,2:T(8,128)(2,1)S(1)} %copy-done.19), kind=kOutput, calls=%fused_computation.1 | convolution fusion | flops 961540608 | bytes 61042688 | tf_op jit(solution)/shard_map/qjh,kjh->jqk/dot_general | solution.py:224
  1140.1 24.9 %multiply_convert_fusion = bf16[7,512,2048]{2,1,0:T(8,128)(2,1)} fusion(f32[7,512,2048]{2,1,0:T(8,128)} %get-tuple-element.187, f32[7,512,2048]{2,1,0:T(8,128)} %get-tuple-element.181, f32[7,512]{1,0:T(8,128)S(1)} %get-tuple-element.186, f32[7,512]{1,0:T(8,128)S(1)} %log_add_fusion), kind=kLoop, calls=%fused_computation | loop fusion | flops 29360128 | bytes 73428992 | tf_op jit(solution)/shard_map/convert_element_type | solution.py:228
  1182.3 9.9 broadcast_multiply_fusion.1
  1193.1 10.6 broadcast_multiply_fusion
  1311.4 64.6 %reduce-scatter.47.cloned.1.call-done = bf16[1600,256]{1,0:T(8,128)(2,1)} async-done(((bf16[1600,2048]{1,0:T(8,128)(2,1)}), bf16[1600,256]{1,0:T(8,128)(2,1)}) %reduce-scatter.47.cloned.1.call-update) | async-done | bytes 819216 | tf_op jit(solution)/shard_map/reduce_scatter | solution.py:330
  1376.0 66.7 %reduce-scatter.49.cloned.1.call-done = bf16[1600,256]{1,0:T(8,128)(2,1)} async-done(((bf16[1600,2048]{1,0:T(8,128)(2,1)}), bf16[1600,256]{1,0:T(8,128)(2,1)}) %reduce-scatter.49.cloned.1.call-update) | async-done | bytes 819216 | tf_op jit(solution)/shard_map/reduce_scatter | solution.py:330
  1445.4 63.7 %reduce-scatter.43.cloned.1.call-done = bf16[256,1600]{0,1:T(8,128)(2,1)} async-done(((bf16[2048,1600]{0,1:T(8,128)(2,1)}), bf16[256,1600]{0,1:T(8,128)(2,1)}) %reduce-scatter.43.cloned.1.call-update) | async-done | bytes 819216 | tf_op jit(solution)/shard_map/reduce_scatter | solution.py:327
  1509.1 66.7 %reduce-scatter.45.cloned.1.call-done = bf16[256,1600]{0,1:T(8,128)(2,1)} async-done(((bf16[2048,1600]{0,1:T(8,128)(2,1)}), bf16[256,1600]{0,1:T(8,128)(2,1)}) %reduce-scatter.45.cloned.1.call-update) | async-done | bytes 819216 | tf_op jit(solution)/shard_map/reduce_scatter | solution.py:327
  1578.6 63.6 %reduce-scatter.39.cloned.1.call-done = bf16[256,1600]{0,1:T(8,128)(2,1)} async-done(((bf16[2048,1600]{0,1:T(8,128)(2,1)}), bf16[256,1600]{0,1:T(8,128)(2,1)}) %reduce-scatter.39.cloned.1.call-update) | async-done | bytes 819216 | tf_op jit(solution)/shard_map/reduce_scatter | solution.py:324
  1642.2 66.8 %reduce-scatter.41.cloned.1.call-done = bf16[256,1600]{0,1:T(8,128)(2,1)} async-done(((bf16[2048,1600]{0,1:T(8,128)(2,1)}), bf16[256,1600]{0,1:T(8,128)(2,1)}) %reduce-scatter.41.cloned.1.call-update) | async-done | bytes 819216 | tf_op jit(solution)/shard_map/reduce_scatter | solution.py:324
  1711.9 43.4 %reduce-scatter.33.cloned.1.call-done = bf16[128,2048]{1,0:T(8,128)(2,1)} async-done(((bf16[512,2048]{1,0:T(8,128)(2,1)}), bf16[128,2048]{1,0:T(8,128)(2,1)}) %reduce-scatter.33.cloned.1.call-update) | async-done | bytes 524304 | tf_op jit(solution)/shard_map/reduce_scatter | solution.py:273
  1755.2 46.1 %reduce-scatter.27.cloned.1.call-done = bf16[128,2048]{1,0:T(8,128)(2,1)} async-done(((bf16[512,2048]{1,0:T(8,128)(2,1)}), bf16[128,2048]{1,0:T(8,128)(2,1)}) %reduce-scatter.27.cloned.1.call-update) | async-done | bytes 524304 | tf_op jit(solution)/shard_map/reduce_scatter | solution.py:273
  1803.5 42.3 %all-reduce.14 = (f32[2048]{0:T(1024)S(1)}, f32[128]{0:T(128)S(1)}, f32[2048]{0:T(1024)S(1)}) all-reduce(f32[2048]{0:T(1024)S(1)} %add.336, f32[128]{0:T(128)S(1)} %maximum_add_fusion, f32[2048]{0:T(1024)S(1)} %add.340), channel_id=17, replica_groups=mesh['dp'=2,'seq'=4,'heads'=4] {'dp','seq','heads'}, use_global_device_ids=true, to_apply=%region_37.38.clone | all-reduce | flops 4224 | bytes 33792
  1850.8 117.9 %reduce-scatter.51.cloned.1.call-done = f32[64,896]{1,0:T(8,128)} async-done(((f32[2048,896]{1,0:T(8,128)}), f32[64,896]{1,0:T(8,128)}) %reduce-scatter.51.cloned.1.call-update) | async-done | bytes 229392 | tf_op jit(solution)/shard_map/reduce_scatter | solution.py:335
  1968.7 318.3 %reduce-scatter.53.cloned.1.call-done = f32[1792,64]{0,1:T(8,128)} async-done(((f32[1792,2048]{0,1:T(8,128)}), f32[1792,64]{0,1:T(8,128)}) %reduce-scatter.53.cloned.1.call-update) | async-done | bytes 458768 | tf_op jit(solution)/shard_map/reduce_scatter | solution.py:336
  (454 shorter events, 354.9 us)
Async XLA Ops:
  7.2 95.9 %all-gather.35.cloned.1.call-start = ((), (), s32[]{:S(2)}) async-start(), calls=%async_computation.32 | async-start | bytes 2621440 | tf_op jit(solution)/shard_map/all_gather | solution.py:133
  9.3 93.8 %copy-start.90 = (f32[128]{0:T(128)}, f32[128]{0:T(128)S(1)}, u32[]{:S(2)}) copy-start(f32[128]{0:T(128)S(1)} %fusion.180) | copy-start | bytes 1540
  9.3 93.8 %copy-start.92 = (f32[128]{0:T(128)}, f32[128]{0:T(128)S(1)}, u32[]{:S(2)}) copy-start(f32[128]{0:T(128)S(1)} %fusion.182) | copy-start | bytes 1540
  57.2 73.6 %all-gather.23.cloned.1.call-start = ((), (), s32[]{:S(2)}) async-start(), calls=%async_computation.25 | async-start | bytes 2064384 | tf_op jit(solution)/shard_map/all_gather | solution.py:304
  57.9 120.9 %all-gather.17.cloned.1.call-start = ((), (), s32[]{:S(2)}) async-start(), calls=%async_computation.22 | async-start | bytes 2621440 | tf_op jit(solution)/shard_map/all_gather | solution.py:133
  58.6 182.0 %all-gather.19.cloned.1.call-start = ((), (), s32[]{:S(2)}) async-start(), calls=%async_computation.23 | async-start | bytes 3784704 | tf_op jit(solution)/shard_map/all_gather | solution.py:310
  59.2 225.8 %all-gather.21.cloned.1.call-start = ((), (), s32[]{:S(2)}) async-start(), calls=%async_computation.24 | async-start | bytes 4587520 | tf_op jit(solution)/shard_map/all_gather | solution.py:149
  59.9 122.6 %copy-start.88 = (f32[64]{0:T(128)}, f32[64]{0:T(128)S(1)}, u32[]{:S(2)}) copy-start(f32[64]{0:T(128)S(1)} %get-tuple-element.175) | copy-start | bytes 772
  59.9 189.8 %copy-start.86 = (f32[64]{0:T(128)}, f32[64]{0:T(128)S(1)}, u32[]{:S(2)}) copy-start(f32[64]{0:T(128)S(1)} %get-tuple-element.174) | copy-start | bytes 772
  61.8 191.3 %copy-start.38 = (f32[512,64]{0,1:T(8,128)}, f32[512,64]{0,1:T(8,128)S(1)}, u32[]{:S(2)}) copy-start(f32[512,64]{0,1:T(8,128)S(1)} %get-tuple-element.139) | copy-start | bytes 393220
  63.9 189.1 %copy-start.40 = (f32[512,64]{0,1:T(8,128)}, f32[512,64]{0,1:T(8,128)S(1)}, u32[]{:S(2)}) copy-start(f32[512,64]{0,1:T(8,128)S(1)} %get-tuple-element.143) | copy-start | bytes 393220
  254.5 114.3 %all-gather.25.cloned.1.call-start = ((), (), s32[]{:S(2)}) async-start(), calls=%async_computation.26 | async-start | bytes 7569408 | tf_op jit(solution)/shard_map/all_gather | solution.py:311
  255.1 146.4 %all-gather.37.cloned.1.call-start = ((), (), s32[]{:S(2)}) async-start(), calls=%async_computation.33 | async-start | bytes 4587520 | tf_op jit(solution)/shard_map/all_gather | solution.py:149
  257.4 193.9 %all-gather.31.cloned.1.call-start = ((), (), s32[]{:S(2)}) async-start(), calls=%async_computation.29 | async-start | bytes 7372800 | tf_op jit(solution)/shard_map/all_gather | solution.py:306
  258.3 147.2 %copy-start.82 = (s32[7]{0:T(128)}, s32[7]{0:T(128)S(1)}, u32[]{:S(2)}) copy-start(s32[7]{0:T(128)S(1)} %and_select_fusion) | copy-start | bytes 88
  333.2 30.6 %all-to-all-start = ((bf16[4,128,448]{1,2,0:T(8,128)(2,1)}), bf16[4,128,448]{1,2,0:T(8,128)(2,1)S(1)}, u32[]{:S(2)}, u32[]{:S(2)}) async-start(bf16[4,128,448]{1,2,0:T(8,128)(2,1)} %copy.191), calls=%async_computation | async-start | bytes 917504 | tf_op jit(solution)/shard_map/all_to_all | solution.py:180
  337.8 161.5 %all-gather.27.cloned.1.call-start = ((), (), s32[]{:S(2)}) async-start(), calls=%async_computation.27 | async-start | bytes 2621440 | tf_op jit(solution)/shard_map/all_gather | solution.py:185
  375.7 172.0 %all-gather.29.cloned.1.call-start = ((), (), s32[]{:S(2)}) async-start(), calls=%async_computation.28 | async-start | bytes 7372800 | tf_op jit(solution)/shard_map/all_gather | solution.py:305
  376.2 219.5 %all-gather.41.cloned.1.call-start = ((), (), s32[]{:S(2)}) async-start(), calls=%async_computation.50 | async-start | bytes 2621440 | tf_op jit(solution)/shard_map/all_gather | solution.py:196
  378.7 265.4 %all-gather.33.cloned.1.call-start = ((), (), s32[]{:S(2)}) async-start(), calls=%async_computation.30 | async-start | bytes 7372800 | tf_op jit(solution)/shard_map/all_gather | solution.py:307
  379.3 340.7 %reduce-scatter.23.cloned.1.call-start = ((), (), s32[]{:S(2)}) async-start(), calls=%async_computation.36 | async-start | bytes 2621440 | tf_op jit(solution)/shard_map/reduce_scatter | solution.py:207
  668.3 100.8 %all-gather.39.cloned.1.call-start = ((), (), s32[]{:S(2)}) async-start(), calls=%async_computation.34 | async-start | bytes 2621440 | tf_op jit(solution)/shard_map/all_gather | solution.py:185
  722.8 93.0 %all-gather.43.cloned.1.call-start = ((), (), s32[]{:S(2)}) async-start(), calls=%async_computation.51 | async-start | bytes 2621440 | tf_op jit(solution)/shard_map/all_gather | solution.py:196
  723.4 162.4 %reduce-scatter.29.cloned.1.call-start = ((), (), s32[]{:S(2)}) async-start(), calls=%async_computation.39 | async-start | bytes 2621440 | tf_op jit(solution)/shard_map/reduce_scatter | solution.py:207
  843.0 88.1 %reduce-scatter.19.cloned.1.call-start = ((), (), s32[]{:S(2)}) async-start(), calls=%async_computation.31 | async-start | bytes 2621440 | tf_op jit(solution)/shard_map/reduce_scatter | solution.py:189
  851.9 124.7 %reduce-scatter.21.cloned.1.call-start = ((), (), s32[]{:S(2)}) async-start(), calls=%async_computation.35 | async-start | bytes 2621440 | tf_op jit(solution)/shard_map/reduce_scatter | solution.py:189
  986.5 16.6 all-to-all-start.2
  1003.1 44.9 %all-to-all-start.3 = ((bf16[128,4,448]{0,2,1:T(8,128)(2,1)}), bf16[128,4,448]{0,2,1:T(8,128)(2,1)}, u32[]{:S(2)}, u32[]{:S(2)}) async-start(bf16[128,4,448]{0,2,1:T(8,128)(2,1)} %bitcast.290), calls=%async_computation.9 | async-start | bytes 917504 | tf_op jit(solution)/shard_map/all_to_all | solution.py:219
  1007.3 257.0 %reduce-scatter.25.cloned.1.call-start = ((), (), s32[]{:S(2)}) async-start(), calls=%async_computation.37 | async-start | bytes 4587520 | tf_op jit(solution)/shard_map/reduce_scatter | solution.py:253
  1113.4 153.1 %reduce-scatter.31.cloned.1.call-start = ((), (), s32[]{:S(2)}) async-start(), calls=%async_computation.40 | async-start | bytes 4587520 | tf_op jit(solution)/shard_map/reduce_scatter | solution.py:253
  1180.8 127.4 %reduce-scatter.37.cloned.1.call-start = ((), (), s32[]{:S(2)}) async-start(), calls=%async_computation.43 | async-start | bytes 2064384 | tf_op jit(solution)/shard_map/reduce_scatter | solution.py:321
  1210.0 99.5 %reduce-scatter.35.cloned.1.call-start = ((), (), s32[]{:S(2)}) async-start(), calls=%async_computation.42 | async-start | bytes 2064384 | tf_op jit(solution)/shard_map/reduce_scatter | solution.py:321
  1212.4 163.5 %reduce-scatter.47.cloned.1.call-start = ((), (), s32[]{:S(2)}) async-start(), calls=%async_computation.48 | async-start | bytes 7372800 | tf_op jit(solution)/shard_map/reduce_scatter | solution.py:330
  1221.2 221.5 %reduce-scatter.49.cloned.1.call-start = ((), (), s32[]{:S(2)}) async-start(), calls=%async_computation.49 | async-start | bytes 7372800 | tf_op jit(solution)/shard_map/reduce_scatter | solution.py:330
  1229.7 279.4 %reduce-scatter.43.cloned.1.call-start = ((), (), s32[]{:S(2)}) async-start(), calls=%async_computation.46 | async-start | bytes 7372800 | tf_op jit(solution)/shard_map/reduce_scatter | solution.py:327
  1238.3 337.6 %reduce-scatter.45.cloned.1.call-start = ((), (), s32[]{:S(2)}) async-start(), calls=%async_computation.47 | async-start | bytes 7372800 | tf_op jit(solution)/shard_map/reduce_scatter | solution.py:327
  1246.8 395.5 %reduce-scatter.39.cloned.1.call-start = ((), (), s32[]{:S(2)}) async-start(), calls=%async_computation.44 | async-start | bytes 7372800 | tf_op jit(solution)/shard_map/reduce_scatter | solution.py:324
  1255.5 453.5 %reduce-scatter.41.cloned.1.call-start = ((), (), s32[]{:S(2)}) async-start(), calls=%async_computation.45 | async-start | bytes 7372800 | tf_op jit(solution)/shard_map/reduce_scatter | solution.py:324
  1264.0 491.3 %reduce-scatter.33.cloned.1.call-start = ((), (), s32[]{:S(2)}) async-start(), calls=%async_computation.41 | async-start | bytes 2621440 | tf_op jit(solution)/shard_map/reduce_scatter | solution.py:273
  1277.5 523.7 %reduce-scatter.27.cloned.1.call-start = ((), (), s32[]{:S(2)}) async-start(), calls=%async_computation.38 | async-start | bytes 2621440 | tf_op jit(solution)/shard_map/reduce_scatter | solution.py:273
  1284.9 683.8 %reduce-scatter.51.cloned.1.call-start = ((), (), s32[]{:S(2)}) async-start(), calls=%async_computation.52 | async-start | bytes 7569408 | tf_op jit(solution)/shard_map/reduce_scatter | solution.py:335
  1295.1 992.0 %reduce-scatter.53.cloned.1.call-start = ((), (), s32[]{:S(2)}) async-start(), calls=%async_computation.53 | async-start | bytes 15138816 | tf_op jit(solution)/shard_map/reduce_scatter | solution.py:336
  1445.4 355.9 %copy-start.1 = (bf16[2,1,128,2048]{3,2,1,0:T(8,128)(2,1)S(1)}, bf16[2,1,128,2048]{3,2,1,0:T(8,128)(2,1)}, u32[]{:S(2)}) copy-start(bf16[2,1,128,2048]{3,2,1,0:T(8,128)(2,1)} %param.12) | copy-start | bytes 3145732
  1445.4 355.9 %copy-start.79 = (f32[2048]{0:T(1024)S(1)}, f32[2048]{0:T(1024)}, u32[]{:S(2)}) copy-start(f32[2048]{0:T(1024)} %copy-done.78) | copy-start | bytes 24580
  1445.4 355.9 %copy-start.91 = (f32[128]{0:T(128)S(1)}, f32[128]{0:T(128)}, u32[]{:S(2)}) copy-start(f32[128]{0:T(128)} %copy-done.90) | copy-start | bytes 1540
  1445.4 355.9 %copy-start.93 = (f32[128]{0:T(128)S(1)}, f32[128]{0:T(128)}, u32[]{:S(2)}) copy-start(f32[128]{0:T(128)} %copy-done.92) | copy-start | bytes 1540
  1578.6 269.0 %copy-start.96 = (f32[128]{0:T(128)S(1)}, f32[128]{0:T(128)}, u32[]{:S(2)}) copy-start(f32[128]{0:T(128)} %copy-done.95) | copy-start | bytes 1540
  1578.6 269.0 %copy-start.98 = (f32[128]{0:T(128)S(1)}, f32[128]{0:T(128)}, u32[]{:S(2)}) copy-start(f32[128]{0:T(128)} %copy-done.97) | copy-start | bytes 1540
  (96 other events, 677.6 us)
Sparse Core Ops, SparseCore 0:
  57.3 45.7 all-gather.34
  104.9 25.7 all-gather.22
  132.9 45.9 all-gather.16
  181.5 59.0 all-gather.18
  254.6 30.3 all-gather.20
  287.7 81.0 all-gather.24
  370.9 30.4 all-gather.36
  403.3 47.8 all-gather.30
  453.4 45.9 all-gather.26
  501.1 46.5 all-gather.28
  549.8 45.9 all-gather.40
  597.5 46.5 all-gather.32
  668.5 51.1 reduce-scatter.22
  722.9 46.1 all-gather.38
  771.2 44.6 all-gather.42
  843.2 42.5 reduce-scatter.28
  887.9 43.1 reduce-scatter.18
  933.4 43.1 reduce-scatter.20
  1113.6 42.5 reduce-scatter.24
  1180.9 42.4 reduce-scatter.30
  1226.7 39.6 reduce-scatter.36
  1269.8 39.6 reduce-scatter.34
  1312.9 62.9 reduce-scatter.46
  1379.7 62.9 reduce-scatter.48
  1446.1 62.9 reduce-scatter.42
  1512.8 62.9 reduce-scatter.44
  1579.2 62.9 reduce-scatter.38
  1646.0 62.9 reduce-scatter.40
  1711.3 43.8 reduce-scatter.32
  1758.0 43.1 reduce-scatter.26
  1804.2 164.4 reduce-scatter.50
  1971.6 315.3 reduce-scatter.52
where the time goes:
time: 2300 us; the launch traced here: 2290 us
  waiting for transfers between devices  1560 us (68%)
  matrix products  410 us (18%)
  other arithmetic  131 us (6%)
  blocking collectives  115 us (5%)
  local copies, waits for them, and re-layouts  49.7 us (2%)
    reduce_scatter x1, waiting for transfers between devices, on_device(): lax.psum_scatter(grads[5], ('dp', 'seq', 'heads'), scatter_dimension=1, t...  318 us
    reduce_scatter x2, waiting for transfers between devices, on_device(): lax.psum_scatter(grads[3].astype(jnp.bfloat16), ('dp', 'seq'), scatter_di...  131 us
    reduce_scatter x2, waiting for transfers between devices, on_device(): lax.psum_scatter(grads[2].astype(jnp.bfloat16), ('dp', 'seq'), scatter_di...  130 us
    reduce_scatter x2, waiting for transfers between devices, on_device(): lax.psum_scatter(grads[1].astype(jnp.bfloat16), ('dp', 'seq'), scatter_di...  130 us
    reduce_scatter x1, waiting for transfers between devices, on_device(): lax.psum_scatter(grads[4], ('dp', 'seq', 'heads'), scatter_dimension=0, t...  118 us
    all_gather x2, waiting for transfers between devices, one_batch(): feed_block = lax.all_gather(feed_rows, 'heads', axis=0, tiled=True)  93.3 us
    reduce_scatter x2, waiting for transfers between devices, one_batch(): lax.psum_scatter((by_transpose(d_query_raw, query_full) + by_transpose(d_...  89.4 us
    reduce_scatter x2, waiting for transfers between devices, one_batch(): lax.psum_scatter(jnp.dot(activated, down_full, preferred_element_type=jnp...  88.9 us
  transfers between devices with their start and end apart: 35, of which 30 were waited for; matrix products, arithmetic and copies ran while one was open for 19% of the time, Pallas kernels for 0%

commit v1 on v0

v1 whole, which is shorter than its diff:
```python
import math

import jax
import jax.numpy as jnp
from jax import lax
from jax.experimental import pallas as pl
from jax.experimental.pallas import tpu as pltpu
from jax.sharding import PartitionSpec as P

QUERY_HEADS = 28
KEY_VALUE_HEADS = 7
HEAD_SIZE = 64
GROUP = QUERY_HEADS // KEY_VALUE_HEADS

EPSILON = 1e-06
SCORE_SCALE = 0.125
MASKED = -1e30
LANES = 128
CHUNK = 256

BF = jnp.bfloat16
F32 = jnp.float32


def dot_nn(left, right):
    return lax.dot_general(left, right, (((1,), (0,)), ((), ())), preferred_element_type=F32)


def dot_nt(left, right):
    return lax.dot_general(left, right, (((1,), (1,)), ((), ())), preferred_element_type=F32)


def dot_tn(left, right):
    return lax.dot_general(left, right, (((0,), (0,)), ((), ())), preferred_element_type=F32)


def pad_heads(tile, low, keep_low):
    rows = tile.shape[0]
    parts = []
    for pair in range(GROUP // 2):
        both = tile[:, pair * LANES : (pair + 1) * LANES].astype(F32)
        turned = pltpu.roll(both, HEAD_SIZE, 1)
        first, second = (both, turned) if keep_low else (turned, both)
        keep = low[:rows] if keep_low else jnp.logical_not(low[:rows])
        parts.append(jnp.where(keep, first, 0.0))
        parts.append(jnp.where(keep, second, 0.0))
    return jnp.concatenate(parts, axis=0).astype(BF)


def four_wide(row):
    return jnp.concatenate([row] * GROUP, axis=1)


def heads_back(stacked, rows):
    parts = []
    for pair in range(GROUP // 2):
        start = 2 * pair * rows
        both = jnp.concatenate(
            [stacked[:, start : start + rows], stacked[:, start + rows : start + 2 * rows]], axis=0
        )
        parts.append(both.T)
    return jnp.concatenate(parts, axis=1)


def attention_forward_kernel(kv0, kv1, query, bias0, bias1, mixed, lse, expo):
    rows = query.shape[0]
    half = kv0.shape[0]
    low = lax.broadcasted_iota(jnp.int32, (half, LANES), 1) < HEAD_SIZE
    padded = pad_heads(query[...], low, True)
    for part, (kv, bias) in enumerate(((kv0, bias0), (kv1, bias1))):
        for step in range(half // CHUNK):
            span = pl.ds(step * CHUNK, CHUNK)
            scores = dot_nt(kv[span, :], padded)
            weight = jnp.exp(scores + four_wide(bias[span, :]))
            expo[pl.ds(part * half + step * CHUNK, CHUNK), :] = weight.astype(BF)
    total = dot_tn(
        jnp.where(low, 1.0, kv0[...].astype(F32)).astype(BF), expo[pl.ds(0, half), :]
    ) + dot_tn(jnp.where(low, 1.0, kv1[...].astype(F32)).astype(BF), expo[pl.ds(half, half), :])
    lse[...] = jnp.log(total[0:1, :])[None]
    mixed[...] = heads_back(total[HEAD_SIZE:, :] / total[:HEAD_SIZE, :], rows).astype(BF)


def attention_backward_kernel(
    kv0, kv1, query, mixed, d_mixed, bias0, bias1, lse, d_query, d_kv0, d_kv1, d_scores
):
    rows = query.shape[0]
    half = kv0.shape[0]
    low = lax.broadcasted_iota(jnp.int32, (rows, LANES), 1) < HEAD_SIZE
    padded = pad_heads(query[...], low, True)
    d_padded = pad_heads(d_mixed[...], low, False)
    product = d_mixed[...].astype(F32) * mixed[...].astype(F32)
    pick = (
        lax.broadcasted_iota(jnp.int32, (8, GROUP * HEAD_SIZE), 1) // HEAD_SIZE
        == lax.broadcasted_iota(jnp.int32, (8, GROUP * HEAD_SIZE), 0)
    ).astype(F32)
    balance = lax.dot_general(
        pick,
        product,
        (((1,), (1,)), ((), ())),
        precision=lax.Precision.HIGHEST,
        preferred_element_type=F32,
    )
    balance = jnp.concatenate([balance[head : head + 1, :] for head in range(GROUP)], axis=1)
    level = lse[0]
    for part, (kv, bias, d_kv) in enumerate(((kv0, bias0, d_kv0), (kv1, bias1, d_kv1))):
        for step in range(half // CHUNK):
            span = pl.ds(step * CHUNK, CHUNK)
            block = kv[span, :]
            scores = dot_nt(block, padded)
            probs = jnp.exp(scores + four_wide(bias[span, :]) - level)
            d_probs = dot_nt(block, d_padded)
            low_scores = (probs * (d_probs - balance)).astype(BF)
            d_scores[pl.ds(part * half + step * CHUNK, CHUNK), :] = low_scores
            d_kv[span, :] = (
                dot_nn(low_scores, padded) + dot_nn(probs.astype(BF), d_padded)
            ).astype(BF)
    total = dot_tn(kv0[...], d_scores[pl.ds(0, half), :]) + dot_tn(
        kv1[...], d_scores[pl.ds(half, half), :]
    )
    d_query[...] = heads_back(total[:HEAD_SIZE, :] * SCORE_SCALE, rows)


def attention_forward(kv0, kv1, query, bias0, bias1):
    half, rows = bias0.shape
    wide = GROUP * rows
    keys = pl.BlockSpec((half, LANES), lambda c: (0, c))
    heads = pl.BlockSpec((rows, GROUP * HEAD_SIZE), lambda c: (0, c))
    fixed = pl.BlockSpec((half, rows), lambda c: (0, 0))
    return pl.pallas_call(
        attention_forward_kernel,
        grid=(KEY_VALUE_HEADS,),
        in_specs=[keys, keys, heads, fixed, fixed],
        out_specs=[heads, pl.BlockSpec((1, 1, wide), lambda c: (c, 0, 0))],
        out_shape=[
            jax.ShapeDtypeStruct(query.shape, BF),
            jax.ShapeDtypeStruct((KEY_VALUE_HEADS, 1, wide), F32),
        ],
        scratch_shapes=[pltpu.VMEM((2 * half, wide), BF)],
        compiler_params=pltpu.CompilerParams(
            dimension_semantics=("arbitrary",), vmem_limit_bytes=48 * 1024 * 1024
        ),
        cost_estimate=pl.CostEstimate(
            flops=KEY_VALUE_HEADS * 2 * half * wide * LANES * 4 * 2,
            bytes_accessed=2 * half * 896 * 2 + rows * 1792 * 4,
            transcendentals=KEY_VALUE_HEADS * 2 * half * wide,
        ),
        name="attention_forward",
    )(kv0, kv1, query, bias0, bias1)


def attention_backward(kv0, kv1, query, mixed, d_mixed, bias0, bias1, lse):
    half, rows = bias0.shape
    wide = GROUP * rows
    keys = pl.BlockSpec((half, LANES), lambda c: (0, c))
    heads = pl.BlockSpec((rows, GROUP * HEAD_SIZE), lambda c: (0, c))
    fixed = pl.BlockSpec((half, rows), lambda c: (0, 0))
    return pl.pallas_call(
        attention_backward_kernel,
        grid=(KEY_VALUE_HEADS,),
        in_specs=[
            keys,
            keys,
            heads,
            heads,
            heads,
            fixed,
            fixed,
            pl.BlockSpec((1, 1, wide), lambda c: (c, 0, 0)),
        ],
        out_specs=[heads, keys, keys],
        out_shape=[
            jax.ShapeDtypeStruct(query.shape, F32),
            jax.ShapeDtypeStruct(kv0.shape, BF),
            jax.ShapeDtypeStruct(kv1.shape, BF),
        ],
        scratch_shapes=[pltpu.VMEM((2 * half, wide), BF)],
        compiler_params=pltpu.CompilerParams(
            dimension_semantics=("arbitrary",), vmem_limit_bytes=48 * 1024 * 1024
        ),
        cost_estimate=pl.CostEstimate(
            flops=KEY_VALUE_HEADS * 2 * half * wide * LANES * 10 * 2,
            bytes_accessed=2 * half * 896 * 4 + rows * 1792 * 10,
            transcendentals=KEY_VALUE_HEADS * 2 * half * wide,
        ),
        name="attention_backward",
    )(kv0, kv1, query, mixed, d_mixed, bias0, bias1, lse)


def norm_scale(values):
    return lax.rsqrt(jnp.mean(values * values, axis=-1, keepdims=True) + EPSILON)


def apply_norm(values, gain):
    return values * norm_scale(values) * gain


def norm_back(values, gain, grad):
    scale = norm_scale(values)
    lifted = grad * gain
    dots = jnp.mean(values * lifted, axis=-1, keepdims=True)
    d_values = scale * lifted - values * (scale * scale * scale) * dots
    return d_values, jnp.sum(grad * values * scale, axis=tuple(range(values.ndim - 1)))


def rotary_tables(places):
    half_width = HEAD_SIZE // 2
    freqs = jnp.exp(
        jnp.arange(half_width, dtype=F32) * (-2.0 * math.log(10000.0) / HEAD_SIZE)
    )
    angles = places.astype(F32)[:, None] * freqs[None, :]
    cosine_table = jnp.cos(angles)
    sine_table = jnp.sin(angles)
    return (
        jnp.concatenate([cosine_table, cosine_table], -1)[:, None, :],
        jnp.concatenate([sine_table, sine_table], -1)[:, None, :],
    )


def apply_rotary(values, cosine_table, sine_table):
    half_width = values.shape[-1] // 2
    turned = jnp.concatenate([-values[..., half_width:], values[..., :half_width]], -1)
    return values * cosine_table + turned * sine_table


def on_device(
    tokens,
    lengths,
    attention_gain,
    query_weight,
    key_value_matrix,
    per_head_gains,
    output_weight,
    feed_gain,
    gate_weight,
    up_weight,
    down_weight,
    cotangent,
):
    batches = tokens.shape[0]
    rows = tokens.shape[2]
    width = tokens.shape[3]
    dp_size = lax.axis_size("dp")
    seq_size = lax.axis_size("seq")
    heads_size = lax.axis_size("heads")
    assert seq_size == 4 and heads_size == 4
    paired = dp_size == 2
    y = lax.axis_index("dp")
    s = lax.axis_index("seq")
    z = lax.axis_index("heads")
    x = s // 2
    core = s % 2
    kv_width = 2 * KEY_VALUE_HEADS * HEAD_SIZE
    q_width = QUERY_HEADS * HEAD_SIZE

    def swap_x(v):
        return lax.ppermute(v, "seq", [(i, i ^ 2) for i in range(4)])

    def swap_core(v):
        return lax.ppermute(v, "seq", [(i, i ^ 1) for i in range(4)])

    def swap_y(v):
        return lax.ppermute(v, "dp", [(0, 1), (1, 0)])

    def line_gather(v):
        up = [(0, 1), (1, 2), (2, 3)]
        down = [(1, 0), (2, 1), (3, 2)]
        u1 = lax.ppermute(v, "heads", up)
        d1 = lax.ppermute(v, "heads", down)
        u2 = lax.ppermute(u1, "heads", up[1:])
        d2 = lax.ppermute(d1, "heads", down[:-1])
        far = lax.ppermute(jnp.where(z == 1, d2, u2), "heads", [(1, 0), (2, 3)])
        table = ((v, u1, u2, far), (d1, v, u1, u2), (d2, d1, v, u1), (far, d2, d1, v))
        return jnp.stack([lax.select_n(z, *row) for row in table], axis=0)

    def gather_yx(v, x_first):
        def along_x(u):
            return jnp.stack([u, swap_x(u)], axis=-3)

        def along_y(u):
            if paired:
                return jnp.stack([u, swap_y(u)], axis=0)
            return lax.all_gather(u, "dp", axis=0)

        return along_y(along_x(v)) if x_first else along_x(along_y(v))

    def scatter_yx(g, x_last):
        def along_x(u):
            return u[..., 0, :, :] + swap_x(u[..., 1, :, :])

        def along_y(u):
            if paired:
                return u[0] + swap_y(u[1])
            return lax.psum_scatter(u, "dp", scatter_dimension=0)

        return along_x(along_y(g)) if x_last else along_y(along_x(g))

    blocks = 2 * dp_size
    piece = width // blocks

    def relative(v):
        cut = [v[..., i * piece : (i + 1) * piece] for i in range(blocks)]
        place = 2 * y + x if paired else x
        ways = 4 if paired else 2
        place = place.astype(jnp.int32)
        return jnp.concatenate(
            [lax.select_n(place, *[cut[i ^ m] for m in range(ways)]) for i in range(blocks)], axis=-1
        )

    def split_core(v):
        u = v.reshape(v.shape[:-1] + (blocks, 2, piece // 2))
        first, second = u[..., 0, :], u[..., 1, :]
        flat = v.shape[:-1] + (width // 2,)
        mine = jnp.where(core == 0, first, second).reshape(flat)
        other = jnp.where(core == 0, second, first).reshape(flat)
        return mine, other

    def merge_core(mine, other):
        shape = mine.shape[:-1] + (blocks, piece // 2)
        mine, other = mine.reshape(shape), other.reshape(shape)
        first = jnp.where(core == 0, mine, other)
        second = jnp.where(core == 0, other, mine)
        return jnp.stack([first, second], axis=-2).reshape(shape[:-2] + (width,))

    small = key_value_matrix.shape[0]
    per_head = per_head_gains.shape[0]
    kv_local = (
        key_value_matrix.reshape(small, 2, KEY_VALUE_HEADS, HEAD_SIZE)
        .transpose(0, 2, 1, 3)
        .reshape(small, kv_width)
    )
    gains_local = jnp.stack(
        [attention_gain, feed_gain, jnp.pad(per_head_gains, (0, small - per_head))], axis=1
    )
    kvg_local = jnp.concatenate(
        [kv_local, jnp.pad(gains_local, ((0, 0), (0, LANES - gains_local.shape[1])))], axis=1
    )
    kvg_rows = line_gather(kvg_local).reshape(4 * small, kv_width + LANES)
    kvg_mine = gather_yx(kvg_rows, True).reshape(width // 2, kv_width + LANES)
    kvg_other = swap_core(kvg_mine)

    q_part = query_weight.shape[1]
    q_rows = (
        line_gather(query_weight).transpose(1, 0, 2).reshape(query_weight.shape[0], q_width)
    )
    q_mine = gather_yx(q_rows, False).reshape(width // 2, q_width)
    q_other = swap_core(q_mine)

    o_rows = line_gather(output_weight.T).reshape(4 * small, q_width)
    o_mine = gather_yx(o_rows, True).reshape(width // 2, q_width)
    o_other = swap_core(o_mine)

    kv_mine, kv_other = kvg_mine[:, :kv_width], kvg_other[:, :kv_width]
    gains = merge_core(kvg_mine[:, kv_width:].T[:3], kvg_other[:, kv_width:].T[:3]).astype(F32)
    attention_scale = gains[0:1]
    feed_scale = gains[1:2]
    head_scale = relative(gains[2:3]).reshape(-1, small)[:, :per_head].reshape(-1)
    query_scale = head_scale[:HEAD_SIZE]
    key_scale = head_scale[HEAD_SIZE:]

    hidden_part = gate_weight.shape[1] // 2

    def unit_half(v, which):
        return jnp.where(which == 0, v[:, :hidden_part], v[:, hidden_part:])

    down_local = down_weight.T
    three = (gate_weight, up_weight, down_local)
    keep = jnp.concatenate([unit_half(v, core) for v in three], axis=1)
    give = jnp.concatenate([unit_half(v, 1 - core) for v in three], axis=1)
    take = swap_core(give)
    ffn_rows = jnp.where(
        core == 0,
        jnp.concatenate([keep, take], axis=0),
        jnp.concatenate([take, keep], axis=0),
    )
    gate_up = gather_yx(ffn_rows[:, : 2 * hidden_part], True).reshape(width, 2 * hidden_part)
    down = gather_yx(ffn_rows[:, 2 * hidden_part :], False).reshape(width, hidden_part)

    row_length = rows * heads_size * seq_size
    block_rows = rows * heads_size
    places = s * block_rows + z * rows + jnp.arange(rows, dtype=jnp.int32)
    inside = jnp.arange(block_rows, dtype=jnp.int32)

    def key_places(first):
        return jnp.concatenate([first * block_rows + inside, (first ^ 2) * block_rows + inside])

    def bias_for(begin, first):
        keys = key_places(first)[:, None]
        return jnp.where((keys <= places[None, :]) & (keys >= begin[None, :]), 0.0, MASKED)

    begins, biases = [], []
    for batch in range(batches):
        sizes = lengths[batch, 0]
        finish = jnp.cumsum(sizes)
        begin = jnp.sum(
            jnp.where(places[:, None] >= finish[None, :], sizes[None, :], 0), axis=1
        ).astype(jnp.int32)
        begins.append(begin)
        biases.append((bias_for(begin, s), bias_for(begin, s ^ 1)))
    offsets = jnp.concatenate([places - begin for begin in begins])
    cosine_table, sine_table = rotary_tables(offsets)

    residual_in = relative(tokens[:, 0].reshape(batches * rows, width)).astype(F32)
    out_cotangent = relative(cotangent[:, 0].reshape(batches * rows, width))
    normed = apply_norm(residual_in, attention_scale).astype(BF)
    normed_mine, normed_other = split_core(normed)
    kv_raw = dot_nn(normed_mine, kv_mine) + dot_nn(normed_other, kv_other)

    def prepare(raw, gain):
        heads = raw.reshape(raw.shape[0], -1, HEAD_SIZE)
        return apply_rotary(apply_norm(heads, gain), cosine_table, sine_table)

    kv_heads = kv_raw.reshape(-1, KEY_VALUE_HEADS, 2, HEAD_SIZE)
    key_raw = kv_heads[:, :, 0]
    keys_float = prepare(key_raw, key_scale)
    kv_low = (
        jnp.stack([keys_float, kv_heads[:, :, 1]], axis=2).reshape(-1, kv_width).astype(BF)
    )
    q_raw = dot_nn(normed_mine, q_mine) + dot_nn(normed_other, q_other)
    queries_float = prepare(q_raw, query_scale)
    queries = (queries_float * SCORE_SCALE).astype(BF).reshape(-1, q_width)

    def every_kv(v):
        pair = jnp.stack([v, swap_x(v)], axis=0).reshape(2 * rows, kv_width)
        lined = lax.all_gather(pair, "heads", axis=0)
        mine = (
            lined.reshape(heads_size, 2, rows, kv_width)
            .transpose(1, 0, 2, 3)
            .reshape(2 * block_rows, kv_width)
        )
        return mine, swap_core(mine)

    feeds, mixeds, lses, kvs, hiddens = [], [], [], [], []
    for batch in range(batches):
        span = slice(batch * rows, (batch + 1) * rows)
        kv0, kv1 = every_kv(kv_low[span])
        mixed, lse = attention_forward(kv0, kv1, queries[span], *biases[batch])
        hidden_in = residual_in[span] + merge_core(dot_nt(mixed, o_mine), dot_nt(mixed, o_other))
        feed_rows = apply_norm(hidden_in, feed_scale).astype(BF)
        feed_mine = lax.all_gather(feed_rows, "heads", axis=0, tiled=True)
        feeds.append((feed_mine, swap_core(feed_mine)))
        mixeds.append(mixed)
        lses.append(lse)
        kvs.append((kv0, kv1))
        hiddens.append(hidden_in)

    def hidden_units(feed):
        both = dot_nn(feed, gate_up)
        return both[:, :hidden_part], both[:, hidden_part:]

    layer_rows, d_feeds, acts, d_gate_ups, cots = [], [], [], [], []
    for batch in range(batches):
        span = slice(batch * rows, (batch + 1) * rows)
        cot_mine = lax.all_gather(out_cotangent[span], "heads", axis=0, tiled=True)
        cot_pair = (cot_mine, swap_core(cot_mine))
        outs = []
        for feed, cot in zip(feeds[batch], cot_pair):
            gate_pre, up_pre = hidden_units(feed)
            sig = jax.nn.sigmoid(gate_pre)
            silu = gate_pre * sig
            act = (silu * up_pre).astype(BF)
            d_act = dot_nn(cot, down)
            d_gate = d_act * up_pre * sig * (1.0 + gate_pre * (1.0 - sig))
            d_up = d_act * silu
            d_gate_up = jnp.concatenate([d_gate, d_up], axis=1).astype(BF)
            out = dot_nt(act, down).astype(BF)
            d_feed = dot_nt(d_gate_up, gate_up).astype(BF)
            acts.append(act)
            d_gate_ups.append(d_gate_up)
            cots.append(cot)
            outs.append((out, d_feed))
        (out_mine, d_feed_mine), (out_other, d_feed_other) = outs
        d_feed = lax.psum_scatter(
            d_feed_mine + swap_core(d_feed_other), "heads", scatter_dimension=0, tiled=True
        )
        feed_out = lax.psum_scatter(
            out_mine + swap_core(out_other), "heads", scatter_dimension=0, tiled=True
        )
        layer_rows.append((hiddens[batch] + feed_out.astype(F32)).astype(BF))
        d_feeds.append(d_feed.astype(F32))

    feed_all = jnp.concatenate([f for pair in feeds for f in pair], axis=0)
    act_all = jnp.concatenate(acts, axis=0)
    d_gate_up_all = jnp.concatenate(d_gate_ups, axis=0)
    cot_all = jnp.concatenate(cots, axis=0)

    def blocked(g):
        return g.astype(BF).reshape(dp_size, 2, -1, g.shape[-1])

    g_gate_up = scatter_yx(blocked(dot_tn(feed_all, d_gate_up_all)), True)
    g_down = scatter_yx(blocked(dot_tn(cot_all, act_all)), False)
    g_ffn = jnp.concatenate([g_gate_up, g_down], axis=1)
    part_rows = g_ffn.shape[0] // 2
    g_keep = jnp.where(core == 0, g_ffn[:part_rows], g_ffn[part_rows:])
    g_give = jnp.where(core == 0, g_ffn[part_rows:], g_ffn[:part_rows])
    g_take = swap_core(g_give)
    grads_ffn = []
    for index in range(3):
        cut = slice(index * hidden_part, (index + 1) * hidden_part)
        own, got = g_keep[:, cut], g_take[:, cut]
        grads_ffn.append(
            jnp.where(
                core == 0,
                jnp.concatenate([own, got], axis=1),
                jnp.concatenate([got, own], axis=1),
            ).astype(F32)
        )
    grad_gate, grad_up, grad_down = grads_ffn
    grad_down = grad_down.T

    d_hiddens, d_attendeds, d_queries, d_pairs = [], [], [], []
    grad_feed_gain = 0.0
    for batch in range(batches):
        span = slice(batch * rows, (batch + 1) * rows)
        d_norm, grad_gain = norm_back(hiddens[batch], feed_scale, d_feeds[batch])
        grad_feed_gain = grad_feed_gain + grad_gain
        d_hidden = out_cotangent[span].astype(F32) + d_norm
        d_attended = d_hidden.astype(BF)
        d_mine, d_other = split_core(d_attended)
        d_mixed = (dot_nn(d_mine, o_mine) + dot_nn(d_other, o_other)).astype(BF)
        d_query, d_kv0, d_kv1 = attention_backward(
            *kvs[batch], queries[span], mixeds[batch], d_mixed, *biases[batch], lses[batch]
        )
        lined = (d_kv0 + swap_core(d_kv1)).reshape(2, heads_size, rows, kv_width)
        lined = lined.transpose(1, 0, 2, 3).reshape(heads_size * 2 * rows, kv_width)
        pair = lax.psum_scatter(lined, "heads", scatter_dimension=0, tiled=True)
        d_pairs.append(pair[:rows] + swap_x(pair[rows:]))
        d_hiddens.append(d_hidden)
        d_attendeds.append((d_mine, d_other))
        d_queries.append(d_query)

    mixed_all = jnp.concatenate(mixeds, axis=0)
    d_mine_all = jnp.concatenate([pair[0] for pair in d_attendeds], axis=0)
    d_other_all = jnp.concatenate([pair[1] for pair in d_attendeds], axis=0)
    d_hidden_all = jnp.concatenate(d_hiddens, axis=0)
    d_query_all = jnp.concatenate(d_queries, axis=0)
    d_pair_all = jnp.concatenate(d_pairs, axis=0)

    def rows_scatter(mine, other, x_last):
        held = mine.astype(BF) + swap_core(other.astype(BF))
        return scatter_yx(held.reshape(dp_size, 2, -1, held.shape[-1]), x_last)

    g_o = rows_scatter(dot_tn(d_mine_all, mixed_all), dot_tn(d_other_all, mixed_all), True)
    grad_output = lax.psum_scatter(g_o, "heads", scatter_dimension=0, tiled=True).astype(F32).T

    def head_norm_back(raw, gain, grad):
        unused, pull = jax.vjp(prepare, raw, gain)
        return pull(grad)

    d_q_raw, grad_query_gain = head_norm_back(
        q_raw, query_scale, d_query_all.reshape(-1, QUERY_HEADS, HEAD_SIZE)
    )
    d_q_raw = d_q_raw.astype(BF)
    g_q = rows_scatter(dot_tn(normed_mine, d_q_raw), dot_tn(normed_other, d_q_raw), False)
    grad_query = lax.psum_scatter(g_q, "heads", scatter_dimension=1, tiled=True).astype(F32)

    d_kv_heads = d_pair_all.astype(F32).reshape(-1, KEY_VALUE_HEADS, 2, HEAD_SIZE)
    d_key_raw, grad_key_gain = head_norm_back(
        key_raw.reshape(key_raw.shape[0], -1), key_scale, d_kv_heads[:, :, 0]
    )
    d_kv_raw = (
        jnp.stack([d_key_raw.reshape(-1, KEY_VALUE_HEADS, HEAD_SIZE), d_kv_heads[:, :, 1]], axis=2)
        .reshape(-1, kv_width)
        .astype(BF)
    )
    d_normed = merge_core(
        dot_nt(d_q_raw, q_mine) + dot_nt(d_kv_raw, kv_mine),
        dot_nt(d_q_raw, q_other) + dot_nt(d_kv_raw, kv_other),
    )
    d_input, grad_attention_gain = norm_back(residual_in, attention_scale, d_normed)
    input_rows = d_hidden_all + d_input

    head_grads = jnp.concatenate([grad_query_gain, grad_key_gain]).reshape(-1, per_head)
    head_column = relative(jnp.pad(head_grads, ((0, 0), (0, small - per_head))).reshape(1, width))
    gain_mine, gain_other = split_core(
        jnp.concatenate([grad_attention_gain[None], grad_feed_gain[None], head_column], axis=0)
    )

    def with_gains(grad, gain):
        return jnp.concatenate([grad, jnp.pad(gain.T, ((0, 0), (0, LANES - 3)))], axis=1)

    g_kv = rows_scatter(
        with_gains(dot_tn(normed_mine, d_kv_raw), gain_mine),
        with_gains(dot_tn(normed_other, d_kv_raw), gain_other),
        True,
    )
    g_kv = lax.psum_scatter(g_kv, "heads", scatter_dimension=0, tiled=True).astype(F32)
    grad_key_value = (
        g_kv[:, :kv_width]
        .reshape(small, KEY_VALUE_HEADS, 2, HEAD_SIZE)
        .transpose(0, 2, 1, 3)
        .reshape(small, kv_width)
    )

    layer_out = relative(jnp.concatenate(layer_rows, axis=0)).reshape(tokens.shape)
    tokens_grad = relative(input_rows).reshape(tokens.shape)
    return (
        layer_out,
        tokens_grad,
        g_kv[:, kv_width],
        grad_query,
        grad_key_value,
        g_kv[:per_head, kv_width + 2],
        grad_output,
        g_kv[:, kv_width + 1],
        grad_gate,
        grad_up,
        grad_down,
    )


def solution(mesh):
    every = ("dp", "seq", "heads")
    token_spec = P(None, "dp", ("seq", "heads"), None)
    return jax.shard_map(
        on_device,
        mesh=mesh,
        in_specs=(
            token_spec,
            P(None, "dp", None),
            P(every),
            P(("dp", "seq"), "heads"),
            P(every, None),
            P(every),
            P(None, every),
            P(every),
            P(("dp", "seq"), "heads"),
            P(("dp", "seq"), "heads"),
            P("heads", ("dp", "seq")),
            token_spec,
        ),
        out_specs=(
            token_spec,
            token_spec,
            P(every),
            P(("dp", "seq"), "heads"),
            P(every, None),
            P(every),
            P(None, every),
            P(every),
            P(("dp", "seq"), "heads"),
            P(("dp", "seq"), "heads"),
            P("heads", ("dp", "seq")),
        ),
        check_vma=False,
    )
```

time: 2300 us -> 1200 us (0.52)
  waiting for transfers between devices: 1560 us -> 539 us
  matrix products: 410 us -> 182 us
  local copies, waits for them, and re-layouts: 49.7 us -> 182 us
  blocking collectives: 115 us -> 0 us
  Pallas kernels: 0 us -> 65.8 us
  starting transfers between devices: 15.7 us -> 62 us
    reduce_scatter x18 -> x8, waiting for transfers between devices: 1030 us -> 78.2 us  [the longest x2 42.4 us: on_device(): lax.psum_scatter(d_feed_mine + swap_core(d_feed_other), 'heads', scatter_...]
    all_gather x14 -> x6, waiting for transfers between devices: 486 us -> 90.6 us  [the longest x2 46.3 us: on_device(): cot_mine = lax.all_gather(out_cotangent[span], 'heads', axis=0, tiled=True)]
    ppermute x0 -> x59, waiting for transfers between devices: none -> 352 us  [the longest x10 164 us: swap_y(): return lax.ppermute(v, 'dp', [(0, 1), (1, 0)])]
    dot_general x56 -> x40, matrix products: 410 us -> 182 us  [the longest x16 63.9 us: dot_nt(): lax.dot_general(left, right, (((1,), (1,)), ((), ())), preferred_element_...]
    unnamed x2 -> x0, blocking collectives: 84.5 us -> none
    pallas_call x0 -> x4, Pallas kernels: none -> 65.8 us  [the longest x2 45.6 us: attention_backward(): pl.pallas_call(attention_backward_kernel, grid=(KEY_VALUE_HEADS,), in_spe...]
    ppermute x0 -> x59, starting transfers between devices: none -> 60.1 us  [the longest x14 19.3 us: swap_x(): return lax.ppermute(v, 'seq', [(i, i ^ 2) for i in range(4)])]
    reshape x2 -> x18, local copies, waits for them, and re-layouts: 1.37 us -> 39.7 us  [the longest x1 8.57 us: on_device(): gather_yx(ffn_rows[:, 2 * hidden_part:], False).reshape(width, hidden_part)]
  transfers between devices with their start and end apart: 35 -> 74, of which waited for: 30 -> 32; matrix products, arithmetic and copies ran while one was open for 19% -> 38% of each run, Pallas kernels for 0% -> 6%
where the time goes in v1:
time: 1200 us; the launch traced here: 1190 us
  waiting for transfers between devices  539 us (45%)
  local copies, waits for them, and re-layouts  182 us (15%)
  matrix products  182 us (15%)
  other arithmetic  139 us (12%)
  Pallas kernels  65.8 us (5%)
  starting transfers between devices  62 us (5%)
  between operations  16.7 us (1%)
    ppermute x10, waiting for transfers between devices, swap_y(): return lax.ppermute(v, 'dp', [(0, 1), (1, 0)])  164 us
    ppermute x14, waiting for transfers between devices, swap_x(): return lax.ppermute(v, 'seq', [(i, i ^ 2) for i in range(4)])  135 us
    dot_general x16, matrix products, dot_nt(): lax.dot_general(left, right, (((1,), (1,)), ((), ())), preferred_element_...  63.9 us
    dot_general x16, matrix products, dot_nn(): lax.dot_general(left, right, (((1,), (0,)), ((), ())), preferred_element_...  59.5 us
    dot_general x8, matrix products, dot_tn(): lax.dot_general(left, right, (((0,), (0,)), ((), ())), preferred_element_...  58.5 us
    all_gather x2, waiting for transfers between devices, on_device(): cot_mine = lax.all_gather(out_cotangent[span], 'heads', axis=0, tiled=True)  46.3 us
    pallas_call x2, Pallas kernels, attention_backward(): pl.pallas_call(attention_backward_kernel, grid=(KEY_VALUE_HEADS,), in_spe...  45.6 us
    all_gather x2, waiting for transfers between devices, on_device(): feed_mine = lax.all_gather(feed_rows, 'heads', axis=0, tiled=True)  44.2 us
  transfers between devices with their start and end apart: 74, of which 32 were waited for; matrix products, arithmetic and copies ran while one was open for 38% of the time, Pallas kernels for 6%

profile of v1, /device:TPU:0, one launch (start us, length us, event | category | flops | bytes accessed | tf_op | source)
XLA Modules:
  0.0 1186.2 jit_solution(2114198792723606142)
XLA Ops:
  23.3 5.5 collective-permute-done.3
  30.2 5.6 collective-permute-done.4
  37.6 8.8 collective-permute-done.5
  51.9 5.3 collective-permute-start.18
  59.0 8.3 collective-permute-done.6
  76.0 7.4 collective-permute-done.13
  132.8 16.4 %collective-permute-done.22 = bf16[64,1792]{1,0:T(8,128)(2,1)S(1)} collective-permute-done((bf16[64,1792]{1,0:T(8,128)(2,1)S(1)}, bf16[64,1792]{1,0:T(8,128)(2,1)S(1)}, u32[]{:S(2)}, u32[]{:S(2)}) %collective-permute-start.22) | collective-permute-done | bytes 229408 | tf_op jit(solution)/shard_map/ppermute | solution.py:271
  151.8 12.7 %collective-permute-done.16 = bf16[2,256,1792]{1,2,0:T(8,128)(2,1)} collective-permute-done((bf16[2,256,1792]{1,2,0:T(8,128)(2,1)}, bf16[2,256,1792]{1,2,0:T(8,128)(2,1)}, u32[]{:S(2)}, u32[]{:S(2)}) %collective-permute-start.16) | collective-permute-done | bytes 1835040 | tf_op jit(solution)/shard_map/ppermute | solution.py:256
  168.1 6.1 copy.250
  175.7 7.7 collective-permute-done.23
  195.7 27.5 %collective-permute-done.24 = bf16[2,256,1792]{2,1,0:T(8,128)(2,1)} collective-permute-done((bf16[2,256,1792]{2,1,0:T(8,128)(2,1)}, bf16[2,256,1792]{2,1,0:T(8,128)(2,1)}, u32[]{:S(2)}, u32[]{:S(2)}) %collective-permute-start.24) | collective-permute-done | bytes 1835040 | tf_op jit(solution)/shard_map/ppermute | solution.py:262
  253.2 10.2 attention_forward.2
  276.4 10.1 attention_forward.3
  307.4 6.1 maximum_select_fusion
  319.9 34.0 %collective-permute-done.27 = bf16[512,1600]{0,1:T(8,128)(2,1)} collective-permute-done((bf16[512,1600]{0,1:T(8,128)(2,1)}, bf16[512,1600]{0,1:T(8,128)(2,1)}, u32[]{:S(2)}, u32[]{:S(2)}) %collective-permute-start.27) | collective-permute-done | bytes 1638432 | tf_op jit(solution)/shard_map/ppermute | solution.py:256
  353.9 5.1 fusion.165
  362.3 86.2 %collective-permute-done.29 = bf16[512,800]{0,1:T(8,128)(2,1)S(1)} collective-permute-done((bf16[512,800]{0,1:T(8,128)(2,1)S(1)}, bf16[512,800]{0,1:T(8,128)(2,1)S(1)}, u32[]{:S(2)}, u32[]{:S(2)}) %collective-permute-start.29) | collective-permute-done | bytes 819232 | tf_op jit(solution)/shard_map/ppermute | solution.py:262
  452.5 34.1 %collective-permute-done.30 = bf16[2,512,800]{1,2,0:T(8,128)(2,1)} collective-permute-done((bf16[2,512,800]{1,2,0:T(8,128)(2,1)}, bf16[2,512,800]{1,2,0:T(8,128)(2,1)}, u32[]{:S(2)}, u32[]{:S(2)}) %collective-permute-start.30) | collective-permute-done | bytes 1638432 | tf_op jit(solution)/shard_map/ppermute | solution.py:256
  488.8 5.2 copy.260
  494.0 8.6 reshape.620
  502.6 6.2 pad_maximum_fusion
  508.7 9.6 copy.259
  518.4 7.3 fusion.196
  525.7 5.2 multiply_convert_fusion.5
  544.8 5.2 fusion.50
  550.1 42.4 %reduce-scatter.16.cloned.1.call-done = bf16[128,2048]{1,0:T(8,128)(2,1)} async-done(((bf16[512,2048]{1,0:T(8,128)(2,1)}), bf16[128,2048]{1,0:T(8,128)(2,1)}) %reduce-scatter.16.cloned.1.call-update) | async-done | bytes 524304 | tf_op jit(solution)/shard_map/reduce_scatter | solution.py:472
  597.3 44.2 %all-gather.13.cloned.1.call-done = bf16[512,2048]{1,0:T(8,128)(2,1)} async-done(((bf16[128,2048]{1,0:T(8,128)(2,1)}), bf16[512,2048]{1,0:T(8,128)(2,1)}) %all-gather.13.cloned.1.call-update) | async-done | bytes 2097168 | tf_op jit(solution)/shard_map/all_gather | solution.py:439
  641.5 46.3 %all-gather.17.cloned.1.call-done = bf16[512,2048]{1,0:T(8,128)(2,1)} async-done(((bf16[128,2048]{1,0:T(8,128)(2,1)}), bf16[512,2048]{1,0:T(8,128)(2,1)}) %all-gather.17.cloned.1.call-update) | async-done | bytes 2097168 | tf_op jit(solution)/shard_map/all_gather | solution.py:453
  687.8 7.3 fusion.199
  699.8 7.6 convolution_convert_fusion.4
  716.4 5.2 fusion.51
  735.0 6.1 convolution_convert_fusion.8
  741.2 11.1 fusion.36
  752.3 8.5 reshape.640
  760.8 9.0 fusion.176
  773.0 5.3 fusion.49
  778.6 32.2 %fusion.16 = bf16[2048,1600]{0,1:T(8,128)(2,1)} fusion(bf16[512,2048]{1,0:T(8,128)(2,1)} %collective-permute-done.35, bf16[512,2048]{1,0:T(8,128)(2,1)} %all-gather.13.cloned.1.call-done, bf16[512,2048]{1,0:T(8,128)(2,1)} %collective-permute-done.31, bf16[512,2048]{1,0:T(8,128)(2,1)} %all-gather.9.cloned.1.call-done, bf16[512,800]{0,1:T(8,128)(2,1)} %copy-done.139, ...), kind=kOutput, calls=%fused_computation.16 | convolution fusion | flops 13511032832 | bytes 21495808 | tf_op jit(solution)/shard_map/dot_general | solution.py:34
  810.8 5.4 fusion.173
  821.8 33.4 %reduce-scatter.14.cloned.1.call-done = bf16[128,2048]{1,0:T(8,128)(2,1)} async-done(((bf16[512,2048]{1,0:T(8,128)(2,1)}), bf16[128,2048]{1,0:T(8,128)(2,1)}) %reduce-scatter.14.cloned.1.call-update) | async-done | bytes 524304 | tf_op jit(solution)/shard_map/reduce_scatter | solution.py:475
  855.3 5.1 fusion.166
  886.0 22.8 %attention_backward.3 = (f32[128,1792]{1,0:T(8,128)S(1)}, bf16[1024,896]{1,0:T(8,128)(2,1)S(1)}, bf16[1024,896]{1,0:T(8,128)(2,1)}) custom-call(bf16[1024,896]{1,0:T(8,128)(2,1)} %bitcast.88.kv0, bf16[1024,896]{1,0:T(8,128)(2,1)} %collective-permute-done.34.kv1, bf16[128,1792]{1,0:T(8,128)(2,1)S(1)} %copy-done.9, ...), custom_call_target="tpu_custom_call" | custom-call | flops 18790481920 | bytes 9633792 | tf_op jit(solution)/shard_map/attention_backward/pallas_call | solution.py:157
  915.0 22.8 %attention_backward.2 = (f32[128,1792]{1,0:T(8,128)S(1)}, bf16[1024,896]{1,0:T(8,128)(2,1)S(1)}, bf16[1024,896]{1,0:T(8,128)(2,1)}) custom-call(bf16[1024,896]{1,0:T(8,128)(2,1)} %bitcast.370, bf16[1024,896]{1,0:T(8,128)(2,1)} %collective-permute-done.9.kv1, bf16[128,1792]{1,0:T(8,128)(2,1)S(1)} %copy-done.8, bf16[128,1792]{1,0:T(8,128)(2,1)S(1)} %get-tuple-element.21.mixed, ...), custom_call_target="tpu_custom_call" | custom-call | flops 18790481920 | bytes 9633792 | tf_op jit(solution)/shard_map/attention_backward/pallas_call | solution.py:157
  973.9 8.9 collective-permute-done.57
  995.2 14.2 %collective-permute-done.55 = bf16[512,1600]{0,1:T(8,128)(2,1)} collective-permute-done((bf16[512,1600]{0,1:T(8,128)(2,1)}, bf16[512,1600]{0,1:T(8,128)(2,1)}, u32[]{:S(2)}, u32[]{:S(2)}) %collective-permute-start.55) | collective-permute-done | bytes 1638432 | tf_op jit(solution)/shard_map/ppermute | solution.py:256
  1035.0 13.7 %collective-permute-done.49 = bf16[2,256,1792]{1,2,0:T(8,128)(2,1)} collective-permute-done((bf16[2,256,1792]{1,2,0:T(8,128)(2,1)}, bf16[2,256,1792]{1,2,0:T(8,128)(2,1)}, u32[]{:S(2)}, u32[]{:S(2)}) %collective-permute-start.49) | collective-permute-done | bytes 1835040 | tf_op jit(solution)/shard_map/ppermute | solution.py:256
  1089.8 12.4 %collective-permute-done.50 = bf16[256,1792]{0,1:T(8,128)(2,1)S(1)} collective-permute-done((bf16[256,1792]{0,1:T(8,128)(2,1)S(1)}, bf16[256,1792]{0,1:T(8,128)(2,1)S(1)}, u32[]{:S(2)}, u32[]{:S(2)}) %collective-permute-start.50) | collective-permute-done | bytes 917536 | tf_op jit(solution)/shard_map/ppermute | solution.py:262
  1116.0 16.3 %collective-permute-done.46 = bf16[2,256,1024]{1,2,0:T(8,128)(2,1)} collective-permute-done((bf16[2,256,1024]{1,2,0:T(8,128)(2,1)}, bf16[2,256,1024]{1,2,0:T(8,128)(2,1)}, u32[]{:S(2)}, u32[]{:S(2)}) %collective-permute-start.46) | collective-permute-done | bytes 1048608 | tf_op jit(solution)/shard_map/ppermute | solution.py:262
  1158.4 17.7 %reduce-scatter.28.cloned.1.call-done = bf16[64,1024]{1,0:T(8,128)(2,1)} async-done(((bf16[256,1024]{1,0:T(8,128)(2,1)}), bf16[64,1024]{1,0:T(8,128)(2,1)}) %reduce-scatter.28.cloned.1.call-update) | async-done | bytes 131088
  (688 shorter events, 427.1 us)
Async XLA Ops:
  7.2 223.2 %all-gather.7.cloned.1.call-start = ((), (), s32[]{:S(2)}) async-start(), calls=%async_computation.9 | async-start | bytes 2293760 | tf_op jit(solution)/shard_map/all_gather | solution.py:424
  48.2 24.5 %collective-permute-start.10 = (bf16[256,448]{0,1:T(8,128)(2,1)}, bf16[256,448]{0,1:T(8,128)(2,1)}, u32[]{:S(2)}, u32[]{:S(2)}) collective-permute-start(bf16[256,448]{0,1:T(8,128)(2,1)} %param.15), channel_id=1, source_target_pairs={{0,1},{1,2},{2,3},{4,5},{5,6},{6,7},{8,9},{9,10},{10,11},{12,13},{... | collective-permute-start | bytes 688136 | tf_op jit(solution)/shard_map/ppermute | solution.py:267
  50.6 22.7 %collective-permute-start.12 = (bf16[256,448]{0,1:T(8,128)(2,1)}, bf16[256,448]{0,1:T(8,128)(2,1)}, u32[]{:S(2)}, u32[]{:S(2)}) collective-permute-start(bf16[256,448]{0,1:T(8,128)(2,1)} %param.15), channel_id=1, source_target_pairs={{1,0},{2,1},{3,2},{5,4},{6,5},{7,6},{9,8},{10,9},{11,10},{13,12},{... | collective-permute-start | bytes 688136 | tf_op jit(solution)/shard_map/ppermute | solution.py:268
  51.9 70.8 %collective-permute-start.18 = (bf16[64,1792]{1,0:T(8,128)(2,1)}, bf16[64,1792]{1,0:T(8,128)(2,1)}, u32[]{:S(2)}, u32[]{:S(2)}) collective-permute-start(bf16[64,1792]{1,0:T(8,128)(2,1)} %bitcast.56), channel_id=1, source_target_pairs={{0,1},{1,2},{2,3},{4,5},{5,6},{6,7},{8,9},{9,10},{10,11},{12,13},{... | collective-permute-start | bytes 688136 | tf_op jit(solution)/shard_map/ppermute | solution.py:267
  57.2 66.2 %collective-permute-start.20 = (bf16[64,1792]{1,0:T(8,128)(2,1)}, bf16[64,1792]{1,0:T(8,128)(2,1)}, u32[]{:S(2)}, u32[]{:S(2)}) collective-permute-start(bf16[64,1792]{1,0:T(8,128)(2,1)} %bitcast.56), channel_id=1, source_target_pairs={{1,0},{2,1},{3,2},{5,4},{6,5},{7,6},{9,8},{10,9},{11,10},{13,12},{... | collective-permute-start | bytes 688136 | tf_op jit(solution)/shard_map/ppermute | solution.py:268
  72.3 27.0 %collective-permute-start.7 = (bf16[1024,1024]{0,1:T(8,128)(2,1)}, bf16[1024,1024]{0,1:T(8,128)(2,1)}, u32[]{:S(2)}, u32[]{:S(2)}) collective-permute-start(bf16[1024,1024]{0,1:T(8,128)(2,1)} %copy.242), channel_id=1, source_target_pairs={{0,4},{4,0},{8,12},{12,8},{1,5},{5,1},{9,13},{13,9},{2,6},{6,2},{1... | collective-permute-start | bytes 6291464 | tf_op jit(solution)/shard_map/ppermute | solution.py:259
  121.2 43.3 %collective-permute-start.16 = (bf16[2,256,1792]{1,2,0:T(8,128)(2,1)}, bf16[2,256,1792]{1,2,0:T(8,128)(2,1)}, u32[]{:S(2)}, u32[]{:S(2)}) collective-permute-start(bf16[2,256,1792]{1,2,0:T(8,128)(2,1)} %get-tuple-element.159), channel_id=1, source_target_pairs={{0,8},{4,12},{8,0},{12,4},{1,9},{5,13},{9,1},{13,5},{2,10},{6,14},... | collective-permute-start | bytes 5505032 | tf_op jit(solution)/shard_map/ppermute | solution.py:256
  127.5 105.2 %all-gather.11.cloned.1.call-start = ((), (), s32[]{:S(2)}) async-start(), calls=%async_computation.12 | async-start | bytes 2293760 | tf_op jit(solution)/shard_map/all_gather | solution.py:424
  151.7 31.7 %collective-permute-start.23 = (bf16[256,1792]{1,0:T(8,128)(2,1)}, bf16[256,1792]{1,0:T(8,128)(2,1)}, u32[]{:S(2)}, u32[]{:S(2)}) collective-permute-start(bf16[256,1792]{1,0:T(8,128)(2,1)} %bitcast.62), channel_id=1, source_target_pairs={{0,8},{4,12},{8,0},{12,4},{1,9},{5,13},{9,1},{13,5},{2,10},{6,14},... | collective-permute-start | bytes 2752520 | tf_op jit(solution)/shard_map/ppermute | solution.py:256
  174.2 62.0 %collective-permute-start.17 = (bf16[1024,1792]{1,0:T(8,128)(2,1)}, bf16[1024,1792]{1,0:T(8,128)(2,1)}, u32[]{:S(2)}, u32[]{:S(2)}) collective-permute-start(bf16[1024,1792]{1,0:T(8,128)(2,1)} %bitcast.376), channel_id=1, source_target_pairs={{0,4},{4,0},{8,12},{12,8},{1,5},{5,1},{9,13},{13,9},{2,6},{6,2},{1... | collective-permute-start | bytes 11010056 | tf_op jit(solution)/shard_map/ppermute | solution.py:259
  186.4 36.8 %collective-permute-start.24 = (bf16[2,256,1792]{2,1,0:T(8,128)(2,1)}, bf16[2,256,1792]{2,1,0:T(8,128)(2,1)}, u32[]{:S(2)}, u32[]{:S(2)}) collective-permute-start(bf16[2,256,1792]{2,1,0:T(8,128)(2,1)} %get-tuple-element.155), channel_id=1, source_target_pairs={{0,16},{16,0},{1,17},{17,1},{2,18},{18,2},{3,19},{19,3},{4,20},{20... | collective-permute-start | bytes 5505032 | tf_op jit(solution)/shard_map/ppermute | solution.py:262
  190.7 261.3 %all-gather.9.cloned.1.call-start = ((), (), s32[]{:S(2)}) async-start(), calls=%async_computation.10 | async-start | bytes 2621440 | tf_op jit(solution)/shard_map/all_gather | solution.py:439
  195.6 111.8 %collective-permute-start.26 = (bf16[256,2400]{0,1:T(8,128)(2,1)}, bf16[256,2400]{0,1:T(8,128)(2,1)}, u32[]{:S(2)}, u32[]{:S(2)}) collective-permute-start(bf16[256,2400]{0,1:T(8,128)(2,1)} %pad_maximum_fusion.13), channel_id=1, source_target_pairs={{0,4},{4,0},{8,12},{12,8},{1,5},{5,1},{9,13},{13,9},{2,6},{6,2},{1... | collective-permute-start | bytes 3686408 | tf_op jit(solution)/shard_map/ppermute | solution.py:259
  226.9 36.5 %collective-permute-start.25 = (bf16[1024,1792]{1,0:T(8,128)(2,1)}, bf16[1024,1792]{1,0:T(8,128)(2,1)}, u32[]{:S(2)}, u32[]{:S(2)}) collective-permute-start(bf16[1024,1792]{1,0:T(8,128)(2,1)} %bitcast.67), channel_id=1, source_target_pairs={{0,4},{4,0},{8,12},{12,8},{1,5},{5,1},{9,13},{13,9},{2,6},{6,2},{1... | collective-permute-start | bytes 11010056 | tf_op jit(solution)/shard_map/ppermute | solution.py:259
  235.6 40.8 %collective-permute-start.34 = (bf16[1024,896]{1,0:T(8,128)(2,1)}, bf16[1024,896]{1,0:T(8,128)(2,1)}, u32[]{:S(2)}, u32[]{:S(2)}) collective-permute-start(bf16[1024,896]{1,0:T(8,128)(2,1)} %bitcast.88.kv0), channel_id=1, source_target_pairs={{0,4},{4,0},{8,12},{12,8},{1,5},{5,1},{9,13},{13,9},{2,6},{6,2},{1... | collective-permute-start | bytes 5505032 | tf_op jit(solution)/shard_map/ppermute | solution.py:259
  307.3 144.7 %all-gather.15.cloned.1.call-start = ((), (), s32[]{:S(2)}) async-start(), calls=%async_computation.15 | async-start | bytes 2621440 | tf_op jit(solution)/shard_map/all_gather | solution.py:453
  316.0 37.9 %collective-permute-start.27 = (bf16[512,1600]{0,1:T(8,128)(2,1)}, bf16[512,1600]{0,1:T(8,128)(2,1)}, u32[]{:S(2)}, u32[]{:S(2)}) collective-permute-start(bf16[512,1600]{0,1:T(8,128)(2,1)} %get-tuple-element.140), channel_id=1, source_target_pairs={{0,8},{4,12},{8,0},{12,4},{1,9},{5,13},{9,1},{13,5},{2,10},{6,14},... | collective-permute-start | bytes 4915208 | tf_op jit(solution)/shard_map/ppermute | solution.py:256
  319.8 272.7 %reduce-scatter.16.cloned.1.call-start = ((), (), s32[]{:S(2)}) async-start(), calls=%async_computation.16 | async-start | bytes 2621440 | tf_op jit(solution)/shard_map/reduce_scatter | solution.py:472
  359.0 143.6 %collective-permute-start.28 = (bf16[2,512,1600]{1,2,0:T(8,128)(2,1)}, bf16[2,512,1600]{1,2,0:T(8,128)(2,1)}, u32[]{:S(2)}, u32[]{:S(2)}) collective-permute-start(bf16[2,512,1600]{1,2,0:T(8,128)(2,1)} %get-tuple-element.134), channel_id=1, source_target_pairs={{0,16},{16,0},{1,17},{17,1},{2,18},{18,2},{3,19},{19,3},{4,20},{20... | collective-permute-start | bytes 9830408 | tf_op jit(solution)/shard_map/ppermute | solution.py:262
  361.8 86.8 %collective-permute-start.29 = (bf16[512,800]{0,1:T(8,128)(2,1)S(1)}, bf16[512,800]{0,1:T(8,128)(2,1)S(1)}, u32[]{:S(2)}, u32[]{:S(2)}) collective-permute-start(bf16[512,800]{0,1:T(8,128)(2,1)S(1)} %get-tuple-element.138), channel_id=1, source_target_pairs={{0,16},{16,0},{1,17},{17,1},{2,18},{18,2},{3,19},{19,3},{4,20},{20... | collective-permute-start | bytes 2457608 | tf_op jit(solution)/shard_map/ppermute | solution.py:262
  450.5 36.1 %collective-permute-start.30 = (bf16[2,512,800]{1,2,0:T(8,128)(2,1)}, bf16[2,512,800]{1,2,0:T(8,128)(2,1)}, u32[]{:S(2)}, u32[]{:S(2)}) collective-permute-start(bf16[2,512,800]{1,2,0:T(8,128)(2,1)} %get-tuple-element.161), channel_id=1, source_target_pairs={{0,8},{4,12},{8,0},{12,4},{1,9},{5,13},{9,1},{13,5},{2,10},{6,14},... | collective-permute-start | bytes 4915208 | tf_op jit(solution)/shard_map/ppermute | solution.py:256
  452.0 66.4 %collective-permute-start.31 = (bf16[512,2048]{1,0:T(8,128)(2,1)}, bf16[512,2048]{1,0:T(8,128)(2,1)}, u32[]{:S(2)}, u32[]{:S(2)}) collective-permute-start(bf16[512,2048]{1,0:T(8,128)(2,1)} %all-gather.9.cloned.1.call-done), channel_id=1, source_target_pairs={{0,4},{4,0},{8,12},{12,8},{1,5},{5,1},{9,13},{13,9},{2,6},{6,2},{1... | collective-permute-start | bytes 6291464 | tf_op jit(solution)/shard_map/ppermute | solution.py:259
  452.0 73.7 %collective-permute-start.37 = (bf16[512,2048]{1,0:T(8,128)(2,1)}, bf16[512,2048]{1,0:T(8,128)(2,1)}, u32[]{:S(2)}, u32[]{:S(2)}) collective-permute-start(bf16[512,2048]{1,0:T(8,128)(2,1)} %all-gather.15.cloned.1.call-done), channel_id=1, source_target_pairs={{0,4},{4,0},{8,12},{12,8},{1,5},{5,1},{9,13},{13,9},{2,6},{6,2},{1... | collective-permute-start | bytes 6291464 | tf_op jit(solution)/shard_map/ppermute | solution.py:259
  550.1 91.4 %all-gather.13.cloned.1.call-start = ((), (), s32[]{:S(2)}) async-start(), calls=%async_computation.13 | async-start | bytes 2621440 | tf_op jit(solution)/shard_map/all_gather | solution.py:439
  596.1 91.8 %all-gather.17.cloned.1.call-start = ((), (), s32[]{:S(2)}) async-start(), calls=%async_computation.17 | async-start | bytes 2621440 | tf_op jit(solution)/shard_map/all_gather | solution.py:453
  596.8 222.7 %reduce-scatter.18.cloned.1.call-start = ((), (), s32[]{:S(2)}) async-start(), calls=%async_computation.18 | async-start | bytes 2621440 | tf_op jit(solution)/shard_map/reduce_scatter | solution.py:472
  641.5 46.3 %collective-permute-start.35 = (bf16[512,2048]{1,0:T(8,128)(2,1)}, bf16[512,2048]{1,0:T(8,128)(2,1)}, u32[]{:S(2)}, u32[]{:S(2)}) collective-permute-start(bf16[512,2048]{1,0:T(8,128)(2,1)} %all-gather.13.cloned.1.call-done), channel_id=1, source_target_pairs={{0,4},{4,0},{8,12},{12,8},{1,5},{5,1},{9,13},{13,9},{2,6},{6,2},{1... | collective-permute-start | bytes 6291464 | tf_op jit(solution)/shard_map/ppermute | solution.py:259
  721.6 100.2 %reduce-scatter.12.cloned.1.call-start = ((), (), s32[]{:S(2)}) async-start(), calls=%async_computation.11 | async-start | bytes 2621440 | tf_op jit(solution)/shard_map/reduce_scatter | solution.py:475
  734.4 120.8 %reduce-scatter.14.cloned.1.call-start = ((), (), s32[]{:S(2)}) async-start(), calls=%async_computation.14 | async-start | bytes 2621440 | tf_op jit(solution)/shard_map/reduce_scatter | solution.py:475
  741.1 31.9 %collective-permute-start.36 = (bf16[512,2048]{1,0:T(8,128)(2,1)}, bf16[512,2048]{1,0:T(8,128)(2,1)}, u32[]{:S(2)}, u32[]{:S(2)}) collective-permute-start(bf16[512,2048]{1,0:T(8,128)(2,1)} %convolution_convert_fusion.8), channel_id=1, source_target_pairs={{0,4},{4,0},{8,12},{12,8},{1,5},{5,1},{9,13},{13,9},{2,6},{6,2},{1... | collective-permute-start | bytes 6291464 | tf_op jit(solution)/shard_map/ppermute | solution.py:259
  771.5 186.6 %collective-permute-start.56 = (bf16[2,512,800]{1,2,0:T(8,128)(2,1)}, bf16[2,512,800]{1,2,0:T(8,128)(2,1)}, u32[]{:S(2)}, u32[]{:S(2)}) collective-permute-start(bf16[2,512,800]{1,2,0:T(8,128)(2,1)} %bitcast.364), channel_id=1, source_target_pairs={{0,8},{4,12},{8,0},{12,4},{1,9},{5,13},{9,1},{13,5},{2,10},{6,14},... | collective-permute-start | bytes 4915208 | tf_op jit(solution)/shard_map/ppermute | solution.py:256
  778.4 248.7 %reduce-scatter.22.cloned.1.call-start = ((), (), s32[]{:S(2)}) async-start(), calls=%async_computation.20 | async-start | bytes 2293760 | tf_op jit(solution)/shard_map/reduce_scatter | solution.py:525
  818.1 148.6 %collective-permute-start.54 = (bf16[2,512,1600]{1,2,0:T(8,128)(2,1)}, bf16[2,512,1600]{1,2,0:T(8,128)(2,1)}, u32[]{:S(2)}, u32[]{:S(2)}) collective-permute-start(bf16[2,512,1600]{1,2,0:T(8,128)(2,1)} %bitcast.363), channel_id=1, source_target_pairs={{0,16},{16,0},{1,17},{17,1},{2,18},{18,2},{3,19},{19,3},{4,20},{20... | collective-permute-start | bytes 9830408 | tf_op jit(solution)/shard_map/ppermute | solution.py:262
  908.8 40.1 %collective-permute-start.43 = (bf16[1024,896]{1,0:T(8,128)(2,1)}, bf16[1024,896]{1,0:T(8,128)(2,1)}, u32[]{:S(2)}, u32[]{:S(2)}) collective-permute-start(bf16[1024,896]{1,0:T(8,128)(2,1)} %get-tuple-element.30), channel_id=1, source_target_pairs={{0,4},{4,0},{8,12},{12,8},{1,5},{5,1},{9,13},{13,9},{2,6},{6,2},{1... | collective-permute-start | bytes 5505032 | tf_op jit(solution)/shard_map/ppermute | solution.py:259
  952.2 79.6 %reduce-scatter.20.cloned.1.call-start = ((), (), s32[]{:S(2)}) async-start(), calls=%async_computation.19 | async-start | bytes 2293760 | tf_op jit(solution)/shard_map/reduce_scatter | solution.py:525
  958.0 26.9 %collective-permute-start.48 = (bf16[1024,1792]{1,0:T(8,128)(2,1)}, bf16[1024,1792]{1,0:T(8,128)(2,1)}, u32[]{:S(2)}, u32[]{:S(2)}) collective-permute-start(bf16[1024,1792]{1,0:T(8,128)(2,1)} %convolution_convert_fusion.2), channel_id=1, source_target_pairs={{0,4},{4,0},{8,12},{12,8},{1,5},{5,1},{9,13},{13,9},{2,6},{6,2},{1... | collective-permute-start | bytes 11010056 | tf_op jit(solution)/shard_map/ppermute | solution.py:259
  966.7 54.2 %collective-permute-start.51 = (bf16[1024,1792]{1,0:T(8,128)(2,1)}, bf16[1024,1792]{1,0:T(8,128)(2,1)}, u32[]{:S(2)}, u32[]{:S(2)}) collective-permute-start(bf16[1024,1792]{1,0:T(8,128)(2,1)} %convolution_convert_fusion), channel_id=1, source_target_pairs={{0,4},{4,0},{8,12},{12,8},{1,5},{5,1},{9,13},{13,9},{2,6},{6,2},{1... | collective-permute-start | bytes 11010056 | tf_op jit(solution)/shard_map/ppermute | solution.py:259
  970.4 38.9 %collective-permute-start.55 = (bf16[512,1600]{0,1:T(8,128)(2,1)}, bf16[512,1600]{0,1:T(8,128)(2,1)}, u32[]{:S(2)}, u32[]{:S(2)}) collective-permute-start(bf16[512,1600]{0,1:T(8,128)(2,1)} %slice_bitcast_fusion), channel_id=1, source_target_pairs={{0,8},{4,12},{8,0},{12,4},{1,9},{5,13},{9,1},{13,5},{2,10},{6,14},... | collective-permute-start | bytes 4915208 | tf_op jit(solution)/shard_map/ppermute | solution.py:256
  973.8 181.1 %reduce-scatter.24.cloned.1.call-start = ((), (), s32[]{:S(2)}) async-start(), calls=%async_computation.21 | async-start | bytes 1146880 | tf_op jit(solution)/shard_map/reduce_scatter | solution.py:554
  993.7 55.0 %collective-permute-start.49 = (bf16[2,256,1792]{1,2,0:T(8,128)(2,1)}, bf16[2,256,1792]{1,2,0:T(8,128)(2,1)}, u32[]{:S(2)}, u32[]{:S(2)}) collective-permute-start(bf16[2,256,1792]{1,2,0:T(8,128)(2,1)} %bitcast.456), channel_id=1, source_target_pairs={{0,8},{4,12},{8,0},{12,4},{1,9},{5,13},{9,1},{13,5},{2,10},{6,14},... | collective-permute-start | bytes 5505032 | tf_op jit(solution)/shard_map/ppermute | solution.py:256
  1013.2 68.6 %collective-permute-start.58 = (bf16[256,2400]{0,1:T(8,128)(2,1)}, bf16[256,2400]{0,1:T(8,128)(2,1)}, u32[]{:S(2)}, u32[]{:S(2)}) collective-permute-start(bf16[256,2400]{0,1:T(8,128)(2,1)} %get-tuple-element.136), channel_id=1, source_target_pairs={{0,4},{4,0},{8,12},{12,8},{1,5},{5,1},{9,13},{13,9},{2,6},{6,2},{1... | collective-permute-start | bytes 3686408 | tf_op jit(solution)/shard_map/ppermute | solution.py:259
  1026.5 57.6 %collective-permute-start.52 = (bf16[2,256,1792]{2,1,0:T(8,128)(2,1)}, bf16[2,256,1792]{2,1,0:T(8,128)(2,1)}, u32[]{:S(2)}, u32[]{:S(2)}) collective-permute-start(bf16[2,256,1792]{2,1,0:T(8,128)(2,1)} %bitcast.134), channel_id=1, source_target_pairs={{0,16},{16,0},{1,17},{17,1},{2,18},{18,2},{3,19},{19,3},{4,20},{20... | collective-permute-start | bytes 5505032 | tf_op jit(solution)/shard_map/ppermute | solution.py:262
  1028.0 25.6 %collective-permute-start.44 = (bf16[128,896]{1,0:T(8,128)(2,1)S(1)}, bf16[128,896]{1,0:T(8,128)(2,1)}, u32[]{:S(2)}, u32[]{:S(2)}) collective-permute-start(bf16[128,896]{1,0:T(8,128)(2,1)S(1)} %slice.558), channel_id=1, source_target_pairs={{0,8},{4,12},{8,0},{12,4},{1,9},{5,13},{9,1},{13,5},{2,10},{6,14},... | collective-permute-start | bytes 688136 | tf_op jit(solution)/shard_map/ppermute | solution.py:256
  1033.5 24.6 %collective-permute-start.42 = (bf16[128,896]{1,0:T(8,128)(2,1)}, bf16[128,896]{1,0:T(8,128)(2,1)}, u32[]{:S(2)}, u32[]{:S(2)}) collective-permute-start(bf16[128,896]{1,0:T(8,128)(2,1)} %slice.556), channel_id=1, source_target_pairs={{0,8},{4,12},{8,0},{12,4},{1,9},{5,13},{9,1},{13,5},{2,10},{6,14},... | collective-permute-start | bytes 688136 | tf_op jit(solution)/shard_map/ppermute | solution.py:256
  1079.3 24.9 %collective-permute-start.45 = (bf16[1024,1024]{0,1:T(8,128)(2,1)}, bf16[1024,1024]{0,1:T(8,128)(2,1)}, u32[]{:S(2)}, u32[]{:S(2)}) collective-permute-start(bf16[1024,1024]{0,1:T(8,128)(2,1)} %fusion.61), channel_id=1, source_target_pairs={{0,4},{4,0},{8,12},{12,8},{1,5},{5,1},{9,13},{13,9},{2,6},{6,2},{1... | collective-permute-start | bytes 6291464 | tf_op jit(solution)/shard_map/ppermute | solution.py:259
  1103.2 53.4 %reduce-scatter.26.cloned.1.call-start = ((), (), s32[]{:S(2)}) async-start(), calls=%async_computation.22 | async-start | bytes 1146880 | tf_op jit(solution)/shard_map/reduce_scatter | solution.py:543
  1107.9 24.4 %collective-permute-start.46 = (bf16[2,256,1024]{1,2,0:T(8,128)(2,1)}, bf16[2,256,1024]{1,2,0:T(8,128)(2,1)}, u32[]{:S(2)}, u32[]{:S(2)}) collective-permute-start(bf16[2,256,1024]{1,2,0:T(8,128)(2,1)} %bitcast.365), channel_id=1, source_target_pairs={{0,16},{16,0},{1,17},{17,1},{2,18},{18,2},{3,19},{19,3},{4,20},{20... | collective-permute-start | bytes 3145736 | tf_op jit(solution)/shard_map/ppermute | solution.py:262
  1113.0 63.1 %reduce-scatter.28.cloned.1.call-start = ((), (), s32[]{:S(2)}) async-start(), calls=%async_computation.23 | async-start | bytes 655360
  (170 other events, 2067.4 us)
Sparse Core Ops, SparseCore 0:
  127.6 41.6 all-gather.6
  190.8 38.6 all-gather.10
  307.5 44.1 all-gather.8
  353.1 44.6 all-gather.14
  550.2 42.3 reduce-scatter.15
  596.2 45.2 all-gather.12
  643.1 44.6 all-gather.16
  721.8 42.4 reduce-scatter.17
  766.6 43.1 reduce-scatter.11
  812.1 43.1 reduce-scatter.13
  952.4 38.7 reduce-scatter.21
  993.3 38.5 reduce-scatter.19
  1103.4 23.6 reduce-scatter.23
  1129.2 24.0 reduce-scatter.25
  1155.5 20.6 reduce-scatter.27

commit v2 on v1

v2 whole, which is shorter than its diff:
```python
import functools
import math

import jax
import jax.numpy as jnp
from jax import lax
from jax.experimental import pallas as pl
from jax.experimental.pallas import tpu as pltpu
from jax.sharding import PartitionSpec as P

QUERY_HEADS = 28
KEY_VALUE_HEADS = 7
HEAD_SIZE = 64
GROUP = QUERY_HEADS // KEY_VALUE_HEADS
GROUP_WIDTH = GROUP * HEAD_SIZE
Q_WIDTH = QUERY_HEADS * HEAD_SIZE
KV_WIDTH = 2 * KEY_VALUE_HEADS * HEAD_SIZE

EPSILON = 1e-06
SCORE_SCALE = 0.125
MASKED = -1e30
LANES = 128
CHUNK = 256
BLOCK = 256
FFN_ROWS = 256
ATTENTION_GAIN, FEED_GAIN, HEAD_GAIN = 0, 1, 2

BF = jnp.bfloat16
F32 = jnp.float32


def dot_nn(left, right):
    return lax.dot_general(left, right, (((1,), (0,)), ((), ())), preferred_element_type=F32)


def dot_nt(left, right):
    return lax.dot_general(left, right, (((1,), (1,)), ((), ())), preferred_element_type=F32)


def dot_tn(left, right):
    return lax.dot_general(left, right, (((0,), (0,)), ((), ())), preferred_element_type=F32)


def shape(dims, kind):
    return jax.ShapeDtypeStruct(dims, kind)


def whole(array):
    dims = array.shape
    return pl.BlockSpec(
        dims, lambda *unused: (0,) * len(dims), pipeline_mode=pl.Buffered(1)
    )


def fixed_out(dims):
    return pl.BlockSpec(dims, lambda *unused: (0,) * len(dims))


def kernel_call(body, name, grid, in_specs, out_specs, out_shape, scratch, flops, table=None):
    outs = out_shape if isinstance(out_shape, (list, tuple)) else [out_shape]
    moved = sum(math.prod(o.shape) * jnp.dtype(o.dtype).itemsize for o in outs)
    kwargs = dict(
        out_shape=out_shape,
        compiler_params=pltpu.CompilerParams(
            dimension_semantics=("arbitrary",) * len(grid), vmem_limit_bytes=56 * 1024 * 1024
        ),
        name=name,
    )

    def call(*operands):
        size = moved + sum(math.prod(o.shape) * o.dtype.itemsize for o in operands)
        cost = pl.CostEstimate(
            flops=flops,
            bytes_accessed=size,
            transcendentals=0,
        )
        if table is None:
            return pl.pallas_call(
                body,
                grid=grid,
                in_specs=in_specs,
                out_specs=out_specs,
                scratch_shapes=scratch,
                cost_estimate=cost,
                **kwargs,
            )(*operands)
        return pl.pallas_call(
            body,
            grid_spec=pltpu.PrefetchScalarGridSpec(
                num_scalar_prefetch=1,
                grid=grid,
                in_specs=in_specs,
                out_specs=out_specs,
                scratch_shapes=scratch,
            ),
            cost_estimate=cost,
            **kwargs,
        )(table, *operands)

    return call


def half_lanes(rows):
    return lax.broadcasted_iota(jnp.int32, (rows, LANES), 1) < HEAD_SIZE


def half_means(values, low):
    first = jnp.sum(jnp.where(low, values, 0.0), axis=1, keepdims=True) / HEAD_SIZE
    second = jnp.sum(jnp.where(low, 0.0, values), axis=1, keepdims=True) / HEAD_SIZE
    return jnp.where(low, first, second)


def turn(values):
    lane = lax.broadcasted_iota(jnp.int32, values.shape, 1)
    early = (lane & (HEAD_SIZE // 2)) == 0
    return jnp.where(
        early, pltpu.roll(values, LANES - HEAD_SIZE // 2, 1), pltpu.roll(values, HEAD_SIZE // 2, 1)
    )


def head_norm(tile, gain, cosine, sine, low):
    normed = tile * lax.rsqrt(half_means(tile * tile, low) + EPSILON) * gain
    return normed * cosine + turn(normed) * sine


def head_norm_back(tile, gain, cosine, sine, low, grad):
    grad = grad * cosine - turn(grad) * sine
    scale = lax.rsqrt(half_means(tile * tile, low) + EPSILON)
    lifted = grad * gain
    dots = half_means(tile * lifted, low)
    d_tile = scale * lifted - tile * (scale * scale * scale) * dots
    return d_tile, jnp.sum(grad * tile * scale, axis=0, keepdims=True)


def place(table, j):
    return pl.ds(pl.multiple_of(table[j] * BLOCK, BLOCK), BLOCK)


def span(j, size=BLOCK):
    return slice(j * size, (j + 1) * size)


def over_pieces(left, pieces, columns=None):
    total, start = None, 0
    for piece in pieces:
        size = piece.shape[0]
        right = piece[...] if columns is None else piece[:, columns]
        term = dot_nn(left[:, start : start + size], right)
        total = term if total is None else total + term
        start += size
    return total


def add_back(target, left, pieces, columns=None):
    start = 0
    for piece in pieces:
        size = piece.shape[0]
        right = piece[...] if columns is None else piece[:, columns]
        target[:, start : start + size] += dot_nt(left, right)
        start += size


def key_value_kernel(table, tokens, cosine, sine, gain, *refs):
    kvg = refs[:-4]
    normed, kv_raw, kv_low, gains = refs[-4:]
    rows, width = tokens.shape
    count = width // BLOCK
    columns = jnp.concatenate([part[:, KV_WIDTH:].astype(F32).T for part in kvg], axis=1)
    gains[...] = columns[:8]
    squares = 0.0
    for j in range(count):
        block = tokens[:, place(table, j)].astype(F32)
        squares = squares + jnp.sum(block * block, axis=1, keepdims=True)
    scale = lax.rsqrt(squares / width + EPSILON)
    for j in range(count):
        block = tokens[:, place(table, j)].astype(F32)
        normed[:, span(j)] = (
            block * scale * columns[ATTENTION_GAIN : ATTENTION_GAIN + 1, span(j)]
        ).astype(BF)
    raw = over_pieces(normed, kvg, slice(0, KV_WIDTH))
    kv_raw[...] = raw
    low = half_lanes(rows)
    for c in range(KEY_VALUE_HEADS):
        tile = raw[:, span(c, LANES)]
        key = head_norm(tile, gain[...], cosine[...], sine[...], low)
        kv_low[:, span(c, LANES)] = jnp.where(low, key, tile).astype(BF)


def project_key_value(table, tokens, cosine, sine, gain, kvg):
    rows, width = tokens.shape
    operands = (tokens, cosine, sine, gain, *kvg)
    return kernel_call(
        key_value_kernel,
        "project_key_value",
        (1,),
        [whole(o) for o in operands],
        [
            fixed_out((rows, width)),
            fixed_out((rows, KV_WIDTH)),
            fixed_out((rows, KV_WIDTH)),
            fixed_out((8, width)),
        ],
        [
            shape((rows, width), BF),
            shape((rows, KV_WIDTH), F32),
            shape((rows, KV_WIDTH), BF),
            shape((8, width), F32),
        ],
        [],
        2 * rows * width * KV_WIDTH,
        table,
    )(*operands)


def query_kernel(normed, cosine, sine, gain, *refs):
    q_raw, queries = refs[-2:]
    rows = normed.shape[0]
    raw = over_pieces(normed, refs[:-2])
    q_raw[...] = raw
    low = half_lanes(rows)
    for tile_index in range(GROUP_WIDTH // LANES):
        tile = raw[:, span(tile_index, LANES)]
        turned = head_norm(tile, gain[...], cosine[...], sine[...], low)
        queries[:, span(tile_index, LANES)] = (turned * SCORE_SCALE).astype(BF)


def column_parts(pieces):
    return [pl.BlockSpec((piece.shape[0], GROUP_WIDTH), lambda c, *t: (0, c)) for piece in pieces]


def project_query(normed, cosine, sine, gain, weight):
    rows, width = normed.shape
    out = pl.BlockSpec((rows, GROUP_WIDTH), lambda c: (0, c))
    return kernel_call(
        query_kernel,
        "project_query",
        (KEY_VALUE_HEADS,),
        [whole(normed), whole(cosine), whole(sine), whole(gain), *column_parts(weight)],
        [out, out],
        [shape((rows, Q_WIDTH), F32), shape((rows, Q_WIDTH), BF)],
        [],
        2 * rows * width * Q_WIDTH,
    )(normed, cosine, sine, gain, *weight)


def output_kernel(table, mixed, tokens, gains, *refs):
    hidden, feed = refs[-2:]
    width = hidden.shape[1]
    step = pl.program_id(0)

    @pl.when(step == 0)
    def _():
        for j in range(width // BLOCK):
            hidden[:, span(j)] = tokens[:, place(table, j)].astype(F32)

    add_back(hidden, mixed[...], refs[:-2])

    @pl.when(step == pl.num_programs(0) - 1)
    def _():
        values = hidden[...]
        scale = lax.rsqrt(jnp.mean(values * values, axis=1, keepdims=True) + EPSILON)
        feed[...] = (values * scale * gains[FEED_GAIN : FEED_GAIN + 1, :]).astype(BF)


def project_output(table, mixed, tokens, batch, gains, weight):
    rows = mixed.shape[0]
    width = tokens.shape[1]
    return kernel_call(
        output_kernel,
        "project_output",
        (KEY_VALUE_HEADS,),
        [
            pl.BlockSpec((rows, GROUP_WIDTH), lambda c, t: (0, c)),
            pl.BlockSpec((rows, width), lambda c, t: (batch, 0)),
            whole(gains),
            *column_parts(weight),
        ],
        [fixed_out((rows, width)), fixed_out((rows, width))],
        [shape((rows, width), F32), shape((rows, width), BF)],
        [],
        2 * rows * width * Q_WIDTH,
        table,
    )(mixed, tokens, gains, *weight)


def hidden_back_kernel(table, d_feed, hidden, cot, gains, *refs):
    d_hidden, d_attended, gain_grad, d_mixed = refs[-4:]
    width = hidden.shape[1]

    @pl.when(pl.program_id(0) == 0)
    def _():
        values = hidden[...]
        grad = d_feed[...].astype(F32)
        scale = lax.rsqrt(jnp.mean(values * values, axis=1, keepdims=True) + EPSILON)
        lifted = grad * gains[FEED_GAIN : FEED_GAIN + 1, :]
        dots = jnp.mean(values * lifted, axis=1, keepdims=True)
        d_norm = scale * lifted - values * (scale * scale * scale) * dots
        gain_grad[...] = jnp.broadcast_to(
            jnp.sum(grad * values * scale, axis=0, keepdims=True), gain_grad.shape
        )
        for j in range(width // BLOCK):
            total = cot[:, place(table, j)].astype(F32) + d_norm[:, span(j)]
            d_hidden[:, span(j)] = total
            d_attended[:, span(j)] = total.astype(BF)

    d_mixed[...] = over_pieces(d_attended, refs[:-4]).astype(BF)


def hidden_back(table, d_feed, hidden, cot, batch, gains, weight):
    rows, width = hidden.shape
    return kernel_call(
        hidden_back_kernel,
        "hidden_back",
        (KEY_VALUE_HEADS,),
        [
            whole(d_feed),
            whole(hidden),
            pl.BlockSpec((rows, width), lambda c, t: (batch, 0)),
            whole(gains),
            *column_parts(weight),
        ],
        [
            fixed_out((rows, width)),
            fixed_out((rows, width)),
            fixed_out((8, width)),
            pl.BlockSpec((rows, GROUP_WIDTH), lambda c, t: (0, c)),
        ],
        [
            shape((rows, width), F32),
            shape((rows, width), BF),
            shape((8, width), F32),
            shape((rows, Q_WIDTH), BF),
        ],
        [],
        2 * rows * width * Q_WIDTH,
        table,
    )(d_feed, hidden, cot, gains, *weight)


def query_back_kernel(d_q, *refs):
    out = refs[-1]

    @pl.when(pl.program_id(0) == 0)
    def _():
        out[...] = jnp.zeros_like(out)

    add_back(out, d_q[...], refs[:-1])


def query_back(d_q, weight):
    rows = d_q.shape[0]
    width = sum(piece.shape[0] for piece in weight)
    return kernel_call(
        query_back_kernel,
        "query_back",
        (KEY_VALUE_HEADS,),
        [pl.BlockSpec((rows, GROUP_WIDTH), lambda c: (0, c)), *column_parts(weight)],
        fixed_out((rows, width)),
        shape((rows, width), F32),
        [],
        2 * rows * width * Q_WIDTH,
    )(d_q, *weight)


def input_back_kernel(
    table,
    d_pair,
    kv_raw,
    cosine,
    sine,
    gain,
    d_normed_q,
    d_hidden0,
    d_hidden1,
    tokens,
    gains,
    *refs,
):
    kvg = refs[:-5]
    d_kv_raw, head_grad, tokens_grad, gain_grad, d_normed = refs[-5:]
    rows, width = tokens.shape
    part = d_hidden0.shape[0]
    low = half_lanes(rows)
    total = 0.0
    for c in range(KEY_VALUE_HEADS):
        grad = d_pair[:, span(c, LANES)].astype(F32)
        d_tile, g_tile = head_norm_back(
            kv_raw[:, span(c, LANES)], gain[...], cosine[...], sine[...], low, grad
        )
        total = total + g_tile
        d_kv_raw[:, span(c, LANES)] = jnp.where(low, d_tile, grad).astype(BF)
    head_grad[...] = jnp.broadcast_to(total, head_grad.shape)
    d_kv = d_kv_raw[...]
    d_normed[...] = d_normed_q[...]
    add_back(d_normed, d_kv, kvg, slice(0, KV_WIDTH))
    squares, dots = 0.0, 0.0
    for j in range(width // BLOCK):
        block = tokens[:, place(table, j)].astype(F32)
        lifted = d_normed[:, span(j)] * gains[ATTENTION_GAIN : ATTENTION_GAIN + 1, span(j)]
        squares = squares + jnp.sum(block * block, axis=1, keepdims=True)
        dots = dots + jnp.sum(block * lifted, axis=1, keepdims=True)
    scale = lax.rsqrt(squares / width + EPSILON)
    dots = dots / width * (scale * scale * scale)
    for j in range(width // BLOCK):
        block = tokens[:, place(table, j)].astype(F32)
        grad = d_normed[:, span(j)]
        lifted = grad * gains[ATTENTION_GAIN : ATTENTION_GAIN + 1, span(j)]
        d_input = scale * lifted - block * dots
        for batch, d_hidden in enumerate((d_hidden0, d_hidden1)):
            tokens_grad[span(batch, part), place(table, j)] = (
                d_hidden[:, span(j)] + d_input[span(batch, part), :]
            )
        gain_grad[:, span(j)] = jnp.broadcast_to(
            jnp.sum(grad * block * scale, axis=0, keepdims=True), (8, BLOCK)
        )


def input_back(table, *operands):
    tokens = operands[8]
    rows, width = tokens.shape
    return kernel_call(
        input_back_kernel,
        "input_back",
        (1,),
        [whole(o) for o in operands],
        [
            fixed_out((rows, KV_WIDTH)),
            fixed_out((8, LANES)),
            fixed_out((rows, width)),
            fixed_out((8, width)),
        ],
        [
            shape((rows, KV_WIDTH), BF),
            shape((8, LANES), F32),
            shape((rows, width), F32),
            shape((8, width), F32),
        ],
        [pltpu.VMEM((rows, width), F32)],
        2 * rows * width * KV_WIDTH,
        table,
    )(*operands)


def layer_out_kernel(table, hidden0, hidden1, added0, added1, out):
    part = hidden0.shape[0]
    for batch, (hidden, added) in enumerate(((hidden0, added0), (hidden1, added1))):
        for j in range(hidden.shape[1] // BLOCK):
            out[span(batch, part), place(table, j)] = (
                hidden[:, span(j)] + added[:, span(j)].astype(F32)
            ).astype(BF)


def finish_layer(table, *operands):
    rows, width = operands[0].shape
    return kernel_call(
        layer_out_kernel,
        "finish_layer",
        (1,),
        [whole(o) for o in operands],
        fixed_out((2 * rows, width)),
        shape((2 * rows, width), BF),
        [],
        0,
        table,
    )(*operands)


def key_value_grad_kernel(normed, d_kv_raw, gain_grads, out0, out1):
    half = normed.shape[1] // 2
    for index, out in enumerate((out0, out1)):
        cut = span(index, half)
        out[:, :KV_WIDTH] = dot_tn(normed[:, cut], d_kv_raw[...]).astype(BF)
        rows = gain_grads[:, cut]
        rows = jnp.concatenate([rows, jnp.zeros((LANES - 8, half), F32)], axis=0)
        out[:, KV_WIDTH:] = rows.T.astype(BF)


def key_value_grad(normed, d_kv_raw, gain_grads):
    rows, width = normed.shape
    dims = (width // 2, KV_WIDTH + LANES)
    return kernel_call(
        key_value_grad_kernel,
        "key_value_grad",
        (1,),
        [whole(normed), whole(d_kv_raw), whole(gain_grads)],
        [fixed_out(dims), fixed_out(dims)],
        [shape(dims, BF), shape(dims, BF)],
        [],
        2 * rows * width * KV_WIDTH,
    )(normed, d_kv_raw, gain_grads)


def pad_heads(tile, low, keep_low):
    parts = []
    for pair in range(GROUP // 2):
        both = tile[:, span(pair, LANES)].astype(F32)
        turned = pltpu.roll(both, HEAD_SIZE, 1)
        first, second = (both, turned) if keep_low else (turned, both)
        keep = low if keep_low else jnp.logical_not(low)
        parts.append(jnp.where(keep, first, 0.0))
        parts.append(jnp.where(keep, second, 0.0))
    return jnp.concatenate(parts, axis=0).astype(BF)


def four_wide(row):
    return jnp.concatenate([row] * GROUP, axis=1)


def heads_back(stacked, rows):
    parts = []
    for pair in range(GROUP // 2):
        start = 2 * pair * rows
        both = jnp.concatenate(
            [stacked[:, start : start + rows], stacked[:, start + rows : start + 2 * rows]], axis=0
        )
        parts.append(both.T)
    return jnp.concatenate(parts, axis=1)


def key_rows(kv, cut):
    rows = kv.shape[2]
    block = kv[cut.start // rows : cut.stop // rows, 0]
    return block.reshape(cut.stop - cut.start, kv.shape[3])


def every_row(kv):
    return key_rows(kv, slice(0, kv.shape[0] * kv.shape[2]))


def ones_and_values(kv):
    values = every_row(kv)
    return jnp.where(half_lanes(values.shape[0]), 1.0, values.astype(F32)).astype(BF)


def attention_forward_kernel(kv0, kv1, query, bias0, bias1, mixed, lse, expo):
    rows = query.shape[0]
    half = bias0.shape[0]
    padded = pad_heads(query[...], half_lanes(rows), True)
    for part, (kv, bias) in enumerate(((kv0, bias0), (kv1, bias1))):
        for step in range(half // CHUNK):
            cut = span(step, CHUNK)
            weight = jnp.exp(dot_nt(key_rows(kv, cut), padded) + four_wide(bias[cut, :]))
            expo[part * half + step * CHUNK : part * half + (step + 1) * CHUNK, :] = weight.astype(BF)
    total = dot_tn(ones_and_values(kv0), expo[:half, :]) + dot_tn(
        ones_and_values(kv1), expo[half:, :]
    )
    lse[...] = jnp.log(total[0:1, :])[None]
    mixed[...] = heads_back(total[HEAD_SIZE:, :] / total[:HEAD_SIZE, :], rows).astype(BF)


def attention_forward(kv0, kv1, query, batch, bias0, bias1):
    half, rows = bias0.shape
    wide = GROUP * rows
    keys = pl.BlockSpec((half // rows, 1, rows, LANES), lambda c: (0, batch, 0, c))
    kv0, kv1 = (kv.reshape(half // rows, -1, rows, KV_WIDTH) for kv in (kv0, kv1))
    return kernel_call(
        attention_forward_kernel,
        "attention_forward",
        (KEY_VALUE_HEADS,),
        [
            keys,
            keys,
            pl.BlockSpec((rows, GROUP_WIDTH), lambda c: (batch, c)),
            whole(bias0),
            whole(bias1),
        ],
        [
            pl.BlockSpec((rows, GROUP_WIDTH), lambda c: (0, c)),
            pl.BlockSpec((1, 1, wide), lambda c: (c, 0, 0)),
        ],
        [shape((rows, Q_WIDTH), BF), shape((KEY_VALUE_HEADS, 1, wide), F32)],
        [pltpu.VMEM((2 * half, wide), BF)],
        KEY_VALUE_HEADS * 2 * half * wide * LANES * 12,
    )(kv0, kv1, query, bias0, bias1)


def attention_backward_kernel(
    kv0,
    kv1,
    query,
    mixed,
    d_mixed,
    bias0,
    bias1,
    lse,
    q_raw,
    cosine,
    sine,
    gain,
    d_q_raw,
    d_kv0,
    d_kv1,
    gain_grad,
    d_scores,
):
    rows = query.shape[0]
    half = bias0.shape[0]
    low = half_lanes(rows)
    padded = pad_heads(query[...], low, True)
    d_padded = pad_heads(d_mixed[...], low, False)
    product = d_mixed[...].astype(F32) * mixed[...].astype(F32)
    pick = (
        lax.broadcasted_iota(jnp.int32, (8, GROUP_WIDTH), 1) // HEAD_SIZE
        == lax.broadcasted_iota(jnp.int32, (8, GROUP_WIDTH), 0)
    ).astype(F32)
    balance = lax.dot_general(
        pick,
        product,
        (((1,), (1,)), ((), ())),
        precision=lax.Precision.HIGHEST,
        preferred_element_type=F32,
    )
    balance = jnp.concatenate([balance[head : head + 1, :] for head in range(GROUP)], axis=1)
    level = lse[0]
    for part, (kv, bias, d_kv) in enumerate(((kv0, bias0, d_kv0), (kv1, bias1, d_kv1))):
        for step in range(half // CHUNK):
            cut = span(step, CHUNK)
            block = key_rows(kv, cut)
            probs = jnp.exp(dot_nt(block, padded) + four_wide(bias[cut, :]) - level)
            d_probs = dot_nt(block, d_padded)
            low_scores = (probs * (d_probs - balance)).astype(BF)
            d_scores[part * half + step * CHUNK : part * half + (step + 1) * CHUNK, :] = low_scores
            d_kv[cut, :] = (
                dot_nn(low_scores, padded) + dot_nn(probs.astype(BF), d_padded)
            ).astype(BF)
    total = dot_tn(every_row(kv0), d_scores[:half, :]) + dot_tn(
        every_row(kv1), d_scores[half:, :]
    )
    d_query = heads_back(total[:HEAD_SIZE, :] * SCORE_SCALE, rows)
    grads = 0.0
    for tile_index in range(GROUP_WIDTH // LANES):
        cut = span(tile_index, LANES)
        d_tile, g_tile = head_norm_back(
            q_raw[:, cut], gain[...], cosine[...], sine[...], low, d_query[:, cut]
        )
        d_q_raw[:, cut] = d_tile.astype(BF)
        grads = grads + g_tile

    @pl.when(pl.program_id(0) == 0)
    def _():
        gain_grad[...] = jnp.zeros_like(gain_grad)

    gain_grad[...] += jnp.broadcast_to(grads, gain_grad.shape)


def attention_backward(
    kv0, kv1, query, batch, mixed, d_mixed, bias0, bias1, lse, q_raw, cosine, sine, gain
):
    half, rows = bias0.shape
    wide = GROUP * rows
    keys = pl.BlockSpec((half // rows, 1, rows, LANES), lambda c: (0, batch, 0, c))
    kv0, kv1 = (kv.reshape(half // rows, -1, rows, KV_WIDTH) for kv in (kv0, kv1))
    d_keys = pl.BlockSpec((half, LANES), lambda c: (0, c))
    heads = pl.BlockSpec((rows, GROUP_WIDTH), lambda c: (0, c))
    part = pl.BlockSpec((rows, GROUP_WIDTH), lambda c: (batch, c))
    table = pl.BlockSpec((rows, LANES), lambda c: (batch, 0))
    return kernel_call(
        attention_backward_kernel,
        "attention_backward",
        (KEY_VALUE_HEADS,),
        [
            keys,
            keys,
            part,
            heads,
            heads,
            whole(bias0),
            whole(bias1),
            pl.BlockSpec((1, 1, wide), lambda c: (c, 0, 0)),
            part,
            table,
            table,
            whole(gain),
        ],
        [heads, d_keys, d_keys, fixed_out((8, LANES))],
        [
            shape((rows, Q_WIDTH), BF),
            shape((half, KV_WIDTH), BF),
            shape((half, KV_WIDTH), BF),
            shape((8, LANES), F32),
        ],
        [pltpu.VMEM((2 * half, wide), BF)],
        KEY_VALUE_HEADS * 2 * half * wide * LANES * 28,
    )(kv0, kv1, query, mixed, d_mixed, bias0, bias1, lse, q_raw, cosine, sine, gain)


def swap_halves(values):
    half = values.shape[1] // 2
    return jnp.concatenate([values[:, half:], values[:, :half]], axis=1)


def feed_forward_kernel(count, units, *refs):
    feed0, feed1, cot0, cot1 = refs[:4]
    gate_up = refs[4 : 4 + count]
    down = refs[4 + count : 4 + 2 * count]
    act_out, d_units_out, out0, out1, d_feed0, d_feed1 = refs[4 + 2 * count :]
    first = pl.program_id(0) < pl.num_programs(0) // 2
    rows, width = feed0.shape
    half = width // 2
    size = down[0].shape[0] // 2
    feed = jnp.where(first, swap_halves(feed0[...]), feed1[...])
    cot = jnp.where(first, swap_halves(cot0[...]), cot1[...])

    def over(left, pieces):
        total = None
        for b, piece in enumerate(pieces):
            both = jnp.concatenate(
                [left[:, b * size : (b + 1) * size], left[:, half + b * size : half + (b + 1) * size]],
                axis=1,
            )
            term = dot_nn(both, piece[...])
            total = term if total is None else total + term
        return total

    both = over(feed, gate_up)
    gate_pre, up_pre = both[:, :units], both[:, units : 2 * units]
    sig = 1.0 / (1.0 + jnp.exp(-gate_pre))
    silu = gate_pre * sig
    act = (silu * up_pre).astype(BF)
    act = jnp.concatenate([act, jnp.zeros((rows, down[0].shape[1] - units), BF)], axis=1)
    act_out[...] = act
    d_act = over(cot, down)[:, :units]
    d_gate = d_act * up_pre * (sig * (1.0 + gate_pre * (1.0 - sig)))
    d_units = jnp.concatenate(
        [
            d_gate.astype(BF),
            (d_act * silu).astype(BF),
            jnp.zeros((rows, gate_up[0].shape[1] - 2 * units), BF),
        ],
        axis=1,
    )
    d_units_out[...] = d_units

    def write(target, left, pieces, swapped):
        for b, piece in enumerate(pieces):
            block = dot_nt(left, piece[...]).astype(BF)
            early, late = (half, 0) if swapped else (0, half)
            target[:, early + b * size : early + (b + 1) * size] = block[:, :size]
            target[:, late + b * size : late + (b + 1) * size] = block[:, size:]

    @pl.when(first)
    def _():
        write(d_feed0, d_units, gate_up, True)
        write(out0, act, down, True)

    @pl.when(jnp.logical_not(first))
    def _():
        write(d_feed1, d_units, gate_up, False)
        write(out1, act, down, False)


def feed_forward(feeds, cots, gate_up, down, units):
    tokens, width = feeds[0].shape
    steps = tokens // FFN_ROWS
    early = pl.BlockSpec((FFN_ROWS, width), lambda i: (jnp.minimum(i, steps - 1), 0))
    late = pl.BlockSpec((FFN_ROWS, width), lambda i: (jnp.maximum(i - steps, 0), 0))
    act_width, units_width = down[0].shape[1], gate_up[0].shape[1]
    return kernel_call(
        functools.partial(feed_forward_kernel, len(down), units),
        "feed_forward",
        (2 * steps,),
        [early, late, early, late, *[whole(w) for w in (*gate_up, *down)]],
        [
            pl.BlockSpec((FFN_ROWS, act_width), lambda i: (i, 0)),
            pl.BlockSpec((FFN_ROWS, units_width), lambda i: (i, 0)),
            early,
            late,
            early,
            late,
        ],
        [
            shape((2 * tokens, act_width), BF),
            shape((2 * tokens, units_width), BF),
            *[shape((tokens, width), BF)] * 4,
        ],
        [],
        2 * tokens * 2 * width * units * 6,
    )(*feeds, *cots, *gate_up, *down)


def weight_grad_kernel(count, columns, *refs):
    lefts = refs[: 2 * count]
    rights = refs[2 * count : -1]
    out = refs[-1]
    rows = lefts[0].shape[0]
    each = count // len(rights)
    total = None
    for index in range(count):
        left = jnp.concatenate([lefts[2 * index][...], lefts[2 * index + 1][...]], axis=1)
        right = rights[index // each]
        term = dot_tn(left, right[span(index % each, rows), columns])
        total = term if total is None else total + term
    out[...] = total.astype(BF)


def weight_grad(lefts, rights, columns, steps, stride, offset):
    rows, width = lefts[0].shape
    units = columns.stop - columns.start
    half = width // 2 // BLOCK
    mine = pl.BlockSpec((rows, BLOCK), lambda i: (0, i * stride + offset))
    other = pl.BlockSpec((rows, BLOCK), lambda i: (0, half + i * stride + offset))
    specs, operands = [], []
    for index, left in enumerate(lefts):
        specs += [other, mine] if index % 2 == 0 else [mine, other]
        operands += [left, left]
    return kernel_call(
        functools.partial(weight_grad_kernel, len(lefts), columns),
        "weight_grad",
        (steps,),
        [*specs, *[whole(r) for r in rights]],
        pl.BlockSpec((2 * BLOCK, units), lambda i: (i, 0)),
        shape((2 * BLOCK * steps, units), BF),
        [],
        2 * len(lefts) * rows * 2 * BLOCK * steps * units,
    )(*operands, *rights)


def rotary_tables(places):
    half_width = HEAD_SIZE // 2
    freqs = jnp.exp(jnp.arange(half_width, dtype=F32) * (-2.0 * math.log(10000.0) / HEAD_SIZE))
    angles = places.astype(F32)[:, None] * freqs[None, :]
    cosine, sine = jnp.cos(angles), jnp.sin(angles)
    return (
        jnp.concatenate([cosine] * 4, axis=1),
        jnp.concatenate([-sine, sine, -sine, sine], axis=1),
    )


def padded_columns(values, columns):
    return jnp.pad(values, ((0, 0), (0, columns - values.shape[1])))


def up_to(size):
    return -(-size // LANES) * LANES


def on_device(
    tokens,
    lengths,
    attention_gain,
    query_weight,
    key_value_matrix,
    per_head_gains,
    output_weight,
    feed_gain,
    gate_weight,
    up_weight,
    down_weight,
    cotangent,
):
    batches = tokens.shape[0]
    rows = tokens.shape[2]
    width = tokens.shape[3]
    dp_size = lax.axis_size("dp")
    heads_size = lax.axis_size("heads")
    seq_size = lax.axis_size("seq")
    assert seq_size == 4 and heads_size == 4 and batches == 2
    paired = dp_size == 2
    y = lax.axis_index("dp").astype(jnp.int32)
    s = lax.axis_index("seq").astype(jnp.int32)
    z = lax.axis_index("heads").astype(jnp.int32)
    x = s // 2
    core = s % 2

    def after(v, *others):
        return lax.optimization_barrier((v, others))[0]

    def swap_x(v):
        return lax.ppermute(v, "seq", [(i, i ^ 2) for i in range(4)])

    def swap_core(v):
        return lax.ppermute(v, "seq", [(i, i ^ 1) for i in range(4)])

    def swap_y(v):
        return lax.ppermute(v, "dp", [(0, 1), (1, 0)])

    def pair_scatter(v, axis):
        def step(u, upper, distance):
            low, high = jnp.split(u, 2, axis=axis)
            sent = lax.ppermute(
                jnp.where(upper, low, high), "heads", [(i, i ^ distance) for i in range(4)]
            )
            return jnp.where(upper, high, low) + sent

        return step(step(v, z >= 2, 2), z % 2 == 1, 1)

    def gather_near(v):
        if not paired:
            both = jnp.stack([v, swap_x(v)], axis=0)
            return [lax.all_gather(both, "dp", axis=0).reshape(-1, v.shape[-1])]
        return [v, swap_x(v), swap_y(v)]

    def gather_far(near, x_first):
        if not paired:
            return near
        return [*near, swap_y(near[1]) if x_first else swap_x(near[2])]

    def pair_gather(v, axis):
        def step(u, upper, distance):
            got = lax.ppermute(u, "heads", [(i, i ^ distance) for i in range(4)])
            return jnp.where(
                upper,
                jnp.concatenate([got, u], axis=axis),
                jnp.concatenate([u, got], axis=axis),
            )

        return step(step(v, z % 2 == 1, 1), z >= 2, 2)

    def both_cores(pieces):
        return [*pieces, *[swap_core(v) for v in pieces]]

    def unit_pieces(pieces):
        if paired:
            return pieces
        g = pieces[0].reshape(blocks, 2, -1, pieces[0].shape[-1])
        return [g.transpose(1, 0, 2, 3).reshape(pieces[0].shape)]

    def scatter_yx(g, x_last, first=(), second=()):
        def along_x(u, late):
            return u[..., 0, :, :] + after(swap_x(u[..., 1, :, :]), late)

        def along_y(u, late):
            if paired:
                return u[0] + after(swap_y(u[1]), late)
            return lax.psum_scatter(u, "dp", scatter_dimension=0)

        if x_last:
            return along_x(along_y(g, first), second)
        return along_y(along_x(g, first), second)

    blocks = 2 * dp_size
    piece = width // blocks

    if paired:
        own = (2 * y + x) * 2 + core
        places_of = jnp.array([b * 2 + c for c in range(2) for b in range(4)], jnp.int32)
        table = places_of ^ own

        def to_order(v):
            return v

        from_order = to_order
    else:
        table = jnp.arange(width // BLOCK, dtype=jnp.int32)

        def flip(v):
            u = v.reshape(v.shape[:-1] + (dp_size, 2, 2, piece // 2))
            u = jnp.where(x == 1, u[..., ::-1, :, :], u)
            return jnp.where(core == 1, u[..., ::-1, :], u)

        def to_order(v):
            return jnp.moveaxis(flip(v), -2, -4).reshape(v.shape)

        def from_order(v):
            u = v.reshape(v.shape[:-1] + (2, dp_size, 2, piece // 2))
            return flip(jnp.moveaxis(u, -4, -2).reshape(v.shape)).reshape(v.shape)

    def small_order(v, back):
        if not paired:
            return from_order(v) if back else to_order(v)
        cut = v.reshape(8, -1)
        return jnp.concatenate(
            [
                lax.select_n(own, *[cut[held(i, m, back)] for m in range(8)])
                for i in range(8)
            ]
        ).reshape(v.shape)

    def held(i, m, back):
        if back:
            source = i ^ m
            return (source % 2) * 4 + source // 2
        return ((i % 4) * 2 + i // 4) ^ m

    small = key_value_matrix.shape[0]
    per_head = per_head_gains.shape[0]
    kv_local = (
        key_value_matrix.reshape(small, 2, KEY_VALUE_HEADS, HEAD_SIZE)
        .transpose(0, 2, 1, 3)
        .reshape(small, KV_WIDTH)
    )
    gains_local = jnp.stack(
        [attention_gain, feed_gain, jnp.pad(per_head_gains, (0, small - per_head))], axis=1
    )
    kvg_local = jnp.concatenate([kv_local, padded_columns(gains_local, LANES)], axis=1)
    kvg_rows = pair_gather(kvg_local, 0)
    kvg_near = gather_near(kvg_rows)

    tokens_in = to_order(tokens[:, 0].reshape(batches * rows, width))
    cot_in = to_order(cotangent[:, 0].reshape(batches * rows, width))
    cot_held = order_columns(table, cot_in) if paired else cot_in
    lined = lax.all_gather(
        jnp.concatenate(
            [
                cot_held,
                padded_columns(query_weight.reshape(small, Q_WIDTH), width),
                padded_columns(output_weight.T, width),
            ],
            axis=0,
        ),
        "heads",
        axis=0,
    )
    cots_mine = [
        lined[:, span(batch, rows)].reshape(heads_size * rows, width) for batch in range(batches)
    ]
    q_rows = (
        lined[:, batches * rows : batches * rows + small, :Q_WIDTH]
        .reshape(heads_size, query_weight.shape[0], query_weight.shape[1])
        .transpose(1, 0, 2)
        .reshape(query_weight.shape[0], Q_WIDTH)
    )
    o_rows = lined[:, batches * rows + small :, :Q_WIDTH].reshape(4 * small, Q_WIDTH)
    q_near = gather_near(q_rows)
    q_full = both_cores(gather_far(q_near, False))
    o_near = gather_near(after(o_rows, q_near))
    o_full = both_cores(gather_far(o_near, True))

    units = gate_weight.shape[1] // 2
    act_width, units_width = up_to(units), up_to(2 * units)

    def unit_half(v, which):
        return jnp.where(which == 0, v[:, :units], v[:, units:])

    down_local = down_weight.T

    def halves(which):
        gate_up = jnp.concatenate([unit_half(gate_weight, which), unit_half(up_weight, which)], axis=1)
        return jnp.concatenate(
            [padded_columns(gate_up, units_width), padded_columns(unit_half(down_local, which), act_width)],
            axis=1,
        )

    keep = halves(core)
    take = swap_core(halves(1 - core))
    ffn_rows = jnp.concatenate([keep, take], axis=0)
    down_near = gather_near(ffn_rows[:, units_width:])
    gate_up_near = gather_near(after(ffn_rows[:, :units_width], kvg_near))
    gate_up = unit_pieces(gather_far(gate_up_near, True))
    down = unit_pieces(gather_far(down_near, False))
    kvg = both_cores(gather_far(after(kvg_near, down_near), True))

    head_column = jnp.concatenate([part[:, KV_WIDTH + HEAD_GAIN] for part in kvg])
    head_scale = small_order(head_column.astype(F32)[None], True)
    head_scale = head_scale.reshape(-1, small)[:, :per_head].reshape(1, -1)
    query_gain = jnp.concatenate([head_scale[:, :HEAD_SIZE]] * 2, axis=1)
    key_gain = jnp.concatenate([head_scale[:, HEAD_SIZE:]] * 2, axis=1)

    block_rows = rows * heads_size
    spots = s * block_rows + z * rows + jnp.arange(rows, dtype=jnp.int32)
    inside = jnp.arange(rows, dtype=jnp.int32)

    def key_spots(first):
        lines = jnp.arange(heads_size, dtype=jnp.int32)[:, None, None] * rows
        fronts = jnp.stack([first, first ^ 2])[None, :, None] * block_rows
        return (lines + fronts + inside[None, None, :]).reshape(-1)

    def bias_for(begin, first):
        keys = key_spots(first)[:, None]
        return jnp.where((keys <= spots[None, :]) & (keys >= begin[None, :]), 0.0, MASKED)

    begins, biases = [], []
    for batch in range(batches):
        sizes = lengths[batch, 0]
        finish = jnp.cumsum(sizes)
        begin = jnp.sum(
            jnp.where(spots[:, None] >= finish[None, :], sizes[None, :], 0), axis=1
        ).astype(jnp.int32)
        begins.append(begin)
        biases.append((bias_for(begin, s), bias_for(begin, s ^ 1)))
    cosine, sine = rotary_tables(jnp.concatenate([spots - begin for begin in begins]))

    normed, kv_raw, kv_low, gains = project_key_value(
        table, after(tokens_in, down_near), cosine, sine, key_gain, kvg
    )
    q_raw, queries = project_query(normed, cosine, sine, query_gain, q_full)

    kv_lined = lax.all_gather(
        after(jnp.concatenate([kv_low, swap_x(kv_low)], axis=0), gate_up_near), "heads", axis=0, tiled=True
    )
    kv_lined = after(kv_lined, q_full[:4], o_near)
    kv_other = swap_core(kv_lined)
    kvs = (kv_lined, kv_other)
    feeds, mixeds, lses, hiddens = [], [], [], []
    for batch in range(batches):
        query = queries if batch == 0 else after(queries, hiddens[0])
        mixed, lse = attention_forward(*kvs, query, batch, *biases[batch])
        mixed_tied = mixed if batch == 0 else after(mixed, gate_up, down)
        hidden_in, feed_rows = project_output(
            table, mixed_tied, tokens_in, batch, gains, o_full
        )
        feed_mine = lax.all_gather(feed_rows, "heads", axis=0, tiled=True)
        feeds.append((swap_core(feed_mine), feed_mine))
        mixeds.append(mixed)
        lses.append(lse)
        hiddens.append(hidden_in)

    d_feeds, acts, d_units, cots, outs = [], [], [], [], []
    for batch in range(batches):
        cot_pair = (swap_core(cots_mine[batch]), cots_mine[batch])
        act, d_unit, out_other, out_mine, d_feed_other, d_feed_mine = feed_forward(
            feeds[batch], cot_pair, gate_up, down, units
        )
        acts.append(act)
        d_units.append(d_unit)
        cots.append(cot_pair)
        outs.append((out_mine, out_other))
        d_feed = d_feed_mine + swap_core(d_feed_other)
        if batch + 1 < batches:
            d_feed = after(d_feed, feeds[batch + 1])
        d_feeds.append(lax.psum_scatter(d_feed, "heads", scatter_dimension=0, tiled=True))

    feed_all = [f for pair in feeds for f in pair]
    cot_all = [c for pair in cots for c in pair]
    count = width // 2 // BLOCK

    def unit_order(g):
        g = g.reshape(count, 2, BLOCK, -1).transpose(1, 0, 2, 3)
        g = g.reshape(2, blocks, piece // 2, -1).transpose(1, 0, 2, 3)
        return g.reshape(dp_size, 2, piece, -1)

    cut_at = up_to(units)

    def both_grads(left, right):
        return [dot_tn(left[:, span(i, width // 2)], right).astype(BF) for i in range(2)]

    def split_rows(mine, got, along_y=True):
        if not paired:
            return mine + got, None
        size = mine.shape[0] // 4
        far = (2, 3) if along_y else (1, 3)
        near = (0, 1) if along_y else (0, 2)

        def pick(v, blocks_of):
            return jnp.concatenate([v[span(b, size)] for b in blocks_of], axis=0)

        return pick(mine, far) + pick(got, far), pick(mine, near) + pick(got, near)

    def send_parts(v, swap, *rows_of):
        parts, start = [], 0
        for size in rows_of:
            parts.append(swap(v[start : start + size]))
            start += size
        assert start == v.shape[0]
        return parts

    def halved(total):
        near = total.shape[0] // 2
        return total[near:], total[:near]

    def fold(parts, kept, *late):
        return halved(kept + after(jnp.concatenate(parts, axis=0), late))

    def fold_whole(sent):
        g = sent.reshape(dp_size, 2, -1, sent.shape[-1])
        g = lax.psum_scatter(g, "dp", scatter_dimension=0)
        return g[0] + swap_x(g[1])

    d_hiddens, d_attendeds, d_q_raws, d_lined = [], [], [], []
    feed_gain_grads, query_gain_grads = [], []
    mixed_all = jnp.concatenate(mixeds, axis=0)
    first_cut, second_cut = slice(0, cut_at), slice(cut_at, up_to(2 * units))
    if paired:
        first_far = weight_grad(feed_all, d_units, first_cut, 2, 1, 2)
        first_parts = send_parts(first_far, swap_y, 384, 640)
        second_far = weight_grad(feed_all, after(d_units, first_far), second_cut, 2, 2, 1)
        second_parts = send_parts(second_far, swap_x, 384, 640)
        d_feeds[0] = after(d_feeds[0], second_far)
    for batch in range(batches):
        d_feed = d_feeds[batch]
        if batch == 1:
            d_feed = after(d_feed, d_q_raws[0])
            if paired:
                tied = after(acts, d_q_raws[0], first_parts[1], second_parts[1])
                down_far = weight_grad(cot_all, tied, slice(0, act_width), 2, 2, 1)
                down_parts = send_parts(down_far, swap_x, 256, 640, 128)
                d_feed = after(d_feed, down_far, last_kv)
        d_hidden, d_attended, feed_grad, d_mixed = hidden_back(
            table, d_feed, hiddens[batch], cot_in, batch, gains, o_full
        )
        d_hiddens.append(d_hidden)
        d_attendeds.append(d_attended)
        if batch == 0 and paired:
            d_mixed = after(d_mixed, first_parts[0], second_parts[0])
        if batch == 1:
            if paired:
                d_attendeds[1] = after(d_attended, down_parts[0])
            o_grads = both_grads(jnp.concatenate(d_attendeds, axis=0), mixed_all)
            o_send, o_keep = split_rows(o_grads[0], swap_core(o_grads[1]))
            d_mixed = after(d_mixed, o_send)
            if paired:
                o_parts = send_parts(o_send, swap_y, 320, 128, 64)
        d_q_raw, d_kv0, d_kv1, query_grad = attention_backward(
            *kvs,
            queries,
            batch,
            mixeds[batch],
            d_mixed,
            *biases[batch],
            lses[batch],
            q_raw,
            cosine,
            sine,
            query_gain,
        )
        d_kv = d_kv0 + swap_core(d_kv1)
        last_kv = d_kv
        d_lined.append(lax.psum_scatter(d_kv, "heads", scatter_dimension=0, tiled=True))
        d_q_raws.append(d_q_raw)
        feed_gain_grads.append(feed_grad)
        query_gain_grads.append(query_grad)

    d_pairs = [pair[:rows] + swap_x(pair[rows:]) for pair in d_lined]
    d_q_raw_all = jnp.concatenate(d_q_raws, axis=0)
    late = (down_parts[1], o_parts[0]) if paired else ()
    q_grads = both_grads(after(normed, d_q_raws[1], late), d_q_raw_all)
    q_send, q_keep = split_rows(q_grads[0], swap_core(q_grads[1]), False)
    d_normed_q = query_back(after(d_q_raw_all, q_send, d_pairs[0]), q_full)
    if paired:
        q_parts = send_parts(q_send, swap_x, 128, 192, 192)
        tied = after(d_units, d_normed_q, q_parts[0], o_parts[1])
        second_got = jnp.concatenate(second_parts, axis=0)
        second_half = weight_grad(feed_all, tied, second_cut, 2, 2, 0) + second_got
        second_last = send_parts(second_half[2 * BLOCK :], swap_y, 320, 192)
        tied = after(acts, second_half, q_parts[1], o_parts[2])
        down_got = jnp.concatenate(down_parts, axis=0)
        half = weight_grad(cot_all, tied, slice(0, act_width), 2, 2, 0) + down_got
        o_send, o_keep = fold(o_parts, o_keep, half)
        o_parts = send_parts(o_send, swap_x, 128, 128)
        before_input = (half, q_parts[2], second_last[0])
    else:
        every_unit = slice(0, units_width)
        g_gate_up = scatter_yx(
            unit_order(weight_grad(feed_all, d_units, every_unit, count, 1, 0)), True
        )
        g_down = scatter_yx(
            unit_order(weight_grad(cot_all, acts, slice(0, act_width), count, 1, 0)), False
        )
        before_input = ()
    d_pair_all = after(jnp.concatenate(d_pairs, axis=0), before_input)

    d_kv_raw, key_grad, tokens_grad, attention_grad = input_back(
        table,
        d_pair_all,
        kv_raw,
        cosine,
        sine,
        key_gain,
        d_normed_q,
        *d_hiddens,
        tokens_in,
        gains,
        *kvg,
    )
    if paired:
        d_kv_raw = after(d_kv_raw, o_parts[0], second_last[1])
    query_grad = query_gain_grads[0][0] + query_gain_grads[1][0]
    head_grads = jnp.concatenate(
        [query_grad[:HEAD_SIZE] + query_grad[HEAD_SIZE:], key_grad[0, :HEAD_SIZE]]
    ).reshape(-1, per_head)
    head_row = small_order(
        jnp.pad(head_grads, ((0, 0), (0, small - per_head))).reshape(1, width), False
    )
    gain_grads = jnp.concatenate(
        [
            attention_grad[0:1],
            feed_gain_grads[0][0:1] + feed_gain_grads[1][0:1],
            head_row,
            jnp.zeros((5, width), F32),
        ],
        axis=0,
    )
    kv_mine, kv_other = key_value_grad(normed, d_kv_raw, gain_grads)
    kv_send, kv_keep = split_rows(kv_mine, swap_core(kv_other))
    if paired:
        kv_got = swap_y(kv_send)
        tied = after(d_units, kv_send)
        first_got = jnp.concatenate(first_parts, axis=0)
        first_half = weight_grad(feed_all, tied, first_cut, 2, 1, 0) + first_got
        first_last = swap_x(first_half[2 * BLOCK :])
        q_send, q_keep = fold(q_parts, q_keep, first_half)
        q_got = swap_y(q_send)
        kv_send, kv_keep = fold([kv_got], kv_keep, first_half)
        g_kv = kv_keep + swap_x(kv_send)
        g_q = q_keep + after(q_got, g_kv)
        g_o = o_keep + after(jnp.concatenate(o_parts, axis=0), first_half)
        down_last = swap_y(half[2 * BLOCK :])
        first_last, second_last, down_last = after((first_last, second_last, down_last), g_q)
        second_got = jnp.concatenate(second_last, axis=0)
        g_gate_up = jnp.concatenate(
            [first_half[: 2 * BLOCK] + first_last, second_half[: 2 * BLOCK] + second_got], axis=1
        )
        g_down = half[: 2 * BLOCK] + down_last
    else:
        g_o, g_q, g_kv = (fold_whole(v) for v in (o_send, q_send, kv_send))
    g_kv = pair_scatter(g_kv, 0).astype(F32)
    grad_output = pair_scatter(g_o, 0).astype(F32).T
    grad_query = pair_scatter(g_q, 1).astype(F32)
    part_rows = g_down.shape[0] // 2
    g_ffn = jnp.concatenate([g_gate_up, g_down], axis=1)
    g_keep = g_ffn[:part_rows]
    g_take = swap_core(g_ffn[part_rows:])
    grads_ffn = []
    for start in (0, units, units_width):
        kept, got = g_keep[:, start : start + units], g_take[:, start : start + units]
        grads_ffn.append(
            jnp.where(
                core == 0,
                jnp.concatenate([kept, got], axis=1),
                jnp.concatenate([got, kept], axis=1),
            ).astype(F32)
        )
    grad_gate, grad_up, grad_down = grads_ffn
    grad_down = grad_down.T

    grad_key_value = (
        g_kv[:, :KV_WIDTH]
        .reshape(small, KEY_VALUE_HEADS, 2, HEAD_SIZE)
        .transpose(0, 2, 1, 3)
        .reshape(small, KV_WIDTH)
    )

    added = []
    for out_mine, out_other in outs:
        out = after(out_mine, before_input) + after(swap_core(out_other), before_input)
        added.append(lax.psum_scatter(out, "heads", scatter_dimension=0, tiled=True))
    layer_out = finish_layer(table, *hiddens, *added)

    return (
        from_order(layer_out).reshape(tokens.shape),
        from_order(tokens_grad).reshape(tokens.shape),
        g_kv[:, KV_WIDTH + ATTENTION_GAIN],
        grad_query,
        grad_key_value,
        g_kv[:per_head, KV_WIDTH + HEAD_GAIN],
        grad_output,
        g_kv[:, KV_WIDTH + FEED_GAIN],
        grad_gate,
        grad_up,
        grad_down,
    )


def order_kernel(table, values, out):
    for j in range(values.shape[1] // BLOCK):
        out[:, span(j)] = values[:, place(table, j)]


def order_columns(table, values):
    return kernel_call(
        order_kernel,
        "order_columns",
        (1,),
        [whole(values)],
        fixed_out(values.shape),
        shape(values.shape, values.dtype),
        [],
        0,
        table,
    )(values)


def solution(mesh):
    every = ("dp", "seq", "heads")
    token_spec = P(None, "dp", ("seq", "heads"), None)
    return jax.shard_map(
        on_device,
        mesh=mesh,
        in_specs=(
            token_spec,
            P(None, "dp", None),
            P(every),
            P(("dp", "seq"), "heads"),
            P(every, None),
            P(every),
            P(None, every),
            P(every),
            P(("dp", "seq"), "heads"),
            P(("dp", "seq"), "heads"),
            P("heads", ("dp", "seq")),
            token_spec,
        ),
        out_specs=(
            token_spec,
            token_spec,
            P(every),
            P(("dp", "seq"), "heads"),
            P(every, None),
            P(every),
            P(None, every),
            P(every),
            P(("dp", "seq"), "heads"),
            P(("dp", "seq"), "heads"),
            P("heads", ("dp", "seq")),
        ),
        check_vma=False,
    )
```

time: 1200 us -> 867 us (0.72)
  Pallas kernels: 65.8 us -> 281 us
  waiting for transfers between devices: 539 us -> 332 us
  matrix products: 182 us -> 8.4 us
  local copies, waits for them, and re-layouts: 182 us -> 73.5 us
  other arithmetic: 139 us -> 77.3 us
    pallas_call x4 -> x23, Pallas kernels: 65.8 us -> 281 us  [the longest x15 218 us: call(): pl.pallas_call(body, grid=grid, in_specs=in_specs, out_specs=out_specs, s...]
    dot_general x32 -> x0, matrix products: 123 us -> none  [the longest x16 63.9 us: dot_nt(): lax.dot_general(left, right, (((1,), (1,)), ((), ())), preferred_element_...]
    ppermute x10 -> x18, waiting for transfers between devices: 164 us -> 66.1 us  [swap_y(): return lax.ppermute(v, 'dp', [(0, 1), (1, 0)])]
    reduce_scatter x8 -> x6, waiting for transfers between devices: 78.2 us -> 0.07 us  [the longest x2 0.04 us: on_device(): lax.psum_scatter(out, 'heads', scatter_dimension=0, tiled=True)]
    ppermute x14 -> x22, waiting for transfers between devices: 135 us -> 75.9 us  [swap_x(): return lax.ppermute(v, 'seq', [(i, i ^ 2) for i in range(4)])]
    dot_general x8 -> x4, matrix products: 58.5 us -> 8.4 us  [dot_tn(): lax.dot_general(left, right, (((0,), (0,)), ((), ())), preferred_element_...]
    another operation x24 -> x2, other arithmetic: 40.5 us -> 0.35 us  [the longest x6 19.5 us: along_y(): return jnp.stack([u, swap_y(u)], axis=0)]
    ppermute x15 -> x8, waiting for transfers between devices: 48.4 us -> 86.1 us  [the longest x6 60.7 us: step(): lax.ppermute(jnp.where(upper, low, high), 'heads', [(i, i ^ distance) for...]
  transfers between devices with their start and end apart: 74 -> 86, of which waited for: 32 -> 28; matrix products, arithmetic and copies ran while one was open for 38% -> 15% of each run, Pallas kernels for 6% -> 31%
where the time goes in v2:
time: 867 us; the launch traced here: 856 us
  waiting for transfers between devices  332 us (38%)
  Pallas kernels  281 us (32%)
  other arithmetic  77.3 us (9%)
  local copies, waits for them, and re-layouts  73.5 us (8%)
  starting transfers between devices  68.3 us (8%)
  between operations  16.1 us (2%)
    pallas_call x15, Pallas kernels, call(): pl.pallas_call(body, grid=grid, in_specs=in_specs, out_specs=out_specs, s...  218 us
    ppermute x22, waiting for transfers between devices, swap_x(): return lax.ppermute(v, 'seq', [(i, i ^ 2) for i in range(4)])  75.9 us
    ppermute x18, waiting for transfers between devices, swap_y(): return lax.ppermute(v, 'dp', [(0, 1), (1, 0)])  66.1 us
    pallas_call x8, Pallas kernels, call(): pl.pallas_call(body, grid_spec=pltpu.PrefetchScalarGridSpec(num_scalar_pr...  63.3 us
    ppermute x6, waiting for transfers between devices, step(): lax.ppermute(jnp.where(upper, low, high), 'heads', [(i, i ^ distance) for...  60.7 us
    all_gather x1, waiting for transfers between devices, on_device(): lax.all_gather(after(jnp.concatenate([kv_low, swap_x(kv_low)], axis=0), g...  45.3 us
    all_gather x2, waiting for transfers between devices, on_device(): feed_mine = lax.all_gather(feed_rows, 'heads', axis=0, tiled=True)  45.2 us
    ppermute x22, starting transfers between devices, swap_x(): return lax.ppermute(v, 'seq', [(i, i ^ 2) for i in range(4)])  29.4 us
  transfers between devices with their start and end apart: 86, of which 28 were waited for; matrix products, arithmetic and copies ran while one was open for 15% of the time, Pallas kernels for 31%

profile of v2, /device:TPU:0, one launch (start us, length us, event | category | flops | bytes accessed | tf_op | source)
XLA Modules:
  0.0 856.2 jit_solution(18250466325074378639)
XLA Ops:
  27.0 6.0 collective-permute-done.3
  33.0 6.0 collective-permute-start.4
  39.0 5.5 fusion.7
  49.5 19.5 %collective-permute-done.4 = bf16[128,1024]{1,0:T(8,128)(2,1)} collective-permute-done((bf16[128,1024]{1,0:T(8,128)(2,1)S(1)}, bf16[128,1024]{1,0:T(8,128)(2,1)}, u32[]{:S(2)}, u32[]{:S(2)}) %collective-permute-start.4) | collective-permute-done | bytes 262176 | tf_op jit(solution)/shard_map/ppermute | solution.py:900
  73.7 8.8 %collective-permute-done.6.refs_2_ = bf16[256,1024]{1,0:T(8,128)(2,1)S(1)} collective-permute-done((bf16[256,1024]{1,0:T(8,128)(2,1)S(1)}, bf16[256,1024]{1,0:T(8,128)(2,1)S(1)}, u32[]{:S(2)}, u32[]{:S(2)}) %collective-permute-start.6) | collective-permute-done | bytes 524320 | tf_op jit(solution)/shard_map/ppermute | solution.py:875
  90.8 4.1 collective-permute-done.7.refs_3_
  103.1 7.3 project_key_value.1
  110.4 35.5 %collective-permute-done.12 = bf16[256,896]{1,0:T(8,128)(2,1)S(1)} collective-permute-done((bf16[256,896]{1,0:T(8,128)(2,1)}, bf16[256,896]{1,0:T(8,128)(2,1)S(1)}, u32[]{:S(2)}, u32[]{:S(2)}) %collective-permute-start.12) | collective-permute-done | bytes 458784 | tf_op jit(solution)/shard_map/ppermute | solution.py:869
  156.7 18.8 %collective-permute-done.16.refs_2_ = bf16[256,1792]{1,0:T(8,128)(2,1)} collective-permute-done((bf16[256,1792]{1,0:T(8,128)(2,1)S(1)}, bf16[256,1792]{1,0:T(8,128)(2,1)}, u32[]{:S(2)}, u32[]{:S(2)}) %collective-permute-start.16) | collective-permute-done | bytes 917536 | tf_op jit(solution)/shard_map/ppermute | solution.py:875
  179.8 45.3 %all-gather.6.cloned.1.call-done = bf16[2048,896]{1,0:T(8,128)(2,1)} async-done(((bf16[512,896]{1,0:T(8,128)(2,1)}), bf16[2048,896]{1,0:T(8,128)(2,1)}) %all-gather.6.cloned.1.call-update) | async-done | bytes 3670032 | tf_op jit(solution)/shard_map/all_gather | solution.py:1078
  226.4 6.9 collective-permute-done.21.refs_4_
  237.9 17.7 %collective-permute-done.25.refs_3_ = bf16[256,1792]{1,0:T(8,128)(2,1)S(1)} collective-permute-done((bf16[256,1792]{1,0:T(8,128)(2,1)S(1)}, bf16[256,1792]{1,0:T(8,128)(2,1)S(1)}, u32[]{:S(2)}, u32[]{:S(2)}) %collective-permute-start.25) | collective-permute-done | bytes 917536 | tf_op jit(solution)/shard_map/ppermute | solution.py:875
  255.6 9.8 %project_query.1 = (f32[256,1792]{1,0:T(8,128)}, bf16[256,1792]{1,0:T(8,128)(2,1)}) custom-call(bf16[256,2048]{1,0:T(8,128)(2,1)} %get-tuple-element.154.normed, f32[256,128]{1,0:T(8,128)} %pad_maximum_fusion.8.cosine, f32[256,128]{1,0:T(8,128)} %pad_maximum_fusion.9.sine, f32[1,128]{1,0:T(1,128)} %pad_maximum_fusion.13.gain, bf16[256,1792]{1,0:T(8,128)(2,1)} %copy-done.13, ...), custom_call_target="tpu_custom_call" | custom-call | flops 1879048192 | bytes 11403776 | tf_op jit(solution)/shard_map/project_query/pallas_call | solution.py:78
  265.4 11.0 %attention_forward.2 = (bf16[128,1792]{1,0:T(8,128)(2,1)}, f32[7,1,512]{2,1,0:T(1,128)}) custom-call(bf16[8,2,128,896]{3,2,1,0:T(8,128)(2,1)} %bitcast.89, bf16[8,2,128,896]{3,2,1,0:T(8,128)(2,1)} %bitcast.19.kv1, bf16[256,1792]{1,0:T(8,128)(2,1)} %get-tuple-element.117.query, f32[1024,128]{1,0:T(8,128)} %get-tuple-element.288.bias0, ...), custom_call_target="tpu_custom_call" | custom-call | flops 11274289152 | bytes 9779200 | tf_op jit(solution)/shard_map/attention_forward/pallas_call | solution.py:78
  278.2 9.6 %project_output.2 = (f32[128,2048]{1,0:T(8,128)}, bf16[128,2048]{1,0:T(8,128)(2,1)}) custom-call(s32[8]{0:T(128)} %broadcast_xor_fusion.table, bf16[128,1792]{1,0:T(8,128)(2,1)} %get-tuple-element.114.mixed, bf16[256,2048]{1,0:T(8,128)(2,1)} %bitcast.66, f32[8,2048]{1,0:T(8,128)} %get-tuple-element.115.gains, bf16[256,1792]{1,0:T(8,128)(2,1)} %bitcast.61, ...), custom_call_target="tpu_custom_call" | custom-call | flops 939524096 | bytes 10485760 | tf_op jit(solution)/shard_map/project_output/pallas_call | solution.py:87
  291.0 4.9 fusion.34
  295.8 36.7 %all-gather.8.cloned.1.call-done.refs_1_.refs_2_.refs_3_ = bf16[512,2048]{1,0:T(8,128)(2,1)} async-done(((bf16[128,2048]{1,0:T(8,128)(2,1)}), bf16[512,2048]{1,0:T(8,128)(2,1)}) %all-gather.8.cloned.1.call-update) | async-done | bytes 2097168 | tf_op jit(solution)/shard_map/all_gather | solution.py:1092
  332.6 11.0 %attention_forward.3 = (bf16[128,1792]{1,0:T(8,128)(2,1)}, f32[7,1,512]{2,1,0:T(1,128)}) custom-call(bf16[8,2,128,896]{3,2,1,0:T(8,128)(2,1)} %bitcast.90, bf16[8,2,128,896]{3,2,1,0:T(8,128)(2,1)} %bitcast.19.kv1, bf16[256,1792]{1,0:T(8,128)(2,1)} %get-tuple-element.117.query, f32[1024,128]{1,0:T(8,128)} %get-tuple-element.287.bias0, ...), custom_call_target="tpu_custom_call" | custom-call | flops 11274289152 | bytes 9779200 | tf_op jit(solution)/shard_map/attention_forward/pallas_call | solution.py:78
  343.6 9.6 %project_output.3 = (f32[128,2048]{1,0:T(8,128)}, bf16[128,2048]{1,0:T(8,128)(2,1)}) custom-call(s32[8]{0:T(128)} %broadcast_xor_fusion.table, bf16[128,1792]{1,0:T(8,128)(2,1)} %get-tuple-element.119.mixed, bf16[256,2048]{1,0:T(8,128)(2,1)} %bitcast.67, f32[8,2048]{1,0:T(8,128)} %get-tuple-element.115.gains, bf16[256,1792]{1,0:T(8,128)(2,1)} %bitcast.62, ...), custom_call_target="tpu_custom_call" | custom-call | flops 939524096 | bytes 10485760 | tf_op jit(solution)/shard_map/project_output/pallas_call | solution.py:87
  354.8 34.3 %feed_forward.2 = (bf16[1024,896]{1,0:T(8,128)(2,1)}, bf16[1024,1664]{1,0:T(8,128)(2,1)}, bf16[512,2048]{1,0:T(8,128)(2,1)}, bf16[512,2048]{1,0:T(8,128)(2,1)}, ...) custom-call(bf16[512,2048]{1,0:T(8,128)(2,1)} %copy-done, ...), custom_call_target="tpu_custom_call" | custom-call | flops 20132659200 | bytes 32505856 | tf_op jit(solution)/shard_map/feed_forward/pallas_call | solution.py:78
  389.7 8.5 all-gather.10.cloned.1.call-done.refs_1_.refs_6_.refs_7_
  398.7 4.4 add.304
  406.8 34.4 %feed_forward.3 = (bf16[1024,896]{1,0:T(8,128)(2,1)}, bf16[1024,1664]{1,0:T(8,128)(2,1)}, bf16[512,2048]{1,0:T(8,128)(2,1)}, bf16[512,2048]{1,0:T(8,128)(2,1)}, ...) custom-call(bf16[512,2048]{1,0:T(8,128)(2,1)} %copy-done.1, ...), custom_call_target="tpu_custom_call" | custom-call | flops 20132659200 | bytes 32505856 | tf_op jit(solution)/shard_map/feed_forward/pallas_call | solution.py:78
  441.4 9.7 %weight_grad.6 = bf16[1024,896]{1,0:T(8,128)(2,1)} custom-call(bf16[512,2048]{1,0:T(8,128)(2,1)} %copy-done, bf16[512,2048]{1,0:T(8,128)(2,1)} %copy-done, bf16[512,2048]{1,0:T(8,128)(2,1)} %all-gather.8.cloned.1.call-done.refs_1_.refs_2_.refs_3_, bf16[512,2048]{1,0:T(8,128)(2,1)} %all-gather.8.cloned.1.call-done.refs_1_.refs_2_.refs_3_, ...), custom_call_target="tpu_custom_call" | custom-call | flops 3758096384 | bytes 25427968 | tf_op jit(solution)/shard_map/weight_grad/pallas_call | solution.py:78
  454.5 8.7 %weight_grad.7 = bf16[1024,768]{1,0:T(8,128)(2,1)} custom-call(bf16[512,2048]{1,0:T(8,128)(2,1)} %copy-done, bf16[512,2048]{1,0:T(8,128)(2,1)} %copy-done, bf16[512,2048]{1,0:T(8,128)(2,1)} %all-gather.8.cloned.1.call-done.refs_1_.refs_2_.refs_3_, bf16[512,2048]{1,0:T(8,128)(2,1)} %all-gather.8.cloned.1.call-done.refs_1_.refs_2_.refs_3_, ...), custom_call_target="tpu_custom_call" | custom-call | flops 3221225472 | bytes 25165824 | tf_op jit(solution)/shard_map/weight_grad/pallas_call | solution.py:78
  471.1 9.8 %hidden_back.2 = (f32[128,2048]{1,0:T(8,128)}, bf16[128,2048]{1,0:T(8,128)(2,1)}, f32[8,2048]{1,0:T(8,128)}, bf16[128,1792]{1,0:T(8,128)(2,1)}) custom-call(s32[8]{0:T(128)} %broadcast_xor_fusion.table, bf16[128,2048]{1,0:T(8,128)(2,1)} %reduce-scatter.7.cloned.1.call-done.d_feed, f32[128,2048]{1,0:T(8,128)} %get-tuple-element.116.hidden.hidden0, ...), custom_call_target="tpu_custom_call" | custom-call | flops 939524096 | bytes 12124160 | tf_op jit(solution)/shard_map/hidden_back/pallas_call | solution.py:87
  481.0 24.5 %attention_backward.2 = (bf16[128,1792]{1,0:T(8,128)(2,1)}, bf16[1024,896]{1,0:T(8,128)(2,1)}, bf16[1024,896]{1,0:T(8,128)(2,1)}, f32[8,128]{1,0:T(8,128)}) custom-call(bf16[8,2,128,896]{3,2,1,0:T(8,128)(2,1)} %bitcast.91, bf16[8,2,128,896]{3,2,1,0:T(8,128)(2,1)} %bitcast.19.kv1, bf16[256,1792]{1,0:T(8,128)(2,1)} %get-tuple-element.117.query, ...), custom_call_target="tpu_custom_call" | custom-call | flops 26306674688 | bytes 16468480 | tf_op jit(solution)/shard_map/attention_backward/pallas_call | solution.py:78
  507.1 22.8 %collective-permute-done.41 = bf16[640,768]{1,0:T(8,128)(2,1)S(1)} collective-permute-done((bf16[640,768]{1,0:T(8,128)(2,1)S(1)}, bf16[640,768]{1,0:T(8,128)(2,1)S(1)}, u32[]{:S(2)}, u32[]{:S(2)}) %collective-permute-start.41) | collective-permute-done | bytes 983072 | tf_op jit(solution)/shard_map/ppermute | solution.py:869
  529.8 9.1 %weight_grad.8 = bf16[1024,896]{1,0:T(8,128)(2,1)} custom-call(bf16[512,2048]{1,0:T(8,128)(2,1)} %collective-permute-done.33.refs_2_.refs_0_.refs_1_, bf16[512,2048]{1,0:T(8,128)(2,1)} %collective-permute-done.33.refs_2_.refs_0_.refs_1_, bf16[512,2048]{1,0:T(8,128)(2,1)} %bitcast.26.refs_3_.refs_2_, bf16[512,2048]{1,0:T(8,128)(2,1)} %bitcast.26.refs_3_.refs_2_, ...), custom_call_target="tpu_custom_call" | custom-call | flops 3758096384 | bytes 22282240 | tf_op jit(solution)/shard_map/weight_grad/pallas_call | solution.py:78
  546.0 9.8 %hidden_back.3 = (f32[128,2048]{1,0:T(8,128)}, bf16[128,2048]{1,0:T(8,128)(2,1)}, f32[8,2048]{1,0:T(8,128)}, bf16[128,1792]{1,0:T(8,128)(2,1)}) custom-call(s32[8]{0:T(128)} %broadcast_xor_fusion.table, bf16[128,2048]{1,0:T(8,128)(2,1)} %reduce-scatter.9.cloned.1.call-done.d_feed, f32[128,2048]{1,0:T(8,128)} %get-tuple-element.120.hidden.hidden1, ...), custom_call_target="tpu_custom_call" | custom-call | flops 939524096 | bytes 12124160 | tf_op jit(solution)/shard_map/hidden_back/pallas_call | solution.py:87
  569.6 24.4 %attention_backward.3 = (bf16[128,1792]{1,0:T(8,128)(2,1)}, bf16[1024,896]{1,0:T(8,128)(2,1)}, bf16[1024,896]{1,0:T(8,128)(2,1)}, f32[8,128]{1,0:T(8,128)}) custom-call(bf16[8,2,128,896]{3,2,1,0:T(8,128)(2,1)} %bitcast.92, bf16[8,2,128,896]{3,2,1,0:T(8,128)(2,1)} %bitcast.19.kv1, bf16[256,1792]{1,0:T(8,128)(2,1)} %get-tuple-element.117.query, ...), custom_call_target="tpu_custom_call" | custom-call | flops 26306674688 | bytes 16468480 | tf_op jit(solution)/shard_map/attention_backward/pallas_call | solution.py:78
  615.8 7.5 collective-permute-done.52
  636.9 8.9 %query_back.1.d_normed_q = f32[256,2048]{1,0:T(8,128)} custom-call(bf16[256,1792]{1,0:T(8,128)(2,1)} %copy-done.12, bf16[256,1792]{1,0:T(8,128)(2,1)} %copy-done.13, bf16[256,1792]{1,0:T(8,128)(2,1)} %copy-done.24, bf16[256,1792]{1,0:T(8,128)(2,1)} %collective-permute-done.16.refs_2_, bf16[256,1792]{1,0:T(8,128)(2,1)} %collective-permute-done.17.refs_3_, ...), custom_call_target="tpu_custom_call" | custom-call | flops 1879048192 | bytes 10354688 | tf_op jit(solution)/shard_map/query_back/pallas_call | solution.py:78
  648.6 8.6 %weight_grad.9 = bf16[1024,768]{1,0:T(8,128)(2,1)} custom-call(bf16[512,2048]{1,0:T(8,128)(2,1)} %copy-done, bf16[512,2048]{1,0:T(8,128)(2,1)} %copy-done, bf16[512,2048]{1,0:T(8,128)(2,1)} %all-gather.8.cloned.1.call-done.refs_1_.refs_2_.refs_3_, bf16[512,2048]{1,0:T(8,128)(2,1)} %all-gather.8.cloned.1.call-done.refs_1_.refs_2_.refs_3_, ...), custom_call_target="tpu_custom_call" | custom-call | flops 3221225472 | bytes 25165824 | tf_op jit(solution)/shard_map/weight_grad/pallas_call | solution.py:78
  663.3 8.8 %weight_grad.10 = bf16[1024,896]{1,0:T(8,128)(2,1)} custom-call(bf16[512,2048]{1,0:T(8,128)(2,1)} %collective-permute-done.33.refs_2_.refs_0_.refs_1_, bf16[512,2048]{1,0:T(8,128)(2,1)} %collective-permute-done.33.refs_2_.refs_0_.refs_1_, bf16[512,2048]{1,0:T(8,128)(2,1)} %bitcast.26.refs_3_.refs_2_, bf16[512,2048]{1,0:T(8,128)(2,1)} %bitcast.26.refs_3_.refs_2_, ...), custom_call_target="tpu_custom_call" | custom-call | flops 3758096384 | bytes 22282240 | tf_op jit(solution)/shard_map/weight_grad/pallas_call | solution.py:78
  673.1 4.2 maximum_add_fusion.1
  683.8 10.5 %input_back.1 = (bf16[256,896]{1,0:T(8,128)(2,1)}, f32[8,128]{1,0:T(8,128)}, f32[256,2048]{1,0:T(8,128)}, f32[8,2048]{1,0:T(8,128)}) custom-call(s32[8]{0:T(128)} %broadcast_xor_fusion.table, bf16[256,896]{1,0:T(8,128)(2,1)} %pad_maximum_fusion.7.d_pair, f32[256,896]{1,0:T(8,128)} %get-tuple-element.170.kv_raw, f32[256,128]{1,0:T(8,128)} %pad_maximum_fusion.8.cosine, ...), custom_call_target="tpu_custom_call" | custom-call | flops 939524096 | bytes 13767168 | tf_op jit(solution)/shard_map/input_back/pallas_call | solution.py:87
  695.1 4.5 add.312
  702.3 4.9 key_value_grad.1
  713.5 6.9 collective-permute-done.70
  724.6 9.7 %weight_grad.11 = bf16[1024,896]{1,0:T(8,128)(2,1)} custom-call(bf16[512,2048]{1,0:T(8,128)(2,1)} %copy-done, bf16[512,2048]{1,0:T(8,128)(2,1)} %copy-done, bf16[512,2048]{1,0:T(8,128)(2,1)} %all-gather.8.cloned.1.call-done.refs_1_.refs_2_.refs_3_, bf16[512,2048]{1,0:T(8,128)(2,1)} %all-gather.8.cloned.1.call-done.refs_1_.refs_2_.refs_3_, ...), custom_call_target="tpu_custom_call" | custom-call | flops 3758096384 | bytes 25427968 | tf_op jit(solution)/shard_map/weight_grad/pallas_call | solution.py:78
  740.6 19.4 %collective-permute-done.71 = bf16[128,1792]{1,0:T(8,128)(2,1)S(1)} collective-permute-done((bf16[128,1792]{1,0:T(8,128)(2,1)S(1)}, bf16[128,1792]{1,0:T(8,128)(2,1)S(1)}, u32[]{:S(2)}, u32[]{:S(2)}) %collective-permute-start.71) | collective-permute-done | bytes 458784 | tf_op jit(solution)/shard_map/ppermute | solution.py:880
  765.6 12.4 %collective-permute-done.72 = bf16[64,1792]{1,0:T(8,128)(2,1)S(1)} collective-permute-done((bf16[64,1792]{1,0:T(8,128)(2,1)S(1)}, bf16[64,1792]{1,0:T(8,128)(2,1)S(1)}, u32[]{:S(2)}, u32[]{:S(2)}) %collective-permute-start.72) | collective-permute-done | bytes 229408 | tf_op jit(solution)/shard_map/ppermute | solution.py:880
  779.0 8.5 collective-permute-done.74
  787.4 7.7 collective-permute-done.73
  802.6 18.2 %collective-permute-done.65 = bf16[128,1024]{1,0:T(8,128)(2,1)S(1)} collective-permute-done((bf16[128,1024]{1,0:T(8,128)(2,1)S(1)}, bf16[128,1024]{1,0:T(8,128)(2,1)S(1)}, u32[]{:S(2)}, u32[]{:S(2)}) %collective-permute-start.65) | collective-permute-done | bytes 262176 | tf_op jit(solution)/shard_map/ppermute | solution.py:880
  824.6 5.7 collective-permute-done.68
  835.6 3.8 collective-permute-done.69
  (485 shorter events, 215.7 us)
Async XLA Ops:
  7.2 141.4 %all-gather.12.cloned.1.call-start = ((), (), s32[]{:S(2)}) async-start(), calls=%async_computation.15 | async-start | bytes 7864320 | tf_op jit(solution)/shard_map/all_gather | solution.py:992
  15.5 209.6 %all-gather.6.cloned.1.call-start = ((), (), s32[]{:S(2)}) async-start(), calls=%async_computation.6 | async-start | bytes 4587520 | tf_op jit(solution)/shard_map/all_gather | solution.py:1078
  33.0 35.9 %collective-permute-start.4 = (bf16[128,1024]{1,0:T(8,128)(2,1)S(1)}, bf16[128,1024]{1,0:T(8,128)(2,1)}, u32[]{:S(2)}, u32[]{:S(2)}) collective-permute-start(bf16[128,1024]{1,0:T(8,128)(2,1)S(1)} %maximum_select_fusion.4), channel_id=1, source_target_pairs={{0,2},{1,3},{2,0},{3,1},{4,6},{5,7},{6,4},{7,5},{8,10},{9,11},{10,... | collective-permute-start | bytes 786440 | tf_op jit(solution)/shard_map/ppermute | solution.py:900
  45.6 37.7 %collective-permute-start.2 = (bf16[512,896]{1,0:T(8,128)(2,1)}, bf16[512,896]{1,0:T(8,128)(2,1)}, u32[]{:S(2)}, u32[]{:S(2)}) collective-permute-start(bf16[512,896]{1,0:T(8,128)(2,1)} %slice.729.refs_8_), channel_id=1, source_target_pairs={{0,16},{16,0},{1,17},{17,1},{2,18},{18,2},{3,19},{19,3},{4,20},{20... | collective-permute-start | bytes 2752520 | tf_op jit(solution)/shard_map/ppermute | solution.py:875
  45.6 37.7 %collective-permute-start.1 = (bf16[512,896]{1,0:T(8,128)(2,1)}, bf16[512,896]{1,0:T(8,128)(2,1)}, u32[]{:S(2)}, u32[]{:S(2)}) collective-permute-start(bf16[512,896]{1,0:T(8,128)(2,1)} %slice.729.refs_8_), channel_id=1, source_target_pairs={{0,8},{4,12},{8,0},{12,4},{1,9},{5,13},{9,1},{13,5},{2,10},{6,14},... | collective-permute-start | bytes 2752520 | tf_op jit(solution)/shard_map/ppermute | solution.py:869
  87.4 60.6 %collective-permute-start.14 = (bf16[512,1664]{1,0:T(8,128)(2,1)}, bf16[512,1664]{1,0:T(8,128)(2,1)}, u32[]{:S(2)}, u32[]{:S(2)}) collective-permute-start(bf16[512,1664]{1,0:T(8,128)(2,1)} %slice.744.refs_4_), channel_id=1, source_target_pairs={{0,16},{16,0},{1,17},{17,1},{2,18},{18,2},{3,19},{19,3},{4,20},{20... | collective-permute-start | bytes 5111816 | tf_op jit(solution)/shard_map/ppermute | solution.py:875
  96.1 52.0 %collective-permute-start.13 = (bf16[512,1664]{1,0:T(8,128)(2,1)}, bf16[512,1664]{1,0:T(8,128)(2,1)}, u32[]{:S(2)}, u32[]{:S(2)}) collective-permute-start(bf16[512,1664]{1,0:T(8,128)(2,1)} %slice.744.refs_4_), channel_id=1, source_target_pairs={{0,8},{4,12},{8,0},{12,4},{1,9},{5,13},{9,1},{13,5},{2,10},{6,14},... | collective-permute-start | bytes 5111816 | tf_op jit(solution)/shard_map/ppermute | solution.py:869
  110.4 35.6 %collective-permute-start.12 = (bf16[256,896]{1,0:T(8,128)(2,1)}, bf16[256,896]{1,0:T(8,128)(2,1)S(1)}, u32[]{:S(2)}, u32[]{:S(2)}) collective-permute-start(bf16[256,896]{1,0:T(8,128)(2,1)} %get-tuple-element.107), channel_id=1, source_target_pairs={{0,8},{4,12},{8,0},{12,4},{1,9},{5,13},{9,1},{13,5},{2,10},{6,14},... | collective-permute-start | bytes 1376264 | tf_op jit(solution)/shard_map/ppermute | solution.py:869
  148.0 184.5 %all-gather.8.cloned.1.call-start = ((), (), s32[]{:S(2)}) async-start(), calls=%async_computation.7 | async-start | bytes 2621440 | tf_op jit(solution)/shard_map/all_gather | solution.py:1092
  152.4 23.1 %collective-permute-start.16 = (bf16[256,1792]{1,0:T(8,128)(2,1)S(1)}, bf16[256,1792]{1,0:T(8,128)(2,1)}, u32[]{:S(2)}, u32[]{:S(2)}) collective-permute-start(bf16[256,1792]{1,0:T(8,128)(2,1)S(1)} %copy.120.refs_0_), channel_id=1, source_target_pairs={{0,16},{16,0},{1,17},{17,1},{2,18},{18,2},{3,19},{19,3},{4,20},{20... | collective-permute-start | bytes 2752520 | tf_op jit(solution)/shard_map/ppermute | solution.py:875
  176.9 48.2 %collective-permute-start.17 = (bf16[256,1792]{1,0:T(8,128)(2,1)}, bf16[256,1792]{1,0:T(8,128)(2,1)}, u32[]{:S(2)}, u32[]{:S(2)}) collective-permute-start(bf16[256,1792]{1,0:T(8,128)(2,1)} %collective-permute-done.16.refs_2_), channel_id=1, source_target_pairs={{0,8},{4,12},{8,0},{12,4},{1,9},{5,13},{9,1},{13,5},{2,10},{6,14},... | collective-permute-start | bytes 2752520 | tf_op jit(solution)/shard_map/ppermute | solution.py:869
  178.4 46.7 %collective-permute-start.19 = (bf16[256,1792]{1,0:T(8,128)(2,1)S(1)}, bf16[256,1792]{1,0:T(8,128)(2,1)S(1)}, u32[]{:S(2)}, u32[]{:S(2)}) collective-permute-start(bf16[256,1792]{1,0:T(8,128)(2,1)S(1)} %bitcast.58), channel_id=1, source_target_pairs={{0,16},{16,0},{1,17},{17,1},{2,18},{18,2},{3,19},{19,3},{4,20},{20... | collective-permute-start | bytes 2752520 | tf_op jit(solution)/shard_map/ppermute | solution.py:875
  178.9 46.2 %collective-permute-start.18 = (bf16[256,1792]{1,0:T(8,128)(2,1)S(1)}, bf16[256,1792]{1,0:T(8,128)(2,1)S(1)}, u32[]{:S(2)}, u32[]{:S(2)}) collective-permute-start(bf16[256,1792]{1,0:T(8,128)(2,1)S(1)} %bitcast.59), channel_id=1, source_target_pairs={{0,8},{4,12},{8,0},{12,4},{1,9},{5,13},{9,1},{13,5},{2,10},{6,14},... | collective-permute-start | bytes 2752520 | tf_op jit(solution)/shard_map/ppermute | solution.py:869
  225.1 40.3 %collective-permute-start.20 = (bf16[2048,896]{1,0:T(8,128)(2,1)}, bf16[2048,896]{1,0:T(8,128)(2,1)}, u32[]{:S(2)}, u32[]{:S(2)}) collective-permute-start(bf16[2048,896]{1,0:T(8,128)(2,1)} %all-gather.6.cloned.1.call-done), channel_id=1, source_target_pairs={{0,4},{4,0},{8,12},{12,8},{1,5},{5,1},{9,13},{13,9},{2,6},{6,2},{1... | collective-permute-start | bytes 11010056 | tf_op jit(solution)/shard_map/ppermute | solution.py:872
  237.3 39.1 %collective-permute-start.26 = (bf16[256,1792]{1,0:T(8,128)(2,1)S(1)}, bf16[256,1792]{1,0:T(8,128)(2,1)S(1)}, u32[]{:S(2)}, u32[]{:S(2)}) collective-permute-start(bf16[256,1792]{1,0:T(8,128)(2,1)S(1)} %bitcast.60), channel_id=1, source_target_pairs={{0,4},{4,0},{8,12},{12,8},{1,5},{5,1},{9,13},{13,9},{2,6},{6,2},{1... | collective-permute-start | bytes 2752520 | tf_op jit(solution)/shard_map/ppermute | solution.py:872
  237.4 39.1 %collective-permute-start.28 = (bf16[256,1792]{1,0:T(8,128)(2,1)S(1)}, bf16[256,1792]{1,0:T(8,128)(2,1)S(1)}, u32[]{:S(2)}, u32[]{:S(2)}) collective-permute-start(bf16[256,1792]{1,0:T(8,128)(2,1)S(1)} %collective-permute-done.19.refs_2_), channel_id=1, source_target_pairs={{0,4},{4,0},{8,12},{12,8},{1,5},{5,1},{9,13},{13,9},{2,6},{6,2},{1... | collective-permute-start | bytes 2752520 | tf_op jit(solution)/shard_map/ppermute | solution.py:872
  237.9 38.6 %collective-permute-start.27 = (bf16[256,1792]{1,0:T(8,128)(2,1)S(1)}, bf16[256,1792]{1,0:T(8,128)(2,1)S(1)}, u32[]{:S(2)}, u32[]{:S(2)}) collective-permute-start(bf16[256,1792]{1,0:T(8,128)(2,1)S(1)} %collective-permute-done.18.refs_1_), channel_id=1, source_target_pairs={{0,4},{4,0},{8,12},{12,8},{1,5},{5,1},{9,13},{13,9},{2,6},{6,2},{1... | collective-permute-start | bytes 2752520 | tf_op jit(solution)/shard_map/ppermute | solution.py:872
  287.9 110.3 %all-gather.10.cloned.1.call-start = ((), (), s32[]{:S(2)}) async-start(), calls=%async_computation.8 | async-start | bytes 2621440 | tf_op jit(solution)/shard_map/all_gather | solution.py:1092
  287.9 55.7 %collective-permute-start.30 = (bf16[512,1664]{1,0:T(8,128)(2,1)}, bf16[512,1664]{1,0:T(8,128)(2,1)}, u32[]{:S(2)}, u32[]{:S(2)}) collective-permute-start(bf16[512,1664]{1,0:T(8,128)(2,1)} %collective-permute-done.13.refs_5_), channel_id=1, source_target_pairs={{0,16},{16,0},{1,17},{17,1},{2,18},{18,2},{3,19},{19,3},{4,20},{20... | collective-permute-start | bytes 5111816 | tf_op jit(solution)/shard_map/ppermute | solution.py:875
  289.5 54.1 %collective-permute-start.31 = (bf16[512,896]{1,0:T(8,128)(2,1)}, bf16[512,896]{1,0:T(8,128)(2,1)S(1)}, u32[]{:S(2)}, u32[]{:S(2)}) collective-permute-start(bf16[512,896]{1,0:T(8,128)(2,1)} %collective-permute-done.2.refs_10_), channel_id=1, source_target_pairs={{0,8},{4,12},{8,0},{12,4},{1,9},{5,13},{9,1},{13,5},{2,10},{6,14},... | collective-permute-start | bytes 2752520 | tf_op jit(solution)/shard_map/ppermute | solution.py:869
  295.8 57.7 %collective-permute-start.33 = (bf16[512,2048]{1,0:T(8,128)(2,1)}, bf16[512,2048]{1,0:T(8,128)(2,1)}, u32[]{:S(2)}, u32[]{:S(2)}) collective-permute-start(bf16[512,2048]{1,0:T(8,128)(2,1)} %bitcast.26.refs_3_.refs_2_), channel_id=1, source_target_pairs={{0,4},{4,0},{8,12},{12,8},{1,5},{5,1},{9,13},{13,9},{2,6},{6,2},{1... | collective-permute-start | bytes 6291464 | tf_op jit(solution)/shard_map/ppermute | solution.py:872
  353.3 117.8 %reduce-scatter.7.cloned.1.call-start = ((), (), s32[]{:S(2)}) async-start(), calls=%async_computation.9 | async-start | bytes 2621440 | tf_op jit(solution)/shard_map/reduce_scatter | solution.py:1111
  405.5 136.7 %reduce-scatter.9.cloned.1.call-start = ((), (), s32[]{:S(2)}) async-start(), calls=%async_computation.10 | async-start | bytes 2621440 | tf_op jit(solution)/shard_map/reduce_scatter | solution.py:1111
  441.2 25.4 %collective-permute-start.39 = (bf16[512,2048]{1,0:T(8,128)(2,1)}, bf16[512,2048]{1,0:T(8,128)(2,1)S(1)}, u32[]{:S(2)}, u32[]{:S(2)}) collective-permute-start(bf16[512,2048]{1,0:T(8,128)(2,1)} %get-tuple-element.140), channel_id=1, source_target_pairs={{0,4},{4,0},{8,12},{12,8},{1,5},{5,1},{9,13},{13,9},{2,6},{6,2},{1... | collective-permute-start | bytes 6291464 | tf_op jit(solution)/shard_map/ppermute | solution.py:872
  453.1 27.9 %collective-permute-start.37 = (bf16[384,896]{1,0:T(8,128)(2,1)}, bf16[384,896]{1,0:T(8,128)(2,1)}, u32[]{:S(2)}, u32[]{:S(2)}) collective-permute-start(bf16[384,896]{1,0:T(8,128)(2,1)} %slice.749), channel_id=1, source_target_pairs={{0,16},{16,0},{1,17},{17,1},{2,18},{18,2},{3,19},{19,3},{4,20},{20... | collective-permute-start | bytes 2064392 | tf_op jit(solution)/shard_map/ppermute | solution.py:875
  468.9 134.9 %reduce-scatter.11.cloned.1.call-start = ((), (), s32[]{:S(2)}) async-start(), calls=%async_computation.11 | async-start | bytes 2293760 | tf_op jit(solution)/shard_map/reduce_scatter | solution.py:1208
  470.5 59.3 %collective-permute-start.40 = (bf16[640,896]{1,0:T(8,128)(2,1)S(1)}, bf16[640,896]{1,0:T(8,128)(2,1)}, u32[]{:S(2)}, u32[]{:S(2)}) collective-permute-start(bf16[640,896]{1,0:T(8,128)(2,1)S(1)} %slice.751), channel_id=1, source_target_pairs={{0,16},{16,0},{1,17},{17,1},{2,18},{18,2},{3,19},{19,3},{4,20},{20... | collective-permute-start | bytes 3440648 | tf_op jit(solution)/shard_map/ppermute | solution.py:875
  505.5 36.8 %collective-permute-start.42 = (bf16[1024,896]{1,0:T(8,128)(2,1)}, bf16[1024,896]{1,0:T(8,128)(2,1)}, u32[]{:S(2)}, u32[]{:S(2)}) collective-permute-start(bf16[1024,896]{1,0:T(8,128)(2,1)} %get-tuple-element.145), channel_id=1, source_target_pairs={{0,4},{4,0},{8,12},{12,8},{1,5},{5,1},{9,13},{13,9},{2,6},{6,2},{1... | collective-permute-start | bytes 5505032 | tf_op jit(solution)/shard_map/ppermute | solution.py:872
  505.6 24.2 %collective-permute-start.41 = (bf16[640,768]{1,0:T(8,128)(2,1)S(1)}, bf16[640,768]{1,0:T(8,128)(2,1)S(1)}, u32[]{:S(2)}, u32[]{:S(2)}) collective-permute-start(bf16[640,768]{1,0:T(8,128)(2,1)S(1)} %slice.752), channel_id=1, source_target_pairs={{0,8},{4,12},{8,0},{12,4},{1,9},{5,13},{9,1},{13,5},{2,10},{6,14},... | collective-permute-start | bytes 2949128 | tf_op jit(solution)/shard_map/ppermute | solution.py:869
  561.0 34.1 %collective-permute-start.45 = (bf16[640,896]{1,0:T(8,128)(2,1)}, bf16[640,896]{1,0:T(8,128)(2,1)}, u32[]{:S(2)}, u32[]{:S(2)}) collective-permute-start(bf16[640,896]{1,0:T(8,128)(2,1)} %slice.756), channel_id=1, source_target_pairs={{0,8},{4,12},{8,0},{12,4},{1,9},{5,13},{9,1},{13,5},{2,10},{6,14},... | collective-permute-start | bytes 3440648 | tf_op jit(solution)/shard_map/ppermute | solution.py:869
  561.8 98.9 %reduce-scatter.17.cloned.1.call-start = ((), (), s32[]{:S(2)}) async-start(), calls=%async_computation.14 | async-start | bytes 2293760 | tf_op jit(solution)/shard_map/reduce_scatter | solution.py:1208
  568.5 27.4 %collective-permute-start.46 = (bf16[320,1792]{1,0:T(8,128)(2,1)S(1)}, bf16[320,1792]{1,0:T(8,128)(2,1)S(1)}, u32[]{:S(2)}, u32[]{:S(2)}) collective-permute-start(bf16[320,1792]{1,0:T(8,128)(2,1)S(1)} %slice.757), channel_id=1, source_target_pairs={{0,16},{16,0},{1,17},{17,1},{2,18},{18,2},{3,19},{19,3},{4,20},{20... | collective-permute-start | bytes 3440648 | tf_op jit(solution)/shard_map/ppermute | solution.py:875
  598.9 30.8 %collective-permute-start.47 = (bf16[1024,1792]{1,0:T(8,128)(2,1)}, bf16[1024,1792]{1,0:T(8,128)(2,1)}, u32[]{:S(2)}, u32[]{:S(2)}) collective-permute-start(bf16[1024,1792]{1,0:T(8,128)(2,1)} %convolution_convert_fusion), channel_id=1, source_target_pairs={{0,4},{4,0},{8,12},{12,8},{1,5},{5,1},{9,13},{13,9},{2,6},{6,2},{1... | collective-permute-start | bytes 11010056 | tf_op jit(solution)/shard_map/ppermute | solution.py:872
  599.4 95.6 %collective-permute-start.56 = (bf16[512,2048]{1,0:T(8,128)(2,1)}, bf16[512,2048]{1,0:T(8,128)(2,1)}, u32[]{:S(2)}, u32[]{:S(2)}) collective-permute-start(bf16[512,2048]{1,0:T(8,128)(2,1)} %get-tuple-element.161), channel_id=1, source_target_pairs={{0,4},{4,0},{8,12},{12,8},{1,5},{5,1},{9,13},{13,9},{2,6},{6,2},{1... | collective-permute-start | bytes 6291464 | tf_op jit(solution)/shard_map/ppermute | solution.py:872
  609.4 100.4 %collective-permute-start.57 = (bf16[512,2048]{1,0:T(8,128)(2,1)}, bf16[512,2048]{1,0:T(8,128)(2,1)}, u32[]{:S(2)}, u32[]{:S(2)}) collective-permute-start(bf16[512,2048]{1,0:T(8,128)(2,1)} %get-tuple-element.165), channel_id=1, source_target_pairs={{0,4},{4,0},{8,12},{12,8},{1,5},{5,1},{9,13},{13,9},{2,6},{6,2},{1... | collective-permute-start | bytes 6291464 | tf_op jit(solution)/shard_map/ppermute | solution.py:872
  613.2 207.7 %reduce-scatter.13.cloned.1.call-start = ((), (), s32[]{:S(2)}) async-start(), calls=%async_computation.12 | async-start | bytes 2621440 | tf_op jit(solution)/shard_map/reduce_scatter | solution.py:1326
  623.3 48.8 %collective-permute-start.53 = (bf16[128,896]{1,0:T(8,128)(2,1)}, bf16[128,896]{1,0:T(8,128)(2,1)}, u32[]{:S(2)}, u32[]{:S(2)}) collective-permute-start(bf16[128,896]{1,0:T(8,128)(2,1)} %slice.768), channel_id=1, source_target_pairs={{0,8},{4,12},{8,0},{12,4},{1,9},{5,13},{9,1},{13,5},{2,10},{6,14},... | collective-permute-start | bytes 688136 | tf_op jit(solution)/shard_map/ppermute | solution.py:869
  635.5 26.3 %collective-permute-start.51 = (bf16[192,1792]{1,0:T(8,128)(2,1)}, bf16[192,1792]{1,0:T(8,128)(2,1)S(1)}, u32[]{:S(2)}, u32[]{:S(2)}) collective-permute-start(bf16[192,1792]{1,0:T(8,128)(2,1)} %get-tuple-element.269), channel_id=1, source_target_pairs={{0,8},{4,12},{8,0},{12,4},{1,9},{5,13},{9,1},{13,5},{2,10},{6,14},... | collective-permute-start | bytes 2064392 | tf_op jit(solution)/shard_map/ppermute | solution.py:869
  647.9 34.9 %collective-permute-start.54 = (bf16[192,1792]{1,0:T(8,128)(2,1)}, bf16[192,1792]{1,0:T(8,128)(2,1)S(1)}, u32[]{:S(2)}, u32[]{:S(2)}) collective-permute-start(bf16[192,1792]{1,0:T(8,128)(2,1)} %get-tuple-element.268), channel_id=1, source_target_pairs={{0,8},{4,12},{8,0},{12,4},{1,9},{5,13},{9,1},{13,5},{2,10},{6,14},... | collective-permute-start | bytes 2064392 | tf_op jit(solution)/shard_map/ppermute | solution.py:869
  699.6 121.3 %reduce-scatter.15.cloned.1.call-start = ((), (), s32[]{:S(2)}) async-start(), calls=%async_computation.13 | async-start | bytes 2621440 | tf_op jit(solution)/shard_map/reduce_scatter | solution.py:1326
  723.3 36.8 %collective-permute-start.63 = (bf16[512,1024]{1,0:T(8,128)(2,1)S(1)}, bf16[512,1024]{1,0:T(8,128)(2,1)S(1)}, u32[]{:S(2)}, u32[]{:S(2)}) collective-permute-start(bf16[512,1024]{1,0:T(8,128)(2,1)S(1)} %slice_add_fusion.2), channel_id=1, source_target_pairs={{0,16},{16,0},{1,17},{17,1},{2,18},{18,2},{3,19},{19,3},{4,20},{20... | collective-permute-start | bytes 3145736 | tf_op jit(solution)/shard_map/ppermute | solution.py:875
  737.1 22.8 %collective-permute-start.71 = (bf16[128,1792]{1,0:T(8,128)(2,1)S(1)}, bf16[128,1792]{1,0:T(8,128)(2,1)S(1)}, u32[]{:S(2)}, u32[]{:S(2)}) collective-permute-start(bf16[128,1792]{1,0:T(8,128)(2,1)S(1)} %broadcast_select_fusion), channel_id=1, source_target_pairs={{0,2},{1,3},{2,0},{3,1},{4,6},{5,7},{6,4},{7,5},{8,10},{9,11},{10,... | collective-permute-start | bytes 1376264 | tf_op jit(solution)/shard_map/ppermute | solution.py:880
  739.8 39.1 %collective-permute-start.67 = (bf16[256,1792]{1,0:T(8,128)(2,1)S(1)}, bf16[256,1792]{1,0:T(8,128)(2,1)S(1)}, u32[]{:S(2)}, u32[]{:S(2)}) collective-permute-start(bf16[256,1792]{1,0:T(8,128)(2,1)S(1)} %slice.791), channel_id=1, source_target_pairs={{0,16},{16,0},{1,17},{17,1},{2,18},{18,2},{3,19},{19,3},{4,20},{20... | collective-permute-start | bytes 2752520 | tf_op jit(solution)/shard_map/ppermute | solution.py:875
  763.3 24.1 %collective-permute-start.74 = (bf16[512,896]{1,0:T(8,128)(2,1)S(1)}, bf16[512,896]{1,0:T(8,128)(2,1)S(1)}, u32[]{:S(2)}, u32[]{:S(2)}) collective-permute-start(bf16[512,896]{1,0:T(8,128)(2,1)S(1)} %slice.799), channel_id=1, source_target_pairs={{0,16},{16,0},{1,17},{17,1},{2,18},{18,2},{3,19},{19,3},{4,20},{20... | collective-permute-start | bytes 2752520 | tf_op jit(solution)/shard_map/ppermute | solution.py:875
  765.0 30.2 %collective-permute-start.73 = (bf16[512,896]{1,0:T(8,128)(2,1)S(1)}, bf16[512,896]{1,0:T(8,128)(2,1)S(1)}, u32[]{:S(2)}, u32[]{:S(2)}) collective-permute-start(bf16[512,896]{1,0:T(8,128)(2,1)S(1)} %slice.798), channel_id=1, source_target_pairs={{0,8},{4,12},{8,0},{12,4},{1,9},{5,13},{9,1},{13,5},{2,10},{6,14},... | collective-permute-start | bytes 2752520 | tf_op jit(solution)/shard_map/ppermute | solution.py:869
  795.2 25.6 %collective-permute-start.65 = (bf16[128,1024]{1,0:T(8,128)(2,1)S(1)}, bf16[128,1024]{1,0:T(8,128)(2,1)S(1)}, u32[]{:S(2)}, u32[]{:S(2)}) collective-permute-start(bf16[128,1024]{1,0:T(8,128)(2,1)S(1)} %broadcast_select_fusion.9), channel_id=1, source_target_pairs={{0,2},{1,3},{2,0},{3,1},{4,6},{5,7},{6,4},{7,5},{8,10},{9,11},{10,... | collective-permute-start | bytes 786440 | tf_op jit(solution)/shard_map/ppermute | solution.py:880
  798.5 31.8 %collective-permute-start.68 = (bf16[256,896]{1,0:T(8,128)(2,1)}, bf16[256,896]{1,0:T(8,128)(2,1)}, u32[]{:S(2)}, u32[]{:S(2)}) collective-permute-start(bf16[256,896]{1,0:T(8,128)(2,1)} %broadcast_select_fusion.1), channel_id=1, source_target_pairs={{0,2},{1,3},{2,0},{3,1},{4,6},{5,7},{6,4},{7,5},{8,10},{9,11},{10,... | collective-permute-start | bytes 1376264 | tf_op jit(solution)/shard_map/ppermute | solution.py:880
  802.3 38.1 %collective-permute-start.75 = (bf16[256,2560]{1,0:T(8,128)(2,1)}, bf16[256,2560]{1,0:T(8,128)(2,1)}, u32[]{:S(2)}, u32[]{:S(2)}) collective-permute-start(bf16[256,2560]{1,0:T(8,128)(2,1)} %pad_maximum_fusion.2), channel_id=1, source_target_pairs={{0,4},{4,0},{8,12},{12,8},{1,5},{5,1},{9,13},{13,9},{2,6},{6,2},{1... | collective-permute-start | bytes 3932168 | tf_op jit(solution)/shard_map/ppermute | solution.py:872
  (98 other events, 1018.3 us)
Sparse Core Ops, SparseCore 0:
  15.6 129.2 all-gather.11
  148.2 76.8 all-gather.5
  288.0 44.5 all-gather.7
  353.4 44.7 all-gather.9
  405.7 42.4 reduce-scatter.6
  469.1 40.3 reduce-scatter.8
  561.9 37.0 reduce-scatter.10
  613.3 36.9 reduce-scatter.16
  699.7 42.6 reduce-scatter.12
  744.6 56.5 reduce-scatter.14

commit v3 on v2

--- a/solution.py
+++ b/solution.py
@@ -865,24 +865,28 @@
     def after(v, *others):
         return lax.optimization_barrier((v, others))[0]
 
+    def beside(outs, parts):
+        return lax.optimization_barrier((outs, parts))
+
     def swap_x(v):
         return lax.ppermute(v, "seq", [(i, i ^ 2) for i in range(4)])
 
+    def swap_xy(v):
+        return lax.ppermute(v, ("dp", "seq"), [(i, i ^ 6) for i in range(8)])
+
     def swap_core(v):
         return lax.ppermute(v, "seq", [(i, i ^ 1) for i in range(4)])
 
     def swap_y(v):
         return lax.ppermute(v, "dp", [(0, 1), (1, 0)])
 
-    def pair_scatter(v, axis):
-        def step(u, upper, distance):
-            low, high = jnp.split(u, 2, axis=axis)
-            sent = lax.ppermute(
-                jnp.where(upper, low, high), "heads", [(i, i ^ distance) for i in range(4)]
-            )
-            return jnp.where(upper, high, low) + sent
-
-        return step(step(v, z >= 2, 2), z % 2 == 1, 1)
+    def line_scatter(v, axis):
+        cut = jnp.split(v, 4, axis=axis)
+        total = lax.select_n(z, *cut)
+        for k in range(1, 4):
+            block = lax.select_n(z, *[cut[i ^ k] for i in range(4)])
+            total = total + lax.ppermute(block, "heads", [(i, i ^ k) for i in range(4)])
+        return total
 
     def gather_near(v):
         if not paired:
@@ -1011,11 +1015,6 @@
         .reshape(query_weight.shape[0], Q_WIDTH)
     )
     o_rows = lined[:, batches * rows + small :, :Q_WIDTH].reshape(4 * small, Q_WIDTH)
-    q_near = gather_near(q_rows)
-    q_full = both_cores(gather_far(q_near, False))
-    o_near = gather_near(after(o_rows, q_near))
-    o_full = both_cores(gather_far(o_near, True))
-
     units = gate_weight.shape[1] // 2
     act_width, units_width = up_to(units), up_to(2 * units)
 
@@ -1037,7 +1036,6 @@
     down_near = gather_near(ffn_rows[:, units_width:])
     gate_up_near = gather_near(after(ffn_rows[:, :units_width], kvg_near))
     gate_up = unit_pieces(gather_far(gate_up_near, True))
-    down = unit_pieces(gather_far(down_near, False))
     kvg = both_cores(gather_far(after(kvg_near, down_near), True))
 
     head_column = jnp.concatenate([part[:, KV_WIDTH + HEAD_GAIN] for part in kvg])
@@ -1073,27 +1071,35 @@
     normed, kv_raw, kv_low, gains = project_key_value(
         table, after(tokens_in, down_near), cosine, sine, key_gain, kvg
     )
-    q_raw, queries = project_query(normed, cosine, sine, query_gain, q_full)
-
-    kv_lined = lax.all_gather(
-        after(jnp.concatenate([kv_low, swap_x(kv_low)], axis=0), gate_up_near), "heads", axis=0, tiled=True
-    )
-    kv_lined = after(kv_lined, q_full[:4], o_near)
-    kv_other = swap_core(kv_lined)
-    kvs = (kv_lined, kv_other)
+    kv_pair = jnp.concatenate([kv_low, swap_x(kv_low)], axis=0)
+    kv_lined = lax.all_gather(after(kv_pair, gate_up_near), "heads", axis=0, tiled=True)
+    down = unit_pieces(gather_far(down_near, False))
+    q_near = gather_near(q_rows)
+    q_full = both_cores(gather_far(q_near, False))
+    o_near = gather_near(after(o_rows, q_near))
+    q_raw, queries = project_query(after(normed, o_near), cosine, sine, query_gain, q_full)
+    o_pieces = gather_far(after(o_near, queries), True)
+    kv_lined = after(kv_lined, queries)
+    kvs = (kv_lined, swap_core(kv_lined))
+
     feeds, mixeds, lses, hiddens = [], [], [], []
     for batch in range(batches):
         query = queries if batch == 0 else after(queries, hiddens[0])
         mixed, lse = attention_forward(*kvs, query, batch, *biases[batch])
-        mixed_tied = mixed if batch == 0 else after(mixed, gate_up, down)
+        if batch == 0:
+            o_full = both_cores(after(o_pieces, mixed))
+        else:
+            (mixed, lse), (gate_up, down) = beside((mixed, lse), (gate_up, down))
         hidden_in, feed_rows = project_output(
-            table, mixed_tied, tokens_in, batch, gains, o_full
+            table, mixed, tokens_in, batch, gains, o_full
         )
-        feed_mine = lax.all_gather(feed_rows, "heads", axis=0, tiled=True)
-        feeds.append((swap_core(feed_mine), feed_mine))
+        feeds.append(lax.all_gather(feed_rows, "heads", axis=0, tiled=True))
         mixeds.append(mixed)
         lses.append(lse)
         hiddens.append(hidden_in)
+
+    feeds[0] = after(feeds[0], feed_rows)
+    feeds = [(swap_core(v), v) for v in feeds]
 
     d_feeds, acts, d_units, cots, outs = [], [], [], [], []
     for batch in range(batches):
@@ -1156,6 +1162,7 @@
         g = lax.psum_scatter(g, "dp", scatter_dimension=0)
         return g[0] + swap_x(g[1])
 
+    added = [out_mine + swap_core(out_other) for out_mine, out_other in outs]
     d_hiddens, d_attendeds, d_q_raws, d_lined = [], [], [], []
     feed_gain_grads, query_gain_grads = [], []
     mixed_all = jnp.concatenate(mixeds, axis=0)
@@ -1171,26 +1178,27 @@
         if batch == 1:
             d_feed = after(d_feed, d_q_raws[0])
             if paired:
-                tied = after(acts, d_q_raws[0], first_parts[1], second_parts[1])
+                tied = after(acts, d_q_raws[0], added)
                 down_far = weight_grad(cot_all, tied, slice(0, act_width), 2, 2, 1)
                 down_parts = send_parts(down_far, swap_x, 256, 640, 128)
                 d_feed = after(d_feed, down_far, last_kv)
-        d_hidden, d_attended, feed_grad, d_mixed = hidden_back(
-            table, d_feed, hiddens[batch], cot_in, batch, gains, o_full
-        )
+        back = hidden_back(table, d_feed, hiddens[batch], cot_in, batch, gains, o_full)
+        if paired and batch == 0:
+            back, (first_parts[0], second_parts[0]) = beside(
+                back, (first_parts[0], second_parts[0])
+            )
+        if paired and batch == 1:
+            back, down_parts[0] = beside(back, down_parts[0])
+        d_hidden, d_attended, feed_grad, d_mixed = back
         d_hiddens.append(d_hidden)
         d_attendeds.append(d_attended)
-        if batch == 0 and paired:
-            d_mixed = after(d_mixed, first_parts[0], second_parts[0])
         if batch == 1:
-            if paired:
-                d_attendeds[1] = after(d_attended, down_parts[0])
             o_grads = both_grads(jnp.concatenate(d_attendeds, axis=0), mixed_all)
             o_send, o_keep = split_rows(o_grads[0], swap_core(o_grads[1]))
             d_mixed = after(d_mixed, o_send)
             if paired:
-                o_parts = send_parts(o_send, swap_y, 320, 128, 64)
-        d_q_raw, d_kv0, d_kv1, query_grad = attention_backward(
+                o_parts = send_parts(o_send, swap_y, 256, 128, 128)
+        back = attention_backward(
             *kvs,
             queries,
             batch,
@@ -1203,6 +1211,13 @@
             sine,
             query_gain,
         )
+        if paired and batch == 0:
+            back, (first_parts[1], second_parts[1]) = beside(
+                back, (first_parts[1], second_parts[1])
+            )
+        if paired and batch == 1:
+            back, (down_parts[1], o_parts[0]) = beside(back, (down_parts[1], o_parts[0]))
+        d_q_raw, d_kv0, d_kv1, query_grad = back
         d_kv = d_kv0 + swap_core(d_kv1)
         last_kv = d_kv
         d_lined.append(lax.psum_scatter(d_kv, "heads", scatter_dimension=0, tiled=True))
@@ -1210,24 +1225,26 @@
         feed_gain_grads.append(feed_grad)
         query_gain_grads.append(query_grad)
 
-    d_pairs = [pair[:rows] + swap_x(pair[rows:]) for pair in d_lined]
+    pairs_got = [swap_x(d_lined[0][rows:])]
     d_q_raw_all = jnp.concatenate(d_q_raws, axis=0)
-    late = (down_parts[1], o_parts[0]) if paired else ()
-    q_grads = both_grads(after(normed, d_q_raws[1], late), d_q_raw_all)
+    q_grads = both_grads(after(normed, last_kv), d_q_raw_all)
+    if paired:
+        q_grads, (down_parts[2], o_parts[1], pairs_got) = beside(
+            q_grads, (down_parts[2], o_parts[1], pairs_got)
+        )
     q_send, q_keep = split_rows(q_grads[0], swap_core(q_grads[1]), False)
-    d_normed_q = query_back(after(d_q_raw_all, q_send, d_pairs[0]), q_full)
+    d_normed_q = query_back(after(d_q_raw_all, q_send), q_full)
     if paired:
-        q_parts = send_parts(q_send, swap_x, 128, 192, 192)
-        tied = after(d_units, d_normed_q, q_parts[0], o_parts[1])
-        second_got = jnp.concatenate(second_parts, axis=0)
-        second_half = weight_grad(feed_all, tied, second_cut, 2, 2, 0) + second_got
+        q_parts = send_parts(q_send[: 2 * LANES], swap_x, 128, 128)
+        d_normed_q, (q_parts[0], o_parts[2]) = beside(d_normed_q, (q_parts[0], o_parts[2]))
+        tied = after(d_units, d_normed_q)
+        second_half = weight_grad(feed_all, tied, second_cut, 2, 2, 0)
+        second_half, q_parts[1] = beside(second_half, q_parts[1])
+        second_half = second_half + jnp.concatenate(second_parts, axis=0)
         second_last = send_parts(second_half[2 * BLOCK :], swap_y, 320, 192)
-        tied = after(acts, second_half, q_parts[1], o_parts[2])
-        down_got = jnp.concatenate(down_parts, axis=0)
-        half = weight_grad(cot_all, tied, slice(0, act_width), 2, 2, 0) + down_got
-        o_send, o_keep = fold(o_parts, o_keep, half)
-        o_parts = send_parts(o_send, swap_x, 128, 128)
-        before_input = (half, q_parts[2], second_last[0])
+        d_lined[1] = after(d_lined[1], second_half)
+        pairs_got.append(swap_x(d_lined[1][rows:]))
+        q_parts += send_parts(after(q_send[2 * LANES :], pairs_got[1]), swap_x, 128, 128)
     else:
         every_unit = slice(0, units_width)
         g_gate_up = scatter_yx(
@@ -1236,10 +1253,12 @@
         g_down = scatter_yx(
             unit_order(weight_grad(cot_all, acts, slice(0, act_width), count, 1, 0)), False
         )
-        before_input = ()
-    d_pair_all = after(jnp.concatenate(d_pairs, axis=0), before_input)
-
-    d_kv_raw, key_grad, tokens_grad, attention_grad = input_back(
+        pairs_got.append(swap_x(d_lined[1][rows:]))
+    d_pair_all = jnp.concatenate(
+        [pair[:rows] + got for pair, got in zip(d_lined, pairs_got)], axis=0
+    )
+
+    back = input_back(
         table,
         d_pair_all,
         kv_raw,
@@ -1253,7 +1272,8 @@
         *kvg,
     )
     if paired:
-        d_kv_raw = after(d_kv_raw, o_parts[0], second_last[1])
+        back, (q_parts[2], second_last[0]) = beside(back, (q_parts[2], second_last[0]))
+    d_kv_raw, key_grad, tokens_grad, attention_grad = back
     query_grad = query_gain_grads[0][0] + query_gain_grads[1][0]
     head_grads = jnp.concatenate(
         [query_grad[:HEAD_SIZE] + query_grad[HEAD_SIZE:], key_grad[0, :HEAD_SIZE]]
@@ -1270,32 +1290,41 @@
         ],
         axis=0,
     )
-    kv_mine, kv_other = key_value_grad(normed, d_kv_raw, gain_grads)
-    kv_send, kv_keep = split_rows(kv_mine, swap_core(kv_other))
+    kv_grads = key_value_grad(normed, d_kv_raw, gain_grads)
     if paired:
-        kv_got = swap_y(kv_send)
-        tied = after(d_units, kv_send)
-        first_got = jnp.concatenate(first_parts, axis=0)
-        first_half = weight_grad(feed_all, tied, first_cut, 2, 1, 0) + first_got
-        first_last = swap_x(first_half[2 * BLOCK :])
-        q_send, q_keep = fold(q_parts, q_keep, first_half)
+        kv_grads, second_last[1] = beside(kv_grads, second_last[1])
+        o_send, o_keep = fold(o_parts, o_keep, d_kv_raw)
+        kv_got = swap_core(kv_grads[1])
+        kv_sums = [kv_grads[0][span(b)] + kv_got[span(b)] for b in range(4)]
+        kv_parts = [swap_x(kv_sums[1]), swap_y(kv_sums[2]), swap_xy(kv_sums[3])]
+        o_got = swap_x(after(o_send, kv_sums))
+        tied = after(acts, kv_sums)
+        half = weight_grad(cot_all, tied, slice(0, act_width), 2, 2, 0)
+        half, q_parts[3] = beside(half, q_parts[3])
+        q_send, q_keep = fold(q_parts, q_keep)
         q_got = swap_y(q_send)
-        kv_send, kv_keep = fold([kv_got], kv_keep, first_half)
-        g_kv = kv_keep + swap_x(kv_send)
-        g_q = q_keep + after(q_got, g_kv)
-        g_o = o_keep + after(jnp.concatenate(o_parts, axis=0), first_half)
-        down_last = swap_y(half[2 * BLOCK :])
-        first_last, second_last, down_last = after((first_last, second_last, down_last), g_q)
+        half = half + jnp.concatenate(down_parts, axis=0)
+        tied = after(d_units, half, q_send)
+        first_half = weight_grad(feed_all, tied, first_cut, 2, 1, 0)
+        first_half, kv_parts = beside(first_half, kv_parts)
+        g_kv = kv_sums[0] + kv_parts[0] + kv_parts[1] + kv_parts[2]
+        first_half = first_half + jnp.concatenate(first_parts, axis=0)
+        first_last = swap_x(after(first_half[2 * BLOCK :], g_kv))
+        down_last = swap_y(after(half[2 * BLOCK :], q_send))
+        g_o = o_keep + after(o_got, first_half)
+        g_q = q_keep + after(q_got, first_half)
+        first_last, down_last = after((first_last, down_last), g_o, g_q)
         second_got = jnp.concatenate(second_last, axis=0)
         g_gate_up = jnp.concatenate(
             [first_half[: 2 * BLOCK] + first_last, second_half[: 2 * BLOCK] + second_got], axis=1
         )
         g_down = half[: 2 * BLOCK] + down_last
     else:
+        kv_send = kv_grads[0] + swap_core(kv_grads[1])
         g_o, g_q, g_kv = (fold_whole(v) for v in (o_send, q_send, kv_send))
-    g_kv = pair_scatter(g_kv, 0).astype(F32)
-    grad_output = pair_scatter(g_o, 0).astype(F32).T
-    grad_query = pair_scatter(g_q, 1).astype(F32)
+    g_kv = line_scatter(g_kv, 0).astype(F32)
+    grad_output = line_scatter(g_o, 0).astype(F32).T
+    grad_query = line_scatter(g_q, 1).astype(F32)
     part_rows = g_down.shape[0] // 2
     g_ffn = jnp.concatenate([g_gate_up, g_down], axis=1)
     g_keep = g_ffn[:part_rows]
@@ -1320,10 +1349,10 @@
         .reshape(small, KV_WIDTH)
     )
 
-    added = []
-    for out_mine, out_other in outs:
-        out = after(out_mine, before_input) + after(swap_core(out_other), before_input)
-        added.append(lax.psum_scatter(out, "heads", scatter_dimension=0, tiled=True))
+    added = [
+        lax.psum_scatter(after(v, last_kv), "heads", scatter_dimension=0, tiled=True) for v in added
+    ]
+    added = after(added, (g_kv, grad_output))
     layer_out = finish_layer(table, *hiddens, *added)
 
     return (

time: 867 us -> 805 us (0.928)
  waiting for transfers between devices: 332 us -> 243 us
  local copies, waits for them, and re-layouts: 73.5 us -> 89.3 us
  starting transfers between devices: 68.3 us -> 78.1 us
    all_gather x3, waiting for transfers between devices: 90.5 us -> 9.2 us  [the longest x2 9.18 us: on_device(): feeds.append(lax.all_gather(feed_rows, 'heads', axis=0, tiled=True))]
    ppermute x6 -> x10, waiting for transfers between devices: 60.7 us -> 22.7 us  [the longest x9 22.7 us: line_scatter(): total = total + lax.ppermute(block, 'heads', [(i, i ^ k) for i in range(4)])]
    ppermute x22, waiting for transfers between devices: 75.9 us -> 105 us  [swap_x(): return lax.ppermute(v, 'seq', [(i, i ^ 2) for i in range(4)])]
    unnamed x140 -> x174, local copies, waits for them, and re-layouts: 20.2 us -> 31.6 us
    ppermute x18, waiting for transfers between devices: 66.1 us -> 54.9 us  [swap_y(): return lax.ppermute(v, 'dp', [(0, 1), (1, 0)])]
    ppermute x6 -> x10, starting transfers between devices: 4.14 us -> 14.4 us  [the longest x9 13.7 us: line_scatter(): total = total + lax.ppermute(block, 'heads', [(i, i ^ k) for i in range(4)])]
    add x13 -> x11, other arithmetic: 20.2 us -> 20.3 us  [the longest x2 7.65 us: on_device(): added = [out_mine + swap_core(out_other) for out_mine, out_other in outs]]
  transfers between devices with their start and end apart: 86 -> 90, of which waited for: 28 -> 34; matrix products, arithmetic and copies ran while one was open for 15% -> 17% of each run, Pallas kernels for 31% -> 34%
where the time goes in v3:
time: 805 us; the launch traced here: 792 us
  Pallas kernels  280 us (35%)
  waiting for transfers between devices  243 us (30%)
  local copies, waits for them, and re-layouts  89.3 us (11%)
  starting transfers between devices  78.1 us (10%)
  other arithmetic  74 us (9%)
  between operations  16.2 us (2%)
  matrix products  10.2 us (1%)
    pallas_call x15, Pallas kernels, call(): pl.pallas_call(body, grid=grid, in_specs=in_specs, out_specs=out_specs, s...  217 us
    ppermute x22, waiting for transfers between devices, swap_x(): return lax.ppermute(v, 'seq', [(i, i ^ 2) for i in range(4)])  105 us
    pallas_call x8, Pallas kernels, call(): pl.pallas_call(body, grid_spec=pltpu.PrefetchScalarGridSpec(num_scalar_pr...  63.6 us
    ppermute x18, waiting for transfers between devices, swap_y(): return lax.ppermute(v, 'dp', [(0, 1), (1, 0)])  54.9 us
    unnamed x174, local copies, waits for them, and re-layouts  31.6 us
    ppermute x22, starting transfers between devices, swap_x(): return lax.ppermute(v, 'seq', [(i, i ^ 2) for i in range(4)])  29.1 us
    ppermute x2, waiting for transfers between devices, step(): got = lax.ppermute(u, 'heads', [(i, i ^ distance) for i in range(4)])  25.5 us
    ppermute x9, waiting for transfers between devices, line_scatter(): total = total + lax.ppermute(block, 'heads', [(i, i ^ k) for i in range(4)])  22.7 us
  transfers between devices with their start and end apart: 90, of which 34 were waited for; matrix products, arithmetic and copies ran while one was open for 17% of the time, Pallas kernels for 34%

profile of v3, /device:TPU:0, one launch (start us, length us, event | category | flops | bytes accessed | tf_op | source)
XLA Modules:
  0.0 791.6 jit_solution(6906999159394274153)
XLA Ops:
  27.0 6.0 collective-permute-done.3
  33.1 6.0 collective-permute-start.4
  39.1 5.5 fusion.7
  49.5 19.5 %collective-permute-done.4 = bf16[128,1024]{1,0:T(8,128)(2,1)} collective-permute-done((bf16[128,1024]{1,0:T(8,128)(2,1)S(1)}, bf16[128,1024]{1,0:T(8,128)(2,1)}, u32[]{:S(2)}, u32[]{:S(2)}) %collective-permute-start.4) | collective-permute-done | bytes 262176 | tf_op jit(solution)/shard_map/ppermute | solution.py:904
  73.8 8.8 %collective-permute-done.6.refs_2_ = bf16[256,1024]{1,0:T(8,128)(2,1)S(1)} collective-permute-done((bf16[256,1024]{1,0:T(8,128)(2,1)S(1)}, bf16[256,1024]{1,0:T(8,128)(2,1)S(1)}, u32[]{:S(2)}, u32[]{:S(2)}) %collective-permute-start.6) | collective-permute-done | bytes 524320 | tf_op jit(solution)/shard_map/ppermute | solution.py:881
  90.9 4.1 collective-permute-done.7.refs_3_
  103.1 7.3 project_key_value.1
  110.5 35.6 %collective-permute-done.12 = bf16[256,896]{1,0:T(8,128)(2,1)S(1)} collective-permute-done((bf16[256,896]{1,0:T(8,128)(2,1)}, bf16[256,896]{1,0:T(8,128)(2,1)S(1)}, u32[]{:S(2)}, u32[]{:S(2)}) %collective-permute-start.12) | collective-permute-done | bytes 458784 | tf_op jit(solution)/shard_map/ppermute | solution.py:872
  157.3 18.7 %collective-permute-done.16.refs_2_ = bf16[256,1792]{1,0:T(8,128)(2,1)S(1)} collective-permute-done((bf16[256,1792]{1,0:T(8,128)(2,1)S(1)}, bf16[256,1792]{1,0:T(8,128)(2,1)S(1)}, u32[]{:S(2)}, u32[]{:S(2)}) %collective-permute-start.16) | collective-permute-done | bytes 917536 | tf_op jit(solution)/shard_map/ppermute | solution.py:881
  180.4 20.4 %collective-permute-done.19.refs_3_ = bf16[256,1792]{1,0:T(8,128)(2,1)S(1)} collective-permute-done((bf16[256,1792]{1,0:T(8,128)(2,1)S(1)}, bf16[256,1792]{1,0:T(8,128)(2,1)S(1)}, u32[]{:S(2)}, u32[]{:S(2)}) %collective-permute-start.19) | collective-permute-done | bytes 917536 | tf_op jit(solution)/shard_map/ppermute | solution.py:872
  201.9 16.4 %collective-permute-done.17.refs_1_ = bf16[256,1792]{1,0:T(8,128)(2,1)S(1)} collective-permute-done((bf16[256,1792]{1,0:T(8,128)(2,1)S(1)}, bf16[256,1792]{1,0:T(8,128)(2,1)S(1)}, u32[]{:S(2)}, u32[]{:S(2)}) %collective-permute-start.17) | collective-permute-done | bytes 917536 | tf_op jit(solution)/shard_map/ppermute | solution.py:872
  219.9 9.5 %project_query.1 = (f32[256,1792]{1,0:T(8,128)}, bf16[256,1792]{1,0:T(8,128)(2,1)}) custom-call(bf16[256,2048]{1,0:T(8,128)(2,1)} %get-tuple-element.255.normed, f32[256,128]{1,0:T(8,128)} %pad_maximum_fusion.7.cosine, f32[256,128]{1,0:T(8,128)} %pad_maximum_fusion.8.sine, f32[1,128]{1,0:T(1,128)} %pad_maximum_fusion.12.gain, bf16[256,1792]{1,0:T(8,128)(2,1)} %copy-done.13, ...), custom_call_target="tpu_custom_call" | custom-call | flops 1879048192 | bytes 11403776 | tf_op jit(solution)/shard_map/project_query/pallas_call | solution.py:78
  232.2 4.0 collective-permute-done.24
  236.2 10.9 %attention_forward.2 = (bf16[128,1792]{1,0:T(8,128)(2,1)}, f32[7,1,512]{2,1,0:T(1,128)}) custom-call(bf16[8,2,128,896]{3,2,1,0:T(8,128)(2,1)} %bitcast.89, bf16[8,2,128,896]{3,2,1,0:T(8,128)(2,1)} %bitcast.19.kv1, bf16[256,1792]{1,0:T(8,128)(2,1)} %get-tuple-element.188.query, f32[1024,128]{1,0:T(8,128)} %get-tuple-element.429.bias0, ...), custom_call_target="tpu_custom_call" | custom-call | flops 11274289152 | bytes 9779200 | tf_op jit(solution)/shard_map/attention_forward/pallas_call | solution.py:78
  247.2 7.1 collective-permute-done.25.refs_3_
  261.7 9.8 %project_output.2 = (f32[128,2048]{1,0:T(8,128)}, bf16[128,2048]{1,0:T(8,128)(2,1)}) custom-call(s32[8]{0:T(128)} %broadcast_xor_fusion.table, bf16[128,1792]{1,0:T(8,128)(2,1)} %get-tuple-element.178.mixed, bf16[256,2048]{1,0:T(8,128)(2,1)} %bitcast.66, f32[8,2048]{1,0:T(8,128)} %get-tuple-element.179.gains, bf16[256,1792]{1,0:T(8,128)(2,1)} %bitcast.61, ...), custom_call_target="tpu_custom_call" | custom-call | flops 939524096 | bytes 10485760 | tf_op jit(solution)/shard_map/project_output/pallas_call | solution.py:87
  273.6 4.8 fusion.33
  278.4 11.0 %attention_forward.3 = (bf16[128,1792]{1,0:T(8,128)(2,1)}, f32[7,1,512]{2,1,0:T(1,128)}) custom-call(bf16[8,2,128,896]{3,2,1,0:T(8,128)(2,1)} %bitcast.90, bf16[8,2,128,896]{3,2,1,0:T(8,128)(2,1)} %bitcast.19.kv1, bf16[256,1792]{1,0:T(8,128)(2,1)} %get-tuple-element.188.query, f32[1024,128]{1,0:T(8,128)} %get-tuple-element.428.bias0, ...), custom_call_target="tpu_custom_call" | custom-call | flops 11274289152 | bytes 9779200 | tf_op jit(solution)/shard_map/attention_forward/pallas_call | solution.py:78
  289.4 5.2 collective-permute-done.31.refs_11_
  294.6 16.3 %collective-permute-done.30.refs_7_ = bf16[512,1664]{1,0:T(8,128)(2,1)S(1)} collective-permute-done((bf16[512,1664]{1,0:T(8,128)(2,1)S(1)}, bf16[512,1664]{1,0:T(8,128)(2,1)S(1)}, u32[]{:S(2)}, u32[]{:S(2)}) %collective-permute-start.30) | collective-permute-done | bytes 1703968 | tf_op jit(solution)/shard_map/ppermute | solution.py:881
  312.0 9.7 %project_output.3 = (f32[128,2048]{1,0:T(8,128)}, bf16[128,2048]{1,0:T(8,128)(2,1)}) custom-call(s32[8]{0:T(128)} %broadcast_xor_fusion.table, bf16[128,1792]{1,0:T(8,128)(2,1)} %get-tuple-element.191.mixed, bf16[256,2048]{1,0:T(8,128)(2,1)} %bitcast.67, f32[8,2048]{1,0:T(8,128)} %get-tuple-element.179.gains, bf16[256,1792]{1,0:T(8,128)(2,1)} %bitcast.62, ...), custom_call_target="tpu_custom_call" | custom-call | flops 939524096 | bytes 10485760 | tf_op jit(solution)/shard_map/project_output/pallas_call | solution.py:87
  322.1 4.1 collective-permute-done.32.refs_0_.refs_1_
  327.5 34.2 %feed_forward.2 = (bf16[1024,896]{1,0:T(8,128)(2,1)}, bf16[1024,1664]{1,0:T(8,128)(2,1)}, bf16[512,2048]{1,0:T(8,128)(2,1)}, bf16[512,2048]{1,0:T(8,128)(2,1)}, ...) custom-call(bf16[512,2048]{1,0:T(8,128)(2,1)} %copy-done, ...), custom_call_target="tpu_custom_call" | custom-call | flops 20132659200 | bytes 32505856 | tf_op jit(solution)/shard_map/feed_forward/pallas_call | solution.py:78
  361.9 9.2 %all-gather.10.cloned.1.call-done.refs_1_.refs_6_.refs_7_ = bf16[512,2048]{1,0:T(8,128)(2,1)} async-done(((bf16[128,2048]{1,0:T(8,128)(2,1)}), bf16[512,2048]{1,0:T(8,128)(2,1)}) %all-gather.10.cloned.1.call-update) | async-done | bytes 2097168 | tf_op jit(solution)/shard_map/all_gather | solution.py:1096
  371.6 4.4 add.321
  379.8 34.4 %feed_forward.3 = (bf16[1024,896]{1,0:T(8,128)(2,1)}, bf16[1024,1664]{1,0:T(8,128)(2,1)}, bf16[512,2048]{1,0:T(8,128)(2,1)}, bf16[512,2048]{1,0:T(8,128)(2,1)}, ...) custom-call(bf16[512,2048]{1,0:T(8,128)(2,1)} %copy-done.1, ...), custom_call_target="tpu_custom_call" | custom-call | flops 20132659200 | bytes 32505856 | tf_op jit(solution)/shard_map/feed_forward/pallas_call | solution.py:78
  414.4 9.7 %weight_grad.6 = bf16[1024,896]{1,0:T(8,128)(2,1)} custom-call(bf16[512,2048]{1,0:T(8,128)(2,1)} %copy-done, bf16[512,2048]{1,0:T(8,128)(2,1)} %copy-done, bf16[512,2048]{1,0:T(8,128)(2,1)} %all-gather.8.cloned.1.call-done.refs_1_.refs_2_.refs_3_, bf16[512,2048]{1,0:T(8,128)(2,1)} %all-gather.8.cloned.1.call-done.refs_1_.refs_2_.refs_3_, ...), custom_call_target="tpu_custom_call" | custom-call | flops 3758096384 | bytes 25427968 | tf_op jit(solution)/shard_map/weight_grad/pallas_call | solution.py:78
  427.5 8.7 %weight_grad.7 = bf16[1024,768]{1,0:T(8,128)(2,1)} custom-call(bf16[512,2048]{1,0:T(8,128)(2,1)} %copy-done, bf16[512,2048]{1,0:T(8,128)(2,1)} %copy-done, bf16[512,2048]{1,0:T(8,128)(2,1)} %all-gather.8.cloned.1.call-done.refs_1_.refs_2_.refs_3_, bf16[512,2048]{1,0:T(8,128)(2,1)} %all-gather.8.cloned.1.call-done.refs_1_.refs_2_.refs_3_, ...), custom_call_target="tpu_custom_call" | custom-call | flops 3221225472 | bytes 25165824 | tf_op jit(solution)/shard_map/weight_grad/pallas_call | solution.py:78
  446.6 9.8 %hidden_back.2 = (f32[128,2048]{1,0:T(8,128)}, bf16[128,2048]{1,0:T(8,128)(2,1)}, f32[8,2048]{1,0:T(8,128)}, bf16[128,1792]{1,0:T(8,128)(2,1)}) custom-call(s32[8]{0:T(128)} %broadcast_xor_fusion.table, bf16[128,2048]{1,0:T(8,128)(2,1)} %reduce-scatter.9.cloned.1.call-done.d_feed, f32[128,2048]{1,0:T(8,128)} %get-tuple-element.187.hidden.hidden0, ...), custom_call_target="tpu_custom_call" | custom-call | flops 939524096 | bytes 12124160 | tf_op jit(solution)/shard_map/hidden_back/pallas_call | solution.py:87
  456.6 24.5 %attention_backward.2 = (bf16[128,1792]{1,0:T(8,128)(2,1)}, bf16[1024,896]{1,0:T(8,128)(2,1)}, bf16[1024,896]{1,0:T(8,128)(2,1)}, f32[8,128]{1,0:T(8,128)}) custom-call(bf16[8,2,128,896]{3,2,1,0:T(8,128)(2,1)} %bitcast.91, bf16[8,2,128,896]{3,2,1,0:T(8,128)(2,1)} %bitcast.19.kv1, bf16[256,1792]{1,0:T(8,128)(2,1)} %get-tuple-element.188.query, ...), custom_call_target="tpu_custom_call" | custom-call | flops 26306674688 | bytes 16468480 | tf_op jit(solution)/shard_map/attention_backward/pallas_call | solution.py:78
  483.0 4.0 add.319
  487.0 3.7 add.322
  490.7 8.8 %weight_grad.8 = bf16[1024,896]{1,0:T(8,128)(2,1)} custom-call(bf16[512,2048]{1,0:T(8,128)(2,1)} %collective-permute-done.33.refs_2_.refs_0_.refs_1_, bf16[512,2048]{1,0:T(8,128)(2,1)} %collective-permute-done.33.refs_2_.refs_0_.refs_1_, bf16[512,2048]{1,0:T(8,128)(2,1)} %bitcast.26.refs_3_.refs_2_, bf16[512,2048]{1,0:T(8,128)(2,1)} %bitcast.26.refs_3_.refs_2_, ...), custom_call_target="tpu_custom_call" | custom-call | flops 3758096384 | bytes 22282240 | tf_op jit(solution)/shard_map/weight_grad/pallas_call | solution.py:78
  502.9 3.7 add.323
  506.7 9.8 %hidden_back.3 = (f32[128,2048]{1,0:T(8,128)}, bf16[128,2048]{1,0:T(8,128)(2,1)}, f32[8,2048]{1,0:T(8,128)}, bf16[128,1792]{1,0:T(8,128)(2,1)}) custom-call(s32[8]{0:T(128)} %broadcast_xor_fusion.table, bf16[128,2048]{1,0:T(8,128)(2,1)} %reduce-scatter.7.cloned.1.call-done.d_feed, f32[128,2048]{1,0:T(8,128)} %get-tuple-element.192.hidden.hidden1, ...), custom_call_target="tpu_custom_call" | custom-call | flops 939524096 | bytes 12124160 | tf_op jit(solution)/shard_map/hidden_back/pallas_call | solution.py:87
  523.6 3.7 collective-permute-done.46
  530.6 24.4 %attention_backward.3 = (bf16[128,1792]{1,0:T(8,128)(2,1)}, bf16[1024,896]{1,0:T(8,128)(2,1)}, bf16[1024,896]{1,0:T(8,128)(2,1)}, f32[8,128]{1,0:T(8,128)}) custom-call(bf16[8,2,128,896]{3,2,1,0:T(8,128)(2,1)} %bitcast.92, bf16[8,2,128,896]{3,2,1,0:T(8,128)(2,1)} %bitcast.19.kv1, bf16[256,1792]{1,0:T(8,128)(2,1)} %get-tuple-element.188.query, ...), custom_call_target="tpu_custom_call" | custom-call | flops 26306674688 | bytes 16468480 | tf_op jit(solution)/shard_map/attention_backward/pallas_call | solution.py:78
  590.3 8.7 %query_back.1.d_normed_q = f32[256,2048]{1,0:T(8,128)} custom-call(bf16[256,1792]{1,0:T(8,128)(2,1)} %copy-done.12, bf16[256,1792]{1,0:T(8,128)(2,1)} %copy-done.13, bf16[256,1792]{1,0:T(8,128)(2,1)} %copy-done.30, bf16[256,1792]{1,0:T(8,128)(2,1)} %copy-done.29, bf16[256,1792]{1,0:T(8,128)(2,1)} %copy-done.31, bf16[256,1792]{1,0:T(8,128)(2,1)} %copy-done.32, ...), custom_call_target="tpu_custom_call" | custom-call | flops 1879048192 | bytes 10354688 | tf_op jit(solution)/shard_map/query_back/pallas_call | solution.py:78
  600.7 8.7 %weight_grad.9 = bf16[1024,768]{1,0:T(8,128)(2,1)} custom-call(bf16[512,2048]{1,0:T(8,128)(2,1)} %copy-done, bf16[512,2048]{1,0:T(8,128)(2,1)} %copy-done, bf16[512,2048]{1,0:T(8,128)(2,1)} %all-gather.8.cloned.1.call-done.refs_1_.refs_2_.refs_3_, bf16[512,2048]{1,0:T(8,128)(2,1)} %all-gather.8.cloned.1.call-done.refs_1_.refs_2_.refs_3_, ...), custom_call_target="tpu_custom_call" | custom-call | flops 3221225472 | bytes 25165824 | tf_op jit(solution)/shard_map/weight_grad/pallas_call | solution.py:78
  630.8 10.5 %input_back.1 = (bf16[256,896]{1,0:T(8,128)(2,1)}, f32[8,128]{1,0:T(8,128)}, f32[256,2048]{1,0:T(8,128)}, f32[8,2048]{1,0:T(8,128)}) custom-call(s32[8]{0:T(128)} %broadcast_xor_fusion.table, bf16[256,896]{1,0:T(8,128)(2,1)} %pad_maximum_fusion.6.d_pair, f32[256,896]{1,0:T(8,128)} %get-tuple-element.268.kv_raw, f32[256,128]{1,0:T(8,128)} %pad_maximum_fusion.7.cosine, ...), custom_call_target="tpu_custom_call" | custom-call | flops 939524096 | bytes 13767168 | tf_op jit(solution)/shard_map/input_back/pallas_call | solution.py:87
  644.6 4.6 key_value_grad.1
  662.9 9.0 %weight_grad.10 = bf16[1024,896]{1,0:T(8,128)(2,1)} custom-call(bf16[512,2048]{1,0:T(8,128)(2,1)} %collective-permute-done.33.refs_2_.refs_0_.refs_1_, bf16[512,2048]{1,0:T(8,128)(2,1)} %collective-permute-done.33.refs_2_.refs_0_.refs_1_, bf16[512,2048]{1,0:T(8,128)(2,1)} %bitcast.26.refs_3_.refs_2_, bf16[512,2048]{1,0:T(8,128)(2,1)} %bitcast.26.refs_3_.refs_2_, ...), custom_call_target="tpu_custom_call" | custom-call | flops 3758096384 | bytes 22282240 | tf_op jit(solution)/shard_map/weight_grad/pallas_call | solution.py:78
  682.8 9.7 %weight_grad.11 = bf16[1024,896]{1,0:T(8,128)(2,1)} custom-call(bf16[512,2048]{1,0:T(8,128)(2,1)} %copy-done, bf16[512,2048]{1,0:T(8,128)(2,1)} %copy-done, bf16[512,2048]{1,0:T(8,128)(2,1)} %all-gather.8.cloned.1.call-done.refs_1_.refs_2_.refs_3_, bf16[512,2048]{1,0:T(8,128)(2,1)} %all-gather.8.cloned.1.call-done.refs_1_.refs_2_.refs_3_, ...), custom_call_target="tpu_custom_call" | custom-call | flops 3758096384 | bytes 25427968 | tf_op jit(solution)/shard_map/weight_grad/pallas_call | solution.py:78
  701.4 5.9 collective-permute-done.66
  723.8 7.1 collective-permute-done.69
  733.0 13.4 %collective-permute-done.77 = bf16[512,896]{1,0:T(8,128)(2,1)} collective-permute-done((bf16[512,896]{1,0:T(8,128)(2,1)}, bf16[512,896]{1,0:T(8,128)(2,1)}, u32[]{:S(2)}, u32[]{:S(2)}) %collective-permute-start.77) | collective-permute-done | bytes 917536 | tf_op jit(solution)/shard_map/ppermute | solution.py:872
  762.0 8.7 %collective-permute-done.71 = bf16[64,1792]{1,0:T(8,128)(2,1)} collective-permute-done((bf16[64,1792]{1,0:T(8,128)(2,1)}, bf16[64,1792]{1,0:T(8,128)(2,1)}, u32[]{:S(2)}, u32[]{:S(2)}) %collective-permute-start.71) | collective-permute-done | bytes 229408 | tf_op jit(solution)/shard_map/ppermute | solution.py:888
  772.7 3.7 finish_layer.1
  (518 shorter events, 251.9 us)
Async XLA Ops:
  7.2 141.4 %all-gather.12.cloned.1.call-start = ((), (), s32[]{:S(2)}) async-start(), calls=%async_computation.15 | async-start | bytes 7864320 | tf_op jit(solution)/shard_map/all_gather | solution.py:996
  15.6 213.8 %all-gather.6.cloned.1.call-start = ((), (), s32[]{:S(2)}) async-start(), calls=%async_computation.6 | async-start | bytes 4587520 | tf_op jit(solution)/shard_map/all_gather | solution.py:1075
  33.1 35.9 %collective-permute-start.4 = (bf16[128,1024]{1,0:T(8,128)(2,1)S(1)}, bf16[128,1024]{1,0:T(8,128)(2,1)}, u32[]{:S(2)}, u32[]{:S(2)}) collective-permute-start(bf16[128,1024]{1,0:T(8,128)(2,1)S(1)} %maximum_select_fusion.4), channel_id=1, source_target_pairs={{0,2},{1,3},{2,0},{3,1},{4,6},{5,7},{6,4},{7,5},{8,10},{9,11},{10,... | collective-permute-start | bytes 786440 | tf_op jit(solution)/shard_map/ppermute | solution.py:904
  45.6 37.7 %collective-permute-start.2 = (bf16[512,896]{1,0:T(8,128)(2,1)}, bf16[512,896]{1,0:T(8,128)(2,1)}, u32[]{:S(2)}, u32[]{:S(2)}) collective-permute-start(bf16[512,896]{1,0:T(8,128)(2,1)} %slice.745.refs_8_), channel_id=1, source_target_pairs={{0,16},{16,0},{1,17},{17,1},{2,18},{18,2},{3,19},{19,3},{4,20},{20... | collective-permute-start | bytes 2752520 | tf_op jit(solution)/shard_map/ppermute | solution.py:881
  45.6 37.7 %collective-permute-start.1 = (bf16[512,896]{1,0:T(8,128)(2,1)}, bf16[512,896]{1,0:T(8,128)(2,1)}, u32[]{:S(2)}, u32[]{:S(2)}) collective-permute-start(bf16[512,896]{1,0:T(8,128)(2,1)} %slice.745.refs_8_), channel_id=1, source_target_pairs={{0,8},{4,12},{8,0},{12,4},{1,9},{5,13},{9,1},{13,5},{2,10},{6,14},... | collective-permute-start | bytes 2752520 | tf_op jit(solution)/shard_map/ppermute | solution.py:872
  87.5 60.6 %collective-permute-start.14 = (bf16[512,1664]{1,0:T(8,128)(2,1)}, bf16[512,1664]{1,0:T(8,128)(2,1)}, u32[]{:S(2)}, u32[]{:S(2)}) collective-permute-start(bf16[512,1664]{1,0:T(8,128)(2,1)} %slice.760.refs_4_), channel_id=1, source_target_pairs={{0,16},{16,0},{1,17},{17,1},{2,18},{18,2},{3,19},{19,3},{4,20},{20... | collective-permute-start | bytes 5111816 | tf_op jit(solution)/shard_map/ppermute | solution.py:881
  96.1 52.0 %collective-permute-start.13 = (bf16[512,1664]{1,0:T(8,128)(2,1)}, bf16[512,1664]{1,0:T(8,128)(2,1)S(1)}, u32[]{:S(2)}, u32[]{:S(2)}) collective-permute-start(bf16[512,1664]{1,0:T(8,128)(2,1)} %slice.760.refs_4_), channel_id=1, source_target_pairs={{0,8},{4,12},{8,0},{12,4},{1,9},{5,13},{9,1},{13,5},{2,10},{6,14},... | collective-permute-start | bytes 5111816 | tf_op jit(solution)/shard_map/ppermute | solution.py:872
  110.5 35.6 %collective-permute-start.12 = (bf16[256,896]{1,0:T(8,128)(2,1)}, bf16[256,896]{1,0:T(8,128)(2,1)S(1)}, u32[]{:S(2)}, u32[]{:S(2)}) collective-permute-start(bf16[256,896]{1,0:T(8,128)(2,1)} %get-tuple-element.170), channel_id=1, source_target_pairs={{0,8},{4,12},{8,0},{12,4},{1,9},{5,13},{9,1},{13,5},{2,10},{6,14},... | collective-permute-start | bytes 1376264 | tf_op jit(solution)/shard_map/ppermute | solution.py:872
  148.1 173.7 %all-gather.8.cloned.1.call-start = ((), (), s32[]{:S(2)}) async-start(), calls=%async_computation.7 | async-start | bytes 2621440 | tf_op jit(solution)/shard_map/all_gather | solution.py:1096
  153.1 23.0 %collective-permute-start.16 = (bf16[256,1792]{1,0:T(8,128)(2,1)S(1)}, bf16[256,1792]{1,0:T(8,128)(2,1)S(1)}, u32[]{:S(2)}, u32[]{:S(2)}) collective-permute-start(bf16[256,1792]{1,0:T(8,128)(2,1)S(1)} %copy.120.refs_0_), channel_id=1, source_target_pairs={{0,16},{16,0},{1,17},{17,1},{2,18},{18,2},{3,19},{19,3},{4,20},{20... | collective-permute-start | bytes 2752520 | tf_op jit(solution)/shard_map/ppermute | solution.py:881
  155.6 21.9 %collective-permute-start.15 = (bf16[256,1792]{1,0:T(8,128)(2,1)S(1)}, bf16[256,1792]{1,0:T(8,128)(2,1)S(1)}, u32[]{:S(2)}, u32[]{:S(2)}) collective-permute-start(bf16[256,1792]{1,0:T(8,128)(2,1)S(1)} %copy.120.refs_0_), channel_id=1, source_target_pairs={{0,8},{4,12},{8,0},{12,4},{1,9},{5,13},{9,1},{13,5},{2,10},{6,14},... | collective-permute-start | bytes 2752520 | tf_op jit(solution)/shard_map/ppermute | solution.py:872
  177.5 23.3 %collective-permute-start.19 = (bf16[256,1792]{1,0:T(8,128)(2,1)S(1)}, bf16[256,1792]{1,0:T(8,128)(2,1)S(1)}, u32[]{:S(2)}, u32[]{:S(2)}) collective-permute-start(bf16[256,1792]{1,0:T(8,128)(2,1)S(1)} %collective-permute-done.16.refs_2_), channel_id=1, source_target_pairs={{0,8},{4,12},{8,0},{12,4},{1,9},{5,13},{9,1},{13,5},{2,10},{6,14},... | collective-permute-start | bytes 2752520 | tf_op jit(solution)/shard_map/ppermute | solution.py:872
  179.4 38.9 %collective-permute-start.17 = (bf16[256,1792]{1,0:T(8,128)(2,1)S(1)}, bf16[256,1792]{1,0:T(8,128)(2,1)S(1)}, u32[]{:S(2)}, u32[]{:S(2)}) collective-permute-start(bf16[256,1792]{1,0:T(8,128)(2,1)S(1)} %bitcast.59), channel_id=1, source_target_pairs={{0,8},{4,12},{8,0},{12,4},{1,9},{5,13},{9,1},{13,5},{2,10},{6,14},... | collective-permute-start | bytes 2752520 | tf_op jit(solution)/shard_map/ppermute | solution.py:872
  179.9 38.4 %collective-permute-start.20 = (bf16[256,1792]{1,0:T(8,128)(2,1)}, bf16[256,1792]{1,0:T(8,128)(2,1)S(1)}, u32[]{:S(2)}, u32[]{:S(2)}) collective-permute-start(bf16[256,1792]{1,0:T(8,128)(2,1)} %copy-done.13), channel_id=1, source_target_pairs={{0,4},{4,0},{8,12},{12,8},{1,5},{5,1},{9,13},{13,9},{2,6},{6,2},{1... | collective-permute-start | bytes 2752520 | tf_op jit(solution)/shard_map/ppermute | solution.py:878
  179.9 38.4 %collective-permute-start.22 = (bf16[256,1792]{1,0:T(8,128)(2,1)S(1)}, bf16[256,1792]{1,0:T(8,128)(2,1)S(1)}, u32[]{:S(2)}, u32[]{:S(2)}) collective-permute-start(bf16[256,1792]{1,0:T(8,128)(2,1)S(1)} %collective-permute-done.16.refs_2_), channel_id=1, source_target_pairs={{0,4},{4,0},{8,12},{12,8},{1,5},{5,1},{9,13},{13,9},{2,6},{6,2},{1... | collective-permute-start | bytes 2752520 | tf_op jit(solution)/shard_map/ppermute | solution.py:878
  231.5 22.7 %collective-permute-start.25 = (bf16[256,1792]{1,0:T(8,128)(2,1)S(1)}, bf16[256,1792]{1,0:T(8,128)(2,1)S(1)}, u32[]{:S(2)}, u32[]{:S(2)}) collective-permute-start(bf16[256,1792]{1,0:T(8,128)(2,1)S(1)} %collective-permute-done.17.refs_1_), channel_id=1, source_target_pairs={{0,16},{16,0},{1,17},{17,1},{2,18},{18,2},{3,19},{19,3},{4,20},{20... | collective-permute-start | bytes 2752520 | tf_op jit(solution)/shard_map/ppermute | solution.py:881
  271.5 99.6 %all-gather.10.cloned.1.call-start = ((), (), s32[]{:S(2)}) async-start(), calls=%async_computation.8 | async-start | bytes 2621440 | tf_op jit(solution)/shard_map/all_gather | solution.py:1096
  271.5 39.3 %collective-permute-start.30 = (bf16[512,1664]{1,0:T(8,128)(2,1)S(1)}, bf16[512,1664]{1,0:T(8,128)(2,1)S(1)}, u32[]{:S(2)}, u32[]{:S(2)}) collective-permute-start(bf16[512,1664]{1,0:T(8,128)(2,1)S(1)} %copy-done.73), channel_id=1, source_target_pairs={{0,16},{16,0},{1,17},{17,1},{2,18},{18,2},{3,19},{19,3},{4,20},{20... | collective-permute-start | bytes 5111816 | tf_op jit(solution)/shard_map/ppermute | solution.py:881
  272.2 22.3 %collective-permute-start.31 = (bf16[512,896]{1,0:T(8,128)(2,1)}, bf16[512,896]{1,0:T(8,128)(2,1)S(1)}, u32[]{:S(2)}, u32[]{:S(2)}) collective-permute-start(bf16[512,896]{1,0:T(8,128)(2,1)} %collective-permute-done.2.refs_10_), channel_id=1, source_target_pairs={{0,8},{4,12},{8,0},{12,4},{1,9},{5,13},{9,1},{13,5},{2,10},{6,14},... | collective-permute-start | bytes 2752520 | tf_op jit(solution)/shard_map/ppermute | solution.py:872
  278.4 43.7 %collective-permute-start.33 = (bf16[512,2048]{1,0:T(8,128)(2,1)}, bf16[512,2048]{1,0:T(8,128)(2,1)}, u32[]{:S(2)}, u32[]{:S(2)}) collective-permute-start(bf16[512,2048]{1,0:T(8,128)(2,1)} %bitcast.26.refs_3_.refs_2_), channel_id=1, source_target_pairs={{0,4},{4,0},{8,12},{12,8},{1,5},{5,1},{9,13},{13,9},{2,6},{6,2},{1... | collective-permute-start | bytes 6291464 | tf_op jit(solution)/shard_map/ppermute | solution.py:878
  321.9 124.8 %reduce-scatter.9.cloned.1.call-start = ((), (), s32[]{:S(2)}) async-start(), calls=%async_computation.10 | async-start | bytes 2621440 | tf_op jit(solution)/shard_map/reduce_scatter | solution.py:1117
  378.5 124.4 %reduce-scatter.7.cloned.1.call-start = ((), (), s32[]{:S(2)}) async-start(), calls=%async_computation.9 | async-start | bytes 2621440 | tf_op jit(solution)/shard_map/reduce_scatter | solution.py:1117
  414.2 25.4 %collective-permute-start.37 = (bf16[512,2048]{1,0:T(8,128)(2,1)}, bf16[512,2048]{1,0:T(8,128)(2,1)S(1)}, u32[]{:S(2)}, u32[]{:S(2)}) collective-permute-start(bf16[512,2048]{1,0:T(8,128)(2,1)} %get-tuple-element.207), channel_id=1, source_target_pairs={{0,4},{4,0},{8,12},{12,8},{1,5},{5,1},{9,13},{13,9},{2,6},{6,2},{1... | collective-permute-start | bytes 6291464 | tf_op jit(solution)/shard_map/ppermute | solution.py:878
  426.1 30.5 %collective-permute-start.39 = (bf16[384,896]{1,0:T(8,128)(2,1)}, bf16[384,896]{1,0:T(8,128)(2,1)}, u32[]{:S(2)}, u32[]{:S(2)}) collective-permute-start(bf16[384,896]{1,0:T(8,128)(2,1)} %slice.765), channel_id=1, source_target_pairs={{0,16},{16,0},{1,17},{17,1},{2,18},{18,2},{3,19},{19,3},{4,20},{20... | collective-permute-start | bytes 2064392 | tf_op jit(solution)/shard_map/ppermute | solution.py:881
  441.9 118.2 %reduce-scatter.15.cloned.1.call-start = ((), (), s32[]{:S(2)}) async-start(), calls=%async_computation.13 | async-start | bytes 2293760 | tf_op jit(solution)/shard_map/reduce_scatter | solution.py:1223
  445.5 36.2 %collective-permute-start.34 = (bf16[512,2048]{1,0:T(8,128)(2,1)}, bf16[512,2048]{1,0:T(8,128)(2,1)S(1)}, u32[]{:S(2)}, u32[]{:S(2)}) collective-permute-start(bf16[512,2048]{1,0:T(8,128)(2,1)} %get-tuple-element.205), channel_id=1, source_target_pairs={{0,4},{4,0},{8,12},{12,8},{1,5},{5,1},{9,13},{13,9},{2,6},{6,2},{1... | collective-permute-start | bytes 6291464 | tf_op jit(solution)/shard_map/ppermute | solution.py:878
  445.5 35.6 %collective-permute-start.41 = (bf16[640,896]{1,0:T(8,128)(2,1)}, bf16[640,896]{1,0:T(8,128)(2,1)}, u32[]{:S(2)}, u32[]{:S(2)}) collective-permute-start(bf16[640,896]{1,0:T(8,128)(2,1)} %slice.767), channel_id=1, source_target_pairs={{0,16},{16,0},{1,17},{17,1},{2,18},{18,2},{3,19},{19,3},{4,20},{20... | collective-permute-start | bytes 3440648 | tf_op jit(solution)/shard_map/ppermute | solution.py:881
  446.1 35.1 %collective-permute-start.42 = (bf16[640,768]{1,0:T(8,128)(2,1)}, bf16[640,768]{1,0:T(8,128)(2,1)}, u32[]{:S(2)}, u32[]{:S(2)}) collective-permute-start(bf16[640,768]{1,0:T(8,128)(2,1)} %slice.768), channel_id=1, source_target_pairs={{0,8},{4,12},{8,0},{12,4},{1,9},{5,13},{9,1},{13,5},{2,10},{6,14},... | collective-permute-start | bytes 2949128 | tf_op jit(solution)/shard_map/ppermute | solution.py:872
  456.5 30.5 %collective-permute-start.43 = (bf16[512,2048]{1,0:T(8,128)(2,1)}, bf16[512,2048]{1,0:T(8,128)(2,1)}, u32[]{:S(2)}, u32[]{:S(2)}) collective-permute-start(bf16[512,2048]{1,0:T(8,128)(2,1)} %get-tuple-element.232), channel_id=1, source_target_pairs={{0,4},{4,0},{8,12},{12,8},{1,5},{5,1},{9,13},{13,9},{2,6},{6,2},{1... | collective-permute-start | bytes 6291464 | tf_op jit(solution)/shard_map/ppermute | solution.py:878
  481.1 21.8 %collective-permute-start.44 = (bf16[1024,896]{1,0:T(8,128)(2,1)}, bf16[1024,896]{1,0:T(8,128)(2,1)}, u32[]{:S(2)}, u32[]{:S(2)}) collective-permute-start(bf16[1024,896]{1,0:T(8,128)(2,1)} %get-tuple-element.236), channel_id=1, source_target_pairs={{0,4},{4,0},{8,12},{12,8},{1,5},{5,1},{9,13},{13,9},{2,6},{6,2},{1... | collective-permute-start | bytes 5505032 | tf_op jit(solution)/shard_map/ppermute | solution.py:878
  521.7 33.3 %collective-permute-start.47 = (bf16[640,896]{1,0:T(8,128)(2,1)}, bf16[640,896]{1,0:T(8,128)(2,1)}, u32[]{:S(2)}, u32[]{:S(2)}) collective-permute-start(bf16[640,896]{1,0:T(8,128)(2,1)} %slice.772), channel_id=1, source_target_pairs={{0,8},{4,12},{8,0},{12,4},{1,9},{5,13},{9,1},{13,5},{2,10},{6,14},... | collective-permute-start | bytes 3440648 | tf_op jit(solution)/shard_map/ppermute | solution.py:872
  522.2 92.2 %reduce-scatter.17.cloned.1.call-start = ((), (), s32[]{:S(2)}) async-start(), calls=%async_computation.14 | async-start | bytes 2293760 | tf_op jit(solution)/shard_map/reduce_scatter | solution.py:1223
  529.1 25.9 %collective-permute-start.48 = (bf16[256,1792]{1,0:T(8,128)(2,1)S(1)}, bf16[256,1792]{1,0:T(8,128)(2,1)S(1)}, u32[]{:S(2)}, u32[]{:S(2)}) collective-permute-start(bf16[256,1792]{1,0:T(8,128)(2,1)S(1)} %slice.773), channel_id=1, source_target_pairs={{0,16},{16,0},{1,17},{17,1},{2,18},{18,2},{3,19},{19,3},{4,20},{20... | collective-permute-start | bytes 2752520 | tf_op jit(solution)/shard_map/ppermute | solution.py:881
  576.5 196.2 %reduce-scatter.11.cloned.1.call-start = ((), (), s32[]{:S(2)}) async-start(), calls=%async_computation.11 | async-start | bytes 2621440 | tf_op jit(solution)/shard_map/reduce_scatter | solution.py:1353
  576.9 22.2 %collective-permute-start.55 = (bf16[128,1792]{1,0:T(8,128)(2,1)S(1)}, bf16[128,1792]{1,0:T(8,128)(2,1)S(1)}, u32[]{:S(2)}, u32[]{:S(2)}) collective-permute-start(bf16[128,1792]{1,0:T(8,128)(2,1)S(1)} %get-tuple-element.398), channel_id=1, source_target_pairs={{0,16},{16,0},{1,17},{17,1},{2,18},{18,2},{3,19},{19,3},{4,20},{20... | collective-permute-start | bytes 1376264 | tf_op jit(solution)/shard_map/ppermute | solution.py:881
  618.4 154.3 %reduce-scatter.13.cloned.1.call-start = ((), (), s32[]{:S(2)}) async-start(), calls=%async_computation.12 | async-start | bytes 2621440 | tf_op jit(solution)/shard_map/reduce_scatter | solution.py:1353
  618.6 22.8 %collective-permute-start.59 = (bf16[320,768]{1,0:T(8,128)(2,1)S(1)}, bf16[320,768]{1,0:T(8,128)(2,1)S(1)}, u32[]{:S(2)}, u32[]{:S(2)}) collective-permute-start(bf16[320,768]{1,0:T(8,128)(2,1)S(1)} %slice.784), channel_id=1, source_target_pairs={{0,16},{16,0},{1,17},{17,1},{2,18},{18,2},{3,19},{19,3},{4,20},{20... | collective-permute-start | bytes 1474568 | tf_op jit(solution)/shard_map/ppermute | solution.py:881
  659.3 33.2 %collective-permute-start.65 = (bf16[256,1024]{1,0:T(8,128)(2,1)S(1)}, bf16[256,1024]{1,0:T(8,128)(2,1)S(1)}, u32[]{:S(2)}, u32[]{:S(2)}) collective-permute-start(bf16[256,1024]{1,0:T(8,128)(2,1)S(1)} %get-tuple-element.384), channel_id=1, source_target_pairs={{0,24},{4,28},{8,16},{12,20},{16,8},{20,12},{24,0},{28,4},{1,25},{... | collective-permute-start | bytes 1572872 | tf_op jit(solution)/shard_map/ppermute | solution.py:875
  660.0 32.5 %collective-permute-start.64 = (bf16[256,1024]{1,0:T(8,128)(2,1)S(1)}, bf16[256,1024]{1,0:T(8,128)(2,1)S(1)}, u32[]{:S(2)}, u32[]{:S(2)}) collective-permute-start(bf16[256,1024]{1,0:T(8,128)(2,1)S(1)} %get-tuple-element.385), channel_id=1, source_target_pairs={{0,16},{16,0},{1,17},{17,1},{2,18},{18,2},{3,19},{19,3},{4,20},{20... | collective-permute-start | bytes 1572872 | tf_op jit(solution)/shard_map/ppermute | solution.py:881
  661.5 31.1 %collective-permute-start.63 = (bf16[256,1024]{1,0:T(8,128)(2,1)S(1)}, bf16[256,1024]{1,0:T(8,128)(2,1)S(1)}, u32[]{:S(2)}, u32[]{:S(2)}) collective-permute-start(bf16[256,1024]{1,0:T(8,128)(2,1)S(1)} %get-tuple-element.386), channel_id=1, source_target_pairs={{0,8},{4,12},{8,0},{12,4},{1,9},{5,13},{9,1},{13,5},{2,10},{6,14},... | collective-permute-start | bytes 1572872 | tf_op jit(solution)/shard_map/ppermute | solution.py:872
  680.8 37.3 %collective-permute-start.73 = (bf16[256,1792]{1,0:T(8,128)(2,1)}, bf16[256,1792]{1,0:T(8,128)(2,1)}, u32[]{:S(2)}, u32[]{:S(2)}) collective-permute-start(bf16[256,1792]{1,0:T(8,128)(2,1)} %slice.800), channel_id=1, source_target_pairs={{0,16},{16,0},{1,17},{17,1},{2,18},{18,2},{3,19},{19,3},{4,20},{20... | collective-permute-start | bytes 2752520 | tf_op jit(solution)/shard_map/ppermute | solution.py:881
  681.4 51.7 %collective-permute-start.78 = (bf16[512,896]{1,0:T(8,128)(2,1)}, bf16[512,896]{1,0:T(8,128)(2,1)}, u32[]{:S(2)}, u32[]{:S(2)}) collective-permute-start(bf16[512,896]{1,0:T(8,128)(2,1)} %slice.810), channel_id=1, source_target_pairs={{0,16},{16,0},{1,17},{17,1},{2,18},{18,2},{3,19},{19,3},{4,20},{20... | collective-permute-start | bytes 2752520 | tf_op jit(solution)/shard_map/ppermute | solution.py:881
  707.3 23.6 %collective-permute-start.69 = (bf16[256,1792]{1,0:T(8,128)(2,1)}, bf16[256,1792]{1,0:T(8,128)(2,1)}, u32[]{:S(2)}, u32[]{:S(2)}) collective-permute-start(bf16[256,1792]{1,0:T(8,128)(2,1)} %slice.802), channel_id=1, source_target_pairs={{0,8},{4,12},{8,0},{12,4},{1,9},{5,13},{9,1},{13,5},{2,10},{6,14},... | collective-permute-start | bytes 2752520 | tf_op jit(solution)/shard_map/ppermute | solution.py:872
  710.8 35.6 %collective-permute-start.77 = (bf16[512,896]{1,0:T(8,128)(2,1)}, bf16[512,896]{1,0:T(8,128)(2,1)}, u32[]{:S(2)}, u32[]{:S(2)}) collective-permute-start(bf16[512,896]{1,0:T(8,128)(2,1)} %slice.809), channel_id=1, source_target_pairs={{0,8},{4,12},{8,0},{12,4},{1,9},{5,13},{9,1},{13,5},{2,10},{6,14},... | collective-permute-start | bytes 2752520 | tf_op jit(solution)/shard_map/ppermute | solution.py:872
  719.7 31.5 %collective-permute-start.74 = (bf16[256,448]{1,0:T(8,128)(2,1)S(1)}, bf16[256,448]{1,0:T(8,128)(2,1)S(1)}, u32[]{:S(2)}, u32[]{:S(2)}) collective-permute-start(bf16[256,448]{1,0:T(8,128)(2,1)S(1)} %get-tuple-element.405), channel_id=1, source_target_pairs={{0,1},{1,0},{2,3},{3,2},{4,5},{5,4},{6,7},{7,6},{8,9},{9,8},{10,11... | collective-permute-start | bytes 688136 | tf_op jit(solution)/shard_map/ppermute | solution.py:888
  722.9 29.1 %collective-permute-start.75 = (bf16[256,448]{1,0:T(8,128)(2,1)S(1)}, bf16[256,448]{1,0:T(8,128)(2,1)S(1)}, u32[]{:S(2)}, u32[]{:S(2)}) collective-permute-start(bf16[256,448]{1,0:T(8,128)(2,1)S(1)} %get-tuple-element.406), channel_id=1, source_target_pairs={{0,2},{1,3},{2,0},{3,1},{4,6},{5,7},{6,4},{7,5},{8,10},{9,11},{10,... | collective-permute-start | bytes 688136 | tf_op jit(solution)/shard_map/ppermute | solution.py:888
  730.9 24.7 %collective-permute-start.76 = (bf16[256,448]{1,0:T(8,128)(2,1)S(1)}, bf16[256,448]{1,0:T(8,128)(2,1)S(1)}, u32[]{:S(2)}, u32[]{:S(2)}) collective-permute-start(bf16[256,448]{1,0:T(8,128)(2,1)S(1)} %get-tuple-element.407), channel_id=1, source_target_pairs={{0,3},{1,2},{2,1},{3,0},{4,7},{5,6},{6,5},{7,4},{8,11},{9,10},{10,... | collective-permute-start | bytes 688136 | tf_op jit(solution)/shard_map/ppermute | solution.py:888
  750.3 26.4 %collective-permute-start.79 = (bf16[256,2560]{1,0:T(8,128)(2,1)}, bf16[256,2560]{1,0:T(8,128)(2,1)}, u32[]{:S(2)}, u32[]{:S(2)}) collective-permute-start(bf16[256,2560]{1,0:T(8,128)(2,1)} %pad_maximum_fusion.2), channel_id=1, source_target_pairs={{0,4},{4,0},{8,12},{12,8},{1,5},{5,1},{9,13},{13,9},{2,6},{6,2},{1... | collective-permute-start | bytes 3932168 | tf_op jit(solution)/shard_map/ppermute | solution.py:878
  (119 other events, 1277.1 us)
Sparse Core Ops, SparseCore 0:
  15.7 129.2 all-gather.11
  148.2 76.8 all-gather.5
  271.6 48.9 all-gather.7
  322.0 49.0 all-gather.9
  378.6 42.4 reduce-scatter.8
  442.0 40.3 reduce-scatter.6
  522.4 37.6 reduce-scatter.14
  576.6 37.7 reduce-scatter.16
  618.5 42.0 reduce-scatter.10
  662.9 51.3 reduce-scatter.12

commit v4 on v3

--- a/solution.py
+++ b/solution.py
@@ -551,7 +551,7 @@
 def attention_forward(kv0, kv1, query, batch, bias0, bias1):
     half, rows = bias0.shape
     wide = GROUP * rows
-    keys = pl.BlockSpec((half // rows, 1, rows, LANES), lambda c: (0, batch, 0, c))
+    keys = pl.BlockSpec((half // rows, 1, rows, LANES), lambda c: (0, 0, 0, c))
     kv0, kv1 = (kv.reshape(half // rows, -1, rows, KV_WIDTH) for kv in (kv0, kv1))
     return kernel_call(
         attention_forward_kernel,
@@ -648,7 +648,7 @@
 ):
     half, rows = bias0.shape
     wide = GROUP * rows
-    keys = pl.BlockSpec((half // rows, 1, rows, LANES), lambda c: (0, batch, 0, c))
+    keys = pl.BlockSpec((half // rows, 1, rows, LANES), lambda c: (0, 0, 0, c))
     kv0, kv1 = (kv.reshape(half // rows, -1, rows, KV_WIDTH) for kv in (kv0, kv1))
     d_keys = pl.BlockSpec((half, LANES), lambda c: (0, c))
     heads = pl.BlockSpec((rows, GROUP_WIDTH), lambda c: (0, c))
@@ -993,28 +993,23 @@
     tokens_in = to_order(tokens[:, 0].reshape(batches * rows, width))
     cot_in = to_order(cotangent[:, 0].reshape(batches * rows, width))
     cot_held = order_columns(table, cot_in) if paired else cot_in
-    lined = lax.all_gather(
-        jnp.concatenate(
-            [
-                cot_held,
-                padded_columns(query_weight.reshape(small, Q_WIDTH), width),
-                padded_columns(output_weight.T, width),
-            ],
-            axis=0,
-        ),
+    projections = lax.all_gather(
+        jnp.concatenate([query_weight.reshape(small, Q_WIDTH), output_weight.T], axis=0),
         "heads",
         axis=0,
     )
+    q_rows = (
+        projections[:, :small]
+        .reshape(heads_size, query_weight.shape[0], query_weight.shape[1])
+        .transpose(1, 0, 2)
+        .reshape(query_weight.shape[0], Q_WIDTH)
+    )
+    o_rows = projections[:, small:].reshape(4 * small, Q_WIDTH)
+    lined = lax.all_gather(cot_held, "heads", axis=0)
     cots_mine = [
         lined[:, span(batch, rows)].reshape(heads_size * rows, width) for batch in range(batches)
     ]
-    q_rows = (
-        lined[:, batches * rows : batches * rows + small, :Q_WIDTH]
-        .reshape(heads_size, query_weight.shape[0], query_weight.shape[1])
-        .transpose(1, 0, 2)
-        .reshape(query_weight.shape[0], Q_WIDTH)
-    )
-    o_rows = lined[:, batches * rows + small :, :Q_WIDTH].reshape(4 * small, Q_WIDTH)
+
     units = gate_weight.shape[1] // 2
     act_width, units_width = up_to(units), up_to(2 * units)
 
@@ -1071,21 +1066,27 @@
     normed, kv_raw, kv_low, gains = project_key_value(
         table, after(tokens_in, down_near), cosine, sine, key_gain, kvg
     )
-    kv_pair = jnp.concatenate([kv_low, swap_x(kv_low)], axis=0)
-    kv_lined = lax.all_gather(after(kv_pair, gate_up_near), "heads", axis=0, tiled=True)
+    kv_got = swap_x(kv_low)
+    kv_lined = []
+    for batch in range(batches):
+        cut = span(batch, rows)
+        pair = jnp.concatenate([kv_low[cut], kv_got[cut]], axis=0)
+        if batch == 0:
+            pair = after(pair, gate_up_near, lined)
+        kv_lined.append(lax.all_gather(pair, "heads", axis=0, tiled=True))
     down = unit_pieces(gather_far(down_near, False))
     q_near = gather_near(q_rows)
-    q_full = both_cores(gather_far(q_near, False))
+    q_full = both_cores(gather_far(after(q_near, kv_got), False))
     o_near = gather_near(after(o_rows, q_near))
-    q_raw, queries = project_query(after(normed, o_near), cosine, sine, query_gain, q_full)
+    q_raw, queries = project_query(after(normed, kv_lined[0]), cosine, sine, query_gain, q_full)
     o_pieces = gather_far(after(o_near, queries), True)
-    kv_lined = after(kv_lined, queries)
-    kvs = (kv_lined, swap_core(kv_lined))
+    kv_lined[0] = after(kv_lined[0], queries, o_near)
+    kvs = [(v, swap_core(v)) for v in kv_lined]
 
     feeds, mixeds, lses, hiddens = [], [], [], []
     for batch in range(batches):
         query = queries if batch == 0 else after(queries, hiddens[0])
-        mixed, lse = attention_forward(*kvs, query, batch, *biases[batch])
+        mixed, lse = attention_forward(*kvs[batch], query, batch, *biases[batch])
         if batch == 0:
             o_full = both_cores(after(o_pieces, mixed))
         else:
@@ -1101,8 +1102,11 @@
     feeds[0] = after(feeds[0], feed_rows)
     feeds = [(swap_core(v), v) for v in feeds]
 
-    d_feeds, acts, d_units, cots, outs = [], [], [], [], []
+    d_feeds, acts, d_units, cots = [], [], [], []
+    added = []
     for batch in range(batches):
+        if batch == 1:
+            feeds[1] = after(feeds[1], added[0])
         cot_pair = (swap_core(cots_mine[batch]), cots_mine[batch])
         act, d_unit, out_other, out_mine, d_feed_other, d_feed_mine = feed_forward(
             feeds[batch], cot_pair, gate_up, down, units
@@ -1110,7 +1114,7 @@
         acts.append(act)
         d_units.append(d_unit)
         cots.append(cot_pair)
-        outs.append((out_mine, out_other))
+        added.append(out_mine + swap_core(out_other))
         d_feed = d_feed_mine + swap_core(d_feed_other)
         if batch + 1 < batches:
             d_feed = after(d_feed, feeds[batch + 1])
@@ -1162,7 +1166,6 @@
         g = lax.psum_scatter(g, "dp", scatter_dimension=0)
         return g[0] + swap_x(g[1])
 
-    added = [out_mine + swap_core(out_other) for out_mine, out_other in outs]
     d_hiddens, d_attendeds, d_q_raws, d_lined = [], [], [], []
     feed_gain_grads, query_gain_grads = [], []
     mixed_all = jnp.concatenate(mixeds, axis=0)
@@ -1178,7 +1181,7 @@
         if batch == 1:
             d_feed = after(d_feed, d_q_raws[0])
             if paired:
-                tied = after(acts, d_q_raws[0], added)
+                tied = after(acts, d_q_raws[0])
                 down_far = weight_grad(cot_all, tied, slice(0, act_width), 2, 2, 1)
                 down_parts = send_parts(down_far, swap_x, 256, 640, 128)
                 d_feed = after(d_feed, down_far, last_kv)
@@ -1199,7 +1202,7 @@
             if paired:
                 o_parts = send_parts(o_send, swap_y, 256, 128, 128)
         back = attention_backward(
-            *kvs,
+            *kvs[batch],
             queries,
             batch,
             mixeds[batch],

time: 805 us -> 780 us (0.969)
  waiting for transfers between devices: 243 us -> 226 us
    unnamed x174 -> x172, local copies, waits for them, and re-layouts: 31.6 us -> 27.5 us
    ppermute x28 -> x29, waiting for transfers between devices: 21.3 us -> 17.8 us  [swap_core(): return lax.ppermute(v, 'seq', [(i, i ^ 1) for i in range(4)])]
  transfers between devices with their start and end apart: 90 -> 93, of which waited for: 34 -> 37; matrix products, arithmetic and copies ran while one was open for 17% -> 18% of each run, Pallas kernels for 34% -> 36%
where the time goes in v4:
time: 780 us; the launch traced here: 772 us
  Pallas kernels  281 us (36%)
  waiting for transfers between devices  226 us (29%)
  local copies, waits for them, and re-layouts  85 us (11%)
  starting transfers between devices  80.9 us (10%)
  other arithmetic  72.4 us (9%)
  between operations  16 us (2%)
  matrix products  10.4 us (1%)
    pallas_call x15, Pallas kernels, call(): pl.pallas_call(body, grid=grid, in_specs=in_specs, out_specs=out_specs, s...  217 us
    ppermute x22, waiting for transfers between devices, swap_x(): return lax.ppermute(v, 'seq', [(i, i ^ 2) for i in range(4)])  106 us
    pallas_call x8, Pallas kernels, call(): pl.pallas_call(body, grid_spec=pltpu.PrefetchScalarGridSpec(num_scalar_pr...  64 us
    ppermute x18, waiting for transfers between devices, swap_y(): return lax.ppermute(v, 'dp', [(0, 1), (1, 0)])  49 us
    unnamed x172, local copies, waits for them, and re-layouts  27.5 us
    ppermute x22, starting transfers between devices, swap_x(): return lax.ppermute(v, 'seq', [(i, i ^ 2) for i in range(4)])  27.4 us
    ppermute x18, starting transfers between devices, swap_y(): return lax.ppermute(v, 'dp', [(0, 1), (1, 0)])  21.2 us
    ppermute x2, waiting for transfers between devices, step(): got = lax.ppermute(u, 'heads', [(i, i ^ distance) for i in range(4)])  18.8 us
  transfers between devices with their start and end apart: 93, of which 37 were waited for; matrix products, arithmetic and copies ran while one was open for 18% of the time, Pallas kernels for 36%

profile of v4, /device:TPU:0, one launch (start us, length us, event | category | flops | bytes accessed | tf_op | source)
XLA Modules:
  0.0 772.1 jit_solution(17302238379810109969)
XLA Ops:
  26.4 8.3 %collective-permute-start.4 = (bf16[128,1024]{1,0:T(8,128)(2,1)S(1)}, bf16[128,1024]{1,0:T(8,128)(2,1)}, u32[]{:S(2)}, u32[]{:S(2)}) collective-permute-start(bf16[128,1024]{1,0:T(8,128)(2,1)S(1)} %maximum_select_fusion.4), channel_id=1, source_target_pairs={{0,2},{1,3},{2,0},{3,1},{4,6},{5,7},{6,4},{7,5},{8,10},{9,11},{10,... | collective-permute-start | bytes 786440 | tf_op jit(solution)/shard_map/ppermute | solution.py:904
  35.8 5.5 fusion.4
  45.4 16.8 %collective-permute-done.4 = bf16[128,1024]{1,0:T(8,128)(2,1)} collective-permute-done((bf16[128,1024]{1,0:T(8,128)(2,1)S(1)}, bf16[128,1024]{1,0:T(8,128)(2,1)}, u32[]{:S(2)}, u32[]{:S(2)}) %collective-permute-start.4) | collective-permute-done | bytes 262176 | tf_op jit(solution)/shard_map/ppermute | solution.py:904
  66.4 7.9 %collective-permute-done.6.refs_2_ = bf16[256,1024]{1,0:T(8,128)(2,1)S(1)} collective-permute-done((bf16[256,1024]{1,0:T(8,128)(2,1)S(1)}, bf16[256,1024]{1,0:T(8,128)(2,1)S(1)}, u32[]{:S(2)}, u32[]{:S(2)}) %collective-permute-start.6) | collective-permute-done | bytes 524320 | tf_op jit(solution)/shard_map/ppermute | solution.py:881
  83.4 5.1 collective-permute-done.7.refs_3_
  96.0 7.3 project_key_value.1
  110.0 29.4 %collective-permute-done.12 = bf16[256,896]{1,0:T(8,128)(2,1)} collective-permute-done((bf16[256,896]{1,0:T(8,128)(2,1)}, bf16[256,896]{1,0:T(8,128)(2,1)}, u32[]{:S(2)}, u32[]{:S(2)}) %collective-permute-start.12) | collective-permute-done | bytes 458784 | tf_op jit(solution)/shard_map/ppermute | solution.py:872
  141.2 6.7 all-gather.17.cloned.1.call-done
  150.1 20.8 %collective-permute-done.15.refs_1_ = bf16[256,1792]{1,0:T(8,128)(2,1)S(1)} collective-permute-done((bf16[256,1792]{1,0:T(8,128)(2,1)}, bf16[256,1792]{1,0:T(8,128)(2,1)S(1)}, u32[]{:S(2)}, u32[]{:S(2)}) %collective-permute-start.15) | collective-permute-done | bytes 917536 | tf_op jit(solution)/shard_map/ppermute | solution.py:872
  174.6 18.9 %collective-permute-done.17.refs_3_ = bf16[256,1792]{1,0:T(8,128)(2,1)} collective-permute-done((bf16[256,1792]{1,0:T(8,128)(2,1)}, bf16[256,1792]{1,0:T(8,128)(2,1)}, u32[]{:S(2)}, u32[]{:S(2)}) %collective-permute-start.17) | collective-permute-done | bytes 917536 | tf_op jit(solution)/shard_map/ppermute | solution.py:872
  198.0 9.5 %project_query.1 = (f32[256,1792]{1,0:T(8,128)}, bf16[256,1792]{1,0:T(8,128)(2,1)}) custom-call(bf16[256,2048]{1,0:T(8,128)(2,1)} %get-tuple-element.265.normed, f32[256,128]{1,0:T(8,128)} %pad_maximum_fusion.9.cosine, f32[256,128]{1,0:T(8,128)} %pad_maximum_fusion.10.sine, f32[1,128]{1,0:T(1,128)} %pad_maximum_fusion.14.gain, bf16[256,1792]{1,0:T(8,128)(2,1)} %copy-done.13, ...), custom_call_target="tpu_custom_call" | custom-call | flops 1879048192 | bytes 11403776 | tf_op jit(solution)/shard_map/project_query/pallas_call | solution.py:78
  207.5 8.8 %collective-permute-done.23.refs_2_ = bf16[256,1792]{1,0:T(8,128)(2,1)S(1)} collective-permute-done((bf16[256,1792]{1,0:T(8,128)(2,1)S(1)}, bf16[256,1792]{1,0:T(8,128)(2,1)S(1)}, u32[]{:S(2)}, u32[]{:S(2)}) %collective-permute-start.23) | collective-permute-done | bytes 917536 | tf_op jit(solution)/shard_map/ppermute | solution.py:881
  222.5 11.1 %attention_forward.2 = (bf16[128,1792]{1,0:T(8,128)(2,1)}, f32[7,1,512]{2,1,0:T(1,128)}) custom-call(bf16[8,1,128,896]{3,2,1,0:T(8,128)(2,1)} %bitcast.19.kv0, bf16[8,1,128,896]{3,2,1,0:T(8,128)(2,1)} %bitcast.20.kv1, bf16[256,1792]{1,0:T(8,128)(2,1)} %get-tuple-element.196.query, f32[1024,128]{1,0:T(8,128)} %get-tuple-element.443.bias0, ...), custom_call_target="tpu_custom_call" | custom-call | flops 11274289152 | bytes 6109184 | tf_op jit(solution)/shard_map/attention_forward/pallas_call | solution.py:78
  233.6 10.5 %collective-permute-done.25.refs_3_ = bf16[256,1792]{1,0:T(8,128)(2,1)S(1)} collective-permute-done((bf16[256,1792]{1,0:T(8,128)(2,1)S(1)}, bf16[256,1792]{1,0:T(8,128)(2,1)S(1)}, u32[]{:S(2)}, u32[]{:S(2)}) %collective-permute-start.25) | collective-permute-done | bytes 917536 | tf_op jit(solution)/shard_map/ppermute | solution.py:881
  251.4 9.6 %project_output.2 = (f32[128,2048]{1,0:T(8,128)}, bf16[128,2048]{1,0:T(8,128)(2,1)}) custom-call(s32[8]{0:T(128)} %broadcast_xor_fusion.table, bf16[128,1792]{1,0:T(8,128)(2,1)} %get-tuple-element.186.mixed, bf16[256,2048]{1,0:T(8,128)(2,1)} %bitcast.69, f32[8,2048]{1,0:T(8,128)} %get-tuple-element.187.gains, bf16[256,1792]{1,0:T(8,128)(2,1)} %bitcast.64, ...), custom_call_target="tpu_custom_call" | custom-call | flops 939524096 | bytes 10485760 | tf_op jit(solution)/shard_map/project_output/pallas_call | solution.py:87
  263.4 4.9 fusion.28
  269.5 11.0 %attention_forward.3 = (bf16[128,1792]{1,0:T(8,128)(2,1)}, f32[7,1,512]{2,1,0:T(1,128)}) custom-call(bf16[8,1,128,896]{3,2,1,0:T(8,128)(2,1)} %bitcast.94, bf16[8,1,128,896]{3,2,1,0:T(8,128)(2,1)} %bitcast.96, bf16[256,1792]{1,0:T(8,128)(2,1)} %get-tuple-element.196.query, f32[1024,128]{1,0:T(8,128)} %get-tuple-element.442.bias0, ...), custom_call_target="tpu_custom_call" | custom-call | flops 11274289152 | bytes 6109184 | tf_op jit(solution)/shard_map/attention_forward/pallas_call | solution.py:78
  280.5 4.0 collective-permute-done.32.refs_11_
  284.5 16.6 %collective-permute-done.31.refs_7_ = bf16[512,1664]{1,0:T(8,128)(2,1)} collective-permute-done((bf16[512,1664]{1,0:T(8,128)(2,1)}, bf16[512,1664]{1,0:T(8,128)(2,1)}, u32[]{:S(2)}, u32[]{:S(2)}) %collective-permute-start.31) | collective-permute-done | bytes 1703968 | tf_op jit(solution)/shard_map/ppermute | solution.py:881
  301.1 9.6 %project_output.3 = (f32[128,2048]{1,0:T(8,128)}, bf16[128,2048]{1,0:T(8,128)(2,1)}) custom-call(s32[8]{0:T(128)} %broadcast_xor_fusion.table, bf16[128,1792]{1,0:T(8,128)(2,1)} %get-tuple-element.199.mixed, bf16[256,2048]{1,0:T(8,128)(2,1)} %bitcast.70, f32[8,2048]{1,0:T(8,128)} %get-tuple-element.187.gains, bf16[256,1792]{1,0:T(8,128)(2,1)} %bitcast.65, ...), custom_call_target="tpu_custom_call" | custom-call | flops 939524096 | bytes 10485760 | tf_op jit(solution)/shard_map/project_output/pallas_call | solution.py:87
  311.1 4.1 collective-permute-done.33.refs_0_.refs_1_
  316.6 34.2 %feed_forward.2 = (bf16[1024,896]{1,0:T(8,128)(2,1)}, bf16[1024,1664]{1,0:T(8,128)(2,1)}, bf16[512,2048]{1,0:T(8,128)(2,1)}, bf16[512,2048]{1,0:T(8,128)(2,1)}, ...) custom-call(bf16[512,2048]{1,0:T(8,128)(2,1)} %copy-done, ...), custom_call_target="tpu_custom_call" | custom-call | flops 20132659200 | bytes 32505856 | tf_op jit(solution)/shard_map/feed_forward/pallas_call | solution.py:78
  351.0 4.2 all-gather.15.cloned.1.call-done.refs_1_.refs_6_.refs_7_
  355.7 4.4 add.317
  362.7 5.1 add.315
  367.7 34.2 %feed_forward.3 = (bf16[1024,896]{1,0:T(8,128)(2,1)}, bf16[1024,1664]{1,0:T(8,128)(2,1)}, bf16[512,2048]{1,0:T(8,128)(2,1)}, bf16[512,2048]{1,0:T(8,128)(2,1)}, ...) custom-call(bf16[512,2048]{1,0:T(8,128)(2,1)} %copy-done.1, ...), custom_call_target="tpu_custom_call" | custom-call | flops 20132659200 | bytes 32505856 | tf_op jit(solution)/shard_map/feed_forward/pallas_call | solution.py:78
  402.1 9.7 %weight_grad.6 = bf16[1024,896]{1,0:T(8,128)(2,1)} custom-call(bf16[512,2048]{1,0:T(8,128)(2,1)} %copy-done, bf16[512,2048]{1,0:T(8,128)(2,1)} %copy-done, bf16[512,2048]{1,0:T(8,128)(2,1)} %all-gather.13.cloned.1.call-done.refs_1_.refs_2_.refs_3_, bf16[512,2048]{1,0:T(8,128)(2,1)} %all-gather.13.cloned.1.call-done.refs_1_.refs_2_.refs_3_, ...), custom_call_target="tpu_custom_call" | custom-call | flops 3758096384 | bytes 25427968 | tf_op jit(solution)/shard_map/weight_grad/pallas_call | solution.py:78
  415.3 8.7 %weight_grad.7 = bf16[1024,768]{1,0:T(8,128)(2,1)} custom-call(bf16[512,2048]{1,0:T(8,128)(2,1)} %copy-done, bf16[512,2048]{1,0:T(8,128)(2,1)} %copy-done, bf16[512,2048]{1,0:T(8,128)(2,1)} %all-gather.13.cloned.1.call-done.refs_1_.refs_2_.refs_3_, bf16[512,2048]{1,0:T(8,128)(2,1)} %all-gather.13.cloned.1.call-done.refs_1_.refs_2_.refs_3_, ...), custom_call_target="tpu_custom_call" | custom-call | flops 3221225472 | bytes 25165824 | tf_op jit(solution)/shard_map/weight_grad/pallas_call | solution.py:78
  431.9 10.4 %hidden_back.2 = (f32[128,2048]{1,0:T(8,128)}, bf16[128,2048]{1,0:T(8,128)(2,1)}, f32[8,2048]{1,0:T(8,128)}, bf16[128,1792]{1,0:T(8,128)(2,1)}) custom-call(s32[8]{0:T(128)} %broadcast_xor_fusion.table, bf16[128,2048]{1,0:T(8,128)(2,1)} %reduce-scatter.9.cloned.1.call-done.d_feed, f32[128,2048]{1,0:T(8,128)} %get-tuple-element.195.hidden.hidden0, ...), custom_call_target="tpu_custom_call" | custom-call | flops 939524096 | bytes 12124160 | tf_op jit(solution)/shard_map/hidden_back/pallas_call | solution.py:87
  442.5 24.5 %attention_backward.2 = (bf16[128,1792]{1,0:T(8,128)(2,1)}, bf16[1024,896]{1,0:T(8,128)(2,1)}, bf16[1024,896]{1,0:T(8,128)(2,1)}, f32[8,128]{1,0:T(8,128)}) custom-call(bf16[8,1,128,896]{3,2,1,0:T(8,128)(2,1)} %bitcast.19.kv0, bf16[8,1,128,896]{3,2,1,0:T(8,128)(2,1)} %bitcast.20.kv1, bf16[256,1792]{1,0:T(8,128)(2,1)} %get-tuple-element.196.query, ...), custom_call_target="tpu_custom_call" | custom-call | flops 26306674688 | bytes 12798464 | tf_op jit(solution)/shard_map/attention_backward/pallas_call | solution.py:78
  468.0 8.9 %weight_grad.8 = bf16[1024,896]{1,0:T(8,128)(2,1)} custom-call(bf16[512,2048]{1,0:T(8,128)(2,1)} %collective-permute-done.34.refs_2_.refs_0_.refs_1_, bf16[512,2048]{1,0:T(8,128)(2,1)} %collective-permute-done.34.refs_2_.refs_0_.refs_1_, bf16[512,2048]{1,0:T(8,128)(2,1)} %bitcast.29.refs_3_.refs_2_, bf16[512,2048]{1,0:T(8,128)(2,1)} %bitcast.29.refs_3_.refs_2_, ...), custom_call_target="tpu_custom_call" | custom-call | flops 3758096384 | bytes 22282240 | tf_op jit(solution)/shard_map/weight_grad/pallas_call | solution.py:78
  481.5 9.8 %hidden_back.3 = (f32[128,2048]{1,0:T(8,128)}, bf16[128,2048]{1,0:T(8,128)(2,1)}, f32[8,2048]{1,0:T(8,128)}, bf16[128,1792]{1,0:T(8,128)(2,1)}) custom-call(s32[8]{0:T(128)} %broadcast_xor_fusion.table, bf16[128,2048]{1,0:T(8,128)(2,1)} %reduce-scatter.7.cloned.1.call-done.d_feed, f32[128,2048]{1,0:T(8,128)} %get-tuple-element.200.hidden.hidden1, ...), custom_call_target="tpu_custom_call" | custom-call | flops 939524096 | bytes 12124160 | tf_op jit(solution)/shard_map/hidden_back/pallas_call | solution.py:87
  498.5 3.8 collective-permute-done.46
  505.6 24.6 %attention_backward.3 = (bf16[128,1792]{1,0:T(8,128)(2,1)}, bf16[1024,896]{1,0:T(8,128)(2,1)}, bf16[1024,896]{1,0:T(8,128)(2,1)}, f32[8,128]{1,0:T(8,128)}) custom-call(bf16[8,1,128,896]{3,2,1,0:T(8,128)(2,1)} %bitcast.95, bf16[8,1,128,896]{3,2,1,0:T(8,128)(2,1)} %bitcast.97, bf16[256,1792]{1,0:T(8,128)(2,1)} %get-tuple-element.196.query, ...), custom_call_target="tpu_custom_call" | custom-call | flops 26306674688 | bytes 12798464 | tf_op jit(solution)/shard_map/attention_backward/pallas_call | solution.py:78
  542.2 3.6 add.320
  565.8 8.7 %query_back.1.d_normed_q = f32[256,2048]{1,0:T(8,128)} custom-call(bf16[256,1792]{1,0:T(8,128)(2,1)} %copy-done.12, bf16[256,1792]{1,0:T(8,128)(2,1)} %copy-done.13, bf16[256,1792]{1,0:T(8,128)(2,1)} %copy-done.29, bf16[256,1792]{1,0:T(8,128)(2,1)} %collective-permute-done.16.refs_2_, bf16[256,1792]{1,0:T(8,128)(2,1)} %collective-permute-done.17.refs_3_, ...), custom_call_target="tpu_custom_call" | custom-call | flops 1879048192 | bytes 10354688 | tf_op jit(solution)/shard_map/query_back/pallas_call | solution.py:78
  576.2 8.7 %weight_grad.9 = bf16[1024,768]{1,0:T(8,128)(2,1)} custom-call(bf16[512,2048]{1,0:T(8,128)(2,1)} %copy-done, bf16[512,2048]{1,0:T(8,128)(2,1)} %copy-done, bf16[512,2048]{1,0:T(8,128)(2,1)} %all-gather.13.cloned.1.call-done.refs_1_.refs_2_.refs_3_, bf16[512,2048]{1,0:T(8,128)(2,1)} %all-gather.13.cloned.1.call-done.refs_1_.refs_2_.refs_3_, ...), custom_call_target="tpu_custom_call" | custom-call | flops 3221225472 | bytes 25165824 | tf_op jit(solution)/shard_map/weight_grad/pallas_call | solution.py:78
  606.3 10.6 %input_back.1 = (bf16[256,896]{1,0:T(8,128)(2,1)}, f32[8,128]{1,0:T(8,128)}, f32[256,2048]{1,0:T(8,128)}, f32[8,2048]{1,0:T(8,128)}) custom-call(s32[8]{0:T(128)} %broadcast_xor_fusion.table, bf16[256,896]{1,0:T(8,128)(2,1)} %pad_maximum_fusion.8.d_pair, f32[256,896]{1,0:T(8,128)} %get-tuple-element.278.kv_raw, f32[256,128]{1,0:T(8,128)} %pad_maximum_fusion.9.cosine, ...), custom_call_target="tpu_custom_call" | custom-call | flops 939524096 | bytes 13767168 | tf_op jit(solution)/shard_map/input_back/pallas_call | solution.py:87
  620.1 4.6 key_value_grad.1
  624.6 3.7 add.321
  642.7 9.3 %weight_grad.10 = bf16[1024,896]{1,0:T(8,128)(2,1)} custom-call(bf16[512,2048]{1,0:T(8,128)(2,1)} %collective-permute-done.34.refs_2_.refs_0_.refs_1_, bf16[512,2048]{1,0:T(8,128)(2,1)} %collective-permute-done.34.refs_2_.refs_0_.refs_1_, bf16[512,2048]{1,0:T(8,128)(2,1)} %bitcast.29.refs_3_.refs_2_, bf16[512,2048]{1,0:T(8,128)(2,1)} %bitcast.29.refs_3_.refs_2_, ...), custom_call_target="tpu_custom_call" | custom-call | flops 3758096384 | bytes 22282240 | tf_op jit(solution)/shard_map/weight_grad/pallas_call | solution.py:78
  662.9 9.7 %weight_grad.11 = bf16[1024,896]{1,0:T(8,128)(2,1)} custom-call(bf16[512,2048]{1,0:T(8,128)(2,1)} %copy-done, bf16[512,2048]{1,0:T(8,128)(2,1)} %copy-done, bf16[512,2048]{1,0:T(8,128)(2,1)} %all-gather.13.cloned.1.call-done.refs_1_.refs_2_.refs_3_, bf16[512,2048]{1,0:T(8,128)(2,1)} %all-gather.13.cloned.1.call-done.refs_1_.refs_2_.refs_3_, ...), custom_call_target="tpu_custom_call" | custom-call | flops 3758096384 | bytes 25427968 | tf_op jit(solution)/shard_map/weight_grad/pallas_call | solution.py:78
  681.1 3.9 collective-permute-done.67
  699.2 9.4 %collective-permute-done.70 = bf16[256,1792]{1,0:T(8,128)(2,1)} collective-permute-done((bf16[256,1792]{1,0:T(8,128)(2,1)}, bf16[256,1792]{1,0:T(8,128)(2,1)}, u32[]{:S(2)}, u32[]{:S(2)}) %collective-permute-start.70) | collective-permute-done | bytes 917536 | tf_op jit(solution)/shard_map/ppermute | solution.py:872
  712.4 14.6 %collective-permute-done.78 = bf16[512,896]{1,0:T(8,128)(2,1)} collective-permute-done((bf16[512,896]{1,0:T(8,128)(2,1)}, bf16[512,896]{1,0:T(8,128)(2,1)}, u32[]{:S(2)}, u32[]{:S(2)}) %collective-permute-start.78) | collective-permute-done | bytes 917536 | tf_op jit(solution)/shard_map/ppermute | solution.py:872
  739.2 5.4 collective-permute-done.71
  744.6 6.7 collective-permute-done.72
  753.3 3.7 finish_layer.1
  (528 shorter events, 244.7 us)
Async XLA Ops:
  7.2 96.7 %all-gather.19.cloned.1.call-start = ((), (), s32[]{:S(2)}) async-start(), calls=%async_computation.17 | async-start | bytes 2293760 | tf_op jit(solution)/shard_map/all_gather | solution.py:996
  10.4 137.6 %all-gather.17.cloned.1.call-start = ((), (), s32[]{:S(2)}) async-start(), calls=%async_computation.16 | async-start | bytes 5242880 | tf_op jit(solution)/shard_map/all_gather | solution.py:1008
  23.9 174.1 %all-gather.9.cloned.1.call-start = ((), (), s32[]{:S(2)}) async-start(), calls=%async_computation.6 | async-start | bytes 2293760 | tf_op jit(solution)/shard_map/all_gather | solution.py:1076
  26.4 35.8 %collective-permute-start.4 = (bf16[128,1024]{1,0:T(8,128)(2,1)S(1)}, bf16[128,1024]{1,0:T(8,128)(2,1)}, u32[]{:S(2)}, u32[]{:S(2)}) collective-permute-start(bf16[128,1024]{1,0:T(8,128)(2,1)S(1)} %maximum_select_fusion.4), channel_id=1, source_target_pairs={{0,2},{1,3},{2,0},{3,1},{4,6},{5,7},{6,4},{7,5},{8,10},{9,11},{10,... | collective-permute-start | bytes 786440 | tf_op jit(solution)/shard_map/ppermute | solution.py:904
  42.3 33.5 %collective-permute-start.2 = (bf16[512,896]{1,0:T(8,128)(2,1)}, bf16[512,896]{1,0:T(8,128)(2,1)}, u32[]{:S(2)}, u32[]{:S(2)}) collective-permute-start(bf16[512,896]{1,0:T(8,128)(2,1)} %slice.761.refs_8_), channel_id=1, source_target_pairs={{0,16},{16,0},{1,17},{17,1},{2,18},{18,2},{3,19},{19,3},{4,20},{20... | collective-permute-start | bytes 2752520 | tf_op jit(solution)/shard_map/ppermute | solution.py:881
  43.5 32.4 %collective-permute-start.1 = (bf16[512,896]{1,0:T(8,128)(2,1)}, bf16[512,896]{1,0:T(8,128)(2,1)}, u32[]{:S(2)}, u32[]{:S(2)}) collective-permute-start(bf16[512,896]{1,0:T(8,128)(2,1)} %slice.761.refs_8_), channel_id=1, source_target_pairs={{0,8},{4,12},{8,0},{12,4},{1,9},{5,13},{9,1},{13,5},{2,10},{6,14},... | collective-permute-start | bytes 2752520 | tf_op jit(solution)/shard_map/ppermute | solution.py:872
  80.9 60.3 %collective-permute-start.14 = (bf16[512,1664]{1,0:T(8,128)(2,1)}, bf16[512,1664]{1,0:T(8,128)(2,1)}, u32[]{:S(2)}, u32[]{:S(2)}) collective-permute-start(bf16[512,1664]{1,0:T(8,128)(2,1)} %slice.777.refs_4_), channel_id=1, source_target_pairs={{0,16},{16,0},{1,17},{17,1},{2,18},{18,2},{3,19},{19,3},{4,20},{20... | collective-permute-start | bytes 5111816 | tf_op jit(solution)/shard_map/ppermute | solution.py:881
  89.6 51.7 %collective-permute-start.13 = (bf16[512,1664]{1,0:T(8,128)(2,1)}, bf16[512,1664]{1,0:T(8,128)(2,1)}, u32[]{:S(2)}, u32[]{:S(2)}) collective-permute-start(bf16[512,1664]{1,0:T(8,128)(2,1)} %slice.777.refs_4_), channel_id=1, source_target_pairs={{0,8},{4,12},{8,0},{12,4},{1,9},{5,13},{9,1},{13,5},{2,10},{6,14},... | collective-permute-start | bytes 5111816 | tf_op jit(solution)/shard_map/ppermute | solution.py:872
  103.3 36.1 %collective-permute-start.12 = (bf16[256,896]{1,0:T(8,128)(2,1)}, bf16[256,896]{1,0:T(8,128)(2,1)}, u32[]{:S(2)}, u32[]{:S(2)}) collective-permute-start(bf16[256,896]{1,0:T(8,128)(2,1)} %get-tuple-element.175), channel_id=1, source_target_pairs={{0,8},{4,12},{8,0},{12,4},{1,9},{5,13},{9,1},{13,5},{2,10},{6,14},... | collective-permute-start | bytes 1376264 | tf_op jit(solution)/shard_map/ppermute | solution.py:872
  108.5 41.7 %collective-permute-start.16 = (bf16[256,1792]{1,0:T(8,128)(2,1)}, bf16[256,1792]{1,0:T(8,128)(2,1)}, u32[]{:S(2)}, u32[]{:S(2)}) collective-permute-start(bf16[256,1792]{1,0:T(8,128)(2,1)} %copy.119), channel_id=1, source_target_pairs={{0,16},{16,0},{1,17},{17,1},{2,18},{18,2},{3,19},{19,3},{4,20},{20... | collective-permute-start | bytes 2752520 | tf_op jit(solution)/shard_map/ppermute | solution.py:881
  148.0 113.1 %all-gather.11.cloned.1.call-start = ((), (), s32[]{:S(2)}) async-start(), calls=%async_computation.7 | async-start | bytes 2293760 | tf_op jit(solution)/shard_map/all_gather | solution.py:1076
  148.6 22.4 %collective-permute-start.15 = (bf16[256,1792]{1,0:T(8,128)(2,1)}, bf16[256,1792]{1,0:T(8,128)(2,1)S(1)}, u32[]{:S(2)}, u32[]{:S(2)}) collective-permute-start(bf16[256,1792]{1,0:T(8,128)(2,1)} %copy.119), channel_id=1, source_target_pairs={{0,8},{4,12},{8,0},{12,4},{1,9},{5,13},{9,1},{13,5},{2,10},{6,14},... | collective-permute-start | bytes 2752520 | tf_op jit(solution)/shard_map/ppermute | solution.py:872
  174.1 23.9 %collective-permute-start.20 = (bf16[256,1792]{1,0:T(8,128)(2,1)}, bf16[256,1792]{1,0:T(8,128)(2,1)}, u32[]{:S(2)}, u32[]{:S(2)}) collective-permute-start(bf16[256,1792]{1,0:T(8,128)(2,1)} %collective-permute-done.16.refs_2_), channel_id=1, source_target_pairs={{0,4},{4,0},{8,12},{12,8},{1,5},{5,1},{9,13},{13,9},{2,6},{6,2},{1... | collective-permute-start | bytes 2752520 | tf_op jit(solution)/shard_map/ppermute | solution.py:878
  174.6 23.4 %collective-permute-start.19 = (bf16[256,1792]{1,0:T(8,128)(2,1)}, bf16[256,1792]{1,0:T(8,128)(2,1)}, u32[]{:S(2)}, u32[]{:S(2)}) collective-permute-start(bf16[256,1792]{1,0:T(8,128)(2,1)} %copy-done.29), channel_id=1, source_target_pairs={{0,4},{4,0},{8,12},{12,8},{1,5},{5,1},{9,13},{13,9},{2,6},{6,2},{1... | collective-permute-start | bytes 2752520 | tf_op jit(solution)/shard_map/ppermute | solution.py:878
  193.6 22.8 %collective-permute-start.23 = (bf16[256,1792]{1,0:T(8,128)(2,1)S(1)}, bf16[256,1792]{1,0:T(8,128)(2,1)S(1)}, u32[]{:S(2)}, u32[]{:S(2)}) collective-permute-start(bf16[256,1792]{1,0:T(8,128)(2,1)S(1)} %bitcast.61), channel_id=1, source_target_pairs={{0,16},{16,0},{1,17},{17,1},{2,18},{18,2},{3,19},{19,3},{4,20},{20... | collective-permute-start | bytes 2752520 | tf_op jit(solution)/shard_map/ppermute | solution.py:881
  195.9 22.5 %collective-permute-start.22 = (bf16[256,1792]{1,0:T(8,128)(2,1)S(1)}, bf16[256,1792]{1,0:T(8,128)(2,1)S(1)}, u32[]{:S(2)}, u32[]{:S(2)}) collective-permute-start(bf16[256,1792]{1,0:T(8,128)(2,1)S(1)} %bitcast.62), channel_id=1, source_target_pairs={{0,8},{4,12},{8,0},{12,4},{1,9},{5,13},{9,1},{13,5},{2,10},{6,14},... | collective-permute-start | bytes 2752520 | tf_op jit(solution)/shard_map/ppermute | solution.py:872
  219.5 91.3 %all-gather.13.cloned.1.call-start = ((), (), s32[]{:S(2)}) async-start(), calls=%async_computation.8 | async-start | bytes 2621440 | tf_op jit(solution)/shard_map/all_gather | solution.py:1097
  221.4 22.7 %collective-permute-start.25 = (bf16[256,1792]{1,0:T(8,128)(2,1)S(1)}, bf16[256,1792]{1,0:T(8,128)(2,1)S(1)}, u32[]{:S(2)}, u32[]{:S(2)}) collective-permute-start(bf16[256,1792]{1,0:T(8,128)(2,1)S(1)} %collective-permute-done.22.refs_1_), channel_id=1, source_target_pairs={{0,16},{16,0},{1,17},{17,1},{2,18},{18,2},{3,19},{19,3},{4,20},{20... | collective-permute-start | bytes 2752520 | tf_op jit(solution)/shard_map/ppermute | solution.py:881
  261.1 94.1 %all-gather.15.cloned.1.call-start = ((), (), s32[]{:S(2)}) async-start(), calls=%async_computation.9 | async-start | bytes 2621440 | tf_op jit(solution)/shard_map/all_gather | solution.py:1097
  261.4 39.8 %collective-permute-start.31 = (bf16[512,1664]{1,0:T(8,128)(2,1)}, bf16[512,1664]{1,0:T(8,128)(2,1)}, u32[]{:S(2)}, u32[]{:S(2)}) collective-permute-start(bf16[512,1664]{1,0:T(8,128)(2,1)} %collective-permute-done.13.refs_5_), channel_id=1, source_target_pairs={{0,16},{16,0},{1,17},{17,1},{2,18},{18,2},{3,19},{19,3},{4,20},{20... | collective-permute-start | bytes 5111816 | tf_op jit(solution)/shard_map/ppermute | solution.py:881
  262.0 22.5 %collective-permute-start.32 = (bf16[512,896]{1,0:T(8,128)(2,1)}, bf16[512,896]{1,0:T(8,128)(2,1)S(1)}, u32[]{:S(2)}, u32[]{:S(2)}) collective-permute-start(bf16[512,896]{1,0:T(8,128)(2,1)} %collective-permute-done.2.refs_10_), channel_id=1, source_target_pairs={{0,8},{4,12},{8,0},{12,4},{1,9},{5,13},{9,1},{13,5},{2,10},{6,14},... | collective-permute-start | bytes 2752520 | tf_op jit(solution)/shard_map/ppermute | solution.py:872
  268.2 42.9 %collective-permute-start.34 = (bf16[512,2048]{1,0:T(8,128)(2,1)}, bf16[512,2048]{1,0:T(8,128)(2,1)}, u32[]{:S(2)}, u32[]{:S(2)}) collective-permute-start(bf16[512,2048]{1,0:T(8,128)(2,1)} %bitcast.29.refs_3_.refs_2_), channel_id=1, source_target_pairs={{0,4},{4,0},{8,12},{12,8},{1,5},{5,1},{9,13},{13,9},{2,6},{6,2},{1... | collective-permute-start | bytes 6291464 | tf_op jit(solution)/shard_map/ppermute | solution.py:878
  310.9 121.0 %reduce-scatter.9.cloned.1.call-start = ((), (), s32[]{:S(2)}) async-start(), calls=%async_computation.11 | async-start | bytes 2621440 | tf_op jit(solution)/shard_map/reduce_scatter | solution.py:1121
  362.5 119.0 %reduce-scatter.7.cloned.1.call-start = ((), (), s32[]{:S(2)}) async-start(), calls=%async_computation.10 | async-start | bytes 2621440 | tf_op jit(solution)/shard_map/reduce_scatter | solution.py:1121
  401.9 27.8 %collective-permute-start.38 = (bf16[512,2048]{1,0:T(8,128)(2,1)}, bf16[512,2048]{1,0:T(8,128)(2,1)S(1)}, u32[]{:S(2)}, u32[]{:S(2)}) collective-permute-start(bf16[512,2048]{1,0:T(8,128)(2,1)} %get-tuple-element.217), channel_id=1, source_target_pairs={{0,4},{4,0},{8,12},{12,8},{1,5},{5,1},{9,13},{13,9},{2,6},{6,2},{1... | collective-permute-start | bytes 6291464 | tf_op jit(solution)/shard_map/ppermute | solution.py:878
  413.8 28.7 %collective-permute-start.40 = (bf16[384,896]{1,0:T(8,128)(2,1)}, bf16[384,896]{1,0:T(8,128)(2,1)}, u32[]{:S(2)}, u32[]{:S(2)}) collective-permute-start(bf16[384,896]{1,0:T(8,128)(2,1)} %slice.783), channel_id=1, source_target_pairs={{0,16},{16,0},{1,17},{17,1},{2,18},{18,2},{3,19},{19,3},{4,20},{20... | collective-permute-start | bytes 2064392 | tf_op jit(solution)/shard_map/ppermute | solution.py:881
  428.6 38.5 %collective-permute-start.42 = (bf16[640,896]{1,0:T(8,128)(2,1)S(1)}, bf16[640,896]{1,0:T(8,128)(2,1)S(1)}, u32[]{:S(2)}, u32[]{:S(2)}) collective-permute-start(bf16[640,896]{1,0:T(8,128)(2,1)S(1)} %slice.785), channel_id=1, source_target_pairs={{0,16},{16,0},{1,17},{17,1},{2,18},{18,2},{3,19},{19,3},{4,20},{20... | collective-permute-start | bytes 3440648 | tf_op jit(solution)/shard_map/ppermute | solution.py:881
  429.2 37.9 %collective-permute-start.43 = (bf16[640,768]{1,0:T(8,128)(2,1)}, bf16[640,768]{1,0:T(8,128)(2,1)S(1)}, u32[]{:S(2)}, u32[]{:S(2)}) collective-permute-start(bf16[640,768]{1,0:T(8,128)(2,1)} %slice.786), channel_id=1, source_target_pairs={{0,8},{4,12},{8,0},{12,4},{1,9},{5,13},{9,1},{13,5},{2,10},{6,14},... | collective-permute-start | bytes 2949128 | tf_op jit(solution)/shard_map/ppermute | solution.py:872
  431.8 103.7 %reduce-scatter.15.cloned.1.call-start = ((), (), s32[]{:S(2)}) async-start(), calls=%async_computation.14 | async-start | bytes 2293760 | tf_op jit(solution)/shard_map/reduce_scatter | solution.py:1226
  496.7 33.5 %collective-permute-start.47 = (bf16[640,896]{1,0:T(8,128)(2,1)}, bf16[640,896]{1,0:T(8,128)(2,1)}, u32[]{:S(2)}, u32[]{:S(2)}) collective-permute-start(bf16[640,896]{1,0:T(8,128)(2,1)} %slice.790), channel_id=1, source_target_pairs={{0,8},{4,12},{8,0},{12,4},{1,9},{5,13},{9,1},{13,5},{2,10},{6,14},... | collective-permute-start | bytes 3440648 | tf_op jit(solution)/shard_map/ppermute | solution.py:872
  497.3 92.6 %reduce-scatter.17.cloned.1.call-start = ((), (), s32[]{:S(2)}) async-start(), calls=%async_computation.15 | async-start | bytes 2293760 | tf_op jit(solution)/shard_map/reduce_scatter | solution.py:1226
  504.1 26.1 %collective-permute-start.48 = (bf16[256,1792]{1,0:T(8,128)(2,1)S(1)}, bf16[256,1792]{1,0:T(8,128)(2,1)S(1)}, u32[]{:S(2)}, u32[]{:S(2)}) collective-permute-start(bf16[256,1792]{1,0:T(8,128)(2,1)S(1)} %slice.791), channel_id=1, source_target_pairs={{0,16},{16,0},{1,17},{17,1},{2,18},{18,2},{3,19},{19,3},{4,20},{20... | collective-permute-start | bytes 2752520 | tf_op jit(solution)/shard_map/ppermute | solution.py:881
  552.0 201.3 %reduce-scatter.11.cloned.1.call-start = ((), (), s32[]{:S(2)}) async-start(), calls=%async_computation.12 | async-start | bytes 2621440 | tf_op jit(solution)/shard_map/reduce_scatter | solution.py:1356
  552.2 72.5 %collective-permute-start.50 = (bf16[512,2048]{1,0:T(8,128)(2,1)}, bf16[512,2048]{1,0:T(8,128)(2,1)}, u32[]{:S(2)}, u32[]{:S(2)}) collective-permute-start(bf16[512,2048]{1,0:T(8,128)(2,1)} %get-tuple-element.263), channel_id=1, source_target_pairs={{0,4},{4,0},{8,12},{12,8},{1,5},{5,1},{9,13},{13,9},{2,6},{6,2},{1... | collective-permute-start | bytes 6291464 | tf_op jit(solution)/shard_map/ppermute | solution.py:878
  593.9 159.5 %reduce-scatter.13.cloned.1.call-start = ((), (), s32[]{:S(2)}) async-start(), calls=%async_computation.13 | async-start | bytes 2621440 | tf_op jit(solution)/shard_map/reduce_scatter | solution.py:1356
  594.3 22.6 %collective-permute-start.60 = (bf16[320,768]{1,0:T(8,128)(2,1)S(1)}, bf16[320,768]{1,0:T(8,128)(2,1)}, u32[]{:S(2)}, u32[]{:S(2)}) collective-permute-start(bf16[320,768]{1,0:T(8,128)(2,1)S(1)} %slice.802), channel_id=1, source_target_pairs={{0,16},{16,0},{1,17},{17,1},{2,18},{18,2},{3,19},{19,3},{4,20},{20... | collective-permute-start | bytes 1474568 | tf_op jit(solution)/shard_map/ppermute | solution.py:881
  629.9 22.1 %collective-permute-start.63 = (bf16[128,1792]{1,0:T(8,128)(2,1)}, bf16[128,1792]{1,0:T(8,128)(2,1)S(1)}, u32[]{:S(2)}, u32[]{:S(2)}) collective-permute-start(bf16[128,1792]{1,0:T(8,128)(2,1)} %get-tuple-element.421), channel_id=1, source_target_pairs={{0,8},{4,12},{8,0},{12,4},{1,9},{5,13},{9,1},{13,5},{2,10},{6,14},... | collective-permute-start | bytes 1376264 | tf_op jit(solution)/shard_map/ppermute | solution.py:872
  639.1 33.5 %collective-permute-start.66 = (bf16[256,1024]{1,0:T(8,128)(2,1)S(1)}, bf16[256,1024]{1,0:T(8,128)(2,1)S(1)}, u32[]{:S(2)}, u32[]{:S(2)}) collective-permute-start(bf16[256,1024]{1,0:T(8,128)(2,1)S(1)} %get-tuple-element.390), channel_id=1, source_target_pairs={{0,24},{4,28},{8,16},{12,20},{16,8},{20,12},{24,0},{28,4},{1,25},{... | collective-permute-start | bytes 1572872 | tf_op jit(solution)/shard_map/ppermute | solution.py:875
  639.8 32.8 %collective-permute-start.65 = (bf16[256,1024]{1,0:T(8,128)(2,1)S(1)}, bf16[256,1024]{1,0:T(8,128)(2,1)S(1)}, u32[]{:S(2)}, u32[]{:S(2)}) collective-permute-start(bf16[256,1024]{1,0:T(8,128)(2,1)S(1)} %get-tuple-element.391), channel_id=1, source_target_pairs={{0,16},{16,0},{1,17},{17,1},{2,18},{18,2},{3,19},{19,3},{4,20},{20... | collective-permute-start | bytes 1572872 | tf_op jit(solution)/shard_map/ppermute | solution.py:881
  641.2 31.4 %collective-permute-start.64 = (bf16[256,1024]{1,0:T(8,128)(2,1)S(1)}, bf16[256,1024]{1,0:T(8,128)(2,1)S(1)}, u32[]{:S(2)}, u32[]{:S(2)}) collective-permute-start(bf16[256,1024]{1,0:T(8,128)(2,1)S(1)} %get-tuple-element.392), channel_id=1, source_target_pairs={{0,8},{4,12},{8,0},{12,4},{1,9},{5,13},{9,1},{13,5},{2,10},{6,14},... | collective-permute-start | bytes 1572872 | tf_op jit(solution)/shard_map/ppermute | solution.py:872
  660.9 33.7 %collective-permute-start.74 = (bf16[256,1792]{1,0:T(8,128)(2,1)}, bf16[256,1792]{1,0:T(8,128)(2,1)}, u32[]{:S(2)}, u32[]{:S(2)}) collective-permute-start(bf16[256,1792]{1,0:T(8,128)(2,1)} %slice.818), channel_id=1, source_target_pairs={{0,16},{16,0},{1,17},{17,1},{2,18},{18,2},{3,19},{19,3},{4,20},{20... | collective-permute-start | bytes 2752520 | tf_op jit(solution)/shard_map/ppermute | solution.py:881
  661.4 51.0 %collective-permute-start.79 = (bf16[512,896]{1,0:T(8,128)(2,1)}, bf16[512,896]{1,0:T(8,128)(2,1)}, u32[]{:S(2)}, u32[]{:S(2)}) collective-permute-start(bf16[512,896]{1,0:T(8,128)(2,1)} %slice.828), channel_id=1, source_target_pairs={{0,16},{16,0},{1,17},{17,1},{2,18},{18,2},{3,19},{19,3},{4,20},{20... | collective-permute-start | bytes 2752520 | tf_op jit(solution)/shard_map/ppermute | solution.py:881
  685.0 23.6 %collective-permute-start.70 = (bf16[256,1792]{1,0:T(8,128)(2,1)}, bf16[256,1792]{1,0:T(8,128)(2,1)}, u32[]{:S(2)}, u32[]{:S(2)}) collective-permute-start(bf16[256,1792]{1,0:T(8,128)(2,1)} %slice.820), channel_id=1, source_target_pairs={{0,8},{4,12},{8,0},{12,4},{1,9},{5,13},{9,1},{13,5},{2,10},{6,14},... | collective-permute-start | bytes 2752520 | tf_op jit(solution)/shard_map/ppermute | solution.py:872
  685.8 41.2 %collective-permute-start.78 = (bf16[512,896]{1,0:T(8,128)(2,1)}, bf16[512,896]{1,0:T(8,128)(2,1)}, u32[]{:S(2)}, u32[]{:S(2)}) collective-permute-start(bf16[512,896]{1,0:T(8,128)(2,1)} %slice.827), channel_id=1, source_target_pairs={{0,8},{4,12},{8,0},{12,4},{1,9},{5,13},{9,1},{13,5},{2,10},{6,14},... | collective-permute-start | bytes 2752520 | tf_op jit(solution)/shard_map/ppermute | solution.py:872
  696.2 35.5 %collective-permute-start.75 = (bf16[256,448]{1,0:T(8,128)(2,1)S(1)}, bf16[256,448]{1,0:T(8,128)(2,1)S(1)}, u32[]{:S(2)}, u32[]{:S(2)}) collective-permute-start(bf16[256,448]{1,0:T(8,128)(2,1)S(1)} %get-tuple-element.415), channel_id=1, source_target_pairs={{0,1},{1,0},{2,3},{3,2},{4,5},{5,4},{6,7},{7,6},{8,9},{9,8},{10,11... | collective-permute-start | bytes 688136 | tf_op jit(solution)/shard_map/ppermute | solution.py:888
  698.3 36.2 %collective-permute-start.76 = (bf16[256,448]{1,0:T(8,128)(2,1)S(1)}, bf16[256,448]{1,0:T(8,128)(2,1)S(1)}, u32[]{:S(2)}, u32[]{:S(2)}) collective-permute-start(bf16[256,448]{1,0:T(8,128)(2,1)S(1)} %get-tuple-element.416), channel_id=1, source_target_pairs={{0,2},{1,3},{2,0},{3,1},{4,6},{5,7},{6,4},{7,5},{8,10},{9,11},{10,... | collective-permute-start | bytes 688136 | tf_op jit(solution)/shard_map/ppermute | solution.py:888
  708.6 27.6 %collective-permute-start.77 = (bf16[256,448]{1,0:T(8,128)(2,1)S(1)}, bf16[256,448]{1,0:T(8,128)(2,1)S(1)}, u32[]{:S(2)}, u32[]{:S(2)}) collective-permute-start(bf16[256,448]{1,0:T(8,128)(2,1)S(1)} %get-tuple-element.417), channel_id=1, source_target_pairs={{0,3},{1,2},{2,1},{3,0},{4,7},{5,6},{6,5},{7,4},{8,11},{9,10},{10,... | collective-permute-start | bytes 688136 | tf_op jit(solution)/shard_map/ppermute | solution.py:888
  730.8 26.4 %collective-permute-start.80 = (bf16[256,2560]{1,0:T(8,128)(2,1)}, bf16[256,2560]{1,0:T(8,128)(2,1)}, u32[]{:S(2)}, u32[]{:S(2)}) collective-permute-start(bf16[256,2560]{1,0:T(8,128)(2,1)} %pad_maximum_fusion.2), channel_id=1, source_target_pairs={{0,4},{4,0},{8,12},{12,8},{1,5},{5,1},{9,13},{13,9},{2,6},{6,2},{1... | collective-permute-start | bytes 3932168 | tf_op jit(solution)/shard_map/ppermute | solution.py:878
  (121 other events, 1180.3 us)
Sparse Core Ops, SparseCore 0:
  10.5 55.4 all-gather.18
  68.2 79.7 all-gather.16
  150.1 39.9 all-gather.8
  219.6 39.4 all-gather.10
  261.2 44.7 all-gather.12
  311.0 44.0 all-gather.14
  362.7 42.4 reduce-scatter.8
  432.0 42.9 reduce-scatter.6
  497.4 38.0 reduce-scatter.14
  552.1 37.6 reduce-scatter.16
  594.0 42.0 reduce-scatter.10
  638.4 46.9 reduce-scatter.12

commit v5 on v4

--- a/solution.py
+++ b/solution.py
@@ -880,13 +880,16 @@
     def swap_y(v):
         return lax.ppermute(v, "dp", [(0, 1), (1, 0)])
 
-    def line_scatter(v, axis):
+    def line_sends(v, axis):
         cut = jnp.split(v, 4, axis=axis)
-        total = lax.select_n(z, *cut)
+        got = []
         for k in range(1, 4):
             block = lax.select_n(z, *[cut[i ^ k] for i in range(4)])
-            total = total + lax.ppermute(block, "heads", [(i, i ^ k) for i in range(4)])
-        return total
+            got.append(lax.ppermute(block, "heads", [(i, i ^ k) for i in range(4)]))
+        return lax.select_n(z, *cut), got
+
+    def line_sum(own_block, got):
+        return own_block + got[0] + got[1] + got[2]
 
     def gather_near(v):
         if not paired:
@@ -1314,9 +1317,14 @@
         first_half = first_half + jnp.concatenate(first_parts, axis=0)
         first_last = swap_x(after(first_half[2 * BLOCK :], g_kv))
         down_last = swap_y(after(half[2 * BLOCK :], q_send))
-        g_o = o_keep + after(o_got, first_half)
+        kv_own, kv_got = line_sends(g_kv, 0)
+        g_o = o_keep + after(o_got, first_half, kv_got)
         g_q = q_keep + after(q_got, first_half)
-        first_last, down_last = after((first_last, down_last), g_o, g_q)
+        o_own, o_got = line_sends(g_o, 0)
+        q_own, q_got = line_sends(g_q, 1)
+        o_got, q_got[:2] = beside(o_got, q_got[:2])
+        o_final = line_sum(o_own, o_got)
+        first_last, down_last = after((first_last, down_last), o_final)
         second_got = jnp.concatenate(second_last, axis=0)
         g_gate_up = jnp.concatenate(
             [first_half[: 2 * BLOCK] + first_last, second_half[: 2 * BLOCK] + second_got], axis=1
@@ -1325,9 +1333,12 @@
     else:
         kv_send = kv_grads[0] + swap_core(kv_grads[1])
         g_o, g_q, g_kv = (fold_whole(v) for v in (o_send, q_send, kv_send))
-    g_kv = line_scatter(g_kv, 0).astype(F32)
-    grad_output = line_scatter(g_o, 0).astype(F32).T
-    grad_query = line_scatter(g_q, 1).astype(F32)
+        kv_own, kv_got = line_sends(g_kv, 0)
+        q_own, q_got = line_sends(g_q, 1)
+        o_final = line_sum(*line_sends(g_o, 0))
+    g_kv = line_sum(kv_own, kv_got).astype(F32)
+    grad_output = o_final.astype(F32).T
+    grad_query = line_sum(q_own, q_got).astype(F32)
     part_rows = g_down.shape[0] // 2
     g_ffn = jnp.concatenate([g_gate_up, g_down], axis=1)
     g_keep = g_ffn[:part_rows]
@@ -1355,7 +1366,7 @@
     added = [
         lax.psum_scatter(after(v, last_kv), "heads", scatter_dimension=0, tiled=True) for v in added
     ]
-    added = after(added, (g_kv, grad_output))
+    added = after(added, g_o, g_q)
     layer_out = finish_layer(table, *hiddens, *added)
 
     return (

time: 780 us -> 766 us (0.982)
    ppermute x22, waiting for transfers between devices: 106 us -> 82.3 us  [swap_x(): return lax.ppermute(v, 'seq', [(i, i ^ 2) for i in range(4)])]
    ppermute x9, waiting for transfers between devices: 18.3 us -> 31.6 us  [line_sends(): got.append(lax.ppermute(block, 'heads', [(i, i ^ k) for i in range(4)]))]
    ppermute x18, waiting for transfers between devices: 49 us -> 57.3 us  [swap_y(): return lax.ppermute(v, 'dp', [(0, 1), (1, 0)])]
    unnamed x172 -> x174, local copies, waits for them, and re-layouts: 27.5 us -> 24.2 us
  transfers between devices with their start and end apart: 93 -> 93, of which waited for: 37 -> 39; matrix products, arithmetic and copies ran while one was open for 18% -> 18% of each run, Pallas kernels for 36% -> 37%
where the time goes in v5:
time: 766 us; the launch traced here: 760 us
  Pallas kernels  281 us (37%)
  waiting for transfers between devices  224 us (29%)
  local copies, waits for them, and re-layouts  81.6 us (11%)
  other arithmetic  73.7 us (10%)
  starting transfers between devices  73.4 us (10%)
  between operations  15.9 us (2%)
  matrix products  10.3 us (1%)
    pallas_call x15, Pallas kernels, call(): pl.pallas_call(body, grid=grid, in_specs=in_specs, out_specs=out_specs, s...  217 us
    ppermute x22, waiting for transfers between devices, swap_x(): return lax.ppermute(v, 'seq', [(i, i ^ 2) for i in range(4)])  82.3 us
    pallas_call x8, Pallas kernels, call(): pl.pallas_call(body, grid_spec=pltpu.PrefetchScalarGridSpec(num_scalar_pr...  64 us
    ppermute x18, waiting for transfers between devices, swap_y(): return lax.ppermute(v, 'dp', [(0, 1), (1, 0)])  57.3 us
    ppermute x9, waiting for transfers between devices, line_sends(): got.append(lax.ppermute(block, 'heads', [(i, i ^ k) for i in range(4)]))  31.6 us
    ppermute x22, starting transfers between devices, swap_x(): return lax.ppermute(v, 'seq', [(i, i ^ 2) for i in range(4)])  25.9 us
    unnamed x174, local copies, waits for them, and re-layouts  24.2 us
    ppermute x18, starting transfers between devices, swap_y(): return lax.ppermute(v, 'dp', [(0, 1), (1, 0)])  21.5 us
  transfers between devices with their start and end apart: 93, of which 39 were waited for; matrix products, arithmetic and copies ran while one was open for 18% of the time, Pallas kernels for 37%

profile of v5, /device:TPU:0, one launch (start us, length us, event | category | flops | bytes accessed | tf_op | source)
XLA Modules:
  0.0 760.3 jit_solution(4011790278507843317)
XLA Ops:
  26.4 8.3 %collective-permute-start.4 = (bf16[128,1024]{1,0:T(8,128)(2,1)S(1)}, bf16[128,1024]{1,0:T(8,128)(2,1)}, u32[]{:S(2)}, u32[]{:S(2)}) collective-permute-start(bf16[128,1024]{1,0:T(8,128)(2,1)S(1)} %maximum_select_fusion.4), channel_id=1, source_target_pairs={{0,2},{1,3},{2,0},{3,1},{4,6},{5,7},{6,4},{7,5},{8,10},{9,11},{10,... | collective-permute-start | bytes 786440 | tf_op jit(solution)/shard_map/ppermute | solution.py:907
  35.8 5.5 fusion.4
  45.4 16.8 %collective-permute-done.4 = bf16[128,1024]{1,0:T(8,128)(2,1)} collective-permute-done((bf16[128,1024]{1,0:T(8,128)(2,1)S(1)}, bf16[128,1024]{1,0:T(8,128)(2,1)}, u32[]{:S(2)}, u32[]{:S(2)}) %collective-permute-start.4) | collective-permute-done | bytes 262176 | tf_op jit(solution)/shard_map/ppermute | solution.py:907
  66.5 7.9 %collective-permute-done.6.refs_2_ = bf16[256,1024]{1,0:T(8,128)(2,1)S(1)} collective-permute-done((bf16[256,1024]{1,0:T(8,128)(2,1)S(1)}, bf16[256,1024]{1,0:T(8,128)(2,1)S(1)}, u32[]{:S(2)}, u32[]{:S(2)}) %collective-permute-start.6) | collective-permute-done | bytes 524320 | tf_op jit(solution)/shard_map/ppermute | solution.py:881
  83.5 5.0 collective-permute-done.7.refs_3_
  96.0 7.3 project_key_value.1
  110.0 29.4 %collective-permute-done.12 = bf16[256,896]{1,0:T(8,128)(2,1)} collective-permute-done((bf16[256,896]{1,0:T(8,128)(2,1)}, bf16[256,896]{1,0:T(8,128)(2,1)}, u32[]{:S(2)}, u32[]{:S(2)}) %collective-permute-start.12) | collective-permute-done | bytes 458784 | tf_op jit(solution)/shard_map/ppermute | solution.py:872
  141.3 6.7 all-gather.17.cloned.1.call-done
  150.1 20.8 %collective-permute-done.15.refs_1_ = bf16[256,1792]{1,0:T(8,128)(2,1)S(1)} collective-permute-done((bf16[256,1792]{1,0:T(8,128)(2,1)}, bf16[256,1792]{1,0:T(8,128)(2,1)S(1)}, u32[]{:S(2)}, u32[]{:S(2)}) %collective-permute-start.15) | collective-permute-done | bytes 917536 | tf_op jit(solution)/shard_map/ppermute | solution.py:872
  174.6 18.9 %collective-permute-done.17.refs_3_ = bf16[256,1792]{1,0:T(8,128)(2,1)} collective-permute-done((bf16[256,1792]{1,0:T(8,128)(2,1)}, bf16[256,1792]{1,0:T(8,128)(2,1)}, u32[]{:S(2)}, u32[]{:S(2)}) %collective-permute-start.17) | collective-permute-done | bytes 917536 | tf_op jit(solution)/shard_map/ppermute | solution.py:872
  198.0 9.5 %project_query.1 = (f32[256,1792]{1,0:T(8,128)}, bf16[256,1792]{1,0:T(8,128)(2,1)}) custom-call(bf16[256,2048]{1,0:T(8,128)(2,1)} %get-tuple-element.271.normed, f32[256,128]{1,0:T(8,128)} %pad_maximum_fusion.9.cosine, f32[256,128]{1,0:T(8,128)} %pad_maximum_fusion.10.sine, f32[1,128]{1,0:T(1,128)} %pad_maximum_fusion.14.gain, bf16[256,1792]{1,0:T(8,128)(2,1)} %copy-done.13, ...), custom_call_target="tpu_custom_call" | custom-call | flops 1879048192 | bytes 11403776 | tf_op jit(solution)/shard_map/project_query/pallas_call | solution.py:78
  207.4 8.8 %collective-permute-done.23.refs_2_ = bf16[256,1792]{1,0:T(8,128)(2,1)S(1)} collective-permute-done((bf16[256,1792]{1,0:T(8,128)(2,1)S(1)}, bf16[256,1792]{1,0:T(8,128)(2,1)S(1)}, u32[]{:S(2)}, u32[]{:S(2)}) %collective-permute-start.23) | collective-permute-done | bytes 917536 | tf_op jit(solution)/shard_map/ppermute | solution.py:881
  222.5 11.0 %attention_forward.2 = (bf16[128,1792]{1,0:T(8,128)(2,1)}, f32[7,1,512]{2,1,0:T(1,128)}) custom-call(bf16[8,1,128,896]{3,2,1,0:T(8,128)(2,1)} %bitcast.19.kv0, bf16[8,1,128,896]{3,2,1,0:T(8,128)(2,1)} %bitcast.20.kv1, bf16[256,1792]{1,0:T(8,128)(2,1)} %get-tuple-element.201.query, f32[1024,128]{1,0:T(8,128)} %get-tuple-element.455.bias0, ...), custom_call_target="tpu_custom_call" | custom-call | flops 11274289152 | bytes 6109184 | tf_op jit(solution)/shard_map/attention_forward/pallas_call | solution.py:78
  233.5 10.5 %collective-permute-done.25.refs_3_ = bf16[256,1792]{1,0:T(8,128)(2,1)S(1)} collective-permute-done((bf16[256,1792]{1,0:T(8,128)(2,1)S(1)}, bf16[256,1792]{1,0:T(8,128)(2,1)S(1)}, u32[]{:S(2)}, u32[]{:S(2)}) %collective-permute-start.25) | collective-permute-done | bytes 917536 | tf_op jit(solution)/shard_map/ppermute | solution.py:881
  251.4 9.6 %project_output.2 = (f32[128,2048]{1,0:T(8,128)}, bf16[128,2048]{1,0:T(8,128)(2,1)}) custom-call(s32[8]{0:T(128)} %broadcast_xor_fusion.table, bf16[128,1792]{1,0:T(8,128)(2,1)} %get-tuple-element.191.mixed, bf16[256,2048]{1,0:T(8,128)(2,1)} %bitcast.69, f32[8,2048]{1,0:T(8,128)} %get-tuple-element.192.gains, bf16[256,1792]{1,0:T(8,128)(2,1)} %bitcast.64, ...), custom_call_target="tpu_custom_call" | custom-call | flops 939524096 | bytes 10485760 | tf_op jit(solution)/shard_map/project_output/pallas_call | solution.py:87
  263.4 4.9 fusion.28
  269.5 11.0 %attention_forward.3 = (bf16[128,1792]{1,0:T(8,128)(2,1)}, f32[7,1,512]{2,1,0:T(1,128)}) custom-call(bf16[8,1,128,896]{3,2,1,0:T(8,128)(2,1)} %bitcast.94, bf16[8,1,128,896]{3,2,1,0:T(8,128)(2,1)} %bitcast.96, bf16[256,1792]{1,0:T(8,128)(2,1)} %get-tuple-element.201.query, f32[1024,128]{1,0:T(8,128)} %get-tuple-element.454.bias0, ...), custom_call_target="tpu_custom_call" | custom-call | flops 11274289152 | bytes 6109184 | tf_op jit(solution)/shard_map/attention_forward/pallas_call | solution.py:78
  280.5 4.0 collective-permute-done.32.refs_11_
  284.5 16.6 %collective-permute-done.31.refs_7_ = bf16[512,1664]{1,0:T(8,128)(2,1)} collective-permute-done((bf16[512,1664]{1,0:T(8,128)(2,1)}, bf16[512,1664]{1,0:T(8,128)(2,1)}, u32[]{:S(2)}, u32[]{:S(2)}) %collective-permute-start.31) | collective-permute-done | bytes 1703968 | tf_op jit(solution)/shard_map/ppermute | solution.py:881
  301.1 9.6 %project_output.3 = (f32[128,2048]{1,0:T(8,128)}, bf16[128,2048]{1,0:T(8,128)(2,1)}) custom-call(s32[8]{0:T(128)} %broadcast_xor_fusion.table, bf16[128,1792]{1,0:T(8,128)(2,1)} %get-tuple-element.204.mixed, bf16[256,2048]{1,0:T(8,128)(2,1)} %bitcast.70, f32[8,2048]{1,0:T(8,128)} %get-tuple-element.192.gains, bf16[256,1792]{1,0:T(8,128)(2,1)} %bitcast.65, ...), custom_call_target="tpu_custom_call" | custom-call | flops 939524096 | bytes 10485760 | tf_op jit(solution)/shard_map/project_output/pallas_call | solution.py:87
  311.1 4.1 collective-permute-done.33.refs_0_.refs_1_
  316.5 34.2 %feed_forward.2 = (bf16[1024,896]{1,0:T(8,128)(2,1)}, bf16[1024,1664]{1,0:T(8,128)(2,1)}, bf16[512,2048]{1,0:T(8,128)(2,1)}, bf16[512,2048]{1,0:T(8,128)(2,1)}, ...) custom-call(bf16[512,2048]{1,0:T(8,128)(2,1)} %copy-done, ...), custom_call_target="tpu_custom_call" | custom-call | flops 20132659200 | bytes 32505856 | tf_op jit(solution)/shard_map/feed_forward/pallas_call | solution.py:78
  350.9 4.3 all-gather.15.cloned.1.call-done.refs_1_.refs_6_.refs_7_
  355.7 4.4 add.317
  362.7 5.0 add.315
  367.7 34.2 %feed_forward.3 = (bf16[1024,896]{1,0:T(8,128)(2,1)}, bf16[1024,1664]{1,0:T(8,128)(2,1)}, bf16[512,2048]{1,0:T(8,128)(2,1)}, bf16[512,2048]{1,0:T(8,128)(2,1)}, ...) custom-call(bf16[512,2048]{1,0:T(8,128)(2,1)} %copy-done.1, ...), custom_call_target="tpu_custom_call" | custom-call | flops 20132659200 | bytes 32505856 | tf_op jit(solution)/shard_map/feed_forward/pallas_call | solution.py:78
  402.2 9.7 %weight_grad.6 = bf16[1024,896]{1,0:T(8,128)(2,1)} custom-call(bf16[512,2048]{1,0:T(8,128)(2,1)} %copy-done, bf16[512,2048]{1,0:T(8,128)(2,1)} %copy-done, bf16[512,2048]{1,0:T(8,128)(2,1)} %all-gather.13.cloned.1.call-done.refs_1_.refs_2_.refs_3_, bf16[512,2048]{1,0:T(8,128)(2,1)} %all-gather.13.cloned.1.call-done.refs_1_.refs_2_.refs_3_, ...), custom_call_target="tpu_custom_call" | custom-call | flops 3758096384 | bytes 25427968 | tf_op jit(solution)/shard_map/weight_grad/pallas_call | solution.py:78
  415.4 8.7 %weight_grad.7 = bf16[1024,768]{1,0:T(8,128)(2,1)} custom-call(bf16[512,2048]{1,0:T(8,128)(2,1)} %copy-done, bf16[512,2048]{1,0:T(8,128)(2,1)} %copy-done, bf16[512,2048]{1,0:T(8,128)(2,1)} %all-gather.13.cloned.1.call-done.refs_1_.refs_2_.refs_3_, bf16[512,2048]{1,0:T(8,128)(2,1)} %all-gather.13.cloned.1.call-done.refs_1_.refs_2_.refs_3_, ...), custom_call_target="tpu_custom_call" | custom-call | flops 3221225472 | bytes 25165824 | tf_op jit(solution)/shard_map/weight_grad/pallas_call | solution.py:78
  432.0 10.4 %hidden_back.2 = (f32[128,2048]{1,0:T(8,128)}, bf16[128,2048]{1,0:T(8,128)(2,1)}, f32[8,2048]{1,0:T(8,128)}, bf16[128,1792]{1,0:T(8,128)(2,1)}) custom-call(s32[8]{0:T(128)} %broadcast_xor_fusion.table, bf16[128,2048]{1,0:T(8,128)(2,1)} %reduce-scatter.9.cloned.1.call-done.d_feed, f32[128,2048]{1,0:T(8,128)} %get-tuple-element.200.hidden.hidden0, ...), custom_call_target="tpu_custom_call" | custom-call | flops 939524096 | bytes 12124160 | tf_op jit(solution)/shard_map/hidden_back/pallas_call | solution.py:87
  442.6 24.6 %attention_backward.2 = (bf16[128,1792]{1,0:T(8,128)(2,1)}, bf16[1024,896]{1,0:T(8,128)(2,1)}, bf16[1024,896]{1,0:T(8,128)(2,1)}, f32[8,128]{1,0:T(8,128)}) custom-call(bf16[8,1,128,896]{3,2,1,0:T(8,128)(2,1)} %bitcast.19.kv0, bf16[8,1,128,896]{3,2,1,0:T(8,128)(2,1)} %bitcast.20.kv1, bf16[256,1792]{1,0:T(8,128)(2,1)} %get-tuple-element.201.query, ...), custom_call_target="tpu_custom_call" | custom-call | flops 26306674688 | bytes 12798464 | tf_op jit(solution)/shard_map/attention_backward/pallas_call | solution.py:78
  468.2 8.8 %weight_grad.8 = bf16[1024,896]{1,0:T(8,128)(2,1)} custom-call(bf16[512,2048]{1,0:T(8,128)(2,1)} %collective-permute-done.34.refs_2_.refs_0_.refs_1_, bf16[512,2048]{1,0:T(8,128)(2,1)} %collective-permute-done.34.refs_2_.refs_0_.refs_1_, bf16[512,2048]{1,0:T(8,128)(2,1)} %bitcast.29.refs_3_.refs_2_, bf16[512,2048]{1,0:T(8,128)(2,1)} %bitcast.29.refs_3_.refs_2_, ...), custom_call_target="tpu_custom_call" | custom-call | flops 3758096384 | bytes 22282240 | tf_op jit(solution)/shard_map/weight_grad/pallas_call | solution.py:78
  481.6 9.8 %hidden_back.3 = (f32[128,2048]{1,0:T(8,128)}, bf16[128,2048]{1,0:T(8,128)(2,1)}, f32[8,2048]{1,0:T(8,128)}, bf16[128,1792]{1,0:T(8,128)(2,1)}) custom-call(s32[8]{0:T(128)} %broadcast_xor_fusion.table, bf16[128,2048]{1,0:T(8,128)(2,1)} %reduce-scatter.7.cloned.1.call-done.d_feed, f32[128,2048]{1,0:T(8,128)} %get-tuple-element.205.hidden.hidden1, ...), custom_call_target="tpu_custom_call" | custom-call | flops 939524096 | bytes 12124160 | tf_op jit(solution)/shard_map/hidden_back/pallas_call | solution.py:87
  498.6 3.8 collective-permute-done.46
  505.7 24.6 %attention_backward.3 = (bf16[128,1792]{1,0:T(8,128)(2,1)}, bf16[1024,896]{1,0:T(8,128)(2,1)}, bf16[1024,896]{1,0:T(8,128)(2,1)}, f32[8,128]{1,0:T(8,128)}) custom-call(bf16[8,1,128,896]{3,2,1,0:T(8,128)(2,1)} %bitcast.95, bf16[8,1,128,896]{3,2,1,0:T(8,128)(2,1)} %bitcast.97, bf16[256,1792]{1,0:T(8,128)(2,1)} %get-tuple-element.201.query, ...), custom_call_target="tpu_custom_call" | custom-call | flops 26306674688 | bytes 12798464 | tf_op jit(solution)/shard_map/attention_backward/pallas_call | solution.py:78
  542.3 3.6 add.320
  565.8 8.7 %query_back.1.d_normed_q = f32[256,2048]{1,0:T(8,128)} custom-call(bf16[256,1792]{1,0:T(8,128)(2,1)} %copy-done.12, bf16[256,1792]{1,0:T(8,128)(2,1)} %copy-done.13, bf16[256,1792]{1,0:T(8,128)(2,1)} %copy-done.25, bf16[256,1792]{1,0:T(8,128)(2,1)} %collective-permute-done.16.refs_2_, bf16[256,1792]{1,0:T(8,128)(2,1)} %collective-permute-done.17.refs_3_, ...), custom_call_target="tpu_custom_call" | custom-call | flops 1879048192 | bytes 10354688 | tf_op jit(solution)/shard_map/query_back/pallas_call | solution.py:78
  576.2 8.7 %weight_grad.9 = bf16[1024,768]{1,0:T(8,128)(2,1)} custom-call(bf16[512,2048]{1,0:T(8,128)(2,1)} %copy-done, bf16[512,2048]{1,0:T(8,128)(2,1)} %copy-done, bf16[512,2048]{1,0:T(8,128)(2,1)} %all-gather.13.cloned.1.call-done.refs_1_.refs_2_.refs_3_, bf16[512,2048]{1,0:T(8,128)(2,1)} %all-gather.13.cloned.1.call-done.refs_1_.refs_2_.refs_3_, ...), custom_call_target="tpu_custom_call" | custom-call | flops 3221225472 | bytes 25165824 | tf_op jit(solution)/shard_map/weight_grad/pallas_call | solution.py:78
  606.4 10.5 %input_back.1 = (bf16[256,896]{1,0:T(8,128)(2,1)}, f32[8,128]{1,0:T(8,128)}, f32[256,2048]{1,0:T(8,128)}, f32[8,2048]{1,0:T(8,128)}) custom-call(s32[8]{0:T(128)} %broadcast_xor_fusion.table, bf16[256,896]{1,0:T(8,128)(2,1)} %pad_maximum_fusion.8.d_pair, f32[256,896]{1,0:T(8,128)} %get-tuple-element.286.kv_raw, f32[256,128]{1,0:T(8,128)} %pad_maximum_fusion.9.cosine, ...), custom_call_target="tpu_custom_call" | custom-call | flops 939524096 | bytes 13767168 | tf_op jit(solution)/shard_map/input_back/pallas_call | solution.py:87
  620.1 4.5 key_value_grad.1
  625.4 3.7 add.321
  641.8 9.4 %weight_grad.10 = bf16[1024,896]{1,0:T(8,128)(2,1)} custom-call(bf16[512,2048]{1,0:T(8,128)(2,1)} %collective-permute-done.34.refs_2_.refs_0_.refs_1_, bf16[512,2048]{1,0:T(8,128)(2,1)} %collective-permute-done.34.refs_2_.refs_0_.refs_1_, bf16[512,2048]{1,0:T(8,128)(2,1)} %bitcast.29.refs_3_.refs_2_, bf16[512,2048]{1,0:T(8,128)(2,1)} %bitcast.29.refs_3_.refs_2_, ...), custom_call_target="tpu_custom_call" | custom-call | flops 3758096384 | bytes 22282240 | tf_op jit(solution)/shard_map/weight_grad/pallas_call | solution.py:78
  660.9 9.7 %weight_grad.11 = bf16[1024,896]{1,0:T(8,128)(2,1)} custom-call(bf16[512,2048]{1,0:T(8,128)(2,1)} %copy-done, bf16[512,2048]{1,0:T(8,128)(2,1)} %copy-done, bf16[512,2048]{1,0:T(8,128)(2,1)} %all-gather.13.cloned.1.call-done.refs_1_.refs_2_.refs_3_, bf16[512,2048]{1,0:T(8,128)(2,1)} %all-gather.13.cloned.1.call-done.refs_1_.refs_2_.refs_3_, ...), custom_call_target="tpu_custom_call" | custom-call | flops 3758096384 | bytes 25427968 | tf_op jit(solution)/shard_map/weight_grad/pallas_call | solution.py:78
  676.2 8.3 %collective-permute-done.71 = bf16[256,1792]{1,0:T(8,128)(2,1)} collective-permute-done((bf16[256,1792]{1,0:T(8,128)(2,1)}, bf16[256,1792]{1,0:T(8,128)(2,1)}, u32[]{:S(2)}, u32[]{:S(2)}) %collective-permute-start.71) | collective-permute-done | bytes 917536 | tf_op jit(solution)/shard_map/ppermute | solution.py:881
  687.8 4.0 collective-permute-done.69
  696.4 10.1 %collective-permute-done.76 = bf16[256,448]{1,0:T(8,128)(2,1)S(1)} collective-permute-done((bf16[256,448]{1,0:T(8,128)(2,1)S(1)}, bf16[256,448]{1,0:T(8,128)(2,1)S(1)}, u32[]{:S(2)}, u32[]{:S(2)}) %collective-permute-start.76) | collective-permute-done | bytes 229408 | tf_op jit(solution)/shard_map/ppermute | solution.py:888
  706.6 4.0 collective-permute-done.75
  711.9 12.7 %collective-permute-done.73 = bf16[64,1792]{1,0:T(8,128)(2,1)S(1)} collective-permute-done((bf16[64,1792]{1,0:T(8,128)(2,1)S(1)}, bf16[64,1792]{1,0:T(8,128)(2,1)S(1)}, u32[]{:S(2)}, u32[]{:S(2)}) %collective-permute-start.73) | collective-permute-done | bytes 229408 | tf_op jit(solution)/shard_map/ppermute | solution.py:888
  735.1 3.7 finish_layer.1
  (530 shorter events, 233.8 us)
Async XLA Ops:
  7.2 96.7 %all-gather.19.cloned.1.call-start = ((), (), s32[]{:S(2)}) async-start(), calls=%async_computation.17 | async-start | bytes 2293760 | tf_op jit(solution)/shard_map/all_gather | solution.py:999
  10.4 137.5 %all-gather.17.cloned.1.call-start = ((), (), s32[]{:S(2)}) async-start(), calls=%async_computation.16 | async-start | bytes 5242880 | tf_op jit(solution)/shard_map/all_gather | solution.py:1011
  23.9 174.1 %all-gather.9.cloned.1.call-start = ((), (), s32[]{:S(2)}) async-start(), calls=%async_computation.6 | async-start | bytes 2293760 | tf_op jit(solution)/shard_map/all_gather | solution.py:1079
  26.4 35.8 %collective-permute-start.4 = (bf16[128,1024]{1,0:T(8,128)(2,1)S(1)}, bf16[128,1024]{1,0:T(8,128)(2,1)}, u32[]{:S(2)}, u32[]{:S(2)}) collective-permute-start(bf16[128,1024]{1,0:T(8,128)(2,1)S(1)} %maximum_select_fusion.4), channel_id=1, source_target_pairs={{0,2},{1,3},{2,0},{3,1},{4,6},{5,7},{6,4},{7,5},{8,10},{9,11},{10,... | collective-permute-start | bytes 786440 | tf_op jit(solution)/shard_map/ppermute | solution.py:907
  42.3 33.5 %collective-permute-start.2 = (bf16[512,896]{1,0:T(8,128)(2,1)}, bf16[512,896]{1,0:T(8,128)(2,1)}, u32[]{:S(2)}, u32[]{:S(2)}) collective-permute-start(bf16[512,896]{1,0:T(8,128)(2,1)} %slice.761.refs_8_), channel_id=1, source_target_pairs={{0,16},{16,0},{1,17},{17,1},{2,18},{18,2},{3,19},{19,3},{4,20},{20... | collective-permute-start | bytes 2752520 | tf_op jit(solution)/shard_map/ppermute | solution.py:881
  43.5 32.4 %collective-permute-start.1 = (bf16[512,896]{1,0:T(8,128)(2,1)}, bf16[512,896]{1,0:T(8,128)(2,1)}, u32[]{:S(2)}, u32[]{:S(2)}) collective-permute-start(bf16[512,896]{1,0:T(8,128)(2,1)} %slice.761.refs_8_), channel_id=1, source_target_pairs={{0,8},{4,12},{8,0},{12,4},{1,9},{5,13},{9,1},{13,5},{2,10},{6,14},... | collective-permute-start | bytes 2752520 | tf_op jit(solution)/shard_map/ppermute | solution.py:872
  81.0 60.3 %collective-permute-start.14 = (bf16[512,1664]{1,0:T(8,128)(2,1)}, bf16[512,1664]{1,0:T(8,128)(2,1)}, u32[]{:S(2)}, u32[]{:S(2)}) collective-permute-start(bf16[512,1664]{1,0:T(8,128)(2,1)} %slice.777.refs_4_), channel_id=1, source_target_pairs={{0,16},{16,0},{1,17},{17,1},{2,18},{18,2},{3,19},{19,3},{4,20},{20... | collective-permute-start | bytes 5111816 | tf_op jit(solution)/shard_map/ppermute | solution.py:881
  89.6 51.7 %collective-permute-start.13 = (bf16[512,1664]{1,0:T(8,128)(2,1)}, bf16[512,1664]{1,0:T(8,128)(2,1)}, u32[]{:S(2)}, u32[]{:S(2)}) collective-permute-start(bf16[512,1664]{1,0:T(8,128)(2,1)} %slice.777.refs_4_), channel_id=1, source_target_pairs={{0,8},{4,12},{8,0},{12,4},{1,9},{5,13},{9,1},{13,5},{2,10},{6,14},... | collective-permute-start | bytes 5111816 | tf_op jit(solution)/shard_map/ppermute | solution.py:872
  103.3 36.1 %collective-permute-start.12 = (bf16[256,896]{1,0:T(8,128)(2,1)}, bf16[256,896]{1,0:T(8,128)(2,1)}, u32[]{:S(2)}, u32[]{:S(2)}) collective-permute-start(bf16[256,896]{1,0:T(8,128)(2,1)} %get-tuple-element.180), channel_id=1, source_target_pairs={{0,8},{4,12},{8,0},{12,4},{1,9},{5,13},{9,1},{13,5},{2,10},{6,14},... | collective-permute-start | bytes 1376264 | tf_op jit(solution)/shard_map/ppermute | solution.py:872
  108.5 41.6 %collective-permute-start.16 = (bf16[256,1792]{1,0:T(8,128)(2,1)}, bf16[256,1792]{1,0:T(8,128)(2,1)}, u32[]{:S(2)}, u32[]{:S(2)}) collective-permute-start(bf16[256,1792]{1,0:T(8,128)(2,1)} %copy.119), channel_id=1, source_target_pairs={{0,16},{16,0},{1,17},{17,1},{2,18},{18,2},{3,19},{19,3},{4,20},{20... | collective-permute-start | bytes 2752520 | tf_op jit(solution)/shard_map/ppermute | solution.py:881
  148.0 113.2 %all-gather.11.cloned.1.call-start = ((), (), s32[]{:S(2)}) async-start(), calls=%async_computation.7 | async-start | bytes 2293760 | tf_op jit(solution)/shard_map/all_gather | solution.py:1079
  148.5 22.4 %collective-permute-start.15 = (bf16[256,1792]{1,0:T(8,128)(2,1)}, bf16[256,1792]{1,0:T(8,128)(2,1)S(1)}, u32[]{:S(2)}, u32[]{:S(2)}) collective-permute-start(bf16[256,1792]{1,0:T(8,128)(2,1)} %copy.119), channel_id=1, source_target_pairs={{0,8},{4,12},{8,0},{12,4},{1,9},{5,13},{9,1},{13,5},{2,10},{6,14},... | collective-permute-start | bytes 2752520 | tf_op jit(solution)/shard_map/ppermute | solution.py:872
  171.9 21.7 %collective-permute-start.17 = (bf16[256,1792]{1,0:T(8,128)(2,1)}, bf16[256,1792]{1,0:T(8,128)(2,1)}, u32[]{:S(2)}, u32[]{:S(2)}) collective-permute-start(bf16[256,1792]{1,0:T(8,128)(2,1)} %collective-permute-done.16.refs_2_), channel_id=1, source_target_pairs={{0,8},{4,12},{8,0},{12,4},{1,9},{5,13},{9,1},{13,5},{2,10},{6,14},... | collective-permute-start | bytes 2752520 | tf_op jit(solution)/shard_map/ppermute | solution.py:872
  174.0 21.0 %collective-permute-start.18 = (bf16[256,1792]{1,0:T(8,128)(2,1)S(1)}, bf16[256,1792]{1,0:T(8,128)(2,1)S(1)}, u32[]{:S(2)}, u32[]{:S(2)}) collective-permute-start(bf16[256,1792]{1,0:T(8,128)(2,1)S(1)} %copy.122.refs_0_), channel_id=1, source_target_pairs={{0,4},{4,0},{8,12},{12,8},{1,5},{5,1},{9,13},{13,9},{2,6},{6,2},{1... | collective-permute-start | bytes 2752520 | tf_op jit(solution)/shard_map/ppermute | solution.py:878
  174.0 23.9 %collective-permute-start.20 = (bf16[256,1792]{1,0:T(8,128)(2,1)}, bf16[256,1792]{1,0:T(8,128)(2,1)}, u32[]{:S(2)}, u32[]{:S(2)}) collective-permute-start(bf16[256,1792]{1,0:T(8,128)(2,1)} %collective-permute-done.16.refs_2_), channel_id=1, source_target_pairs={{0,4},{4,0},{8,12},{12,8},{1,5},{5,1},{9,13},{13,9},{2,6},{6,2},{1... | collective-permute-start | bytes 2752520 | tf_op jit(solution)/shard_map/ppermute | solution.py:878
  174.5 23.4 %collective-permute-start.19 = (bf16[256,1792]{1,0:T(8,128)(2,1)}, bf16[256,1792]{1,0:T(8,128)(2,1)}, u32[]{:S(2)}, u32[]{:S(2)}) collective-permute-start(bf16[256,1792]{1,0:T(8,128)(2,1)} %copy-done.25), channel_id=1, source_target_pairs={{0,4},{4,0},{8,12},{12,8},{1,5},{5,1},{9,13},{13,9},{2,6},{6,2},{1... | collective-permute-start | bytes 2752520 | tf_op jit(solution)/shard_map/ppermute | solution.py:878
  193.5 22.8 %collective-permute-start.23 = (bf16[256,1792]{1,0:T(8,128)(2,1)S(1)}, bf16[256,1792]{1,0:T(8,128)(2,1)S(1)}, u32[]{:S(2)}, u32[]{:S(2)}) collective-permute-start(bf16[256,1792]{1,0:T(8,128)(2,1)S(1)} %bitcast.61), channel_id=1, source_target_pairs={{0,16},{16,0},{1,17},{17,1},{2,18},{18,2},{3,19},{19,3},{4,20},{20... | collective-permute-start | bytes 2752520 | tf_op jit(solution)/shard_map/ppermute | solution.py:881
  195.9 22.5 %collective-permute-start.22 = (bf16[256,1792]{1,0:T(8,128)(2,1)S(1)}, bf16[256,1792]{1,0:T(8,128)(2,1)S(1)}, u32[]{:S(2)}, u32[]{:S(2)}) collective-permute-start(bf16[256,1792]{1,0:T(8,128)(2,1)S(1)} %bitcast.62), channel_id=1, source_target_pairs={{0,8},{4,12},{8,0},{12,4},{1,9},{5,13},{9,1},{13,5},{2,10},{6,14},... | collective-permute-start | bytes 2752520 | tf_op jit(solution)/shard_map/ppermute | solution.py:872
  219.5 91.3 %all-gather.13.cloned.1.call-start = ((), (), s32[]{:S(2)}) async-start(), calls=%async_computation.8 | async-start | bytes 2621440 | tf_op jit(solution)/shard_map/all_gather | solution.py:1100
  221.4 22.7 %collective-permute-start.25 = (bf16[256,1792]{1,0:T(8,128)(2,1)S(1)}, bf16[256,1792]{1,0:T(8,128)(2,1)S(1)}, u32[]{:S(2)}, u32[]{:S(2)}) collective-permute-start(bf16[256,1792]{1,0:T(8,128)(2,1)S(1)} %collective-permute-done.22.refs_1_), channel_id=1, source_target_pairs={{0,16},{16,0},{1,17},{17,1},{2,18},{18,2},{3,19},{19,3},{4,20},{20... | collective-permute-start | bytes 2752520 | tf_op jit(solution)/shard_map/ppermute | solution.py:881
  261.0 94.1 %all-gather.15.cloned.1.call-start = ((), (), s32[]{:S(2)}) async-start(), calls=%async_computation.9 | async-start | bytes 2621440 | tf_op jit(solution)/shard_map/all_gather | solution.py:1100
  261.3 39.8 %collective-permute-start.31 = (bf16[512,1664]{1,0:T(8,128)(2,1)}, bf16[512,1664]{1,0:T(8,128)(2,1)}, u32[]{:S(2)}, u32[]{:S(2)}) collective-permute-start(bf16[512,1664]{1,0:T(8,128)(2,1)} %collective-permute-done.13.refs_5_), channel_id=1, source_target_pairs={{0,16},{16,0},{1,17},{17,1},{2,18},{18,2},{3,19},{19,3},{4,20},{20... | collective-permute-start | bytes 5111816 | tf_op jit(solution)/shard_map/ppermute | solution.py:881
  261.9 22.5 %collective-permute-start.32 = (bf16[512,896]{1,0:T(8,128)(2,1)}, bf16[512,896]{1,0:T(8,128)(2,1)S(1)}, u32[]{:S(2)}, u32[]{:S(2)}) collective-permute-start(bf16[512,896]{1,0:T(8,128)(2,1)} %collective-permute-done.2.refs_10_), channel_id=1, source_target_pairs={{0,8},{4,12},{8,0},{12,4},{1,9},{5,13},{9,1},{13,5},{2,10},{6,14},... | collective-permute-start | bytes 2752520 | tf_op jit(solution)/shard_map/ppermute | solution.py:872
  268.2 42.9 %collective-permute-start.34 = (bf16[512,2048]{1,0:T(8,128)(2,1)}, bf16[512,2048]{1,0:T(8,128)(2,1)}, u32[]{:S(2)}, u32[]{:S(2)}) collective-permute-start(bf16[512,2048]{1,0:T(8,128)(2,1)} %bitcast.29.refs_3_.refs_2_), channel_id=1, source_target_pairs={{0,4},{4,0},{8,12},{12,8},{1,5},{5,1},{9,13},{13,9},{2,6},{6,2},{1... | collective-permute-start | bytes 6291464 | tf_op jit(solution)/shard_map/ppermute | solution.py:878
  310.9 121.1 %reduce-scatter.9.cloned.1.call-start = ((), (), s32[]{:S(2)}) async-start(), calls=%async_computation.11 | async-start | bytes 2621440 | tf_op jit(solution)/shard_map/reduce_scatter | solution.py:1124
  362.6 119.1 %reduce-scatter.7.cloned.1.call-start = ((), (), s32[]{:S(2)}) async-start(), calls=%async_computation.10 | async-start | bytes 2621440 | tf_op jit(solution)/shard_map/reduce_scatter | solution.py:1124
  402.0 27.8 %collective-permute-start.38 = (bf16[512,2048]{1,0:T(8,128)(2,1)}, bf16[512,2048]{1,0:T(8,128)(2,1)S(1)}, u32[]{:S(2)}, u32[]{:S(2)}) collective-permute-start(bf16[512,2048]{1,0:T(8,128)(2,1)} %get-tuple-element.222), channel_id=1, source_target_pairs={{0,4},{4,0},{8,12},{12,8},{1,5},{5,1},{9,13},{13,9},{2,6},{6,2},{1... | collective-permute-start | bytes 6291464 | tf_op jit(solution)/shard_map/ppermute | solution.py:878
  413.9 28.7 %collective-permute-start.40 = (bf16[384,896]{1,0:T(8,128)(2,1)}, bf16[384,896]{1,0:T(8,128)(2,1)}, u32[]{:S(2)}, u32[]{:S(2)}) collective-permute-start(bf16[384,896]{1,0:T(8,128)(2,1)} %slice.783), channel_id=1, source_target_pairs={{0,16},{16,0},{1,17},{17,1},{2,18},{18,2},{3,19},{19,3},{4,20},{20... | collective-permute-start | bytes 2064392 | tf_op jit(solution)/shard_map/ppermute | solution.py:881
  428.6 38.6 %collective-permute-start.42 = (bf16[640,896]{1,0:T(8,128)(2,1)S(1)}, bf16[640,896]{1,0:T(8,128)(2,1)S(1)}, u32[]{:S(2)}, u32[]{:S(2)}) collective-permute-start(bf16[640,896]{1,0:T(8,128)(2,1)S(1)} %slice.785), channel_id=1, source_target_pairs={{0,16},{16,0},{1,17},{17,1},{2,18},{18,2},{3,19},{19,3},{4,20},{20... | collective-permute-start | bytes 3440648 | tf_op jit(solution)/shard_map/ppermute | solution.py:881
  429.2 38.0 %collective-permute-start.43 = (bf16[640,768]{1,0:T(8,128)(2,1)}, bf16[640,768]{1,0:T(8,128)(2,1)S(1)}, u32[]{:S(2)}, u32[]{:S(2)}) collective-permute-start(bf16[640,768]{1,0:T(8,128)(2,1)} %slice.786), channel_id=1, source_target_pairs={{0,8},{4,12},{8,0},{12,4},{1,9},{5,13},{9,1},{13,5},{2,10},{6,14},... | collective-permute-start | bytes 2949128 | tf_op jit(solution)/shard_map/ppermute | solution.py:872
  431.9 103.8 %reduce-scatter.15.cloned.1.call-start = ((), (), s32[]{:S(2)}) async-start(), calls=%async_computation.14 | async-start | bytes 2293760 | tf_op jit(solution)/shard_map/reduce_scatter | solution.py:1229
  496.8 33.5 %collective-permute-start.47 = (bf16[640,896]{1,0:T(8,128)(2,1)}, bf16[640,896]{1,0:T(8,128)(2,1)}, u32[]{:S(2)}, u32[]{:S(2)}) collective-permute-start(bf16[640,896]{1,0:T(8,128)(2,1)} %slice.790), channel_id=1, source_target_pairs={{0,8},{4,12},{8,0},{12,4},{1,9},{5,13},{9,1},{13,5},{2,10},{6,14},... | collective-permute-start | bytes 3440648 | tf_op jit(solution)/shard_map/ppermute | solution.py:872
  497.4 92.5 %reduce-scatter.17.cloned.1.call-start = ((), (), s32[]{:S(2)}) async-start(), calls=%async_computation.15 | async-start | bytes 2293760 | tf_op jit(solution)/shard_map/reduce_scatter | solution.py:1229
  504.3 26.1 %collective-permute-start.48 = (bf16[256,1792]{1,0:T(8,128)(2,1)S(1)}, bf16[256,1792]{1,0:T(8,128)(2,1)S(1)}, u32[]{:S(2)}, u32[]{:S(2)}) collective-permute-start(bf16[256,1792]{1,0:T(8,128)(2,1)S(1)} %slice.791), channel_id=1, source_target_pairs={{0,16},{16,0},{1,17},{17,1},{2,18},{18,2},{3,19},{19,3},{4,20},{20... | collective-permute-start | bytes 2752520 | tf_op jit(solution)/shard_map/ppermute | solution.py:881
  552.0 183.1 %reduce-scatter.11.cloned.1.call-start = ((), (), s32[]{:S(2)}) async-start(), calls=%async_computation.12 | async-start | bytes 2621440 | tf_op jit(solution)/shard_map/reduce_scatter | solution.py:1367
  552.2 72.5 %collective-permute-start.50 = (bf16[512,2048]{1,0:T(8,128)(2,1)}, bf16[512,2048]{1,0:T(8,128)(2,1)}, u32[]{:S(2)}, u32[]{:S(2)}) collective-permute-start(bf16[512,2048]{1,0:T(8,128)(2,1)} %get-tuple-element.268), channel_id=1, source_target_pairs={{0,4},{4,0},{8,12},{12,8},{1,5},{5,1},{9,13},{13,9},{2,6},{6,2},{1... | collective-permute-start | bytes 6291464 | tf_op jit(solution)/shard_map/ppermute | solution.py:878
  552.7 21.9 %collective-permute-start.56 = (bf16[128,1792]{1,0:T(8,128)(2,1)S(1)}, bf16[128,1792]{1,0:T(8,128)(2,1)S(1)}, u32[]{:S(2)}, u32[]{:S(2)}) collective-permute-start(bf16[128,1792]{1,0:T(8,128)(2,1)S(1)} %get-tuple-element.418), channel_id=1, source_target_pairs={{0,16},{16,0},{1,17},{17,1},{2,18},{18,2},{3,19},{19,3},{4,20},{20... | collective-permute-start | bytes 1376264 | tf_op jit(solution)/shard_map/ppermute | solution.py:881
  564.3 21.0 %collective-permute-start.57 = (bf16[128,1792]{1,0:T(8,128)(2,1)S(1)}, bf16[128,1792]{1,0:T(8,128)(2,1)S(1)}, u32[]{:S(2)}, u32[]{:S(2)}) collective-permute-start(bf16[128,1792]{1,0:T(8,128)(2,1)S(1)} %get-tuple-element.416), channel_id=1, source_target_pairs={{0,8},{4,12},{8,0},{12,4},{1,9},{5,13},{9,1},{13,5},{2,10},{6,14},... | collective-permute-start | bytes 1376264 | tf_op jit(solution)/shard_map/ppermute | solution.py:872
  594.0 141.2 %reduce-scatter.13.cloned.1.call-start = ((), (), s32[]{:S(2)}) async-start(), calls=%async_computation.13 | async-start | bytes 2621440 | tf_op jit(solution)/shard_map/reduce_scatter | solution.py:1367
  594.4 22.6 %collective-permute-start.60 = (bf16[320,768]{1,0:T(8,128)(2,1)S(1)}, bf16[320,768]{1,0:T(8,128)(2,1)}, u32[]{:S(2)}, u32[]{:S(2)}) collective-permute-start(bf16[320,768]{1,0:T(8,128)(2,1)S(1)} %slice.802), channel_id=1, source_target_pairs={{0,16},{16,0},{1,17},{17,1},{2,18},{18,2},{3,19},{19,3},{4,20},{20... | collective-permute-start | bytes 1474568 | tf_op jit(solution)/shard_map/ppermute | solution.py:881
  603.1 21.6 %collective-permute-start.61 = (bf16[192,768]{1,0:T(8,128)(2,1)}, bf16[192,768]{1,0:T(8,128)(2,1)S(1)}, u32[]{:S(2)}, u32[]{:S(2)}) collective-permute-start(bf16[192,768]{1,0:T(8,128)(2,1)} %slice.813), channel_id=1, source_target_pairs={{0,16},{16,0},{1,17},{17,1},{2,18},{18,2},{3,19},{19,3},{4,20},{20... | collective-permute-start | bytes 884744 | tf_op jit(solution)/shard_map/ppermute | solution.py:881
  638.3 32.2 %collective-permute-start.67 = (bf16[256,1024]{1,0:T(8,128)(2,1)}, bf16[256,1024]{1,0:T(8,128)(2,1)}, u32[]{:S(2)}, u32[]{:S(2)}) collective-permute-start(bf16[256,1024]{1,0:T(8,128)(2,1)} %get-tuple-element.402), channel_id=1, source_target_pairs={{0,24},{4,28},{8,16},{12,20},{16,8},{20,12},{24,0},{28,4},{1,25},{... | collective-permute-start | bytes 1572872 | tf_op jit(solution)/shard_map/ppermute | solution.py:875
  638.9 32.0 %collective-permute-start.66 = (bf16[256,1024]{1,0:T(8,128)(2,1)}, bf16[256,1024]{1,0:T(8,128)(2,1)}, u32[]{:S(2)}, u32[]{:S(2)}) collective-permute-start(bf16[256,1024]{1,0:T(8,128)(2,1)} %get-tuple-element.403), channel_id=1, source_target_pairs={{0,16},{16,0},{1,17},{17,1},{2,18},{18,2},{3,19},{19,3},{4,20},{20... | collective-permute-start | bytes 1572872 | tf_op jit(solution)/shard_map/ppermute | solution.py:881
  640.3 30.5 %collective-permute-start.65 = (bf16[256,1024]{1,0:T(8,128)(2,1)}, bf16[256,1024]{1,0:T(8,128)(2,1)}, u32[]{:S(2)}, u32[]{:S(2)}) collective-permute-start(bf16[256,1024]{1,0:T(8,128)(2,1)} %get-tuple-element.404), channel_id=1, source_target_pairs={{0,8},{4,12},{8,0},{12,4},{1,9},{5,13},{9,1},{13,5},{2,10},{6,14},... | collective-permute-start | bytes 1572872 | tf_op jit(solution)/shard_map/ppermute | solution.py:872
  658.9 25.7 %collective-permute-start.71 = (bf16[256,1792]{1,0:T(8,128)(2,1)}, bf16[256,1792]{1,0:T(8,128)(2,1)}, u32[]{:S(2)}, u32[]{:S(2)}) collective-permute-start(bf16[256,1792]{1,0:T(8,128)(2,1)} %slice.820), channel_id=1, source_target_pairs={{0,16},{16,0},{1,17},{17,1},{2,18},{18,2},{3,19},{19,3},{4,20},{20... | collective-permute-start | bytes 2752520 | tf_op jit(solution)/shard_map/ppermute | solution.py:881
  659.0 66.4 %collective-permute-start.79 = (bf16[512,896]{1,0:T(8,128)(2,1)}, bf16[512,896]{1,0:T(8,128)(2,1)}, u32[]{:S(2)}, u32[]{:S(2)}) collective-permute-start(bf16[512,896]{1,0:T(8,128)(2,1)} %slice.828), channel_id=1, source_target_pairs={{0,16},{16,0},{1,17},{17,1},{2,18},{18,2},{3,19},{19,3},{4,20},{20... | collective-permute-start | bytes 2752520 | tf_op jit(solution)/shard_map/ppermute | solution.py:881
  670.6 23.6 %collective-permute-start.63 = (bf16[256,1792]{1,0:T(8,128)(2,1)}, bf16[256,1792]{1,0:T(8,128)(2,1)S(1)}, u32[]{:S(2)}, u32[]{:S(2)}) collective-permute-start(bf16[256,1792]{1,0:T(8,128)(2,1)} %slice.804), channel_id=1, source_target_pairs={{0,8},{4,12},{8,0},{12,4},{1,9},{5,13},{9,1},{13,5},{2,10},{6,14},... | collective-permute-start | bytes 2752520 | tf_op jit(solution)/shard_map/ppermute | solution.py:872
  686.8 38.7 %collective-permute-start.78 = (bf16[512,896]{1,0:T(8,128)(2,1)S(1)}, bf16[512,896]{1,0:T(8,128)(2,1)S(1)}, u32[]{:S(2)}, u32[]{:S(2)}) collective-permute-start(bf16[512,896]{1,0:T(8,128)(2,1)S(1)} %slice.827), channel_id=1, source_target_pairs={{0,8},{4,12},{8,0},{12,4},{1,9},{5,13},{9,1},{13,5},{2,10},{6,14},... | collective-permute-start | bytes 2752520 | tf_op jit(solution)/shard_map/ppermute | solution.py:872
  (122 other events, 1159.6 us)
Sparse Core Ops, SparseCore 0:
  10.5 55.4 all-gather.18
  68.2 79.6 all-gather.16
  150.1 39.9 all-gather.8
  219.6 39.5 all-gather.10
  261.2 44.7 all-gather.12
  311.0 44.1 all-gather.14
  362.7 42.4 reduce-scatter.8
  432.0 42.8 reduce-scatter.6
  497.5 38.0 reduce-scatter.14
  552.1 37.7 reduce-scatter.16
  594.1 42.0 reduce-scatter.10
  638.5 47.4 reduce-scatter.12

commit v6 on v5

--- a/solution.py
+++ b/solution.py
@@ -1322,7 +1322,7 @@
         g_q = q_keep + after(q_got, first_half)
         o_own, o_got = line_sends(g_o, 0)
         q_own, q_got = line_sends(g_q, 1)
-        o_got, q_got[:2] = beside(o_got, q_got[:2])
+        o_got, q_got = beside(o_got, q_got)
         o_final = line_sum(o_own, o_got)
         first_last, down_last = after((first_last, down_last), o_final)
         second_got = jnp.concatenate(second_last, axis=0)

time: 766 us -> 775 us (1.012)
  waiting for transfers between devices: 224 us -> 235 us
    ppermute x9, waiting for transfers between devices: 31.6 us -> 41.7 us  [line_sends(): got.append(lax.ppermute(block, 'heads', [(i, i ^ k) for i in range(4)]))]
    unnamed x174 -> x176, local copies, waits for them, and re-layouts: 24.2 us -> 24.2 us
  transfers between devices with their start and end apart: 93 -> 93, of which waited for: 39 -> 39; matrix products, arithmetic and copies ran while one was open for 18% -> 17% of each run, Pallas kernels for 37% -> 37%
where the time goes in v6:
time: 775 us; the launch traced here: 769 us
  Pallas kernels  281 us (36%)
  waiting for transfers between devices  235 us (30%)
  local copies, waits for them, and re-layouts  81.7 us (11%)
  other arithmetic  72.9 us (9%)
  starting transfers between devices  72.3 us (9%)
  between operations  15.9 us (2%)
  matrix products  10.3 us (1%)
    pallas_call x15, Pallas kernels, call(): pl.pallas_call(body, grid=grid, in_specs=in_specs, out_specs=out_specs, s...  217 us
    ppermute x22, waiting for transfers between devices, swap_x(): return lax.ppermute(v, 'seq', [(i, i ^ 2) for i in range(4)])  82.8 us
    pallas_call x8, Pallas kernels, call(): pl.pallas_call(body, grid_spec=pltpu.PrefetchScalarGridSpec(num_scalar_pr...  64 us
    ppermute x18, waiting for transfers between devices, swap_y(): return lax.ppermute(v, 'dp', [(0, 1), (1, 0)])  57.3 us
    ppermute x9, waiting for transfers between devices, line_sends(): got.append(lax.ppermute(block, 'heads', [(i, i ^ k) for i in range(4)]))  41.7 us
    ppermute x22, starting transfers between devices, swap_x(): return lax.ppermute(v, 'seq', [(i, i ^ 2) for i in range(4)])  25.9 us
    unnamed x176, local copies, waits for them, and re-layouts  24.2 us
    ppermute x18, starting transfers between devices, swap_y(): return lax.ppermute(v, 'dp', [(0, 1), (1, 0)])  21.4 us
  transfers between devices with their start and end apart: 93, of which 39 were waited for; matrix products, arithmetic and copies ran while one was open for 17% of the time, Pallas kernels for 37%

profile of v6, /device:TPU:0, one launch (start us, length us, event | category | flops | bytes accessed | tf_op | source)
XLA Modules:
  0.0 769.2 jit_solution(14951407664658682770)
XLA Ops:
  26.4 8.3 %collective-permute-start.4 = (bf16[128,1024]{1,0:T(8,128)(2,1)S(1)}, bf16[128,1024]{1,0:T(8,128)(2,1)}, u32[]{:S(2)}, u32[]{:S(2)}) collective-permute-start(bf16[128,1024]{1,0:T(8,128)(2,1)S(1)} %maximum_select_fusion.4), channel_id=1, source_target_pairs={{0,2},{1,3},{2,0},{3,1},{4,6},{5,7},{6,4},{7,5},{8,10},{9,11},{10,... | collective-permute-start | bytes 786440 | tf_op jit(solution)/shard_map/ppermute | solution.py:907
  35.8 5.5 fusion.4
  45.4 16.8 %collective-permute-done.4 = bf16[128,1024]{1,0:T(8,128)(2,1)} collective-permute-done((bf16[128,1024]{1,0:T(8,128)(2,1)S(1)}, bf16[128,1024]{1,0:T(8,128)(2,1)}, u32[]{:S(2)}, u32[]{:S(2)}) %collective-permute-start.4) | collective-permute-done | bytes 262176 | tf_op jit(solution)/shard_map/ppermute | solution.py:907
  66.5 7.9 %collective-permute-done.6.refs_2_ = bf16[256,1024]{1,0:T(8,128)(2,1)S(1)} collective-permute-done((bf16[256,1024]{1,0:T(8,128)(2,1)S(1)}, bf16[256,1024]{1,0:T(8,128)(2,1)S(1)}, u32[]{:S(2)}, u32[]{:S(2)}) %collective-permute-start.6) | collective-permute-done | bytes 524320 | tf_op jit(solution)/shard_map/ppermute | solution.py:881
  83.5 5.0 collective-permute-done.7.refs_3_
  96.0 7.3 project_key_value.1
  110.0 29.3 %collective-permute-done.12 = bf16[256,896]{1,0:T(8,128)(2,1)} collective-permute-done((bf16[256,896]{1,0:T(8,128)(2,1)}, bf16[256,896]{1,0:T(8,128)(2,1)}, u32[]{:S(2)}, u32[]{:S(2)}) %collective-permute-start.12) | collective-permute-done | bytes 458784 | tf_op jit(solution)/shard_map/ppermute | solution.py:872
  141.3 6.7 all-gather.17.cloned.1.call-done
  150.1 20.8 %collective-permute-done.15.refs_1_ = bf16[256,1792]{1,0:T(8,128)(2,1)S(1)} collective-permute-done((bf16[256,1792]{1,0:T(8,128)(2,1)}, bf16[256,1792]{1,0:T(8,128)(2,1)S(1)}, u32[]{:S(2)}, u32[]{:S(2)}) %collective-permute-start.15) | collective-permute-done | bytes 917536 | tf_op jit(solution)/shard_map/ppermute | solution.py:872
  174.6 18.9 %collective-permute-done.17.refs_3_ = bf16[256,1792]{1,0:T(8,128)(2,1)} collective-permute-done((bf16[256,1792]{1,0:T(8,128)(2,1)}, bf16[256,1792]{1,0:T(8,128)(2,1)}, u32[]{:S(2)}, u32[]{:S(2)}) %collective-permute-start.17) | collective-permute-done | bytes 917536 | tf_op jit(solution)/shard_map/ppermute | solution.py:872
  198.0 9.5 %project_query.1 = (f32[256,1792]{1,0:T(8,128)}, bf16[256,1792]{1,0:T(8,128)(2,1)}) custom-call(bf16[256,2048]{1,0:T(8,128)(2,1)} %get-tuple-element.272.normed, f32[256,128]{1,0:T(8,128)} %pad_maximum_fusion.9.cosine, f32[256,128]{1,0:T(8,128)} %pad_maximum_fusion.10.sine, f32[1,128]{1,0:T(1,128)} %pad_maximum_fusion.14.gain, bf16[256,1792]{1,0:T(8,128)(2,1)} %copy-done.13, ...), custom_call_target="tpu_custom_call" | custom-call | flops 1879048192 | bytes 11403776 | tf_op jit(solution)/shard_map/project_query/pallas_call | solution.py:78
  207.5 8.8 %collective-permute-done.23.refs_2_ = bf16[256,1792]{1,0:T(8,128)(2,1)S(1)} collective-permute-done((bf16[256,1792]{1,0:T(8,128)(2,1)S(1)}, bf16[256,1792]{1,0:T(8,128)(2,1)S(1)}, u32[]{:S(2)}, u32[]{:S(2)}) %collective-permute-start.23) | collective-permute-done | bytes 917536 | tf_op jit(solution)/shard_map/ppermute | solution.py:881
  222.5 11.0 %attention_forward.2 = (bf16[128,1792]{1,0:T(8,128)(2,1)}, f32[7,1,512]{2,1,0:T(1,128)}) custom-call(bf16[8,1,128,896]{3,2,1,0:T(8,128)(2,1)} %bitcast.19.kv0, bf16[8,1,128,896]{3,2,1,0:T(8,128)(2,1)} %bitcast.20.kv1, bf16[256,1792]{1,0:T(8,128)(2,1)} %get-tuple-element.202.query, f32[1024,128]{1,0:T(8,128)} %get-tuple-element.457.bias0, ...), custom_call_target="tpu_custom_call" | custom-call | flops 11274289152 | bytes 6109184 | tf_op jit(solution)/shard_map/attention_forward/pallas_call | solution.py:78
  233.6 10.5 %collective-permute-done.25.refs_3_ = bf16[256,1792]{1,0:T(8,128)(2,1)S(1)} collective-permute-done((bf16[256,1792]{1,0:T(8,128)(2,1)S(1)}, bf16[256,1792]{1,0:T(8,128)(2,1)S(1)}, u32[]{:S(2)}, u32[]{:S(2)}) %collective-permute-start.25) | collective-permute-done | bytes 917536 | tf_op jit(solution)/shard_map/ppermute | solution.py:881
  251.4 9.6 %project_output.2 = (f32[128,2048]{1,0:T(8,128)}, bf16[128,2048]{1,0:T(8,128)(2,1)}) custom-call(s32[8]{0:T(128)} %broadcast_xor_fusion.table, bf16[128,1792]{1,0:T(8,128)(2,1)} %get-tuple-element.192.mixed, bf16[256,2048]{1,0:T(8,128)(2,1)} %bitcast.69, f32[8,2048]{1,0:T(8,128)} %get-tuple-element.193.gains, bf16[256,1792]{1,0:T(8,128)(2,1)} %bitcast.64, ...), custom_call_target="tpu_custom_call" | custom-call | flops 939524096 | bytes 10485760 | tf_op jit(solution)/shard_map/project_output/pallas_call | solution.py:87
  263.4 4.8 fusion.28
  269.5 11.0 %attention_forward.3 = (bf16[128,1792]{1,0:T(8,128)(2,1)}, f32[7,1,512]{2,1,0:T(1,128)}) custom-call(bf16[8,1,128,896]{3,2,1,0:T(8,128)(2,1)} %bitcast.94, bf16[8,1,128,896]{3,2,1,0:T(8,128)(2,1)} %bitcast.96, bf16[256,1792]{1,0:T(8,128)(2,1)} %get-tuple-element.202.query, f32[1024,128]{1,0:T(8,128)} %get-tuple-element.456.bias0, ...), custom_call_target="tpu_custom_call" | custom-call | flops 11274289152 | bytes 6109184 | tf_op jit(solution)/shard_map/attention_forward/pallas_call | solution.py:78
  280.5 4.0 collective-permute-done.32.refs_11_
  284.5 16.6 %collective-permute-done.31.refs_7_ = bf16[512,1664]{1,0:T(8,128)(2,1)} collective-permute-done((bf16[512,1664]{1,0:T(8,128)(2,1)}, bf16[512,1664]{1,0:T(8,128)(2,1)}, u32[]{:S(2)}, u32[]{:S(2)}) %collective-permute-start.31) | collective-permute-done | bytes 1703968 | tf_op jit(solution)/shard_map/ppermute | solution.py:881
  301.1 9.6 %project_output.3 = (f32[128,2048]{1,0:T(8,128)}, bf16[128,2048]{1,0:T(8,128)(2,1)}) custom-call(s32[8]{0:T(128)} %broadcast_xor_fusion.table, bf16[128,1792]{1,0:T(8,128)(2,1)} %get-tuple-element.205.mixed, bf16[256,2048]{1,0:T(8,128)(2,1)} %bitcast.70, f32[8,2048]{1,0:T(8,128)} %get-tuple-element.193.gains, bf16[256,1792]{1,0:T(8,128)(2,1)} %bitcast.65, ...), custom_call_target="tpu_custom_call" | custom-call | flops 939524096 | bytes 10485760 | tf_op jit(solution)/shard_map/project_output/pallas_call | solution.py:87
  311.1 4.1 collective-permute-done.33.refs_0_.refs_1_
  316.5 34.2 %feed_forward.2 = (bf16[1024,896]{1,0:T(8,128)(2,1)}, bf16[1024,1664]{1,0:T(8,128)(2,1)}, bf16[512,2048]{1,0:T(8,128)(2,1)}, bf16[512,2048]{1,0:T(8,128)(2,1)}, ...) custom-call(bf16[512,2048]{1,0:T(8,128)(2,1)} %copy-done, ...), custom_call_target="tpu_custom_call" | custom-call | flops 20132659200 | bytes 32505856 | tf_op jit(solution)/shard_map/feed_forward/pallas_call | solution.py:78
  350.9 4.3 all-gather.15.cloned.1.call-done.refs_1_.refs_6_.refs_7_
  355.7 4.4 add.317
  362.7 5.0 add.315
  367.7 34.3 %feed_forward.3 = (bf16[1024,896]{1,0:T(8,128)(2,1)}, bf16[1024,1664]{1,0:T(8,128)(2,1)}, bf16[512,2048]{1,0:T(8,128)(2,1)}, bf16[512,2048]{1,0:T(8,128)(2,1)}, ...) custom-call(bf16[512,2048]{1,0:T(8,128)(2,1)} %copy-done.1, ...), custom_call_target="tpu_custom_call" | custom-call | flops 20132659200 | bytes 32505856 | tf_op jit(solution)/shard_map/feed_forward/pallas_call | solution.py:78
  402.2 9.7 %weight_grad.6 = bf16[1024,896]{1,0:T(8,128)(2,1)} custom-call(bf16[512,2048]{1,0:T(8,128)(2,1)} %copy-done, bf16[512,2048]{1,0:T(8,128)(2,1)} %copy-done, bf16[512,2048]{1,0:T(8,128)(2,1)} %all-gather.13.cloned.1.call-done.refs_1_.refs_2_.refs_3_, bf16[512,2048]{1,0:T(8,128)(2,1)} %all-gather.13.cloned.1.call-done.refs_1_.refs_2_.refs_3_, ...), custom_call_target="tpu_custom_call" | custom-call | flops 3758096384 | bytes 25427968 | tf_op jit(solution)/shard_map/weight_grad/pallas_call | solution.py:78
  415.4 8.7 %weight_grad.7 = bf16[1024,768]{1,0:T(8,128)(2,1)} custom-call(bf16[512,2048]{1,0:T(8,128)(2,1)} %copy-done, bf16[512,2048]{1,0:T(8,128)(2,1)} %copy-done, bf16[512,2048]{1,0:T(8,128)(2,1)} %all-gather.13.cloned.1.call-done.refs_1_.refs_2_.refs_3_, bf16[512,2048]{1,0:T(8,128)(2,1)} %all-gather.13.cloned.1.call-done.refs_1_.refs_2_.refs_3_, ...), custom_call_target="tpu_custom_call" | custom-call | flops 3221225472 | bytes 25165824 | tf_op jit(solution)/shard_map/weight_grad/pallas_call | solution.py:78
  432.0 10.4 %hidden_back.2 = (f32[128,2048]{1,0:T(8,128)}, bf16[128,2048]{1,0:T(8,128)(2,1)}, f32[8,2048]{1,0:T(8,128)}, bf16[128,1792]{1,0:T(8,128)(2,1)}) custom-call(s32[8]{0:T(128)} %broadcast_xor_fusion.table, bf16[128,2048]{1,0:T(8,128)(2,1)} %reduce-scatter.9.cloned.1.call-done.d_feed, f32[128,2048]{1,0:T(8,128)} %get-tuple-element.201.hidden.hidden0, ...), custom_call_target="tpu_custom_call" | custom-call | flops 939524096 | bytes 12124160 | tf_op jit(solution)/shard_map/hidden_back/pallas_call | solution.py:87
  442.6 24.6 %attention_backward.2 = (bf16[128,1792]{1,0:T(8,128)(2,1)}, bf16[1024,896]{1,0:T(8,128)(2,1)}, bf16[1024,896]{1,0:T(8,128)(2,1)}, f32[8,128]{1,0:T(8,128)}) custom-call(bf16[8,1,128,896]{3,2,1,0:T(8,128)(2,1)} %bitcast.19.kv0, bf16[8,1,128,896]{3,2,1,0:T(8,128)(2,1)} %bitcast.20.kv1, bf16[256,1792]{1,0:T(8,128)(2,1)} %get-tuple-element.202.query, ...), custom_call_target="tpu_custom_call" | custom-call | flops 26306674688 | bytes 12798464 | tf_op jit(solution)/shard_map/attention_backward/pallas_call | solution.py:78
  468.2 8.9 %weight_grad.8 = bf16[1024,896]{1,0:T(8,128)(2,1)} custom-call(bf16[512,2048]{1,0:T(8,128)(2,1)} %collective-permute-done.34.refs_2_.refs_0_.refs_1_, bf16[512,2048]{1,0:T(8,128)(2,1)} %collective-permute-done.34.refs_2_.refs_0_.refs_1_, bf16[512,2048]{1,0:T(8,128)(2,1)} %bitcast.29.refs_3_.refs_2_, bf16[512,2048]{1,0:T(8,128)(2,1)} %bitcast.29.refs_3_.refs_2_, ...), custom_call_target="tpu_custom_call" | custom-call | flops 3758096384 | bytes 22282240 | tf_op jit(solution)/shard_map/weight_grad/pallas_call | solution.py:78
  481.6 9.8 %hidden_back.3 = (f32[128,2048]{1,0:T(8,128)}, bf16[128,2048]{1,0:T(8,128)(2,1)}, f32[8,2048]{1,0:T(8,128)}, bf16[128,1792]{1,0:T(8,128)(2,1)}) custom-call(s32[8]{0:T(128)} %broadcast_xor_fusion.table, bf16[128,2048]{1,0:T(8,128)(2,1)} %reduce-scatter.7.cloned.1.call-done.d_feed, f32[128,2048]{1,0:T(8,128)} %get-tuple-element.206.hidden.hidden1, ...), custom_call_target="tpu_custom_call" | custom-call | flops 939524096 | bytes 12124160 | tf_op jit(solution)/shard_map/hidden_back/pallas_call | solution.py:87
  498.6 3.8 collective-permute-done.46
  505.6 24.6 %attention_backward.3 = (bf16[128,1792]{1,0:T(8,128)(2,1)}, bf16[1024,896]{1,0:T(8,128)(2,1)}, bf16[1024,896]{1,0:T(8,128)(2,1)}, f32[8,128]{1,0:T(8,128)}) custom-call(bf16[8,1,128,896]{3,2,1,0:T(8,128)(2,1)} %bitcast.95, bf16[8,1,128,896]{3,2,1,0:T(8,128)(2,1)} %bitcast.97, bf16[256,1792]{1,0:T(8,128)(2,1)} %get-tuple-element.202.query, ...), custom_call_target="tpu_custom_call" | custom-call | flops 26306674688 | bytes 12798464 | tf_op jit(solution)/shard_map/attention_backward/pallas_call | solution.py:78
  565.8 8.7 %query_back.1.d_normed_q = f32[256,2048]{1,0:T(8,128)} custom-call(bf16[256,1792]{1,0:T(8,128)(2,1)} %copy-done.12, bf16[256,1792]{1,0:T(8,128)(2,1)} %copy-done.13, bf16[256,1792]{1,0:T(8,128)(2,1)} %copy-done.25, bf16[256,1792]{1,0:T(8,128)(2,1)} %collective-permute-done.16.refs_2_, bf16[256,1792]{1,0:T(8,128)(2,1)} %collective-permute-done.17.refs_3_, ...), custom_call_target="tpu_custom_call" | custom-call | flops 1879048192 | bytes 10354688 | tf_op jit(solution)/shard_map/query_back/pallas_call | solution.py:78
  576.2 8.7 %weight_grad.9 = bf16[1024,768]{1,0:T(8,128)(2,1)} custom-call(bf16[512,2048]{1,0:T(8,128)(2,1)} %copy-done, bf16[512,2048]{1,0:T(8,128)(2,1)} %copy-done, bf16[512,2048]{1,0:T(8,128)(2,1)} %all-gather.13.cloned.1.call-done.refs_1_.refs_2_.refs_3_, bf16[512,2048]{1,0:T(8,128)(2,1)} %all-gather.13.cloned.1.call-done.refs_1_.refs_2_.refs_3_, ...), custom_call_target="tpu_custom_call" | custom-call | flops 3221225472 | bytes 25165824 | tf_op jit(solution)/shard_map/weight_grad/pallas_call | solution.py:78
  606.4 10.6 %input_back.1 = (bf16[256,896]{1,0:T(8,128)(2,1)}, f32[8,128]{1,0:T(8,128)}, f32[256,2048]{1,0:T(8,128)}, f32[8,2048]{1,0:T(8,128)}) custom-call(s32[8]{0:T(128)} %broadcast_xor_fusion.table, bf16[256,896]{1,0:T(8,128)(2,1)} %pad_maximum_fusion.8.d_pair, f32[256,896]{1,0:T(8,128)} %get-tuple-element.287.kv_raw, f32[256,128]{1,0:T(8,128)} %pad_maximum_fusion.9.cosine, ...), custom_call_target="tpu_custom_call" | custom-call | flops 939524096 | bytes 13767168 | tf_op jit(solution)/shard_map/input_back/pallas_call | solution.py:87
  620.1 4.6 key_value_grad.1
  625.4 3.7 add.321
  641.8 9.4 %weight_grad.10 = bf16[1024,896]{1,0:T(8,128)(2,1)} custom-call(bf16[512,2048]{1,0:T(8,128)(2,1)} %collective-permute-done.34.refs_2_.refs_0_.refs_1_, bf16[512,2048]{1,0:T(8,128)(2,1)} %collective-permute-done.34.refs_2_.refs_0_.refs_1_, bf16[512,2048]{1,0:T(8,128)(2,1)} %bitcast.29.refs_3_.refs_2_, bf16[512,2048]{1,0:T(8,128)(2,1)} %bitcast.29.refs_3_.refs_2_, ...), custom_call_target="tpu_custom_call" | custom-call | flops 3758096384 | bytes 22282240 | tf_op jit(solution)/shard_map/weight_grad/pallas_call | solution.py:78
  660.9 9.7 %weight_grad.11 = bf16[1024,896]{1,0:T(8,128)(2,1)} custom-call(bf16[512,2048]{1,0:T(8,128)(2,1)} %copy-done, bf16[512,2048]{1,0:T(8,128)(2,1)} %copy-done, bf16[512,2048]{1,0:T(8,128)(2,1)} %all-gather.13.cloned.1.call-done.refs_1_.refs_2_.refs_3_, bf16[512,2048]{1,0:T(8,128)(2,1)} %all-gather.13.cloned.1.call-done.refs_1_.refs_2_.refs_3_, ...), custom_call_target="tpu_custom_call" | custom-call | flops 3758096384 | bytes 25427968 | tf_op jit(solution)/shard_map/weight_grad/pallas_call | solution.py:78
  676.2 8.4 %collective-permute-done.71 = bf16[256,1792]{1,0:T(8,128)(2,1)} collective-permute-done((bf16[256,1792]{1,0:T(8,128)(2,1)}, bf16[256,1792]{1,0:T(8,128)(2,1)}, u32[]{:S(2)}, u32[]{:S(2)}) %collective-permute-start.71) | collective-permute-done | bytes 917536 | tf_op jit(solution)/shard_map/ppermute | solution.py:881
  687.1 4.6 collective-permute-done.69
  696.4 6.4 collective-permute-done.77
  704.3 5.7 collective-permute-done.75
  710.0 16.6 %collective-permute-done.76 = bf16[256,448]{1,0:T(8,128)(2,1)S(1)} collective-permute-done((bf16[256,448]{1,0:T(8,128)(2,1)S(1)}, bf16[256,448]{1,0:T(8,128)(2,1)S(1)}, u32[]{:S(2)}, u32[]{:S(2)}) %collective-permute-start.76) | collective-permute-done | bytes 229408 | tf_op jit(solution)/shard_map/ppermute | solution.py:888
  727.9 6.7 collective-permute-done.73
  744.3 3.7 finish_layer.1
  (532 shorter events, 237.1 us)
Async XLA Ops:
  7.2 96.7 %all-gather.19.cloned.1.call-start = ((), (), s32[]{:S(2)}) async-start(), calls=%async_computation.17 | async-start | bytes 2293760 | tf_op jit(solution)/shard_map/all_gather | solution.py:999
  10.4 137.5 %all-gather.17.cloned.1.call-start = ((), (), s32[]{:S(2)}) async-start(), calls=%async_computation.16 | async-start | bytes 5242880 | tf_op jit(solution)/shard_map/all_gather | solution.py:1011
  23.8 174.1 %all-gather.9.cloned.1.call-start = ((), (), s32[]{:S(2)}) async-start(), calls=%async_computation.6 | async-start | bytes 2293760 | tf_op jit(solution)/shard_map/all_gather | solution.py:1079
  26.4 35.8 %collective-permute-start.4 = (bf16[128,1024]{1,0:T(8,128)(2,1)S(1)}, bf16[128,1024]{1,0:T(8,128)(2,1)}, u32[]{:S(2)}, u32[]{:S(2)}) collective-permute-start(bf16[128,1024]{1,0:T(8,128)(2,1)S(1)} %maximum_select_fusion.4), channel_id=1, source_target_pairs={{0,2},{1,3},{2,0},{3,1},{4,6},{5,7},{6,4},{7,5},{8,10},{9,11},{10,... | collective-permute-start | bytes 786440 | tf_op jit(solution)/shard_map/ppermute | solution.py:907
  42.3 33.5 %collective-permute-start.2 = (bf16[512,896]{1,0:T(8,128)(2,1)}, bf16[512,896]{1,0:T(8,128)(2,1)}, u32[]{:S(2)}, u32[]{:S(2)}) collective-permute-start(bf16[512,896]{1,0:T(8,128)(2,1)} %slice.761.refs_8_), channel_id=1, source_target_pairs={{0,16},{16,0},{1,17},{17,1},{2,18},{18,2},{3,19},{19,3},{4,20},{20... | collective-permute-start | bytes 2752520 | tf_op jit(solution)/shard_map/ppermute | solution.py:881
  43.5 32.4 %collective-permute-start.1 = (bf16[512,896]{1,0:T(8,128)(2,1)}, bf16[512,896]{1,0:T(8,128)(2,1)}, u32[]{:S(2)}, u32[]{:S(2)}) collective-permute-start(bf16[512,896]{1,0:T(8,128)(2,1)} %slice.761.refs_8_), channel_id=1, source_target_pairs={{0,8},{4,12},{8,0},{12,4},{1,9},{5,13},{9,1},{13,5},{2,10},{6,14},... | collective-permute-start | bytes 2752520 | tf_op jit(solution)/shard_map/ppermute | solution.py:872
  81.0 60.3 %collective-permute-start.14 = (bf16[512,1664]{1,0:T(8,128)(2,1)}, bf16[512,1664]{1,0:T(8,128)(2,1)}, u32[]{:S(2)}, u32[]{:S(2)}) collective-permute-start(bf16[512,1664]{1,0:T(8,128)(2,1)} %slice.777.refs_4_), channel_id=1, source_target_pairs={{0,16},{16,0},{1,17},{17,1},{2,18},{18,2},{3,19},{19,3},{4,20},{20... | collective-permute-start | bytes 5111816 | tf_op jit(solution)/shard_map/ppermute | solution.py:881
  89.6 51.7 %collective-permute-start.13 = (bf16[512,1664]{1,0:T(8,128)(2,1)}, bf16[512,1664]{1,0:T(8,128)(2,1)}, u32[]{:S(2)}, u32[]{:S(2)}) collective-permute-start(bf16[512,1664]{1,0:T(8,128)(2,1)} %slice.777.refs_4_), channel_id=1, source_target_pairs={{0,8},{4,12},{8,0},{12,4},{1,9},{5,13},{9,1},{13,5},{2,10},{6,14},... | collective-permute-start | bytes 5111816 | tf_op jit(solution)/shard_map/ppermute | solution.py:872
  103.3 36.1 %collective-permute-start.12 = (bf16[256,896]{1,0:T(8,128)(2,1)}, bf16[256,896]{1,0:T(8,128)(2,1)}, u32[]{:S(2)}, u32[]{:S(2)}) collective-permute-start(bf16[256,896]{1,0:T(8,128)(2,1)} %get-tuple-element.181), channel_id=1, source_target_pairs={{0,8},{4,12},{8,0},{12,4},{1,9},{5,13},{9,1},{13,5},{2,10},{6,14},... | collective-permute-start | bytes 1376264 | tf_op jit(solution)/shard_map/ppermute | solution.py:872
  108.5 41.6 %collective-permute-start.16 = (bf16[256,1792]{1,0:T(8,128)(2,1)}, bf16[256,1792]{1,0:T(8,128)(2,1)}, u32[]{:S(2)}, u32[]{:S(2)}) collective-permute-start(bf16[256,1792]{1,0:T(8,128)(2,1)} %copy.119), channel_id=1, source_target_pairs={{0,16},{16,0},{1,17},{17,1},{2,18},{18,2},{3,19},{19,3},{4,20},{20... | collective-permute-start | bytes 2752520 | tf_op jit(solution)/shard_map/ppermute | solution.py:881
  148.0 113.2 %all-gather.11.cloned.1.call-start = ((), (), s32[]{:S(2)}) async-start(), calls=%async_computation.7 | async-start | bytes 2293760 | tf_op jit(solution)/shard_map/all_gather | solution.py:1079
  148.5 22.4 %collective-permute-start.15 = (bf16[256,1792]{1,0:T(8,128)(2,1)}, bf16[256,1792]{1,0:T(8,128)(2,1)S(1)}, u32[]{:S(2)}, u32[]{:S(2)}) collective-permute-start(bf16[256,1792]{1,0:T(8,128)(2,1)} %copy.119), channel_id=1, source_target_pairs={{0,8},{4,12},{8,0},{12,4},{1,9},{5,13},{9,1},{13,5},{2,10},{6,14},... | collective-permute-start | bytes 2752520 | tf_op jit(solution)/shard_map/ppermute | solution.py:872
  171.9 21.7 %collective-permute-start.17 = (bf16[256,1792]{1,0:T(8,128)(2,1)}, bf16[256,1792]{1,0:T(8,128)(2,1)}, u32[]{:S(2)}, u32[]{:S(2)}) collective-permute-start(bf16[256,1792]{1,0:T(8,128)(2,1)} %collective-permute-done.16.refs_2_), channel_id=1, source_target_pairs={{0,8},{4,12},{8,0},{12,4},{1,9},{5,13},{9,1},{13,5},{2,10},{6,14},... | collective-permute-start | bytes 2752520 | tf_op jit(solution)/shard_map/ppermute | solution.py:872
  174.0 23.9 %collective-permute-start.20 = (bf16[256,1792]{1,0:T(8,128)(2,1)}, bf16[256,1792]{1,0:T(8,128)(2,1)}, u32[]{:S(2)}, u32[]{:S(2)}) collective-permute-start(bf16[256,1792]{1,0:T(8,128)(2,1)} %collective-permute-done.16.refs_2_), channel_id=1, source_target_pairs={{0,4},{4,0},{8,12},{12,8},{1,5},{5,1},{9,13},{13,9},{2,6},{6,2},{1... | collective-permute-start | bytes 2752520 | tf_op jit(solution)/shard_map/ppermute | solution.py:878
  174.5 23.4 %collective-permute-start.19 = (bf16[256,1792]{1,0:T(8,128)(2,1)}, bf16[256,1792]{1,0:T(8,128)(2,1)}, u32[]{:S(2)}, u32[]{:S(2)}) collective-permute-start(bf16[256,1792]{1,0:T(8,128)(2,1)} %copy-done.25), channel_id=1, source_target_pairs={{0,4},{4,0},{8,12},{12,8},{1,5},{5,1},{9,13},{13,9},{2,6},{6,2},{1... | collective-permute-start | bytes 2752520 | tf_op jit(solution)/shard_map/ppermute | solution.py:878
  193.5 22.8 %collective-permute-start.23 = (bf16[256,1792]{1,0:T(8,128)(2,1)S(1)}, bf16[256,1792]{1,0:T(8,128)(2,1)S(1)}, u32[]{:S(2)}, u32[]{:S(2)}) collective-permute-start(bf16[256,1792]{1,0:T(8,128)(2,1)S(1)} %bitcast.61), channel_id=1, source_target_pairs={{0,16},{16,0},{1,17},{17,1},{2,18},{18,2},{3,19},{19,3},{4,20},{20... | collective-permute-start | bytes 2752520 | tf_op jit(solution)/shard_map/ppermute | solution.py:881
  195.9 22.5 %collective-permute-start.22 = (bf16[256,1792]{1,0:T(8,128)(2,1)S(1)}, bf16[256,1792]{1,0:T(8,128)(2,1)S(1)}, u32[]{:S(2)}, u32[]{:S(2)}) collective-permute-start(bf16[256,1792]{1,0:T(8,128)(2,1)S(1)} %bitcast.62), channel_id=1, source_target_pairs={{0,8},{4,12},{8,0},{12,4},{1,9},{5,13},{9,1},{13,5},{2,10},{6,14},... | collective-permute-start | bytes 2752520 | tf_op jit(solution)/shard_map/ppermute | solution.py:872
  219.5 91.3 %all-gather.13.cloned.1.call-start = ((), (), s32[]{:S(2)}) async-start(), calls=%async_computation.8 | async-start | bytes 2621440 | tf_op jit(solution)/shard_map/all_gather | solution.py:1100
  221.4 22.7 %collective-permute-start.25 = (bf16[256,1792]{1,0:T(8,128)(2,1)S(1)}, bf16[256,1792]{1,0:T(8,128)(2,1)S(1)}, u32[]{:S(2)}, u32[]{:S(2)}) collective-permute-start(bf16[256,1792]{1,0:T(8,128)(2,1)S(1)} %collective-permute-done.22.refs_1_), channel_id=1, source_target_pairs={{0,16},{16,0},{1,17},{17,1},{2,18},{18,2},{3,19},{19,3},{4,20},{20... | collective-permute-start | bytes 2752520 | tf_op jit(solution)/shard_map/ppermute | solution.py:881
  261.1 94.1 %all-gather.15.cloned.1.call-start = ((), (), s32[]{:S(2)}) async-start(), calls=%async_computation.9 | async-start | bytes 2621440 | tf_op jit(solution)/shard_map/all_gather | solution.py:1100
  261.3 39.8 %collective-permute-start.31 = (bf16[512,1664]{1,0:T(8,128)(2,1)}, bf16[512,1664]{1,0:T(8,128)(2,1)}, u32[]{:S(2)}, u32[]{:S(2)}) collective-permute-start(bf16[512,1664]{1,0:T(8,128)(2,1)} %collective-permute-done.13.refs_5_), channel_id=1, source_target_pairs={{0,16},{16,0},{1,17},{17,1},{2,18},{18,2},{3,19},{19,3},{4,20},{20... | collective-permute-start | bytes 5111816 | tf_op jit(solution)/shard_map/ppermute | solution.py:881
  261.9 22.5 %collective-permute-start.32 = (bf16[512,896]{1,0:T(8,128)(2,1)}, bf16[512,896]{1,0:T(8,128)(2,1)S(1)}, u32[]{:S(2)}, u32[]{:S(2)}) collective-permute-start(bf16[512,896]{1,0:T(8,128)(2,1)} %collective-permute-done.2.refs_10_), channel_id=1, source_target_pairs={{0,8},{4,12},{8,0},{12,4},{1,9},{5,13},{9,1},{13,5},{2,10},{6,14},... | collective-permute-start | bytes 2752520 | tf_op jit(solution)/shard_map/ppermute | solution.py:872
  268.2 42.9 %collective-permute-start.34 = (bf16[512,2048]{1,0:T(8,128)(2,1)}, bf16[512,2048]{1,0:T(8,128)(2,1)}, u32[]{:S(2)}, u32[]{:S(2)}) collective-permute-start(bf16[512,2048]{1,0:T(8,128)(2,1)} %bitcast.29.refs_3_.refs_2_), channel_id=1, source_target_pairs={{0,4},{4,0},{8,12},{12,8},{1,5},{5,1},{9,13},{13,9},{2,6},{6,2},{1... | collective-permute-start | bytes 6291464 | tf_op jit(solution)/shard_map/ppermute | solution.py:878
  310.9 121.1 %reduce-scatter.9.cloned.1.call-start = ((), (), s32[]{:S(2)}) async-start(), calls=%async_computation.11 | async-start | bytes 2621440 | tf_op jit(solution)/shard_map/reduce_scatter | solution.py:1124
  362.6 119.1 %reduce-scatter.7.cloned.1.call-start = ((), (), s32[]{:S(2)}) async-start(), calls=%async_computation.10 | async-start | bytes 2621440 | tf_op jit(solution)/shard_map/reduce_scatter | solution.py:1124
  402.0 27.8 %collective-permute-start.38 = (bf16[512,2048]{1,0:T(8,128)(2,1)}, bf16[512,2048]{1,0:T(8,128)(2,1)S(1)}, u32[]{:S(2)}, u32[]{:S(2)}) collective-permute-start(bf16[512,2048]{1,0:T(8,128)(2,1)} %get-tuple-element.223), channel_id=1, source_target_pairs={{0,4},{4,0},{8,12},{12,8},{1,5},{5,1},{9,13},{13,9},{2,6},{6,2},{1... | collective-permute-start | bytes 6291464 | tf_op jit(solution)/shard_map/ppermute | solution.py:878
  413.9 28.7 %collective-permute-start.40 = (bf16[384,896]{1,0:T(8,128)(2,1)}, bf16[384,896]{1,0:T(8,128)(2,1)}, u32[]{:S(2)}, u32[]{:S(2)}) collective-permute-start(bf16[384,896]{1,0:T(8,128)(2,1)} %slice.783), channel_id=1, source_target_pairs={{0,16},{16,0},{1,17},{17,1},{2,18},{18,2},{3,19},{19,3},{4,20},{20... | collective-permute-start | bytes 2064392 | tf_op jit(solution)/shard_map/ppermute | solution.py:881
  428.7 38.5 %collective-permute-start.42 = (bf16[640,896]{1,0:T(8,128)(2,1)S(1)}, bf16[640,896]{1,0:T(8,128)(2,1)S(1)}, u32[]{:S(2)}, u32[]{:S(2)}) collective-permute-start(bf16[640,896]{1,0:T(8,128)(2,1)S(1)} %slice.785), channel_id=1, source_target_pairs={{0,16},{16,0},{1,17},{17,1},{2,18},{18,2},{3,19},{19,3},{4,20},{20... | collective-permute-start | bytes 3440648 | tf_op jit(solution)/shard_map/ppermute | solution.py:881
  429.3 37.9 %collective-permute-start.43 = (bf16[640,768]{1,0:T(8,128)(2,1)}, bf16[640,768]{1,0:T(8,128)(2,1)S(1)}, u32[]{:S(2)}, u32[]{:S(2)}) collective-permute-start(bf16[640,768]{1,0:T(8,128)(2,1)} %slice.786), channel_id=1, source_target_pairs={{0,8},{4,12},{8,0},{12,4},{1,9},{5,13},{9,1},{13,5},{2,10},{6,14},... | collective-permute-start | bytes 2949128 | tf_op jit(solution)/shard_map/ppermute | solution.py:872
  432.0 103.7 %reduce-scatter.15.cloned.1.call-start = ((), (), s32[]{:S(2)}) async-start(), calls=%async_computation.14 | async-start | bytes 2293760 | tf_op jit(solution)/shard_map/reduce_scatter | solution.py:1229
  496.7 33.5 %collective-permute-start.47 = (bf16[640,896]{1,0:T(8,128)(2,1)}, bf16[640,896]{1,0:T(8,128)(2,1)}, u32[]{:S(2)}, u32[]{:S(2)}) collective-permute-start(bf16[640,896]{1,0:T(8,128)(2,1)} %slice.790), channel_id=1, source_target_pairs={{0,8},{4,12},{8,0},{12,4},{1,9},{5,13},{9,1},{13,5},{2,10},{6,14},... | collective-permute-start | bytes 3440648 | tf_op jit(solution)/shard_map/ppermute | solution.py:872
  497.4 92.6 %reduce-scatter.17.cloned.1.call-start = ((), (), s32[]{:S(2)}) async-start(), calls=%async_computation.15 | async-start | bytes 2293760 | tf_op jit(solution)/shard_map/reduce_scatter | solution.py:1229
  504.2 26.0 %collective-permute-start.48 = (bf16[256,1792]{1,0:T(8,128)(2,1)S(1)}, bf16[256,1792]{1,0:T(8,128)(2,1)S(1)}, u32[]{:S(2)}, u32[]{:S(2)}) collective-permute-start(bf16[256,1792]{1,0:T(8,128)(2,1)S(1)} %slice.791), channel_id=1, source_target_pairs={{0,16},{16,0},{1,17},{17,1},{2,18},{18,2},{3,19},{19,3},{4,20},{20... | collective-permute-start | bytes 2752520 | tf_op jit(solution)/shard_map/ppermute | solution.py:881
  552.0 192.3 %reduce-scatter.11.cloned.1.call-start = ((), (), s32[]{:S(2)}) async-start(), calls=%async_computation.12 | async-start | bytes 2621440 | tf_op jit(solution)/shard_map/reduce_scatter | solution.py:1367
  552.1 72.6 %collective-permute-start.50 = (bf16[512,2048]{1,0:T(8,128)(2,1)}, bf16[512,2048]{1,0:T(8,128)(2,1)}, u32[]{:S(2)}, u32[]{:S(2)}) collective-permute-start(bf16[512,2048]{1,0:T(8,128)(2,1)} %get-tuple-element.269), channel_id=1, source_target_pairs={{0,4},{4,0},{8,12},{12,8},{1,5},{5,1},{9,13},{13,9},{2,6},{6,2},{1... | collective-permute-start | bytes 6291464 | tf_op jit(solution)/shard_map/ppermute | solution.py:878
  552.6 21.9 %collective-permute-start.56 = (bf16[128,1792]{1,0:T(8,128)(2,1)S(1)}, bf16[128,1792]{1,0:T(8,128)(2,1)S(1)}, u32[]{:S(2)}, u32[]{:S(2)}) collective-permute-start(bf16[128,1792]{1,0:T(8,128)(2,1)S(1)} %get-tuple-element.420), channel_id=1, source_target_pairs={{0,16},{16,0},{1,17},{17,1},{2,18},{18,2},{3,19},{19,3},{4,20},{20... | collective-permute-start | bytes 1376264 | tf_op jit(solution)/shard_map/ppermute | solution.py:881
  593.9 150.4 %reduce-scatter.13.cloned.1.call-start = ((), (), s32[]{:S(2)}) async-start(), calls=%async_computation.13 | async-start | bytes 2621440 | tf_op jit(solution)/shard_map/reduce_scatter | solution.py:1367
  594.3 22.6 %collective-permute-start.60 = (bf16[320,768]{1,0:T(8,128)(2,1)S(1)}, bf16[320,768]{1,0:T(8,128)(2,1)}, u32[]{:S(2)}, u32[]{:S(2)}) collective-permute-start(bf16[320,768]{1,0:T(8,128)(2,1)S(1)} %slice.802), channel_id=1, source_target_pairs={{0,16},{16,0},{1,17},{17,1},{2,18},{18,2},{3,19},{19,3},{4,20},{20... | collective-permute-start | bytes 1474568 | tf_op jit(solution)/shard_map/ppermute | solution.py:881
  638.3 32.2 %collective-permute-start.67 = (bf16[256,1024]{1,0:T(8,128)(2,1)}, bf16[256,1024]{1,0:T(8,128)(2,1)}, u32[]{:S(2)}, u32[]{:S(2)}) collective-permute-start(bf16[256,1024]{1,0:T(8,128)(2,1)} %get-tuple-element.404), channel_id=1, source_target_pairs={{0,24},{4,28},{8,16},{12,20},{16,8},{20,12},{24,0},{28,4},{1,25},{... | collective-permute-start | bytes 1572872 | tf_op jit(solution)/shard_map/ppermute | solution.py:875
  638.9 31.9 %collective-permute-start.66 = (bf16[256,1024]{1,0:T(8,128)(2,1)}, bf16[256,1024]{1,0:T(8,128)(2,1)}, u32[]{:S(2)}, u32[]{:S(2)}) collective-permute-start(bf16[256,1024]{1,0:T(8,128)(2,1)} %get-tuple-element.405), channel_id=1, source_target_pairs={{0,16},{16,0},{1,17},{17,1},{2,18},{18,2},{3,19},{19,3},{4,20},{20... | collective-permute-start | bytes 1572872 | tf_op jit(solution)/shard_map/ppermute | solution.py:881
  640.3 30.5 %collective-permute-start.65 = (bf16[256,1024]{1,0:T(8,128)(2,1)}, bf16[256,1024]{1,0:T(8,128)(2,1)}, u32[]{:S(2)}, u32[]{:S(2)}) collective-permute-start(bf16[256,1024]{1,0:T(8,128)(2,1)} %get-tuple-element.406), channel_id=1, source_target_pairs={{0,8},{4,12},{8,0},{12,4},{1,9},{5,13},{9,1},{13,5},{2,10},{6,14},... | collective-permute-start | bytes 1572872 | tf_op jit(solution)/shard_map/ppermute | solution.py:872
  658.8 25.7 %collective-permute-start.71 = (bf16[256,1792]{1,0:T(8,128)(2,1)}, bf16[256,1792]{1,0:T(8,128)(2,1)}, u32[]{:S(2)}, u32[]{:S(2)}) collective-permute-start(bf16[256,1792]{1,0:T(8,128)(2,1)} %slice.820), channel_id=1, source_target_pairs={{0,16},{16,0},{1,17},{17,1},{2,18},{18,2},{3,19},{19,3},{4,20},{20... | collective-permute-start | bytes 2752520 | tf_op jit(solution)/shard_map/ppermute | solution.py:881
  659.0 78.2 %collective-permute-start.79 = (bf16[512,896]{1,0:T(8,128)(2,1)}, bf16[512,896]{1,0:T(8,128)(2,1)}, u32[]{:S(2)}, u32[]{:S(2)}) collective-permute-start(bf16[512,896]{1,0:T(8,128)(2,1)} %slice.828), channel_id=1, source_target_pairs={{0,16},{16,0},{1,17},{17,1},{2,18},{18,2},{3,19},{19,3},{4,20},{20... | collective-permute-start | bytes 2752520 | tf_op jit(solution)/shard_map/ppermute | solution.py:881
  670.6 23.6 %collective-permute-start.63 = (bf16[256,1792]{1,0:T(8,128)(2,1)}, bf16[256,1792]{1,0:T(8,128)(2,1)S(1)}, u32[]{:S(2)}, u32[]{:S(2)}) collective-permute-start(bf16[256,1792]{1,0:T(8,128)(2,1)} %slice.804), channel_id=1, source_target_pairs={{0,8},{4,12},{8,0},{12,4},{1,9},{5,13},{9,1},{13,5},{2,10},{6,14},... | collective-permute-start | bytes 2752520 | tf_op jit(solution)/shard_map/ppermute | solution.py:872
  686.1 51.1 %collective-permute-start.78 = (bf16[512,896]{1,0:T(8,128)(2,1)S(1)}, bf16[512,896]{1,0:T(8,128)(2,1)S(1)}, u32[]{:S(2)}, u32[]{:S(2)}) collective-permute-start(bf16[512,896]{1,0:T(8,128)(2,1)S(1)} %slice.827), channel_id=1, source_target_pairs={{0,8},{4,12},{8,0},{12,4},{1,9},{5,13},{9,1},{13,5},{2,10},{6,14},... | collective-permute-start | bytes 2752520 | tf_op jit(solution)/shard_map/ppermute | solution.py:872
  694.1 32.4 %collective-permute-start.76 = (bf16[256,448]{1,0:T(8,128)(2,1)S(1)}, bf16[256,448]{1,0:T(8,128)(2,1)S(1)}, u32[]{:S(2)}, u32[]{:S(2)}) collective-permute-start(bf16[256,448]{1,0:T(8,128)(2,1)S(1)} %get-tuple-element.431), channel_id=1, source_target_pairs={{0,2},{1,3},{2,0},{3,1},{4,6},{5,7},{6,4},{7,5},{8,10},{9,11},{10,... | collective-permute-start | bytes 688136 | tf_op jit(solution)/shard_map/ppermute | solution.py:888
  702.8 25.1 %collective-permute-start.74 = (bf16[64,1792]{1,0:T(8,128)(2,1)S(1)}, bf16[64,1792]{1,0:T(8,128)(2,1)S(1)}, u32[]{:S(2)}, u32[]{:S(2)}) collective-permute-start(bf16[64,1792]{1,0:T(8,128)(2,1)S(1)} %get-tuple-element.432), channel_id=1, source_target_pairs={{0,3},{1,2},{2,1},{3,0},{4,7},{5,6},{6,5},{7,4},{8,11},{9,10},{10,... | collective-permute-start | bytes 688136 | tf_op jit(solution)/shard_map/ppermute | solution.py:888
  710.0 24.6 %collective-permute-start.73 = (bf16[64,1792]{1,0:T(8,128)(2,1)S(1)}, bf16[64,1792]{1,0:T(8,128)(2,1)S(1)}, u32[]{:S(2)}, u32[]{:S(2)}) collective-permute-start(bf16[64,1792]{1,0:T(8,128)(2,1)S(1)} %get-tuple-element.433), channel_id=1, source_target_pairs={{0,2},{1,3},{2,0},{3,1},{4,6},{5,7},{6,4},{7,5},{8,10},{9,11},{10,... | collective-permute-start | bytes 688136 | tf_op jit(solution)/shard_map/ppermute | solution.py:888
  (123 other events, 1231.4 us)
Sparse Core Ops, SparseCore 0:
  10.5 55.4 all-gather.18
  68.2 79.6 all-gather.16
  150.1 39.9 all-gather.8
  219.6 39.5 all-gather.10
  261.2 44.7 all-gather.12
  311.0 44.1 all-gather.14
  362.7 42.4 reduce-scatter.8
  432.1 42.8 reduce-scatter.6
  497.5 38.0 reduce-scatter.14
  552.1 37.7 reduce-scatter.16
  594.1 42.1 reduce-scatter.10
  638.5 47.4 reduce-scatter.12
